TPU v7x, 32 devices: a whole 2x2x4 slice. The times are simulated.
32 devices in a mesh: groups: 2 (over y), dp: 4 (over z), tensor: 4 (over x, core).
Axes of the slice: x: 2, y: 2, z: 4, core: 2. Of those that a mesh axis runs over, the one named last changes fastest.
Arguments:
- prompt_kv: bfloat16 [2, 1024, 1024], P(None, ('groups', 'dp'), 'tensor'), parts along dimension 1, may hold values from -8 to 8
- resp_q: bfloat16 [8192, 5120], P(('groups', 'dp'), 'tensor'), parts along dimension 0, may hold values from -8 to 8
- resp_kv: bfloat16 [2, 8192, 1024], P(None, ('groups', 'dp'), 'tensor'), parts along dimension 1, may hold values from -6 to 6
- out_grad: bfloat16 [8192, 5120], P(('groups', 'dp'), 'tensor'), parts along dimension 0, may hold values from -6 to 6
- rewards: float32 [128], P(('groups', 'dp')), parts along dimension 0, may hold values from -12 to 12
- resp_prompt: int32 [128], P('groups'), parts along dimension 0, may hold values from 0 to 3, as said below
- resp_len: int32 [128], P(('groups', 'dp')), parts along dimension 0, may hold values from 16 to 64
Outputs:
- q_grad: bfloat16 [8192, 5120], P(('groups', 'dp'), 'tensor'), parts along dimension 0
- self_kv_grad: bfloat16 [2, 8192, 1024], P(None, ('groups', 'dp'), 'tensor'), parts along dimension 1
- prefix_kv_grad: bfloat16 [2, 1024, 1024], P(None, ('groups', 'dp'), 'tensor'), parts along dimension 1
There are 2 independent parts, one for each index of `groups`. A program takes and returns all parts, laid end to end along the dimension named above; each array names one. Nothing has to cross between parts.
Inputs may be any that keep to these rules, and one draw needn't show every extreme that they name: `resp_prompt`: responses r = i * 16 onward lie on index i of dp, and prompt p on index p of dp. Each prompt has exactly 16 responses, and one index of dp holds at most 4 responses of one prompt.
All inputs are finite; a program needn't handle non-finite values.
Results may differ from a plain program's by a relative error of at most 0.0081.
Values may be sent and summed in bfloat16 or wider, within the bound.
No kernel may reach another device: no remote copies, remote signals or barrier semaphores. Data moves between devices by JAX's collectives and lax.ppermute only.
A program may use at most 128 MiB of HBM per device.

v0:
```python
import math

import jax
import jax.numpy as jnp
from jax import lax
from jax.sharding import PartitionSpec as P

HD = 128


def local_attention(queries, all_keys, all_values, scaled, prompt_len):
    score_scale = 1.0 / math.sqrt(queries.shape[-1])
    scores = (
        jnp.einsum("rtkgd,rskd->rkgts", queries, all_keys, preferred_element_type=jnp.float32)
        * score_scale
    )
    row_pos = jnp.arange(scores.shape[3], dtype=jnp.int32)[:, None]
    col_pos = jnp.arange(scores.shape[4], dtype=jnp.int32)[None, :]
    allowed = (col_pos < prompt_len) | (col_pos - prompt_len <= row_pos)
    scores = jnp.where(allowed, scores, -1e30)
    row_max = jnp.max(scores, axis=-1, keepdims=True)
    exp_scores = jnp.exp(scores - row_max)
    weights = exp_scores / jnp.sum(exp_scores, axis=-1, keepdims=True)
    rounded = weights.astype(jnp.bfloat16)
    attended = jnp.einsum(
        "rkgts,rskd->rtkgd", rounded, all_values, preferred_element_type=jnp.float32
    )
    delta_rows = jnp.sum(scaled.astype(jnp.float32) * attended, axis=-1)
    delta_rows = jnp.transpose(delta_rows, (0, 2, 3, 1))[..., None]
    grad_weights = jnp.einsum(
        "rtkgd,rskd->rkgts", scaled, all_values, preferred_element_type=jnp.float32
    )
    grad_scores = (weights * (grad_weights - delta_rows) * score_scale).astype(jnp.bfloat16)
    query_grad = jnp.einsum(
        "rkgts,rskd->rtkgd", grad_scores, all_keys, preferred_element_type=jnp.float32
    ).astype(jnp.bfloat16)
    key_grad = jnp.einsum(
        "rkgts,rtkgd->rskd", grad_scores, queries, preferred_element_type=jnp.float32
    ).astype(jnp.bfloat16)
    value_grad = jnp.einsum(
        "rkgts,rtkgd->rskd", rounded, scaled, preferred_element_type=jnp.float32
    ).astype(jnp.bfloat16)
    return (query_grad, key_grad, value_grad)


def shards(prompt_kv, resp_q, resp_kv, out_grad, rewards, resp_prompt, resp_len):
    dp_size = lax.axis_size("dp")
    my_index = lax.axis_index("dp")
    resp_count = rewards.shape[0]
    resp_tokens = resp_q.shape[0] // resp_count
    prompt_len = prompt_kv.shape[1]
    kv_width = prompt_kv.shape[2]
    head_dim = HD
    kv_local = kv_width // head_dim
    group_size = resp_q.shape[1] // kv_width
    slots = (resp_count + dp_size - 1) // dp_size
    my_prompts = lax.dynamic_slice_in_dim(resp_prompt, my_index * resp_count, resp_count)
    owners = jnp.arange(dp_size, dtype=jnp.int32)
    member = (my_prompts[:, None] == owners[None, :]).astype(jnp.float32)
    partial_sums = jnp.sum(member * rewards[:, None], axis=0)
    totals = lax.psum(partial_sums, "dp")
    own_total = jnp.sum(member * totals[None, :], axis=1)
    advantage = rewards - own_total / resp_count
    positions = jnp.arange(resp_tokens, dtype=jnp.int32)
    valid_rows = (positions[None, :] < resp_len[:, None]).astype(jnp.float32)
    factor = advantage[:, None] * (resp_tokens / resp_len.astype(jnp.float32))[:, None] * valid_rows
    scaled = (
        out_grad.reshape(resp_count, resp_tokens, -1).astype(jnp.float32) * factor[:, :, None]
    ).astype(jnp.bfloat16)
    gathered = lax.all_gather(prompt_kv, "dp", axis=1, tiled=True)
    gathered = gathered.reshape(2, dp_size, prompt_len, kv_width)
    picked = jnp.take(gathered, my_prompts, axis=1)
    prefix = picked.reshape(2, resp_count, prompt_len, kv_local, head_dim)
    self_kv = resp_kv.reshape(2, resp_count, resp_tokens, kv_local, head_dim)
    joined = jnp.concatenate([prefix, self_kv], axis=2)
    queries = resp_q.reshape(resp_count, resp_tokens, kv_local, group_size, head_dim)
    scaled_heads = scaled.reshape(resp_count, resp_tokens, kv_local, group_size, head_dim)
    query_grad, key_grad, value_grad = local_attention(
        queries, joined[0], joined[1], scaled_heads, prompt_len
    )
    q_out = query_grad.reshape(resp_count * resp_tokens, -1)
    self_out = jnp.stack([key_grad[:, prompt_len:], value_grad[:, prompt_len:]], axis=0).reshape(
        2, resp_count * resp_tokens, kv_width
    )
    per_resp = jnp.stack([key_grad[:, :prompt_len], value_grad[:, :prompt_len]], axis=1).reshape(
        resp_count, -1
    )
    resp_ids = jnp.arange(resp_count, dtype=jnp.int32)
    earlier = (my_prompts[:, None] == my_prompts[None, :]) & (resp_ids[None, :] < resp_ids[:, None])
    slot_rank = jnp.sum(earlier.astype(jnp.int32), axis=1)
    target = my_prompts * slots + slot_rank
    route_onehot = (
        jnp.arange(dp_size * slots, dtype=jnp.int32)[:, None] == target[None, :]
    ).astype(jnp.bfloat16)
    outgoing_grads = jnp.dot(route_onehot, per_resp, preferred_element_type=jnp.float32).astype(
        jnp.bfloat16
    )
    outgoing_grads = outgoing_grads.reshape(dp_size * slots, 2, prompt_len, kv_width)
    incoming_grads = lax.all_to_all(outgoing_grads, "dp", split_axis=0, concat_axis=0, tiled=True)
    prefix_out = jnp.sum(incoming_grads, axis=0, dtype=jnp.float32).astype(jnp.bfloat16)
    return (q_out, self_out, prefix_out)


def solution(mesh):
    in_specs = (
        P(None, ("groups", "dp"), "tensor"),
        P(("groups", "dp"), "tensor"),
        P(None, ("groups", "dp"), "tensor"),
        P(("groups", "dp"), "tensor"),
        P(("groups", "dp")),
        P("groups"),
        P(("groups", "dp")),
    )
    out_specs = (
        P(("groups", "dp"), "tensor"),
        P(None, ("groups", "dp"), "tensor"),
        P(None, ("groups", "dp"), "tensor"),
    )
    return jax.shard_map(shards, mesh=mesh, in_specs=in_specs, out_specs=out_specs, check_vma=False)
```

profile of v0, /device:TPU:0, one launch (start us, length us, event | category | flops | bytes accessed | tf_op | source)
XLA Modules:
  0.0 166.9 jit_solution(10344005108902818908)
XLA Ops:
  2.3 13.5 %psum.7 = f32[4]{0:T(128)S(1)} all-reduce(f32[4]{0:T(128)S(1)} %select_reduce_fusion.1), channel_id=1, replica_groups=mesh['groups'=2,'dp'=4,'tensor'=4] {'dp'}, use_global_device_ids=true, to_apply=%region_3.4 | all-reduce | flops 4 | bytes 32 | tf_op jit(solution)/shard_map/psum | solution.py:61
  17.3 15.1 %all_gather.3 = bf16[2,512,256]{2,1,0:T(8,128)(2,1)S(1)} all-gather(bf16[2,128,256]{2,1,0:T(8,128)(2,1)} %param.7), channel_id=1, replica_groups=mesh['groups'=2,'dp'=4,'tensor'=4] {'dp'}, dimensions={1}, use_global_device_ids=true | all-gather | bytes 655360 | tf_op jit(solution)/shard_map/all_gather | solution.py:70
  32.4 1.3 reshape.98
  34.0 2.0 %gather_fusion = bf16[16,2,128,256]{3,2,1,0:T(8,128)(2,1)} fusion(bf16[2,4,128,256]{3,2,1,0:T(8,128)(2,1)S(1)} %bitcast.71, s32[1024]{0:T(1024)S(1)} %pad_clamp_fusion), kind=kCustom, calls=%fused_computation | custom fusion | bytes 4194368 | tf_op jit(solution)/shard_map/jit(_take)/gather | solution.py:72
  36.0 3.0 %copy.31 = bf16[2,16,128,256]{2,3,1,0:T(8,128)(2,1)S(1)} copy(bf16[2,16,128,256]{3,2,0,1:T(8,128)(2,1)} %bitcast.73) | data formatting | bytes 4194304 | tf_op jit(solution)/shard_map/jit(_take)/gather | solution.py:72
  39.0 2.6 %copy.32 = bf16[2,16,128,2,128]{4,2,3,1,0:T(8,128)(2,1)} copy(bf16[2,16,128,2,128]{2,4,3,1,0:T(8,128)(2,1)S(1)} %bitcast.75) | data formatting | bytes 4194304 | tf_op jit(solution)/shard_map/jit(_take)/gather | solution.py:72
  41.6 7.0 %reshape.99 = bf16[16,64,2,5,128]{4,3,2,1,0:T(8,128)(2,1)} reshape(bf16[1024,1280]{1,0:T(8,128)(2,1)} %param.8) | data formatting | bytes 5242880 | tf_op jit(solution)/shard_map/reshape | solution.py:76
  48.6 7.2 %reshape.103 = f32[16,64,2,5,128]{4,3,2,1,0:T(8,128)} reshape(bf16[1024,1280]{1,0:T(8,128)(2,1)} %param.10) | data formatting | bytes 7864320 | tf_op jit(solution)/shard_map/convert_element_type | solution.py:68
  55.8 1.9 %broadcast_select_fusion = bf16[2,16,128,2,128]{4,2,3,1,0:T(8,128)(2,1)S(1)} fusion(bf16[2,16,128,2,128]{4,2,3,1,0:T(8,128)(2,1)} %copy.32, pred[16]{0:T(512)(128)(4,1)S(1)} %get-tuple-element.3), kind=kLoop, calls=%fused_computation.25 | loop fusion | flops 1048576 | bytes 4194320 | tf_op jit(solution)/shard_map/jit(_take)/select_n | solution.py:72
  57.7 5.3 %fusion.6 = bf16[16,64,2,5,128]{4,1,3,2,0:T(8,128)(2,1)S(1)} fusion(f32[16,64,2,5,128]{4,3,2,1,0:T(8,128)} %reshape.103, f32[16,64]{1,0:T(8,128)S(1)} %fusion.24), kind=kLoop, calls=%fused_computation.13 | loop fusion | flops 2621440 | bytes 7868416 | tf_op jit(solution)/shard_map/convert_element_type | solution.py:69
  63.0 5.4 %fusion.15 = f32[16,2,192,64,5]{2,3,4,1,0:T(8,128)} fusion(bf16[16,64,2,5,128]{4,3,2,1,0:T(8,128)(2,1)S(1)} %copy-done, bf16[2,16,128,2,128]{4,2,3,1,0:T(8,128)(2,1)S(1)} %broadcast_select_fusion, bf16[2,16,64,2,128]{4,2,3,1,0:T(8,128)(2,1)S(1)} %copy.33), kind=kOutput, calls=%fused_computation.31 | convolution fusion | flops 506462208 | bytes 13631488 | tf_op jit(solution)/shard_map/rtkgd,rskd->rkgts/dot_general | solution.py:14
  68.4 14.7 %fusion.33 = (f32[16,2,5,64]{3,2,1,0:T(8,128)S(1)}, f32[16,2,5,64,192]{4,3,2,1,0:T(8,128)}) fusion(f32[16,2,192,64,5]{2,3,4,1,0:T(8,128)} %fusion.15, pred[64,192]{1,0:T(8,128)(4,1)S(1)} %fusion.23), kind=kOutput, calls=%fused_computation.61 | output fusion | flops 11796671 | bytes 15781888 | tf_op jit(solution)/shard_map/sub | solution.py:22
  83.0 5.3 %fusion.10 = bf16[16,2,5,64,192]{4,3,2,1,0:T(8,128)(2,1)S(1)} fusion(f32[16,2,5,64,192]{4,3,2,1,0:T(8,128)} %get-tuple-element.8, f32[16,2,5,64]{3,2,1,0:T(8,128)S(1)} %get-tuple-element.7), kind=kLoop, calls=%fused_computation.18 | loop fusion | flops 3932160 | bytes 11837440 | tf_op jit(solution)/shard_map/convert_element_type | solution.py:24
  88.4 1.7 %fusion.5 = f32[16,64,2,5]{1,3,2,0:T(8,128)S(1)} fusion(bf16[16,64,2,5,128]{4,1,3,2,0:T(8,128)(2,1)S(1)} %fusion.6, bf16[16,2,5,64,192]{4,3,2,1,0:T(8,128)(2,1)S(1)} %fusion.10, bf16[2,16,64,2,128]{4,2,3,1,0:T(8,128)(2,1)S(1)} %copy.33, bf16[2,16,128,2,128]{4,2,3,1,0:T(8,128)(2,1)S(1)} %broadcast_select_fusion), kind=kOutput, calls=%fused_computation.11 | convolution fusion | flops 510384128 | bytes 9740288 | tf_op jit(solution)/shard_map/rkgts,rskd->rtkgd/dot_general | solution.py:25
  90.1 1.8 %fusion.20 = bf16[16,192,2,128]{3,1,2,0:T(8,128)(2,1)S(1)} fusion(bf16[16,64,2,5,128]{4,1,3,2,0:T(8,128)(2,1)S(1)} %fusion.6, bf16[16,2,5,64,192]{4,3,2,1,0:T(8,128)(2,1)S(1)} %fusion.10), kind=kOutput, calls=%fused_computation.34 | convolution fusion | flops 504102912 | bytes 8126464 | tf_op jit(solution)/shard_map/rkgts,rtkgd->rskd/dot_general | solution.py:40
  91.9 8.6 %fusion.3 = bf16[16,2,5,64,192]{4,3,2,1,0:T(8,128)(2,1)S(1)} fusion(f32[16,2,5,64]{3,2,1,0:T(8,128)S(1)} %bitcast.76, f32[16,2,5,64,192]{4,3,2,1,0:T(8,128)} %get-tuple-element.8, f32[16,2,5,64]{3,2,1,0:T(8,128)S(1)} %get-tuple-element.7, bf16[16,64,2,5,128]{4,1,3,2,0:T(8,128)(2,1)S(1)} %fusion.6, bf16[2,16,64,2,128]{4,2,3,1,0:T(8,128)(2,1)S(1)} %copy.33, ...), kind=kOutput, calls=%fused_computation.6 | convolution fusion | flops 516292608 | bytes 17645568 | tf_op jit(solution)/shard_map/rtkgd,rskd->rkgts/dot_general | solution.py:30
  100.5 2.0 %fusion.17 = bf16[16,192,2,128]{3,1,2,0:T(8,128)(2,1)S(1)} fusion(bf16[16,2,5,64,192]{4,3,2,1,0:T(8,128)(2,1)S(1)} %fusion.3, bf16[16,64,2,5,128]{4,3,2,1,0:T(8,128)(2,1)S(1)} %copy-done.1), kind=kOutput, calls=%fused_computation.33 | convolution fusion | flops 504102912 | bytes 8126464 | tf_op jit(solution)/shard_map/rkgts,rtkgd->rskd/dot_general | solution.py:37
  104.0 3.5 %copy.40 = bf16[16,2,128,2,128]{4,3,2,1,0:T(2,128)(2,1)} copy(bf16[16,2,128,2,128]{4,2,3,0,1:T(8,128)(2,1)S(1)} %pad_maximum_fusion) | data formatting | bytes 4194304 | tf_op jit(solution)/shard_map/stack | solution.py:85
  107.5 3.9 %reshape.101 = bf16[16,65536]{1,0:T(8,128)(2,1)} reshape(bf16[16,2,128,2,128]{4,3,2,1,0:T(2,128)(2,1)} %copy.40) | data formatting | bytes 4194304 | tf_op jit(solution)/shard_map/reshape | solution.py:85
  111.4 2.3 %convolution_convert_fusion = bf16[16,65536]{1,0:T(8,128)(2,1)S(1)} fusion(bf16[16,65536]{1,0:T(8,128)(2,1)} %reshape.101, s32[16]{0:T(128)S(1)} %get-tuple-element.5), kind=kOutput, calls=%fused_computation.2 | convolution fusion | flops 34603264 | bytes 4194368 | tf_op jit(solution)/shard_map/dot_general | solution.py:95
  113.6 1.9 %copy.45 = bf16[2,8,256,256]{3,2,1,0:T(8,128)(2,1)} copy(bf16[2,8,256,256]{3,1,2,0:T(8,128)(2,1)S(1)} %bitcast.74) | data formatting | bytes 4194304
  115.5 4.7 %all-to-all-start = ((bf16[16,2,128,256]{3,2,1,0:T(8,128)(2,1)}), bf16[16,2,128,256]{3,2,1,0:T(8,128)(2,1)}, u32[]{:S(2)}, u32[]{:S(2)}) async-start(bf16[16,2,128,256]{3,2,1,0:T(8,128)(2,1)} %bitcast.72), calls=%async_computation | async-start | bytes 4194304 | tf_op jit(solution)/shard_map/all_to_all | solution.py:99
  121.3 1.9 %slice.29 = bf16[16,64,2,128]{3,1,2,0:T(8,128)(2,1)} slice(bf16[16,192,2,128]{3,1,2,0:T(8,128)(2,1)} %copy-done.2), slice={[0:16], [128:192], [0:2], [0:128]} | slice | bytes 1048576 | tf_op jit(solution)/shard_map/slice | solution.py:82
  123.2 1.3 copy.38
  124.5 2.2 %stack.18 = bf16[1,1024,256]{2,1,0:T(8,128)(2,1)} reshape(bf16[16,64,2,128]{3,2,1,0:T(2,128)(2,1)} %copy.38) | data formatting | bytes 1048576 | tf_op jit(solution)/shard_map/stack | solution.py:82
  126.7 2.4 %copy.39 = bf16[16,64,2,128]{3,2,1,0:T(2,128)(2,1)} copy(bf16[16,64,2,128]{3,1,2,0:T(8,128)(2,1)} %slice.29) | data formatting | bytes 1048576 | tf_op jit(solution)/shard_map/slice | solution.py:82
  129.0 2.2 %stack.19 = bf16[1,1024,256]{2,1,0:T(8,128)(2,1)} reshape(bf16[16,64,2,128]{3,2,1,0:T(2,128)(2,1)} %copy.39) | data formatting | bytes 1048576 | tf_op jit(solution)/shard_map/stack | solution.py:82
  131.2 4.0 %convert_bitcast_fusion = bf16[16,64,2,5,128]{4,1,3,2,0:T(8,128)(2,1)S(1)} fusion(bf16[16,2,5,64,192]{4,3,2,1,0:T(8,128)(2,1)} %copy-done.3, bf16[2,16,128,2,128]{4,2,3,1,0:T(8,128)(2,1)S(1)} %broadcast_select_fusion, bf16[2,16,64,2,128]{4,2,3,1,0:T(8,128)(2,1)S(1)} %copy.33), kind=kOutput, calls=%fused_computation.23 | convolution fusion | flops 507772928 | bytes 9699328 | tf_op jit(solution)/shard_map/rkgts,rskd->rtkgd/dot_general | solution.py:34
  135.2 4.0 %copy.36 = bf16[16,64,2,5,128]{4,3,2,1,0:T(8,128)(2,1)} copy(bf16[16,64,2,5,128]{4,1,3,2,0:T(8,128)(2,1)S(1)} %convert_bitcast_fusion) | data formatting | bytes 5242880 | tf_op jit(solution)/shard_map/convert_element_type | solution.py:36
  139.2 7.1 %reshape.100 = bf16[1024,1280]{1,0:T(8,128)(2,1)} reshape(bf16[16,64,2,5,128]{4,3,2,1,0:T(8,128)(2,1)} %copy.36) | data formatting | bytes 5242880 | tf_op jit(solution)/shard_map/reshape | solution.py:81
  147.4 16.9 %all-to-all-done = bf16[16,2,128,256]{3,2,1,0:T(8,128)(2,1)} async-done(((bf16[16,2,128,256]{3,2,1,0:T(8,128)(2,1)}), bf16[16,2,128,256]{3,2,1,0:T(8,128)(2,1)}, u32[]{:S(2)}, u32[]{:S(2)}) %all-to-all-start) | async-done | bytes 2097184 | tf_op jit(solution)/shard_map/all_to_all | solution.py:99
  164.4 2.6 %reduce_sum.62 = bf16[2,128,256]{2,1,0:T(8,128)(2,1)} reduce(bf16[16,2,128,256]{3,2,1,0:T(8,128)(2,1)} %all-to-all-done, bf16[]{:T(256)} %constant.48.clone.1), dimensions={0}, to_apply=%region_7.8 | reduce | flops 983040 | bytes 2228226 | tf_op jit(solution)/shard_map/reduce_sum | solution.py:100
  (30 shorter events, 7.2 us)
Async XLA Ops:
  57.7 5.3 %copy-start = (bf16[16,64,2,5,128]{4,3,2,1,0:T(8,128)(2,1)S(1)}, bf16[16,64,2,5,128]{4,3,2,1,0:T(8,128)(2,1)}, u32[]{:S(2)}) copy-start(bf16[16,64,2,5,128]{4,3,2,1,0:T(8,128)(2,1)} %reshape.99) | copy-start | bytes 7864324
  91.8 10.6 %copy-start.2 = (bf16[16,192,2,128]{3,1,2,0:T(8,128)(2,1)}, bf16[16,192,2,128]{3,1,2,0:T(8,128)(2,1)S(1)}, u32[]{:S(2)}) copy-start(bf16[16,192,2,128]{3,1,2,0:T(8,128)(2,1)S(1)} %fusion.20) | copy-start | bytes 4718596
  91.9 8.6 %copy-start.1 = (bf16[16,64,2,5,128]{4,3,2,1,0:T(8,128)(2,1)S(1)}, bf16[16,64,2,5,128]{4,3,2,1,0:T(8,128)(2,1)}, u32[]{:S(2)}) copy-start(bf16[16,64,2,5,128]{4,3,2,1,0:T(8,128)(2,1)} %reshape.99) | copy-start | bytes 7864324
  100.5 2.3 %copy-start.3 = (bf16[16,2,5,64,192]{4,3,2,1,0:T(8,128)(2,1)}, bf16[16,2,5,64,192]{4,3,2,1,0:T(8,128)(2,1)S(1)}, u32[]{:S(2)}) copy-start(bf16[16,2,5,64,192]{4,3,2,1,0:T(8,128)(2,1)S(1)} %fusion.3) | copy-start | bytes 11796484
  102.8 1.2 copy-start.6
  115.5 48.9 %all-to-all-start = ((bf16[16,2,128,256]{3,2,1,0:T(8,128)(2,1)}), bf16[16,2,128,256]{3,2,1,0:T(8,128)(2,1)}, u32[]{:S(2)}, u32[]{:S(2)}) async-start(bf16[16,2,128,256]{3,2,1,0:T(8,128)(2,1)} %bitcast.72), calls=%async_computation | async-start | bytes 4194304 | tf_op jit(solution)/shard_map/all_to_all | solution.py:99
  139.2 7.1 %copy-start.4 = (bf16[1,1024,256]{2,1,0:T(8,128)(2,1)S(1)}, bf16[1,1024,256]{2,1,0:T(8,128)(2,1)}, u32[]{:S(2)}) copy-start(bf16[1,1024,256]{2,1,0:T(8,128)(2,1)} %stack.18) | copy-start | bytes 1572868
  139.2 7.1 %copy-start.5 = (bf16[1,1024,256]{2,1,0:T(8,128)(2,1)S(1)}, bf16[1,1024,256]{2,1,0:T(8,128)(2,1)}, u32[]{:S(2)}) copy-start(bf16[1,1024,256]{2,1,0:T(8,128)(2,1)} %stack.19) | copy-start | bytes 1572868
where the time goes:
time: 168 us; the launch traced here: 167 us
  local copies, waits for them, and re-layouts  56.2 us (33%)
  other arithmetic  34.2 us (20%)
  blocking collectives  28.5 us (17%)
  matrix products  25.7 us (15%)
  waiting for transfers between devices  16.9 us (10%)
  starting transfers between devices  4.68 us (3%)
    all_to_all x1, waiting for transfers between devices, shards(): lax.all_to_all(outgoing_grads, 'dp', split_axis=0, concat_axis=0, tiled=T...  16.9 us
    all_gather x1, blocking collectives, shards(): gathered = lax.all_gather(prompt_kv, 'dp', axis=1, tiled=True)  15.1 us
    sub x1, other arithmetic, local_attention(): exp_scores = jnp.exp(scores - row_max)  14.7 us
    psum x1, blocking collectives, shards(): totals = lax.psum(partial_sums, 'dp')  13.5 us
    dot_general x1, matrix products, local_attention(): jnp.einsum('rtkgd,rskd->rkgts', scaled, all_values, preferred_element_typ...  8.58 us
    gather x3, local copies, waits for them, and re-layouts, shards(): picked = jnp.take(gathered, my_prompts, axis=1)  7.63 us
    convert_element_type x1, local copies, waits for them, and re-layouts, shards(): out_grad.reshape(resp_count, resp_tokens, -1).astype(jnp.float32)  7.17 us
    reshape x1, local copies, waits for them, and re-layouts, shards(): q_out = query_grad.reshape(resp_count * resp_tokens, -1)  7.12 us
  transfers between devices with their start and end apart: 1, of which 1 were waited for; matrix products, arithmetic and copies ran while one was open for 16% of the time, Pallas kernels for 0%

commit v1 on v0

v1 whole, which is shorter than its diff:
```python
import functools
import math

import jax
import jax.numpy as jnp
from jax import lax
from jax.experimental import pallas as pl
from jax.experimental.pallas import tpu as pltpu
from jax.sharding import PartitionSpec as P

HD = 128
NEG = -1e30
F32 = jnp.float32
BF16 = jnp.bfloat16


def dot(a, b, dims):
    return lax.dot_general(a, b, (dims, ((), ())), preferred_element_type=F32)


NN = ((1,), (0,))
NT = ((1,), (1,))
TN = ((0,), (0,))


def softmax_grads(scores_p, scores_s, gw_p, gw_s, factor, mask, scale):
    c = scale * math.log2(math.e)
    scores_s = jnp.where(mask, scores_s, NEG)
    top = jnp.maximum(
        jnp.max(scores_p, axis=0, keepdims=True), jnp.max(scores_s, axis=0, keepdims=True)
    )
    e_p = jnp.exp2((scores_p - top) * c)
    e_s = jnp.exp2((scores_s - top) * c)
    total = jnp.sum(e_p, axis=0, keepdims=True) + jnp.sum(e_s, axis=0, keepdims=True)
    weighted = jnp.sum(e_p * gw_p, axis=0, keepdims=True) + jnp.sum(
        e_s * gw_s, axis=0, keepdims=True
    )
    inverse = 1.0 / total
    delta = weighted * inverse
    gain = inverse * factor
    w_p, w_s = e_p * gain, e_s * gain
    return (
        w_p.astype(BF16),
        w_s.astype(BF16),
        (w_p * (gw_p - delta)).astype(BF16),
        (w_s * (gw_s - delta)).astype(BF16),
    )


def lane_masks(tokens, lanes):
    lane = lax.broadcasted_iota(jnp.int32, (1, lanes), 1)
    return lane, lax.rem(lane, tokens)


def causal(tokens, lanes):
    key = lax.broadcasted_iota(jnp.int32, (tokens, lanes), 0)
    lane = lax.broadcasted_iota(jnp.int32, (tokens, lanes), 1)
    return key <= lax.rem(lane, tokens)


def attend_group(slots, base, group_size, kv_heads, tokens, prefix_len, q, og, kv, prefix, lens, factors, out, self_out, prefix_out):
    scale = 1.0 / math.sqrt(HD)
    whole = group_size - group_size % 2
    wide = whole * tokens
    pairs = [(j, j + 1) if j + 1 < slots else (j, None) for j in range(0, slots, 2)]

    def head(k, h):
        at = (k * group_size + h) * HD
        return slice(at, at + HD)

    def rows(ref, k, blocks):
        return jnp.concatenate([ref[base + j, :, head(k, h)] for j, h in blocks], axis=0)

    def row_factor(j, lanes):
        _, t = lane_masks(tokens, lanes)
        return jnp.where(t < lens[j], factors[j], 0.0)

    for k in range(kv_heads):
        cols = slice(k * HD, (k + 1) * HD)
        key_p, value_p = prefix[0, :, cols], prefix[1, :, cols]
        key_pt = key_p.T
        key_acc = jnp.zeros((prefix_len, HD), F32)
        value_acc = jnp.zeros((prefix_len, HD), F32)
        for pair in pairs:
            members = [j for j in pair if j is not None]
            key_s = {j: kv[base + j, 0, :, cols] for j in members}
            value_s = {j: kv[base + j, 1, :, cols] for j in members}
            second = members[-1]
            key_pair = jnp.concatenate([key_s[pair[0]], key_s[second]], axis=0)
            value_pair = jnp.concatenate([value_s[pair[0]], value_s[second]], axis=0)
            key_t = jnp.concatenate([key_pt, key_pair.T], axis=1)
            key_self = {}
            value_self = {}
            empty = jnp.zeros((tokens, wide), BF16)
            for place, j in enumerate(members):
                blocks = [(j, h) for h in range(whole)]
                q_rows, g_rows = rows(q, k, blocks), rows(og, k, blocks)
                scores = dot(jnp.concatenate([key_p, key_s[j]], axis=0), q_rows, NT)
                gw = dot(jnp.concatenate([value_p, value_s[j]], axis=0), g_rows, NT)
                w_p, w_s, d_p, d_s = softmax_grads(
                    scores[:prefix_len],
                    scores[prefix_len:],
                    gw[:prefix_len],
                    gw[prefix_len:],
                    row_factor(j, wide),
                    causal(tokens, wide),
                    scale,
                )
                d_wide = jnp.concatenate(
                    [d_p, d_s, empty] if place == 0 else [d_p, empty, d_s], axis=0
                )
                q_grad = (dot(key_t, d_wide, NN) * scale).astype(BF16).T
                for n, (_, h) in enumerate(blocks):
                    out[base + j, :, head(k, h)] = q_grad[n * tokens : (n + 1) * tokens]
                kg = dot(jnp.concatenate([d_p, d_s], axis=0), q_rows, NN)
                vg = dot(jnp.concatenate([w_p, w_s], axis=0), g_rows, NN)
                key_acc += kg[:prefix_len]
                value_acc += vg[:prefix_len]
                key_self[j] = kg[prefix_len:]
                value_self[j] = vg[prefix_len:]
            if group_size % 2:
                blocks = [(pair[0], group_size - 1), (second, group_size - 1)]
                q_rows, g_rows = rows(q, k, blocks), rows(og, k, blocks)
                lanes = 2 * tokens
                lane, t = lane_masks(tokens, lanes)
                left = lane < tokens
                length = jnp.where(left, lens[pair[0]], lens[second] if len(members) > 1 else 0)
                gain = jnp.where(left, factors[pair[0]], factors[second])
                factor = jnp.where(t < length, gain, 0.0)
                scores = dot(jnp.concatenate([key_p, key_pair], axis=0), q_rows, NT)
                gw = dot(jnp.concatenate([value_p, value_pair], axis=0), g_rows, NT)

                def own(both):
                    return jnp.where(left, both[:tokens], both[tokens:])

                w_p, w_s, d_p, d_s = softmax_grads(
                    scores[:prefix_len],
                    own(scores[prefix_len:]),
                    gw[:prefix_len],
                    own(gw[prefix_len:]),
                    factor,
                    causal(tokens, lanes),
                    scale,
                )

                def spread(part):
                    none = jnp.zeros_like(part)
                    return jnp.concatenate(
                        [jnp.where(left, part, none), jnp.where(left, none, part)], axis=0
                    )

                d_all = jnp.concatenate([d_p, spread(d_s)], axis=0)
                w_all = jnp.concatenate([w_p, spread(w_s)], axis=0)
                q_grad = (dot(key_t, d_all, NN) * scale).astype(BF16).T
                for n, j in enumerate(members):
                    out[base + j, :, head(k, group_size - 1)] = q_grad[n * tokens : (n + 1) * tokens]
                kg = dot(d_all, q_rows, NN)
                vg = dot(w_all, g_rows, NN)
                key_acc += kg[:prefix_len]
                value_acc += vg[:prefix_len]
                for n, j in enumerate(members):
                    at = prefix_len + n * tokens
                    key_self[j] += kg[at : at + tokens]
                    value_self[j] += vg[at : at + tokens]
            for j in members:
                self_out[base + j, 0, :, cols] = (key_self[j] * scale).astype(BF16)
                self_out[base + j, 1, :, cols] = value_self[j].astype(BF16)
        prefix_out[0, :, cols] = (key_acc * scale).astype(BF16)
        prefix_out[1, :, cols] = value_acc.astype(BF16)


def attention_kernel(dims, *refs):
    n_dp, count, slots, kv_heads, group_size, tokens, prefix_len, near = dims
    groups = count // slots
    n_prompts = n_dp if near else 1
    refs = list(refs)
    resp_prompt, resp_len = refs[:2]
    rewards = refs[2 : 2 + n_prompts]
    q_hbm, og_hbm, kv_hbm = refs[2 + n_prompts : 5 + n_prompts]
    prompts = refs[5 + n_prompts : 5 + 2 * n_prompts]
    q_out, self_out = refs[5 + 2 * n_prompts : 7 + 2 * n_prompts]
    n_out = groups if near else 1
    prefix_outs = refs[7 + 2 * n_prompts : 7 + 2 * n_prompts + n_out]
    (order, seen, totals, lens, factors, q, og, kv, prefix, out, own, grads, sem_in, sem_prefix, sem_out, sem_grads) = refs[
        7 + 2 * n_prompts + n_out :
    ]
    me = lax.axis_index("dp")
    width = kv_heads * HD

    for p in range(n_dp):
        seen[p] = 0
        totals[p] = 0.0

    def place(i, _):
        prompt = resp_prompt[me * count + i]
        if near:
            turn = lax.rem(prompt - me + n_dp, n_dp)
            order[turn * slots + seen[turn]] = i
            seen[turn] = seen[turn] + 1
        else:
            order[i] = i
        return 0

    lax.fori_loop(0, count, place, 0)

    def at_rows(slot):
        return pl.ds(pl.multiple_of(order[slot] * tokens, tokens), tokens)

    def copies_in(slot):
        rows = at_rows(slot)
        return (
            pltpu.make_async_copy(q_hbm.at[rows], q.at[slot], sem_in.at[slot, 0]),
            pltpu.make_async_copy(og_hbm.at[rows], og.at[slot], sem_in.at[slot, 1]),
            pltpu.make_async_copy(kv_hbm.at[0, rows], kv.at[slot, 0], sem_in.at[slot, 2]),
            pltpu.make_async_copy(kv_hbm.at[1, rows], kv.at[slot, 1], sem_in.at[slot, 3]),
        )

    def prefix_copy(g):
        if near:
            return pltpu.make_async_copy(prompts[g], prefix.at[g], sem_prefix.at[g])
        prompt = resp_prompt[me * count + g]
        return pltpu.make_async_copy(prompts[0].at[prompt], prefix.at[g], sem_prefix.at[g])

    def copies_out(slot):
        rows = at_rows(slot)
        return (
            pltpu.make_async_copy(out.at[slot], q_out.at[rows], sem_out.at[slot, 0]),
            pltpu.make_async_copy(own.at[slot, 0], self_out.at[0, rows], sem_out.at[slot, 1]),
            pltpu.make_async_copy(own.at[slot, 1], self_out.at[1, rows], sem_out.at[slot, 2]),
        )

    def grads_copy(g):
        target = prefix_outs[g] if near else prefix_outs[0].at[g]
        return pltpu.make_async_copy(grads.at[g], target, sem_grads.at[g])

    for g in range(groups):
        prefix_copy(g).start()

        def start(n, _):
            for copy in copies_in(g * slots + n):
                copy.start()
            return 0

        lax.fori_loop(0, slots, start, 0)

    if near:
        for s in range(n_dp):
            source = lax.rem(me + s, n_dp)

            def add(i, _):
                prompt = resp_prompt[source * count + i]
                totals[prompt] = totals[prompt] + rewards[s][i]
                return 0

            lax.fori_loop(0, count, add, 0)
    else:

        def add_one(i, _):
            prompt = resp_prompt[i]
            totals[prompt] = totals[prompt] + rewards[0][i]
            return 0

        lax.fori_loop(0, n_dp * count, add_one, 0)

    own_rewards = rewards[0]

    def find_factor(slot, _):
        i = order[slot]
        length = resp_len[i]
        reward = own_rewards[i] if near else own_rewards[me * count + i]
        advantage = reward - totals[resp_prompt[me * count + i]] / count
        lens[slot] = length
        factors[slot] = advantage * (tokens / length.astype(F32))
        return 0

    lax.fori_loop(0, count, find_factor, 0)

    def one_group(g, _):
        base = g * slots

        def wait(n, _):
            for copy in copies_in(base + n):
                copy.wait()
            return 0

        lax.fori_loop(0, slots, wait, 0)
        attend_group(
            slots, base, group_size, kv_heads, tokens, prefix_len, q, og, kv, prefix.at[g],
            [lens[base + j] for j in range(slots)], [factors[base + j] for j in range(slots)],
            out, own, grads.at[g],
        )

        def send(n, _):
            for copy in copies_out(base + n):
                copy.start()
            return 0

        lax.fori_loop(0, slots, send, 0)
        return 0

    for g in range(groups):
        prefix_copy(g).wait()
    lax.fori_loop(0, groups, one_group, 0)
    for g in range(groups):
        grads_copy(g).start()

    def finish(slot, _):
        for copy in copies_out(slot):
            copy.wait()
        return 0

    lax.fori_loop(0, count, finish, 0)
    for g in range(groups):
        grads_copy(g).wait()


def shards(prompt_kv, resp_q, resp_kv, out_grad, rewards, resp_prompt, resp_len):
    n_dp = lax.axis_size("dp")
    count = rewards.shape[0]
    tokens = resp_q.shape[0] // count
    prefix_len, width = prompt_kv.shape[1:]
    kv_heads = width // HD
    group_size = resp_q.shape[1] // width
    slots = (count + n_dp - 1) // n_dp
    groups = count // slots
    near = groups == n_dp

    if near:
        def from_ahead(x, s):
            return lax.ppermute(x, "dp", [((i + s) % n_dp, i) for i in range(n_dp)])

        reward_parts = [rewards] + [from_ahead(rewards, s) for s in range(1, n_dp)]
        prompt_parts = [prompt_kv] + [from_ahead(prompt_kv, s) for s in range(1, n_dp)]
        prefix_shapes = [jax.ShapeDtypeStruct(prompt_kv.shape, BF16)] * groups
    else:
        reward_parts = [lax.all_gather(rewards, "dp", axis=0, tiled=True)]
        prompt_parts = [lax.all_gather(prompt_kv, "dp", axis=0)]
        prefix_shapes = [jax.ShapeDtypeStruct((groups,) + prompt_kv.shape, BF16)]

    dims = (n_dp, count, slots, kv_heads, group_size, tokens, prefix_len, near)
    smem = pl.BlockSpec(memory_space=pltpu.SMEM)
    anywhere = pl.BlockSpec(memory_space=pl.ANY)
    results = pl.pallas_call(
        functools.partial(attention_kernel, dims),
        out_shape=[
            jax.ShapeDtypeStruct(resp_q.shape, BF16),
            jax.ShapeDtypeStruct(resp_kv.shape, BF16),
        ]
        + prefix_shapes,
        in_specs=[smem] * (2 + len(reward_parts)) + [anywhere] * (3 + len(prompt_parts)),
        out_specs=[anywhere] * (2 + len(prefix_shapes)),
        scratch_shapes=[
            pltpu.SMEM((count,), jnp.int32),
            pltpu.SMEM((n_dp,), jnp.int32),
            pltpu.SMEM((n_dp,), F32),
            pltpu.SMEM((count,), jnp.int32),
            pltpu.SMEM((count,), F32),
            pltpu.VMEM((count, tokens, resp_q.shape[1]), BF16),
            pltpu.VMEM((count, tokens, resp_q.shape[1]), BF16),
            pltpu.VMEM((count, 2, tokens, width), BF16),
            pltpu.VMEM((groups, 2, prefix_len, width), BF16),
            pltpu.VMEM((count, tokens, resp_q.shape[1]), BF16),
            pltpu.VMEM((count, 2, tokens, width), BF16),
            pltpu.VMEM((groups, 2, prefix_len, width), BF16),
            pltpu.SemaphoreType.DMA((count, 4)),
            pltpu.SemaphoreType.DMA((groups,)),
            pltpu.SemaphoreType.DMA((count, 3)),
            pltpu.SemaphoreType.DMA((groups,)),
        ],
        compiler_params=pltpu.CompilerParams(vmem_limit_bytes=48 * 1024 * 1024),
        cost_estimate=pl.CostEstimate(
            flops=2 * 5 * count * tokens * group_size * kv_heads * (prefix_len + tokens) * HD,
            bytes_accessed=2 * (3 * resp_q.size + 2 * resp_kv.size),
            transcendentals=0,
        ),
        name="attention_grads",
    )(resp_prompt, resp_len, *reward_parts, resp_q, out_grad, resp_kv, *prompt_parts)
    q_out, self_out = results[:2]

    if near:
        arrived = [results[2]] + [
            lax.ppermute(results[2 + s], "dp", [(i, (i + s) % n_dp) for i in range(n_dp)])
            for s in range(1, n_dp)
        ]
        prefix_out = sum(part.astype(F32) for part in arrived).astype(BF16)
    else:
        mine = lax.dynamic_slice_in_dim(resp_prompt, lax.axis_index("dp") * count, count)
        route = (jnp.arange(n_dp, dtype=jnp.int32)[:, None] == mine[None, :]).astype(BF16)
        outgoing = jnp.dot(
            route, results[2].reshape(groups, -1), preferred_element_type=F32
        ).astype(BF16)
        outgoing = outgoing.reshape((n_dp,) + prompt_kv.shape)
        incoming = lax.all_to_all(outgoing, "dp", split_axis=0, concat_axis=0, tiled=True)
        prefix_out = jnp.sum(incoming, axis=0, dtype=F32).astype(BF16)
    return (q_out, self_out, prefix_out)


def solution(mesh):
    in_specs = (
        P(None, ("groups", "dp"), "tensor"),
        P(("groups", "dp"), "tensor"),
        P(None, ("groups", "dp"), "tensor"),
        P(("groups", "dp"), "tensor"),
        P(("groups", "dp")),
        P("groups"),
        P(("groups", "dp")),
    )
    out_specs = (
        P(("groups", "dp"), "tensor"),
        P(None, ("groups", "dp"), "tensor"),
        P(None, ("groups", "dp"), "tensor"),
    )
    return jax.shard_map(shards, mesh=mesh, in_specs=in_specs, out_specs=out_specs, check_vma=False)
```

time: 168 us -> 65.8 us (0.39)
  local copies, waits for them, and re-layouts: 56.2 us -> 5.83 us
  other arithmetic: 34.2 us -> 0.73 us
  blocking collectives: 28.5 us -> 0 us
  matrix products: 25.7 us -> 0 us
  Pallas kernels: 0 us -> 24.9 us
  starting transfers between devices: 4.68 us -> 14.8 us
  waiting for transfers between devices: 16.9 us -> 18.6 us
    dot_general x7 -> x0, matrix products: 25.7 us -> none  [the longest x1 8.58 us: local_attention(): jnp.einsum('rtkgd,rskd->rkgts', scaled, all_values, preferred_element_typ...]
    pallas_call x0 -> x1, Pallas kernels: none -> 24.9 us  [shards(): pl.pallas_call(functools.partial(attention_kernel, dims), out_shape=[jax....]
    reshape x5 -> x0, local copies, waits for them, and re-layouts: 19.6 us -> none  [the longest x1 7.12 us: shards(): q_out = query_grad.reshape(resp_count * resp_tokens, -1)]
    ppermute x0 -> x9, waiting for transfers between devices: none -> 18.6 us  [the longest x6 10.7 us: from_ahead(): return lax.ppermute(x, 'dp', [((i + s) % n_dp, i) for i in range(n_dp)])]
    all_to_all x1 -> x0, waiting for transfers between devices: 16.9 us -> none  [shards(): lax.all_to_all(outgoing_grads, 'dp', split_axis=0, concat_axis=0, tiled=T...]
    all_gather x1 -> x0, blocking collectives: 15.1 us -> none  [shards(): gathered = lax.all_gather(prompt_kv, 'dp', axis=1, tiled=True)]
    ppermute x0 -> x9, starting transfers between devices: none -> 14.8 us  [the longest x6 11 us: from_ahead(): return lax.ppermute(x, 'dp', [((i + s) % n_dp, i) for i in range(n_dp)])]
    sub x2 -> x0, other arithmetic: 14.7 us -> none  [the longest x1 14.7 us: local_attention(): exp_scores = jnp.exp(scores - row_max)]
  transfers between devices with their start and end apart: 1 -> 9, of which waited for: 1 -> 4; matrix products, arithmetic and copies ran while one was open for 16% -> 0% of each run, Pallas kernels for 0% -> 0%
where the time goes in v1:
time: 65.8 us; the launch traced here: 65.6 us
  Pallas kernels  24.9 us (38%)
  waiting for transfers between devices  18.6 us (28%)
  starting transfers between devices  14.8 us (22%)
  local copies, waits for them, and re-layouts  5.83 us (9%)
  other arithmetic  0.73 us (1%)
  between operations  0.67 us (1%)
    pallas_call x1, Pallas kernels, shards(): pl.pallas_call(functools.partial(attention_kernel, dims), out_shape=[jax....  24.9 us
    ppermute x6, starting transfers between devices, from_ahead(): return lax.ppermute(x, 'dp', [((i + s) % n_dp, i) for i in range(n_dp)])  11 us
    ppermute x6, waiting for transfers between devices, from_ahead(): return lax.ppermute(x, 'dp', [((i + s) % n_dp, i) for i in range(n_dp)])  10.7 us
    ppermute x3, waiting for transfers between devices, shards(): lax.ppermute(results[2 + s], 'dp', [(i, (i + s) % n_dp) for i in range(n_...  7.82 us
    unnamed x12, local copies, waits for them, and re-layouts  5.83 us
    ppermute x3, starting transfers between devices, shards(): lax.ppermute(results[2 + s], 'dp', [(i, (i + s) % n_dp) for i in range(n_...  3.87 us
  transfers between devices with their start and end apart: 9, of which 4 were waited for; matrix products, arithmetic and copies ran while one was open for 0% of the time, Pallas kernels for 0%

profile of v1, /device:TPU:0, one launch (start us, length us, event | category | flops | bytes accessed | tf_op | source)
XLA Modules:
  0.0 65.6 jit_solution(4660960646625272661)
XLA Ops:
  0.6 4.1 %collective-permute-start.4 = (bf16[2,128,256]{2,1,0:T(8,128)(2,1)}, bf16[2,128,256]{2,1,0:T(8,128)(2,1)S(1)}, u32[]{:S(2)}, u32[]{:S(2)}) collective-permute-start(bf16[2,128,256]{2,1,0:T(8,128)(2,1)} %refs_9_.1), channel_id=1, source_target_pairs={{8,0},{12,4},{0,8},{4,12},{9,1},{13,5},{1,9},{5,13},{10,2},{14,6},... | collective-permute-start | bytes 393224 | tf_op jit(solution)/shard_map/ppermute | solution.py:330
  4.7 1.3 %collective-permute-start.3 = (bf16[2,128,256]{2,1,0:T(8,128)(2,1)}, bf16[2,128,256]{2,1,0:T(8,128)(2,1)S(1)}, u32[]{:S(2)}, u32[]{:S(2)}) collective-permute-start(bf16[2,128,256]{2,1,0:T(8,128)(2,1)} %refs_9_.1), channel_id=1, source_target_pairs={{4,0},{8,4},{12,8},{0,12},{5,1},{9,5},{13,9},{1,13},{6,2},{10,6},{... | collective-permute-start | bytes 393224 | tf_op jit(solution)/shard_map/ppermute | solution.py:330
  6.1 0.7 %collective-permute-start.5 = (bf16[2,128,256]{2,1,0:T(8,128)(2,1)}, bf16[2,128,256]{2,1,0:T(8,128)(2,1)S(1)}, u32[]{:S(2)}, u32[]{:S(2)}) collective-permute-start(bf16[2,128,256]{2,1,0:T(8,128)(2,1)} %refs_9_.1), channel_id=1, source_target_pairs={{12,0},{0,4},{4,8},{8,12},{13,1},{1,5},{5,9},{9,13},{14,2},{2,6},{... | collective-permute-start | bytes 393224 | tf_op jit(solution)/shard_map/ppermute | solution.py:330
  6.8 1.0 %collective-permute-start.1 = (f32[16]{0:T(128)}, f32[16]{0:T(128)S(1)}, u32[]{:S(2)}, u32[]{:S(2)}) collective-permute-start(f32[16]{0:T(128)} %refs_2_.1), channel_id=1, source_target_pairs={{8,0},{12,4},{0,8},{4,12},{9,1},{13,5},{1,9},{5,13},{10,2},{14,6},... | collective-permute-start | bytes 200 | tf_op jit(solution)/shard_map/ppermute | solution.py:330
  7.8 2.9 %collective-permute-start = (f32[16]{0:T(128)}, f32[16]{0:T(128)S(1)}, u32[]{:S(2)}, u32[]{:S(2)}) collective-permute-start(f32[16]{0:T(128)} %refs_2_.1), channel_id=1, source_target_pairs={{4,0},{8,4},{12,8},{0,12},{5,1},{9,5},{13,9},{1,13},{6,2},{10,6},{... | collective-permute-start | bytes 200 | tf_op jit(solution)/shard_map/ppermute | solution.py:330
  10.7 6.2 %collective-permute-done.1.refs_4_ = f32[16]{0:T(128)S(1)} collective-permute-done((f32[16]{0:T(128)}, f32[16]{0:T(128)S(1)}, u32[]{:S(2)}, u32[]{:S(2)}) %collective-permute-start.1) | collective-permute-done | bytes 96 | tf_op jit(solution)/shard_map/ppermute | solution.py:330
  16.9 0.9 %collective-permute-start.2 = (f32[16]{0:T(128)}, f32[16]{0:T(128)S(1)}, u32[]{:S(2)}, u32[]{:S(2)}) collective-permute-start(f32[16]{0:T(128)} %refs_2_.1), channel_id=1, source_target_pairs={{12,0},{0,4},{4,8},{8,12},{13,1},{1,5},{5,9},{9,13},{14,2},{2,6},{... | collective-permute-start | bytes 200 | tf_op jit(solution)/shard_map/ppermute | solution.py:330
  17.8 0.0 collective-permute-done.refs_3_
  17.8 4.6 %collective-permute-done.2.refs_5_ = f32[16]{0:T(128)S(1)} collective-permute-done((f32[16]{0:T(128)}, f32[16]{0:T(128)S(1)}, u32[]{:S(2)}, u32[]{:S(2)}) %collective-permute-start.2) | collective-permute-done | bytes 96 | tf_op jit(solution)/shard_map/ppermute | solution.py:330
  22.3 0.0 collective-permute-done.4.refs_11_
  22.3 0.0 collective-permute-done.3.refs_10_
  22.3 0.0 collective-permute-done.5.refs_12_
  22.4 0.0 copy-start
  22.4 1.7 %copy-done = bf16[1024,1280]{1,0:T(8,128)(2,1)S(1)} copy-done((bf16[1024,1280]{1,0:T(8,128)(2,1)S(1)}, bf16[1024,1280]{1,0:T(8,128)(2,1)}, u32[]{:S(2)}) %copy-start) | copy-done | bytes 2621464
  24.1 0.0 copy-start.1
  24.1 1.2 %copy-done.1 = bf16[2,1024,256]{2,1,0:T(8,128)(2,1)S(1)} copy-done((bf16[2,1024,256]{2,1,0:T(8,128)(2,1)S(1)}, bf16[2,1024,256]{2,1,0:T(8,128)(2,1)}, u32[]{:S(2)}) %copy-start.1) | copy-done | bytes 1048600
  25.3 0.0 copy-start.2
  25.3 0.9 %copy-done.2 = bf16[2,128,256]{2,1,0:T(8,128)(2,1)S(1)} copy-done((bf16[2,128,256]{2,1,0:T(8,128)(2,1)S(1)}, bf16[2,128,256]{2,1,0:T(8,128)(2,1)}, u32[]{:S(2)}) %copy-start.2) | copy-done | bytes 131096
  26.2 0.0 copy-start.3
  26.2 0.7 copy-done.3
  26.9 0.0 copy-start.4
  26.9 0.7 copy-done.4
  27.5 0.0 copy-start.5
  27.5 0.7 copy-done.5
  28.2 24.9 %attention_grads.1 = (bf16[1024,1280]{1,0:T(8,128)(2,1)}, bf16[2,1024,256]{2,1,0:T(8,128)(2,1)}, bf16[2,128,256]{2,1,0:T(8,128)(2,1)S(1)}, bf16[2,128,256]{2,1,0...) custom-call(s32[64]{0:T(128)S(1)} %copy-done.3, s32[16]{0:T(128)S(1)} %copy-done.4, ...), custom_call_target="tpu_custom_call" | custom-call | flops 2516582400 | bytes 9961472 | tf_op jit(solution)/shard_map/attention_grads/pallas_call | solution.py:343
  53.1 0.1 collective-permute-start.6
  53.2 2.3 %collective-permute-start.7 = (bf16[2,128,256]{2,1,0:T(8,128)(2,1)S(1)}, bf16[2,128,256]{2,1,0:T(8,128)(2,1)S(1)}, u32[]{:S(2)}, u32[]{:S(2)}) collective-permute-start(bf16[2,128,256]{2,1,0:T(8,128)(2,1)S(1)} %get-tuple-element.13), channel_id=1, source_target_pairs={{0,8},{4,12},{8,0},{12,4},{1,9},{5,13},{9,1},{13,5},{2,10},{6,14},... | collective-permute-start | bytes 393224 | tf_op jit(solution)/shard_map/ppermute | solution.py:382
  55.6 1.5 %collective-permute-start.8 = (bf16[2,128,256]{2,1,0:T(8,128)(2,1)S(1)}, bf16[2,128,256]{2,1,0:T(8,128)(2,1)S(1)}, u32[]{:S(2)}, u32[]{:S(2)}) collective-permute-start(bf16[2,128,256]{2,1,0:T(8,128)(2,1)S(1)} %get-tuple-element.14), channel_id=1, source_target_pairs={{0,12},{4,0},{8,4},{12,8},{1,13},{5,1},{9,5},{13,9},{2,14},{6,2},{... | collective-permute-start | bytes 393224 | tf_op jit(solution)/shard_map/ppermute | solution.py:382
  57.0 4.5 %collective-permute-done.6 = bf16[2,128,256]{2,1,0:T(8,128)(2,1)S(1)} collective-permute-done((bf16[2,128,256]{2,1,0:T(8,128)(2,1)S(1)}, bf16[2,128,256]{2,1,0:T(8,128)(2,1)S(1)}, u32[]{:S(2)}, u32[]{:S(2)}) %collective-permute-start.6) | collective-permute-done | bytes 131104 | tf_op jit(solution)/shard_map/ppermute | solution.py:382
  61.5 3.4 %collective-permute-done.7 = bf16[2,128,256]{2,1,0:T(8,128)(2,1)S(1)} collective-permute-done((bf16[2,128,256]{2,1,0:T(8,128)(2,1)S(1)}, bf16[2,128,256]{2,1,0:T(8,128)(2,1)S(1)}, u32[]{:S(2)}, u32[]{:S(2)}) %collective-permute-start.7) | collective-permute-done | bytes 131104 | tf_op jit(solution)/shard_map/ppermute | solution.py:382
  64.8 0.0 collective-permute-done.8
  64.8 0.7 %add_convert_fusion = bf16[2,128,256]{2,1,0:T(8,128)(2,1)} fusion(bf16[2,128,256]{2,1,0:T(8,128)(2,1)S(1)} %collective-permute-done.8, bf16[2,128,256]{2,1,0:T(8,128)(2,1)S(1)} %collective-permute-done.7, bf16[2,128,256]{2,1,0:T(8,128)(2,1)S(1)} %collective-permute-done.6, bf16[2,128,256]{2,1,0:T(8,128)(2,1)S(1)} %get-tuple-element.11), kind=kLoop, calls=%fused_computation | loop fusion | flops 524288 | bytes 655360 | tf_op jit(solution)/shard_map/convert_element_type | solution.py:385
Async XLA Ops:
  0.6 21.7 %collective-permute-start.4 = (bf16[2,128,256]{2,1,0:T(8,128)(2,1)}, bf16[2,128,256]{2,1,0:T(8,128)(2,1)S(1)}, u32[]{:S(2)}, u32[]{:S(2)}) collective-permute-start(bf16[2,128,256]{2,1,0:T(8,128)(2,1)} %refs_9_.1), channel_id=1, source_target_pairs={{8,0},{12,4},{0,8},{4,12},{9,1},{13,5},{1,9},{5,13},{10,2},{14,6},... | collective-permute-start | bytes 393224 | tf_op jit(solution)/shard_map/ppermute | solution.py:330
  4.7 17.6 %collective-permute-start.3 = (bf16[2,128,256]{2,1,0:T(8,128)(2,1)}, bf16[2,128,256]{2,1,0:T(8,128)(2,1)S(1)}, u32[]{:S(2)}, u32[]{:S(2)}) collective-permute-start(bf16[2,128,256]{2,1,0:T(8,128)(2,1)} %refs_9_.1), channel_id=1, source_target_pairs={{4,0},{8,4},{12,8},{0,12},{5,1},{9,5},{13,9},{1,13},{6,2},{10,6},{... | collective-permute-start | bytes 393224 | tf_op jit(solution)/shard_map/ppermute | solution.py:330
  6.1 16.3 %collective-permute-start.5 = (bf16[2,128,256]{2,1,0:T(8,128)(2,1)}, bf16[2,128,256]{2,1,0:T(8,128)(2,1)S(1)}, u32[]{:S(2)}, u32[]{:S(2)}) collective-permute-start(bf16[2,128,256]{2,1,0:T(8,128)(2,1)} %refs_9_.1), channel_id=1, source_target_pairs={{12,0},{0,4},{4,8},{8,12},{13,1},{1,5},{5,9},{9,13},{14,2},{2,6},{... | collective-permute-start | bytes 393224 | tf_op jit(solution)/shard_map/ppermute | solution.py:330
  6.8 10.1 %collective-permute-start.1 = (f32[16]{0:T(128)}, f32[16]{0:T(128)S(1)}, u32[]{:S(2)}, u32[]{:S(2)}) collective-permute-start(f32[16]{0:T(128)} %refs_2_.1), channel_id=1, source_target_pairs={{8,0},{12,4},{0,8},{4,12},{9,1},{13,5},{1,9},{5,13},{10,2},{14,6},... | collective-permute-start | bytes 200 | tf_op jit(solution)/shard_map/ppermute | solution.py:330
  7.8 10.0 %collective-permute-start = (f32[16]{0:T(128)}, f32[16]{0:T(128)S(1)}, u32[]{:S(2)}, u32[]{:S(2)}) collective-permute-start(f32[16]{0:T(128)} %refs_2_.1), channel_id=1, source_target_pairs={{4,0},{8,4},{12,8},{0,12},{5,1},{9,5},{13,9},{1,13},{6,2},{10,6},{... | collective-permute-start | bytes 200 | tf_op jit(solution)/shard_map/ppermute | solution.py:330
  16.9 5.5 %collective-permute-start.2 = (f32[16]{0:T(128)}, f32[16]{0:T(128)S(1)}, u32[]{:S(2)}, u32[]{:S(2)}) collective-permute-start(f32[16]{0:T(128)} %refs_2_.1), channel_id=1, source_target_pairs={{12,0},{0,4},{4,8},{8,12},{13,1},{1,5},{5,9},{9,13},{14,2},{2,6},{... | collective-permute-start | bytes 200 | tf_op jit(solution)/shard_map/ppermute | solution.py:330
  22.4 1.7 %copy-start = (bf16[1024,1280]{1,0:T(8,128)(2,1)S(1)}, bf16[1024,1280]{1,0:T(8,128)(2,1)}, u32[]{:S(2)}) copy-start(bf16[1024,1280]{1,0:T(8,128)(2,1)} %refs_6_.1) | copy-start | bytes 7864324
  24.1 1.2 %copy-start.1 = (bf16[2,1024,256]{2,1,0:T(8,128)(2,1)S(1)}, bf16[2,1024,256]{2,1,0:T(8,128)(2,1)}, u32[]{:S(2)}) copy-start(bf16[2,1024,256]{2,1,0:T(8,128)(2,1)} %refs_8_.1) | copy-start | bytes 3145732
  25.3 0.9 %copy-start.2 = (bf16[2,128,256]{2,1,0:T(8,128)(2,1)S(1)}, bf16[2,128,256]{2,1,0:T(8,128)(2,1)}, u32[]{:S(2)}) copy-start(bf16[2,128,256]{2,1,0:T(8,128)(2,1)} %refs_9_.1) | copy-start | bytes 393220
  26.2 0.7 copy-start.3
  26.9 0.7 copy-start.4
  27.5 0.7 copy-start.5
  53.1 8.3 %collective-permute-start.6 = (bf16[2,128,256]{2,1,0:T(8,128)(2,1)S(1)}, bf16[2,128,256]{2,1,0:T(8,128)(2,1)S(1)}, u32[]{:S(2)}, u32[]{:S(2)}) collective-permute-start(bf16[2,128,256]{2,1,0:T(8,128)(2,1)S(1)} %get-tuple-element.12), channel_id=1, source_target_pairs={{0,4},{4,8},{8,12},{12,0},{1,5},{5,9},{9,13},{13,1},{2,6},{6,10},{... | collective-permute-start | bytes 393224 | tf_op jit(solution)/shard_map/ppermute | solution.py:382
  53.2 11.6 %collective-permute-start.7 = (bf16[2,128,256]{2,1,0:T(8,128)(2,1)S(1)}, bf16[2,128,256]{2,1,0:T(8,128)(2,1)S(1)}, u32[]{:S(2)}, u32[]{:S(2)}) collective-permute-start(bf16[2,128,256]{2,1,0:T(8,128)(2,1)S(1)} %get-tuple-element.13), channel_id=1, source_target_pairs={{0,8},{4,12},{8,0},{12,4},{1,9},{5,13},{9,1},{13,5},{2,10},{6,14},... | collective-permute-start | bytes 393224 | tf_op jit(solution)/shard_map/ppermute | solution.py:382
  55.6 9.3 %collective-permute-start.8 = (bf16[2,128,256]{2,1,0:T(8,128)(2,1)S(1)}, bf16[2,128,256]{2,1,0:T(8,128)(2,1)S(1)}, u32[]{:S(2)}, u32[]{:S(2)}) collective-permute-start(bf16[2,128,256]{2,1,0:T(8,128)(2,1)S(1)} %get-tuple-element.14), channel_id=1, source_target_pairs={{0,12},{4,0},{8,4},{12,8},{1,13},{5,1},{9,5},{13,9},{2,14},{6,2},{... | collective-permute-start | bytes 393224 | tf_op jit(solution)/shard_map/ppermute | solution.py:382

commit v2 on v1

--- a/solution.py
+++ b/solution.py
@@ -10,6 +10,8 @@
 
 HD = 128
 NEG = -1e30
+TAIL = 16
+FIRST = 1
 F32 = jnp.float32
 BF16 = jnp.bfloat16
 
@@ -169,42 +171,155 @@
         prefix_out[1, :, cols] = value_acc.astype(BF16)
 
 
-def attention_kernel(dims, *refs):
-    n_dp, count, slots, kv_heads, group_size, tokens, prefix_len, near = dims
-    groups = count // slots
-    n_prompts = n_dp if near else 1
+def group_kernel(turn, dims, refs):
+    n_dp, count, slots, kv_heads, group_size, tokens, prefix_len = dims
     refs = list(refs)
-    resp_prompt, resp_len = refs[:2]
-    rewards = refs[2 : 2 + n_prompts]
-    q_hbm, og_hbm, kv_hbm = refs[2 + n_prompts : 5 + n_prompts]
-    prompts = refs[5 + n_prompts : 5 + 2 * n_prompts]
-    q_out, self_out = refs[5 + 2 * n_prompts : 7 + 2 * n_prompts]
-    n_out = groups if near else 1
-    prefix_outs = refs[7 + 2 * n_prompts : 7 + 2 * n_prompts + n_out]
-    (order, seen, totals, lens, factors, q, og, kv, prefix, out, own, grads, sem_in, sem_prefix, sem_out, sem_grads) = refs[
-        7 + 2 * n_prompts + n_out :
+    small_hbm = refs[:3]
+    payloads = refs[3 : 3 + n_dp]
+    q_hbm, og_hbm, kv_hbm = refs[3 + n_dp : 6 + n_dp]
+    refs = refs[6 + n_dp + (2 if turn != FIRST else 0) :]
+    q_out, self_out, grads_out = refs[:3]
+    (resp_prompt, resp_len, rewards, order, q, og, kv, prefix, tails, out, own, grads,
+     sem_small, sem_prefix, sem_in, sem_out) = refs[3:]
+    me = lax.axis_index("dp")
+    prompt = lax.rem(me + turn, n_dp)
+
+    small = [
+        pltpu.make_async_copy(src, dst, sem_small.at[n])
+        for n, (src, dst) in enumerate(zip(small_hbm, (resp_prompt, resp_len, rewards)))
     ]
+    for copy in small:
+        copy.start()
+    own_rows = [
+        pltpu.make_async_copy(payloads[s].at[0, pl.ds(prefix_len, TAIL)], tails.at[s], sem_small.at[3 + s])
+        for s in range(n_dp)
+    ]
+    prefix_copies = [
+        pltpu.make_async_copy(payloads[turn].at[n, pl.ds(0, prefix_len)], prefix.at[n], sem_prefix.at[n])
+        for n in range(2)
+    ]
+    for copy in own_rows + prefix_copies:
+        copy.start()
+    small[0].wait()
+    found = 0
+    for i in range(count):
+        order[found] = i
+        found = found + (resp_prompt[me * count + i] == prompt).astype(jnp.int32)
+
+    picked = [order[j] for j in range(slots)]
+    rows = [pl.ds(pl.multiple_of(i * tokens, tokens), tokens) for i in picked]
+    copies_in, copies_out = [], []
+    for j in range(slots):
+        copies_in += [
+            pltpu.make_async_copy(q_hbm.at[rows[j]], q.at[j], sem_in.at[j, 0]),
+            pltpu.make_async_copy(og_hbm.at[rows[j]], og.at[j], sem_in.at[j, 1]),
+            pltpu.make_async_copy(kv_hbm.at[0, rows[j]], kv.at[j, 0], sem_in.at[j, 2]),
+            pltpu.make_async_copy(kv_hbm.at[1, rows[j]], kv.at[j, 1], sem_in.at[j, 3]),
+        ]
+        copies_out += [
+            pltpu.make_async_copy(out.at[j], q_out.at[rows[j]], sem_out.at[j, 0]),
+            pltpu.make_async_copy(own.at[j, 0], self_out.at[0, rows[j]], sem_out.at[j, 1]),
+            pltpu.make_async_copy(own.at[j, 1], self_out.at[1, rows[j]], sem_out.at[j, 2]),
+        ]
+    for copy in copies_in:
+        copy.start()
+
+    for copy in small[1:] + own_rows:
+        copy.wait()
+    member = jnp.zeros((1, tails.shape[2]), F32)
+    for s in range(n_dp):
+        tail = tails[s].astype(F32)
+        reward = tail[0:1] + tail[1:2] + tail[2:3]
+        member += jnp.where(tail[3:4] == prompt.astype(F32), reward, 0.0)
+    total = jnp.sum(member, axis=1, keepdims=True)
+    lens = [resp_len[i] for i in picked]
+    factors = [
+        (rewards[i] - total / count) * (tokens / length.astype(F32))
+        for i, length in zip(picked, lens)
+    ]
+    for copy in prefix_copies + copies_in:
+        copy.wait()
+    attend_group(
+        slots, 0, group_size, kv_heads, tokens, prefix_len, q, og, kv, prefix, lens, factors, out, own, grads
+    )
+    last = pltpu.make_async_copy(grads, grads_out, sem_prefix.at[0])
+    last.start()
+    for copy in copies_out:
+        copy.start()
+    for copy in copies_out + [last]:
+        copy.wait()
+
+
+def near_grads(turn, dims, small, payloads, resp_q, out_grad, resp_kv, earlier):
+    n_dp, count, slots, kv_heads, group_size, tokens, prefix_len = dims
+    width = kv_heads * HD
+    anywhere = pl.BlockSpec(memory_space=pl.ANY)
+    operands = [*small, *payloads, resp_q, out_grad, resp_kv, *earlier]
+    lanes = resp_q.shape[1]
+    return pl.pallas_call(
+        lambda *refs: group_kernel(turn, dims, refs),
+        out_shape=[
+            jax.ShapeDtypeStruct(resp_q.shape, BF16),
+            jax.ShapeDtypeStruct(resp_kv.shape, BF16),
+            jax.ShapeDtypeStruct((2, prefix_len, width), BF16),
+        ],
+        in_specs=[anywhere] * len(operands),
+        out_specs=[anywhere] * 3,
+        input_output_aliases={len(operands) - 2: 0, len(operands) - 1: 1} if earlier else {},
+        scratch_shapes=[
+            pltpu.SMEM(small[0].shape, jnp.int32),
+            pltpu.SMEM(small[1].shape, jnp.int32),
+            pltpu.SMEM(small[2].shape, F32),
+            pltpu.SMEM((slots + 1,), jnp.int32),
+            pltpu.VMEM((slots, tokens, lanes), BF16),
+            pltpu.VMEM((slots, tokens, lanes), BF16),
+            pltpu.VMEM((slots, 2, tokens, width), BF16),
+            pltpu.VMEM((2, prefix_len, width), BF16),
+            pltpu.VMEM((n_dp, TAIL, width), BF16),
+            pltpu.VMEM((slots, tokens, lanes), BF16),
+            pltpu.VMEM((slots, 2, tokens, width), BF16),
+            pltpu.VMEM((2, prefix_len, width), BF16),
+            pltpu.SemaphoreType.DMA((3 + n_dp,)),
+            pltpu.SemaphoreType.DMA((2,)),
+            pltpu.SemaphoreType.DMA((slots, 4)),
+            pltpu.SemaphoreType.DMA((slots, 3)),
+        ],
+        compiler_params=pltpu.CompilerParams(vmem_limit_bytes=48 * 1024 * 1024),
+        cost_estimate=pl.CostEstimate(
+            flops=2 * 5 * slots * tokens * group_size * kv_heads * (prefix_len + tokens) * HD,
+            bytes_accessed=2 * slots * tokens * (3 * lanes + 4 * width),
+            transcendentals=0,
+        ),
+        name="group_grads",
+    )(*operands)
+
+
+def make_payload(prompt_kv, rewards, my_prompts):
+    high = lax.reduce_precision(rewards, 8, 7)
+    middle = lax.reduce_precision(rewards - high, 8, 7)
+    low = rewards - high - middle
+    rows = jnp.stack([high, middle, low, my_prompts.astype(F32)]).astype(BF16)
+    rows = jnp.pad(
+        rows,
+        ((0, TAIL - rows.shape[0]), (0, prompt_kv.shape[2] - rows.shape[1])),
+        constant_values=-1,
+    )
+    return jnp.concatenate([prompt_kv, jnp.broadcast_to(rows, (2,) + rows.shape)], axis=1)
+
+
+def far_kernel(dims, *refs):
+    n_dp, count, slots, kv_heads, group_size, tokens, prefix_len = dims
+    groups = count
+    (resp_prompt, resp_len, rewards, q_hbm, og_hbm, kv_hbm, prompts, q_out, self_out, prefix_outs,
+     totals, lens, factors, q, og, kv, prefix, out, own, grads, sem_in, sem_prefix, sem_out, sem_grads) = refs
     me = lax.axis_index("dp")
     width = kv_heads * HD
 
     for p in range(n_dp):
-        seen[p] = 0
         totals[p] = 0.0
 
-    def place(i, _):
-        prompt = resp_prompt[me * count + i]
-        if near:
-            turn = lax.rem(prompt - me + n_dp, n_dp)
-            order[turn * slots + seen[turn]] = i
-            seen[turn] = seen[turn] + 1
-        else:
-            order[i] = i
-        return 0
-
-    lax.fori_loop(0, count, place, 0)
-
     def at_rows(slot):
-        return pl.ds(pl.multiple_of(order[slot] * tokens, tokens), tokens)
+        return pl.ds(pl.multiple_of(slot * tokens, tokens), tokens)
 
     def copies_in(slot):
         rows = at_rows(slot)
@@ -216,10 +331,8 @@
         )
 
     def prefix_copy(g):
-        if near:
-            return pltpu.make_async_copy(prompts[g], prefix.at[g], sem_prefix.at[g])
         prompt = resp_prompt[me * count + g]
-        return pltpu.make_async_copy(prompts[0].at[prompt], prefix.at[g], sem_prefix.at[g])
+        return pltpu.make_async_copy(prompts.at[prompt], prefix.at[g], sem_prefix.at[g])
 
     def copies_out(slot):
         rows = at_rows(slot)
@@ -230,8 +343,7 @@
         )
 
     def grads_copy(g):
-        target = prefix_outs[g] if near else prefix_outs[0].at[g]
-        return pltpu.make_async_copy(grads.at[g], target, sem_grads.at[g])
+        return pltpu.make_async_copy(grads.at[g], prefix_outs.at[g], sem_grads.at[g])
 
     for g in range(groups):
         prefix_copy(g).start()
@@ -243,32 +355,17 @@
 
         lax.fori_loop(0, slots, start, 0)
 
-    if near:
-        for s in range(n_dp):
-            source = lax.rem(me + s, n_dp)
-
-            def add(i, _):
-                prompt = resp_prompt[source * count + i]
-                totals[prompt] = totals[prompt] + rewards[s][i]
-                return 0
-
-            lax.fori_loop(0, count, add, 0)
-    else:
-
-        def add_one(i, _):
-            prompt = resp_prompt[i]
-            totals[prompt] = totals[prompt] + rewards[0][i]
-            return 0
-
-        lax.fori_loop(0, n_dp * count, add_one, 0)
-
-    own_rewards = rewards[0]
+    def add(i, _):
+        prompt = resp_prompt[i]
+        totals[prompt] = totals[prompt] + rewards[i]
+        return 0
+
+    lax.fori_loop(0, n_dp * count, add, 0)
 
     def find_factor(slot, _):
-        i = order[slot]
-        length = resp_len[i]
-        reward = own_rewards[i] if near else own_rewards[me * count + i]
-        advantage = reward - totals[resp_prompt[me * count + i]] / count
+        length = resp_len[slot]
+        place = me * count + slot
+        advantage = rewards[place] - totals[resp_prompt[place]] / count
         lens[slot] = length
         factors[slot] = advantage * (tokens / length.astype(F32))
         return 0
@@ -312,6 +409,57 @@
     lax.fori_loop(0, count, finish, 0)
     for g in range(groups):
         grads_copy(g).wait()
+
+
+def far_shards(dims, prompt_kv, resp_q, resp_kv, out_grad, rewards, resp_prompt, resp_len, my_prompts):
+    n_dp, count, slots, kv_heads, group_size, tokens, prefix_len = dims
+    assert slots == 1
+    width = kv_heads * HD
+    lanes = resp_q.shape[1]
+    smem = pl.BlockSpec(memory_space=pltpu.SMEM)
+    anywhere = pl.BlockSpec(memory_space=pl.ANY)
+    q_out, self_out, per_resp = pl.pallas_call(
+        functools.partial(far_kernel, dims),
+        out_shape=[
+            jax.ShapeDtypeStruct(resp_q.shape, BF16),
+            jax.ShapeDtypeStruct(resp_kv.shape, BF16),
+            jax.ShapeDtypeStruct((count, 2, prefix_len, width), BF16),
+        ],
+        in_specs=[smem] * 3 + [anywhere] * 4,
+        out_specs=[anywhere] * 3,
+        scratch_shapes=[
+            pltpu.SMEM((n_dp,), F32),
+            pltpu.SMEM((count,), jnp.int32),
+            pltpu.SMEM((count,), F32),
+            pltpu.VMEM((count, tokens, lanes), BF16),
+            pltpu.VMEM((count, tokens, lanes), BF16),
+            pltpu.VMEM((count, 2, tokens, width), BF16),
+            pltpu.VMEM((count, 2, prefix_len, width), BF16),
+            pltpu.VMEM((count, tokens, lanes), BF16),
+            pltpu.VMEM((count, 2, tokens, width), BF16),
+            pltpu.VMEM((count, 2, prefix_len, width), BF16),
+            pltpu.SemaphoreType.DMA((count, 4)),
+            pltpu.SemaphoreType.DMA((count,)),
+            pltpu.SemaphoreType.DMA((count, 3)),
+            pltpu.SemaphoreType.DMA((count,)),
+        ],
+        compiler_params=pltpu.CompilerParams(vmem_limit_bytes=48 * 1024 * 1024),
+        name="far_grads",
+    )(
+        resp_prompt,
+        resp_len,
+        lax.all_gather(rewards, "dp", axis=0, tiled=True),
+        resp_q,
+        out_grad,
+        resp_kv,
+        lax.all_gather(prompt_kv, "dp", axis=0),
+    )
+    route = (jnp.arange(n_dp, dtype=jnp.int32)[:, None] == my_prompts[None, :]).astype(BF16)
+    outgoing = jnp.dot(route, per_resp.reshape(count, -1), preferred_element_type=F32).astype(BF16)
+    outgoing = outgoing.reshape((n_dp,) + prompt_kv.shape)
+    incoming = lax.all_to_all(outgoing, "dp", split_axis=0, concat_axis=0, tiled=True)
+    prefix_out = jnp.sum(incoming, axis=0, dtype=F32).astype(BF16)
+    return (q_out, self_out, prefix_out)
 
 
 def shards(prompt_kv, resp_q, resp_kv, out_grad, rewards, resp_prompt, resp_len):
@@ -322,77 +470,27 @@
     kv_heads = width // HD
     group_size = resp_q.shape[1] // width
     slots = (count + n_dp - 1) // n_dp
-    groups = count // slots
-    near = groups == n_dp
-
-    if near:
-        def from_ahead(x, s):
-            return lax.ppermute(x, "dp", [((i + s) % n_dp, i) for i in range(n_dp)])
-
-        reward_parts = [rewards] + [from_ahead(rewards, s) for s in range(1, n_dp)]
-        prompt_parts = [prompt_kv] + [from_ahead(prompt_kv, s) for s in range(1, n_dp)]
-        prefix_shapes = [jax.ShapeDtypeStruct(prompt_kv.shape, BF16)] * groups
-    else:
-        reward_parts = [lax.all_gather(rewards, "dp", axis=0, tiled=True)]
-        prompt_parts = [lax.all_gather(prompt_kv, "dp", axis=0)]
-        prefix_shapes = [jax.ShapeDtypeStruct((groups,) + prompt_kv.shape, BF16)]
-
-    dims = (n_dp, count, slots, kv_heads, group_size, tokens, prefix_len, near)
-    smem = pl.BlockSpec(memory_space=pltpu.SMEM)
-    anywhere = pl.BlockSpec(memory_space=pl.ANY)
-    results = pl.pallas_call(
-        functools.partial(attention_kernel, dims),
-        out_shape=[
-            jax.ShapeDtypeStruct(resp_q.shape, BF16),
-            jax.ShapeDtypeStruct(resp_kv.shape, BF16),
-        ]
-        + prefix_shapes,
-        in_specs=[smem] * (2 + len(reward_parts)) + [anywhere] * (3 + len(prompt_parts)),
-        out_specs=[anywhere] * (2 + len(prefix_shapes)),
-        scratch_shapes=[
-            pltpu.SMEM((count,), jnp.int32),
-            pltpu.SMEM((n_dp,), jnp.int32),
-            pltpu.SMEM((n_dp,), F32),
-            pltpu.SMEM((count,), jnp.int32),
-            pltpu.SMEM((count,), F32),
-            pltpu.VMEM((count, tokens, resp_q.shape[1]), BF16),
-            pltpu.VMEM((count, tokens, resp_q.shape[1]), BF16),
-            pltpu.VMEM((count, 2, tokens, width), BF16),
-            pltpu.VMEM((groups, 2, prefix_len, width), BF16),
-            pltpu.VMEM((count, tokens, resp_q.shape[1]), BF16),
-            pltpu.VMEM((count, 2, tokens, width), BF16),
-            pltpu.VMEM((groups, 2, prefix_len, width), BF16),
-            pltpu.SemaphoreType.DMA((count, 4)),
-            pltpu.SemaphoreType.DMA((groups,)),
-            pltpu.SemaphoreType.DMA((count, 3)),
-            pltpu.SemaphoreType.DMA((groups,)),
-        ],
-        compiler_params=pltpu.CompilerParams(vmem_limit_bytes=48 * 1024 * 1024),
-        cost_estimate=pl.CostEstimate(
-            flops=2 * 5 * count * tokens * group_size * kv_heads * (prefix_len + tokens) * HD,
-            bytes_accessed=2 * (3 * resp_q.size + 2 * resp_kv.size),
-            transcendentals=0,
-        ),
-        name="attention_grads",
-    )(resp_prompt, resp_len, *reward_parts, resp_q, out_grad, resp_kv, *prompt_parts)
-    q_out, self_out = results[:2]
-
-    if near:
-        arrived = [results[2]] + [
-            lax.ppermute(results[2 + s], "dp", [(i, (i + s) % n_dp) for i in range(n_dp)])
-            for s in range(1, n_dp)
-        ]
-        prefix_out = sum(part.astype(F32) for part in arrived).astype(BF16)
-    else:
-        mine = lax.dynamic_slice_in_dim(resp_prompt, lax.axis_index("dp") * count, count)
-        route = (jnp.arange(n_dp, dtype=jnp.int32)[:, None] == mine[None, :]).astype(BF16)
-        outgoing = jnp.dot(
-            route, results[2].reshape(groups, -1), preferred_element_type=F32
-        ).astype(BF16)
-        outgoing = outgoing.reshape((n_dp,) + prompt_kv.shape)
-        incoming = lax.all_to_all(outgoing, "dp", split_axis=0, concat_axis=0, tiled=True)
-        prefix_out = jnp.sum(incoming, axis=0, dtype=F32).astype(BF16)
-    return (q_out, self_out, prefix_out)
+    dims = (n_dp, count, slots, kv_heads, group_size, tokens, prefix_len)
+    my_prompts = lax.dynamic_slice_in_dim(resp_prompt, lax.axis_index("dp") * count, count)
+    if count // slots != n_dp:
+        return far_shards(dims, prompt_kv, resp_q, resp_kv, out_grad, rewards, resp_prompt, resp_len, my_prompts)
+
+    payload = make_payload(prompt_kv, rewards, my_prompts)
+    payloads = [payload] + [
+        lax.ppermute(payload, "dp", [((i + s) % n_dp, i) for i in range(n_dp)])
+        for s in range(1, n_dp)
+    ]
+    earlier = ()
+    arrived = []
+    for turn in [*range(FIRST, n_dp), *range(FIRST)]:
+        *earlier, grads = near_grads(
+            turn, dims, (resp_prompt, resp_len, rewards), payloads, resp_q, out_grad, resp_kv, earlier
+        )
+        if turn:
+            grads = lax.ppermute(grads, "dp", [(i, (i + turn) % n_dp) for i in range(n_dp)])
+        arrived.append(grads)
+    prefix_out = sum(part.astype(F32) for part in arrived).astype(BF16)
+    return (*earlier, prefix_out)
 
 
 def solution(mesh):

time: 65.8 us -> 64.6 us (0.982)
  waiting for transfers between devices: 18.6 us -> 12.2 us
  Pallas kernels: 24.9 us -> 30.9 us
  starting transfers between devices: 14.8 us -> 12.4 us
  other arithmetic: 0.73 us -> 3.05 us
  local copies, waits for them, and re-layouts: 5.83 us -> 4.94 us
    ppermute x9 -> x6, waiting for transfers between devices: 18.6 us -> 12.2 us  [the longest x3 8.35 us: shards(): lax.ppermute(payload, 'dp', [((i + s) % n_dp, i) for i in range(n_dp)])]
    pallas_call x1 -> x4, Pallas kernels: 24.9 us -> 30.9 us  [near_grads(): pl.pallas_call(lambda *refs: group_kernel(turn, dims, refs), out_shape=[j...]
    ppermute x9 -> x6, starting transfers between devices: 14.8 us -> 12.4 us  [the longest x3 7.01 us: shards(): lax.ppermute(payload, 'dp', [((i + s) % n_dp, i) for i in range(n_dp)])]
    another operation x0 -> x3, other arithmetic: none -> 1.41 us  [make_payload(): rows = jnp.stack([high, middle, low, my_prompts.astype(F32)]).astype(BF16)]
    concatenate x0 -> x1, other arithmetic: none -> 0.92 us  [make_payload(): jnp.concatenate([prompt_kv, jnp.broadcast_to(rows, (2,) + rows.shape)], a...]
    unnamed x12 -> x10, local copies, waits for them, and re-layouts: 5.83 us -> 4.93 us
  transfers between devices with their start and end apart: 9 -> 6, of which waited for: 4 -> 3; matrix products, arithmetic and copies ran while one was open for 0% -> 0% of each run, Pallas kernels for 0% -> 12%
where the time goes in v2:
time: 64.6 us; the launch traced here: 64.2 us
  Pallas kernels  30.9 us (48%)
  starting transfers between devices  12.4 us (19%)
  waiting for transfers between devices  12.2 us (19%)
  local copies, waits for them, and re-layouts  4.94 us (8%)
  other arithmetic  3.05 us (5%)
  between operations  0.69 us (1%)
    pallas_call x4, Pallas kernels, near_grads(): pl.pallas_call(lambda *refs: group_kernel(turn, dims, refs), out_shape=[j...  30.9 us
    ppermute x3, waiting for transfers between devices, shards(): lax.ppermute(payload, 'dp', [((i + s) % n_dp, i) for i in range(n_dp)])  8.35 us
    ppermute x3, starting transfers between devices, shards(): lax.ppermute(payload, 'dp', [((i + s) % n_dp, i) for i in range(n_dp)])  7.01 us
    ppermute x3, starting transfers between devices, shards(): lax.ppermute(grads, 'dp', [(i, (i + turn) % n_dp) for i in range(n_dp)])  5.39 us
    unnamed x10, local copies, waits for them, and re-layouts  4.93 us
    ppermute x3, waiting for transfers between devices, shards(): lax.ppermute(grads, 'dp', [(i, (i + turn) % n_dp) for i in range(n_dp)])  3.83 us
    another operation x3, other arithmetic, make_payload(): rows = jnp.stack([high, middle, low, my_prompts.astype(F32)]).astype(BF16)  1.41 us
  transfers between devices with their start and end apart: 6, of which 3 were waited for; matrix products, arithmetic and copies ran while one was open for 0% of the time, Pallas kernels for 12%

profile of v2, /device:TPU:0, one launch (start us, length us, event | category | flops | bytes accessed | tf_op | source)
XLA Modules:
  0.0 64.2 jit_solution(3029756374113708020)
XLA Ops:
  0.6 0.7 %fusion.12 = (bf16[1,16]{1,0:T(2,128)(2,1)S(1)}, bf16[1,16]{1,0:T(2,128)(2,1)S(1)}, bf16[1,16]{1,0:T(2,128)(2,1)S(1)}) fusion(f32[16]{0:T(128)} %refs_2_.7), kind=kLoop, calls=%fused_computation.20 | loop fusion | flops 112 | bytes 160 | tf_op jit(solution)/shard_map/stack | solution.py:301
  1.3 0.7 %convert_bitcast_fusion = bf16[1,16]{1,0:T(2,128)(2,1)S(1)} fusion(s32[64]{0:T(128)} %refs_0_.7, s32[]{:T(128)S(6)} %select_n.3), kind=kLoop, calls=%fused_computation.24 | loop fusion | flops 32 | bytes 100 | tf_op jit(solution)/shard_map/stack | solution.py:301
  2.1 0.9 %pad_maximum_fusion.refs_3_ = bf16[2,144,256]{2,1,0:T(8,128)(2,1)S(1)} fusion(bf16[2,16,256]{2,1,0:T(8,128)(2,1)S(1)} %broadcast_in_dim.3, bf16[2,128,256]{2,1,0:T(8,128)(2,1)} %param.7), kind=kLoop, calls=%fused_computation.1 | loop fusion | flops 294912 | bytes 294912 | tf_op jit(solution)/shard_map/concatenate | solution.py:307
  3.0 3.1 %collective-permute-start.2 = (bf16[2,144,256]{2,1,0:T(8,128)(2,1)S(1)}, bf16[2,144,256]{2,1,0:T(8,128)(2,1)S(1)}, u32[]{:S(2)}, u32[]{:S(2)}) collective-permute-start(bf16[2,144,256]{2,1,0:T(8,128)(2,1)S(1)} %pad_maximum_fusion.refs_3_), channel_id=1, source_target_pairs={{12,0},{0,4},{4,8},{8,12},{13,1},{1,5},{5,9},{9,13},{14,2},{2,6},{... | collective-permute-start | bytes 442376 | tf_op jit(solution)/shard_map/ppermute | solution.py:480
  6.1 2.6 %collective-permute-start.1 = (bf16[2,144,256]{2,1,0:T(8,128)(2,1)S(1)}, bf16[2,144,256]{2,1,0:T(8,128)(2,1)S(1)}, u32[]{:S(2)}, u32[]{:S(2)}) collective-permute-start(bf16[2,144,256]{2,1,0:T(8,128)(2,1)S(1)} %pad_maximum_fusion.refs_3_), channel_id=1, source_target_pairs={{8,0},{12,4},{0,8},{4,12},{9,1},{13,5},{1,9},{5,13},{10,2},{14,6},... | collective-permute-start | bytes 442376 | tf_op jit(solution)/shard_map/ppermute | solution.py:480
  8.6 1.3 %collective-permute-start = (bf16[2,144,256]{2,1,0:T(8,128)(2,1)S(1)}, bf16[2,144,256]{2,1,0:T(8,128)(2,1)S(1)}, u32[]{:S(2)}, u32[]{:S(2)}) collective-permute-start(bf16[2,144,256]{2,1,0:T(8,128)(2,1)S(1)} %pad_maximum_fusion.refs_3_), channel_id=1, source_target_pairs={{4,0},{8,4},{12,8},{0,12},{5,1},{9,5},{13,9},{1,13},{6,2},{10,6},{... | collective-permute-start | bytes 442376 | tf_op jit(solution)/shard_map/ppermute | solution.py:480
  10.0 2.9 %collective-permute-done.2.refs_6_ = bf16[2,144,256]{2,1,0:T(8,128)(2,1)S(1)} collective-permute-done((bf16[2,144,256]{2,1,0:T(8,128)(2,1)S(1)}, bf16[2,144,256]{2,1,0:T(8,128)(2,1)S(1)}, u32[]{:S(2)}, u32[]{:S(2)}) %collective-permute-start.2) | collective-permute-done | bytes 147488 | tf_op jit(solution)/shard_map/ppermute | solution.py:480
  12.9 5.5 %collective-permute-done.1.refs_5_ = bf16[2,144,256]{2,1,0:T(8,128)(2,1)S(1)} collective-permute-done((bf16[2,144,256]{2,1,0:T(8,128)(2,1)S(1)}, bf16[2,144,256]{2,1,0:T(8,128)(2,1)S(1)}, u32[]{:S(2)}, u32[]{:S(2)}) %collective-permute-start.1) | collective-permute-done | bytes 147488 | tf_op jit(solution)/shard_map/ppermute | solution.py:480
  18.3 0.0 collective-permute-done.refs_4_
  18.3 0.0 copy-start
  18.3 1.7 %copy-done = bf16[1024,1280]{1,0:T(8,128)(2,1)S(1)} copy-done((bf16[1024,1280]{1,0:T(8,128)(2,1)S(1)}, bf16[1024,1280]{1,0:T(8,128)(2,1)}, u32[]{:S(2)}) %copy-start) | copy-done | bytes 2621464
  20.1 0.0 copy-start.1
  20.1 1.2 %copy-done.1 = bf16[2,1024,256]{2,1,0:T(8,128)(2,1)S(1)} copy-done((bf16[2,1024,256]{2,1,0:T(8,128)(2,1)S(1)}, bf16[2,1024,256]{2,1,0:T(8,128)(2,1)}, u32[]{:S(2)}) %copy-start.1) | copy-done | bytes 1048600
  21.3 0.0 copy-start.2
  21.3 0.7 %copy-done.2 = f32[16]{0:T(128)S(1)} copy-done((f32[16]{0:T(128)S(1)}, f32[16]{0:T(128)}, u32[]{:S(2)}) %copy-start.2) | copy-done | bytes 88
  22.0 0.0 copy-start.3
  22.0 0.7 %copy-done.3 = s32[64]{0:T(128)S(1)} copy-done((s32[64]{0:T(128)S(1)}, s32[64]{0:T(128)}, u32[]{:S(2)}) %copy-start.3) | copy-done | bytes 280
  22.6 0.0 copy-start.4
  22.6 0.7 %copy-done.4 = s32[16]{0:T(128)S(1)} copy-done((s32[16]{0:T(128)S(1)}, s32[16]{0:T(128)}, u32[]{:S(2)}) %copy-start.4) | copy-done | bytes 88
  23.3 7.7 %group_grads.4 = (bf16[1024,1280]{1,0:T(8,128)(2,1)}, bf16[2,1024,256]{2,1,0:T(8,128)(2,1)}, bf16[2,128,256]{2,1,0:T(8,128)(2,1)S(1)}) custom-call(s32[64]{0:T(128)S(1)} %copy-done.3, s32[16]{0:T(128)S(1)} %copy-done.4, f32[16]{0:T(128)S(1)} %copy-done.2, bf16[2,144,256]{2,1,0:T(8,128)(2,1)S(1)} %pad_maximum_fusion.refs_3_, ...), custom_call_target="tpu_custom_call" | custom-call | flops 629145600 | bytes 2490368 | tf_op jit(solution)/shard_map/group_grads/pallas_call | solution.py:259
  31.0 7.7 %group_grads.5 = (bf16[1024,1280]{1,0:T(8,128)(2,1)}, bf16[2,1024,256]{2,1,0:T(8,128)(2,1)}, bf16[2,128,256]{2,1,0:T(8,128)(2,1)S(1)}) custom-call(s32[64]{0:T(128)S(1)} %copy-done.3, s32[16]{0:T(128)S(1)} %copy-done.4, f32[16]{0:T(128)S(1)} %copy-done.2, ...), custom_call_target="tpu_custom_call", output_to_operand_aliasing={{0}: (10, {}), {1}: (11, {})} | custom-call | flops 629145600 | bytes 2490368 | tf_op jit(solution)/shard_map/group_grads/pallas_call | solution.py:259
  38.8 7.7 %group_grads.6 = (bf16[1024,1280]{1,0:T(8,128)(2,1)}, bf16[2,1024,256]{2,1,0:T(8,128)(2,1)}, bf16[2,128,256]{2,1,0:T(8,128)(2,1)S(1)}) custom-call(s32[64]{0:T(128)S(1)} %copy-done.3, s32[16]{0:T(128)S(1)} %copy-done.4, f32[16]{0:T(128)S(1)} %copy-done.2, ...), custom_call_target="tpu_custom_call", output_to_operand_aliasing={{0}: (10, {}), {1}: (11, {})} | custom-call | flops 629145600 | bytes 2490368 | tf_op jit(solution)/shard_map/group_grads/pallas_call | solution.py:259
  46.5 4.7 %collective-permute-start.5 = (bf16[2,128,256]{2,1,0:T(8,128)(2,1)S(1)}, bf16[2,128,256]{2,1,0:T(8,128)(2,1)S(1)}, u32[]{:S(2)}, u32[]{:S(2)}) collective-permute-start(bf16[2,128,256]{2,1,0:T(8,128)(2,1)S(1)} %get-tuple-element.25), channel_id=1, source_target_pairs={{0,12},{4,0},{8,4},{12,8},{1,13},{5,1},{9,5},{13,9},{2,14},{6,2},{... | collective-permute-start | bytes 393224 | tf_op jit(solution)/shard_map/ppermute | solution.py:490
  51.3 0.4 collective-permute-start.4
  51.7 0.2 collective-permute-start.3
  51.9 7.7 %group_grads.7 = (bf16[1024,1280]{1,0:T(8,128)(2,1)}, bf16[2,1024,256]{2,1,0:T(8,128)(2,1)}, bf16[2,128,256]{2,1,0:T(8,128)(2,1)S(1)}) custom-call(s32[64]{0:T(128)S(1)} %copy-done.3, s32[16]{0:T(128)S(1)} %copy-done.4, f32[16]{0:T(128)S(1)} %copy-done.2, ...), custom_call_target="tpu_custom_call", output_to_operand_aliasing={{0}: (10, {}), {1}: (11, {})} | custom-call | flops 629145600 | bytes 2490368 | tf_op jit(solution)/shard_map/group_grads/pallas_call | solution.py:259
  59.7 0.0 collective-permute-done.5
  59.7 3.8 %collective-permute-done.4 = bf16[2,128,256]{2,1,0:T(8,128)(2,1)S(1)} collective-permute-done((bf16[2,128,256]{2,1,0:T(8,128)(2,1)S(1)}, bf16[2,128,256]{2,1,0:T(8,128)(2,1)S(1)}, u32[]{:S(2)}, u32[]{:S(2)}) %collective-permute-start.4) | collective-permute-done | bytes 131104 | tf_op jit(solution)/shard_map/ppermute | solution.py:490
  63.5 0.0 collective-permute-done.3
  63.5 0.7 %add_convert_fusion = bf16[2,128,256]{2,1,0:T(8,128)(2,1)} fusion(bf16[2,128,256]{2,1,0:T(8,128)(2,1)S(1)} %get-tuple-element.26, bf16[2,128,256]{2,1,0:T(8,128)(2,1)S(1)} %collective-permute-done.5, bf16[2,128,256]{2,1,0:T(8,128)(2,1)S(1)} %collective-permute-done.4, bf16[2,128,256]{2,1,0:T(8,128)(2,1)S(1)} %collective-permute-done.3), kind=kLoop, calls=%fused_computation | loop fusion | flops 524288 | bytes 655360 | tf_op jit(solution)/shard_map/convert_element_type | solution.py:492
  (2 shorter events, 0.0 us)
Async XLA Ops:
  3.0 9.9 %collective-permute-start.2 = (bf16[2,144,256]{2,1,0:T(8,128)(2,1)S(1)}, bf16[2,144,256]{2,1,0:T(8,128)(2,1)S(1)}, u32[]{:S(2)}, u32[]{:S(2)}) collective-permute-start(bf16[2,144,256]{2,1,0:T(8,128)(2,1)S(1)} %pad_maximum_fusion.refs_3_), channel_id=1, source_target_pairs={{12,0},{0,4},{4,8},{8,12},{13,1},{1,5},{5,9},{9,13},{14,2},{2,6},{... | collective-permute-start | bytes 442376 | tf_op jit(solution)/shard_map/ppermute | solution.py:480
  6.1 12.3 %collective-permute-start.1 = (bf16[2,144,256]{2,1,0:T(8,128)(2,1)S(1)}, bf16[2,144,256]{2,1,0:T(8,128)(2,1)S(1)}, u32[]{:S(2)}, u32[]{:S(2)}) collective-permute-start(bf16[2,144,256]{2,1,0:T(8,128)(2,1)S(1)} %pad_maximum_fusion.refs_3_), channel_id=1, source_target_pairs={{8,0},{12,4},{0,8},{4,12},{9,1},{13,5},{1,9},{5,13},{10,2},{14,6},... | collective-permute-start | bytes 442376 | tf_op jit(solution)/shard_map/ppermute | solution.py:480
  8.6 9.7 %collective-permute-start = (bf16[2,144,256]{2,1,0:T(8,128)(2,1)S(1)}, bf16[2,144,256]{2,1,0:T(8,128)(2,1)S(1)}, u32[]{:S(2)}, u32[]{:S(2)}) collective-permute-start(bf16[2,144,256]{2,1,0:T(8,128)(2,1)S(1)} %pad_maximum_fusion.refs_3_), channel_id=1, source_target_pairs={{4,0},{8,4},{12,8},{0,12},{5,1},{9,5},{13,9},{1,13},{6,2},{10,6},{... | collective-permute-start | bytes 442376 | tf_op jit(solution)/shard_map/ppermute | solution.py:480
  18.3 1.7 %copy-start = (bf16[1024,1280]{1,0:T(8,128)(2,1)S(1)}, bf16[1024,1280]{1,0:T(8,128)(2,1)}, u32[]{:S(2)}) copy-start(bf16[1024,1280]{1,0:T(8,128)(2,1)} %refs_7_.7) | copy-start | bytes 7864324
  20.1 1.2 %copy-start.1 = (bf16[2,1024,256]{2,1,0:T(8,128)(2,1)S(1)}, bf16[2,1024,256]{2,1,0:T(8,128)(2,1)}, u32[]{:S(2)}) copy-start(bf16[2,1024,256]{2,1,0:T(8,128)(2,1)} %refs_9_.7) | copy-start | bytes 3145732
  21.3 0.7 %copy-start.2 = (f32[16]{0:T(128)S(1)}, f32[16]{0:T(128)}, u32[]{:S(2)}) copy-start(f32[16]{0:T(128)} %refs_2_.7) | copy-start | bytes 196
  22.0 0.7 %copy-start.3 = (s32[64]{0:T(128)S(1)}, s32[64]{0:T(128)}, u32[]{:S(2)}) copy-start(s32[64]{0:T(128)} %refs_0_.7) | copy-start | bytes 772
  22.6 0.7 %copy-start.4 = (s32[16]{0:T(128)S(1)}, s32[16]{0:T(128)}, u32[]{:S(2)}) copy-start(s32[16]{0:T(128)} %refs_1_.7) | copy-start | bytes 196
  46.5 13.1 %collective-permute-start.5 = (bf16[2,128,256]{2,1,0:T(8,128)(2,1)S(1)}, bf16[2,128,256]{2,1,0:T(8,128)(2,1)S(1)}, u32[]{:S(2)}, u32[]{:S(2)}) collective-permute-start(bf16[2,128,256]{2,1,0:T(8,128)(2,1)S(1)} %get-tuple-element.25), channel_id=1, source_target_pairs={{0,12},{4,0},{8,4},{12,8},{1,13},{5,1},{9,5},{13,9},{2,14},{6,2},{... | collective-permute-start | bytes 393224 | tf_op jit(solution)/shard_map/ppermute | solution.py:490
  51.3 12.2 %collective-permute-start.4 = (bf16[2,128,256]{2,1,0:T(8,128)(2,1)S(1)}, bf16[2,128,256]{2,1,0:T(8,128)(2,1)S(1)}, u32[]{:S(2)}, u32[]{:S(2)}) collective-permute-start(bf16[2,128,256]{2,1,0:T(8,128)(2,1)S(1)} %get-tuple-element.24), channel_id=1, source_target_pairs={{0,8},{4,12},{8,0},{12,4},{1,9},{5,13},{9,1},{13,5},{2,10},{6,14},... | collective-permute-start | bytes 393224 | tf_op jit(solution)/shard_map/ppermute | solution.py:490
  51.7 11.8 %collective-permute-start.3 = (bf16[2,128,256]{2,1,0:T(8,128)(2,1)S(1)}, bf16[2,128,256]{2,1,0:T(8,128)(2,1)S(1)}, u32[]{:S(2)}, u32[]{:S(2)}) collective-permute-start(bf16[2,128,256]{2,1,0:T(8,128)(2,1)S(1)} %get-tuple-element.23), channel_id=1, source_target_pairs={{0,4},{4,8},{8,12},{12,0},{1,5},{5,9},{9,13},{13,1},{2,6},{6,10},{... | collective-permute-start | bytes 393224 | tf_op jit(solution)/shard_map/ppermute | solution.py:490

commit v3 on v2

v3 whole, which is shorter than its diff:
```python
import functools
import math

import jax
import jax.numpy as jnp
from jax import lax
from jax.experimental import pallas as pl
from jax.experimental.pallas import tpu as pltpu
from jax.sharding import PartitionSpec as P

HD = 128
NEG = -1e30
FIRST = 1
F32 = jnp.float32
BF16 = jnp.bfloat16


def dot(a, b, dims):
    return lax.dot_general(a, b, (dims, ((), ())), preferred_element_type=F32)


NN = ((1,), (0,))
NT = ((1,), (1,))
TN = ((0,), (0,))


def attend_group(slots, base, group_size, kv_heads, tokens, prefix_len, q, og, kv, prefix, lens, factors, out, self_out, prefix_out):
    scale = 1.0 / math.sqrt(HD)
    log_scale = scale * math.log2(math.e)
    whole = group_size - group_size % 2
    pairs = [(j, j + 1) if j + 1 < slots else (j, j) for j in range(0, slots, 2)]
    most = max(whole, 2) * tokens
    assert tokens & (tokens - 1) == 0
    lane = lax.broadcasted_iota(jnp.int32, (1, most), 1)
    token = lane & (tokens - 1)
    key = lax.broadcasted_iota(jnp.int32, (tokens, most), 0)
    causal = key <= (lax.broadcasted_iota(jnp.int32, (tokens, most), 1) & (tokens - 1))
    left = lane[:, : 2 * tokens] < tokens

    def head(k, h):
        at = (k * group_size + h) * HD
        return slice(at, at + HD)

    def rows(ref, k, blocks):
        return jnp.concatenate([ref[base + j, :, head(k, h)] for j, h in blocks], axis=0)

    class Heads:
        pass

    heads, chunks = [], []
    for k in range(kv_heads):
        t = Heads()
        t.cols = slice(k * HD, (k + 1) * HD)
        t.key_p, t.value_p = prefix[0, :, t.cols], prefix[1, :, t.cols]
        t.key_pt = t.key_p.T
        t.key_acc = t.value_acc = None
        t.key_self, t.value_self, t.left_over = {}, {}, 0
        heads.append(t)
        for pair in pairs:
            p = Heads()
            p.keys = [kv[base + j, 0, :, t.cols] for j in pair]
            p.values = [kv[base + j, 1, :, t.cols] for j in pair]
            p.key_pair = jnp.concatenate(p.keys, axis=0)
            p.value_pair = jnp.concatenate(p.values, axis=0)
            p.key_t = jnp.concatenate([t.key_pt, p.key_pair.T], axis=1)
            for n in range(2 if pair[0] != pair[1] else 1):
                c = Heads()
                c.k, c.t, c.p, c.pair, c.place = k, t, p, pair, n
                c.blocks = [(pair[n], h) for h in range(whole)]
                c.shared = False
                chunks.append(c)
            if group_size % 2:
                c = Heads()
                c.k, c.t, c.p, c.pair = k, t, p, pair
                c.blocks = [(j, group_size - 1) for j in pair]
                c.shared = True
                chunks.append(c)
        t.left_over = len([c for c in chunks if c.t is t])

    def own(both):
        return jnp.where(left, both[:tokens], both[tokens:])

    def spread(part):
        none = jnp.zeros_like(part)
        return jnp.concatenate([jnp.where(left, part, none), jnp.where(left, none, part)], axis=0)

    def products(c):
        t, p = c.t, c.p
        c.q_rows, c.g_rows = rows(q, c.k, c.blocks), rows(og, c.k, c.blocks)
        key_s, value_s = (
            (p.key_pair, p.value_pair) if c.shared else (p.keys[c.place], p.values[c.place])
        )
        c.scores = dot(jnp.concatenate([t.key_p, key_s], axis=0), c.q_rows, NT)
        c.gw = dot(jnp.concatenate([t.value_p, value_s], axis=0), c.g_rows, NT)

    def weigh(c):
        lanes = len(c.blocks) * tokens
        scores_p, scores_s = c.scores[:prefix_len], c.scores[prefix_len:]
        c.gw_p, c.gw_s = c.gw[:prefix_len], c.gw[prefix_len:]
        if c.shared:
            scores_s, c.gw_s = own(scores_s), own(c.gw_s)
        scores_s = jnp.where(causal[:, :lanes], scores_s, NEG)
        top = jnp.maximum(
            jnp.max(scores_p, axis=0, keepdims=True), jnp.max(scores_s, axis=0, keepdims=True)
        )
        c.e_p = jnp.exp2((scores_p - top) * log_scale)
        c.e_s = jnp.exp2((scores_s - top) * log_scale)
        total = jnp.sum(c.e_p, axis=0, keepdims=True) + jnp.sum(c.e_s, axis=0, keepdims=True)
        weighted = jnp.sum(c.e_p * c.gw_p, axis=0, keepdims=True) + jnp.sum(
            c.e_s * c.gw_s, axis=0, keepdims=True
        )
        if c.shared:
            first, second = c.pair
            length = jnp.where(left, lens[first], lens[second] if first != second else 0)
            gain = jnp.where(left, factors[first], factors[second])
        else:
            length, gain = lens[c.pair[c.place]], factors[c.pair[c.place]]
        inverse = 1.0 / total
        c.delta = weighted * inverse
        c.gain = inverse * jnp.where(token[:, :lanes] < length, gain, 0.0)

    def gradients(c):
        w_p, w_s = c.e_p * c.gain, c.e_s * c.gain
        d_p = (w_p * (c.gw_p - c.delta)).astype(BF16)
        d_s = (w_s * (c.gw_s - c.delta)).astype(BF16)
        w_p, w_s = w_p.astype(BF16), w_s.astype(BF16)
        if c.shared:
            d_s, w_s = spread(d_s), spread(w_s)
            c.d_all = c.d_wide = jnp.concatenate([d_p, d_s], axis=0)
        else:
            c.d_all = jnp.concatenate([d_p, d_s], axis=0)
            empty = jnp.zeros_like(d_s)
            c.d_wide = jnp.concatenate([d_p, d_s, empty] if c.place == 0 else [d_p, empty, d_s], axis=0)
        c.w_all = jnp.concatenate([w_p, w_s], axis=0)

    def outgoing(c):
        t = c.t
        q_grad = (dot(c.p.key_t, c.d_wide, NN) * scale).astype(BF16).T
        kg = dot(c.d_all, c.q_rows, NN)
        vg = dot(c.w_all, c.g_rows, NN)
        targets = list(dict.fromkeys(c.pair)) if c.shared else [c.pair[c.place]]
        for n, (j, h) in enumerate(c.blocks):
            if not c.shared or n < len(targets):
                out[base + j, :, head(c.k, h)] = q_grad[n * tokens : (n + 1) * tokens]
        t.key_acc = kg[:prefix_len] if t.key_acc is None else t.key_acc + kg[:prefix_len]
        t.value_acc = vg[:prefix_len] if t.value_acc is None else t.value_acc + vg[:prefix_len]
        for n, j in enumerate(targets):
            at = slice(prefix_len + n * tokens, prefix_len + (n + 1) * tokens)
            t.key_self.setdefault(j, []).append(kg[at])
            t.value_self.setdefault(j, []).append(vg[at])
        t.left_over -= 1
        if t.left_over == 0:
            for j in range(slots):
                self_out[base + j, 0, :, t.cols] = (sum(t.key_self[j]) * scale).astype(BF16)
                self_out[base + j, 1, :, t.cols] = sum(t.value_self[j]).astype(BF16)
            prefix_out[0, :, t.cols] = (t.key_acc * scale).astype(BF16)
            prefix_out[1, :, t.cols] = t.value_acc.astype(BF16)

    stages = (products, weigh, gradients, outgoing)
    for step in range(len(chunks) + len(stages) - 1):
        for late, stage in enumerate(stages):
            if 0 <= step - late < len(chunks):
                stage(chunks[step - late])


def group_kernel(turn, dims, refs):
    n_dp, count, slots, kv_heads, group_size, tokens, prefix_len = dims
    refs = list(refs)
    n_small = 2 + n_dp
    small_hbm = refs[:n_small]
    prompt_hbm, q_hbm, og_hbm, kv_hbm = refs[n_small : n_small + 4]
    refs = refs[n_small + 4 + (2 if turn != FIRST else 0) :]
    q_out, self_out, grads_out = refs[:3]
    resp_prompt, resp_len, *rewards = refs[3 : 3 + n_small]
    order, q, og, kv, prefix, out, own, grads, sem_small, sem_prefix, sem_in, sem_out = refs[3 + n_small :]
    me = lax.axis_index("dp")
    prompt = lax.rem(me + turn, n_dp)

    small = [
        pltpu.make_async_copy(src, dst, sem_small.at[n])
        for n, (src, dst) in enumerate(zip(small_hbm, (resp_prompt, resp_len, *rewards)))
    ]
    prefix_copy = pltpu.make_async_copy(prompt_hbm, prefix, sem_prefix.at[0])
    for copy in small + [prefix_copy]:
        copy.start()
    small[0].wait()
    found = 0
    for i in range(count):
        order[found] = i
        found = found + (resp_prompt[me * count + i] == prompt).astype(jnp.int32)

    picked = [order[j] for j in range(slots)]
    rows = [pl.ds(pl.multiple_of(i * tokens, tokens), tokens) for i in picked]
    copies_in, copies_out = [], []
    for j in range(slots):
        copies_in += [
            pltpu.make_async_copy(q_hbm.at[rows[j]], q.at[j], sem_in.at[j, 0]),
            pltpu.make_async_copy(og_hbm.at[rows[j]], og.at[j], sem_in.at[j, 1]),
            pltpu.make_async_copy(kv_hbm.at[0, rows[j]], kv.at[j, 0], sem_in.at[j, 2]),
            pltpu.make_async_copy(kv_hbm.at[1, rows[j]], kv.at[j, 1], sem_in.at[j, 3]),
        ]
        copies_out += [
            pltpu.make_async_copy(out.at[j], q_out.at[rows[j]], sem_out.at[j, 0]),
            pltpu.make_async_copy(own.at[j, 0], self_out.at[0, rows[j]], sem_out.at[j, 1]),
            pltpu.make_async_copy(own.at[j, 1], self_out.at[1, rows[j]], sem_out.at[j, 2]),
        ]
    for copy in copies_in:
        copy.start()

    for copy in small[1:]:
        copy.wait()
    total = jnp.float32(0.0)
    for away in range(n_dp):
        source = lax.rem(me + away, n_dp) * count
        for i in range(count):
            total += jnp.where(resp_prompt[source + i] == prompt, rewards[away][i], 0.0)
    lens = [resp_len[i] for i in picked]
    factors = [
        (rewards[0][i] - total / count) * (tokens / length.astype(F32))
        for i, length in zip(picked, lens)
    ]
    for copy in [prefix_copy] + copies_in:
        copy.wait()
    attend_group(
        slots, 0, group_size, kv_heads, tokens, prefix_len, q, og, kv, prefix, lens, factors, out, own, grads
    )
    last = pltpu.make_async_copy(grads, grads_out, sem_prefix.at[0])
    last.start()
    for copy in copies_out:
        copy.start()
    for copy in copies_out + [last]:
        copy.wait()


def near_grads(turn, dims, small, prompt, resp_q, out_grad, resp_kv, earlier):
    n_dp, count, slots, kv_heads, group_size, tokens, prefix_len = dims
    width = kv_heads * HD
    anywhere = pl.BlockSpec(memory_space=pltpu.HBM)
    operands = [*small, prompt, resp_q, out_grad, resp_kv, *earlier]
    lanes = resp_q.shape[1]
    return pl.pallas_call(
        lambda *refs: group_kernel(turn, dims, refs),
        out_shape=[
            jax.ShapeDtypeStruct(resp_q.shape, BF16),
            jax.ShapeDtypeStruct(resp_kv.shape, BF16),
            jax.ShapeDtypeStruct((2, prefix_len, width), BF16),
        ],
        in_specs=[anywhere] * len(operands),
        out_specs=[anywhere] * 3,
        input_output_aliases={len(operands) - 2: 0, len(operands) - 1: 1} if earlier else {},
        scratch_shapes=[
            *[pltpu.SMEM(x.shape, x.dtype) for x in small],
            pltpu.SMEM((slots + 1,), jnp.int32),
            pltpu.VMEM((slots, tokens, lanes), BF16),
            pltpu.VMEM((slots, tokens, lanes), BF16),
            pltpu.VMEM((slots, 2, tokens, width), BF16),
            pltpu.VMEM((2, prefix_len, width), BF16),
            pltpu.VMEM((slots, tokens, lanes), BF16),
            pltpu.VMEM((slots, 2, tokens, width), BF16),
            pltpu.VMEM((2, prefix_len, width), BF16),
            pltpu.SemaphoreType.DMA((len(small),)),
            pltpu.SemaphoreType.DMA((2,)),
            pltpu.SemaphoreType.DMA((slots, 4)),
            pltpu.SemaphoreType.DMA((slots, 3)),
        ],
        compiler_params=pltpu.CompilerParams(vmem_limit_bytes=48 * 1024 * 1024),
        cost_estimate=pl.CostEstimate(
            flops=2 * 5 * slots * tokens * group_size * kv_heads * (prefix_len + tokens) * HD,
            bytes_accessed=2 * slots * tokens * (3 * lanes + 4 * width),
            transcendentals=0,
        ),
        name="group_grads",
    )(*operands)


def far_kernel(dims, *refs):
    n_dp, count, slots, kv_heads, group_size, tokens, prefix_len = dims
    groups = count
    (resp_prompt, resp_len, rewards, q_hbm, og_hbm, kv_hbm, prompts, q_out, self_out, prefix_outs,
     totals, lens, factors, q, og, kv, prefix, out, own, grads, sem_in, sem_prefix, sem_out, sem_grads) = refs
    me = lax.axis_index("dp")
    width = kv_heads * HD

    for p in range(n_dp):
        totals[p] = 0.0

    def at_rows(slot):
        return pl.ds(pl.multiple_of(slot * tokens, tokens), tokens)

    def copies_in(slot):
        rows = at_rows(slot)
        return (
            pltpu.make_async_copy(q_hbm.at[rows], q.at[slot], sem_in.at[slot, 0]),
            pltpu.make_async_copy(og_hbm.at[rows], og.at[slot], sem_in.at[slot, 1]),
            pltpu.make_async_copy(kv_hbm.at[0, rows], kv.at[slot, 0], sem_in.at[slot, 2]),
            pltpu.make_async_copy(kv_hbm.at[1, rows], kv.at[slot, 1], sem_in.at[slot, 3]),
        )

    def prefix_copy(g):
        prompt = resp_prompt[me * count + g]
        return pltpu.make_async_copy(prompts.at[prompt], prefix.at[g], sem_prefix.at[g])

    def copies_out(slot):
        rows = at_rows(slot)
        return (
            pltpu.make_async_copy(out.at[slot], q_out.at[rows], sem_out.at[slot, 0]),
            pltpu.make_async_copy(own.at[slot, 0], self_out.at[0, rows], sem_out.at[slot, 1]),
            pltpu.make_async_copy(own.at[slot, 1], self_out.at[1, rows], sem_out.at[slot, 2]),
        )

    def grads_copy(g):
        return pltpu.make_async_copy(grads.at[g], prefix_outs.at[g], sem_grads.at[g])

    for g in range(groups):
        prefix_copy(g).start()

        def start(n, _):
            for copy in copies_in(g * slots + n):
                copy.start()
            return 0

        lax.fori_loop(0, slots, start, 0)

    def add(i, _):
        prompt = resp_prompt[i]
        totals[prompt] = totals[prompt] + rewards[i]
        return 0

    lax.fori_loop(0, n_dp * count, add, 0)

    def find_factor(slot, _):
        length = resp_len[slot]
        place = me * count + slot
        advantage = rewards[place] - totals[resp_prompt[place]] / count
        lens[slot] = length
        factors[slot] = advantage * (tokens / length.astype(F32))
        return 0

    lax.fori_loop(0, count, find_factor, 0)

    def one_group(g, _):
        base = g * slots

        def wait(n, _):
            for copy in copies_in(base + n):
                copy.wait()
            return 0

        lax.fori_loop(0, slots, wait, 0)
        attend_group(
            slots, base, group_size, kv_heads, tokens, prefix_len, q, og, kv, prefix.at[g],
            [lens[base + j] for j in range(slots)], [factors[base + j] for j in range(slots)],
            out, own, grads.at[g],
        )

        def send(n, _):
            for copy in copies_out(base + n):
                copy.start()
            return 0

        lax.fori_loop(0, slots, send, 0)
        return 0

    for g in range(groups):
        prefix_copy(g).wait()
    lax.fori_loop(0, groups, one_group, 0)
    for g in range(groups):
        grads_copy(g).start()

    def finish(slot, _):
        for copy in copies_out(slot):
            copy.wait()
        return 0

    lax.fori_loop(0, count, finish, 0)
    for g in range(groups):
        grads_copy(g).wait()


def far_shards(dims, prompt_kv, resp_q, resp_kv, out_grad, rewards, resp_prompt, resp_len, my_prompts):
    n_dp, count, slots, kv_heads, group_size, tokens, prefix_len = dims
    assert slots == 1
    width = kv_heads * HD
    lanes = resp_q.shape[1]
    smem = pl.BlockSpec(memory_space=pltpu.SMEM)
    anywhere = pl.BlockSpec(memory_space=pl.ANY)
    q_out, self_out, per_resp = pl.pallas_call(
        functools.partial(far_kernel, dims),
        out_shape=[
            jax.ShapeDtypeStruct(resp_q.shape, BF16),
            jax.ShapeDtypeStruct(resp_kv.shape, BF16),
            jax.ShapeDtypeStruct((count, 2, prefix_len, width), BF16),
        ],
        in_specs=[smem] * 3 + [anywhere] * 4,
        out_specs=[anywhere] * 3,
        scratch_shapes=[
            pltpu.SMEM((n_dp,), F32),
            pltpu.SMEM((count,), jnp.int32),
            pltpu.SMEM((count,), F32),
            pltpu.VMEM((count, tokens, lanes), BF16),
            pltpu.VMEM((count, tokens, lanes), BF16),
            pltpu.VMEM((count, 2, tokens, width), BF16),
            pltpu.VMEM((count, 2, prefix_len, width), BF16),
            pltpu.VMEM((count, tokens, lanes), BF16),
            pltpu.VMEM((count, 2, tokens, width), BF16),
            pltpu.VMEM((count, 2, prefix_len, width), BF16),
            pltpu.SemaphoreType.DMA((count, 4)),
            pltpu.SemaphoreType.DMA((count,)),
            pltpu.SemaphoreType.DMA((count, 3)),
            pltpu.SemaphoreType.DMA((count,)),
        ],
        compiler_params=pltpu.CompilerParams(vmem_limit_bytes=48 * 1024 * 1024),
        name="far_grads",
    )(
        resp_prompt,
        resp_len,
        lax.all_gather(rewards, "dp", axis=0, tiled=True),
        resp_q,
        out_grad,
        resp_kv,
        lax.all_gather(prompt_kv, "dp", axis=0),
    )
    route = (jnp.arange(n_dp, dtype=jnp.int32)[:, None] == my_prompts[None, :]).astype(BF16)
    outgoing = jnp.dot(route, per_resp.reshape(count, -1), preferred_element_type=F32).astype(BF16)
    outgoing = outgoing.reshape((n_dp,) + prompt_kv.shape)
    incoming = lax.all_to_all(outgoing, "dp", split_axis=0, concat_axis=0, tiled=True)
    prefix_out = jnp.sum(incoming, axis=0, dtype=F32).astype(BF16)
    return (q_out, self_out, prefix_out)


def shards(prompt_kv, resp_q, resp_kv, out_grad, rewards, resp_prompt, resp_len):
    n_dp = lax.axis_size("dp")
    count = rewards.shape[0]
    tokens = resp_q.shape[0] // count
    prefix_len, width = prompt_kv.shape[1:]
    kv_heads = width // HD
    group_size = resp_q.shape[1] // width
    slots = (count + n_dp - 1) // n_dp
    dims = (n_dp, count, slots, kv_heads, group_size, tokens, prefix_len)
    my_prompts = lax.dynamic_slice_in_dim(resp_prompt, lax.axis_index("dp") * count, count)
    if count // slots != n_dp:
        return far_shards(dims, prompt_kv, resp_q, resp_kv, out_grad, rewards, resp_prompt, resp_len, my_prompts)

    def from_ahead(x, s):
        return lax.ppermute(x, "dp", [((i + s) % n_dp, i) for i in range(n_dp)])

    all_rewards = [rewards] + [from_ahead(rewards, s) for s in range(1, n_dp)]
    prompts = [prompt_kv] + [from_ahead(prompt_kv, s) for s in range(1, n_dp)]
    earlier = ()
    arrived = []
    for turn in [*range(FIRST, n_dp), *range(FIRST)]:
        *earlier, grads = near_grads(
            turn, dims, (resp_prompt, resp_len, *all_rewards), prompts[turn], resp_q, out_grad, resp_kv, earlier
        )
        if turn:
            grads = lax.ppermute(grads, "dp", [(i, (i + turn) % n_dp) for i in range(n_dp)])
        arrived.append(grads)
    prefix_out = sum(part.astype(F32) for part in arrived).astype(BF16)
    return (*earlier, prefix_out)


def solution(mesh):
    in_specs = (
        P(None, ("groups", "dp"), "tensor"),
        P(("groups", "dp"), "tensor"),
        P(None, ("groups", "dp"), "tensor"),
        P(("groups", "dp"), "tensor"),
        P(("groups", "dp")),
        P("groups"),
        P(("groups", "dp")),
    )
    out_specs = (
        P(("groups", "dp"), "tensor"),
        P(None, ("groups", "dp"), "tensor"),
        P(None, ("groups", "dp"), "tensor"),
    )
    return jax.shard_map(shards, mesh=mesh, in_specs=in_specs, out_specs=out_specs, check_vma=False)
```

time: 64.6 us -> 57.8 us (0.89)
  Pallas kernels: 30.9 us -> 23.2 us
  starting transfers between devices: 12.4 us -> 17.1 us
  other arithmetic: 3.05 us -> 0.72 us
  waiting for transfers between devices: 12.2 us -> 10.7 us
    pallas_call x4, Pallas kernels: 30.9 us -> 23.2 us  [near_grads(): pl.pallas_call(lambda *refs: group_kernel(turn, dims, refs), out_shape=[j...]
    ppermute x3 -> x6, starting transfers between devices: 7.01 us -> 11.1 us  [from_ahead(): return lax.ppermute(x, 'dp', [((i + s) % n_dp, i) for i in range(n_dp)])]
    another operation x3 -> x0, other arithmetic: 1.41 us -> none  [make_payload(): rows = jnp.stack([high, middle, low, my_prompts.astype(F32)]).astype(BF16)]
    ppermute x3, waiting for transfers between devices: 3.83 us -> 2.84 us  [shards(): lax.ppermute(grads, 'dp', [(i, (i + turn) % n_dp) for i in range(n_dp)])]
    concatenate x1 -> x0, other arithmetic: 0.92 us -> none  [make_payload(): jnp.concatenate([prompt_kv, jnp.broadcast_to(rows, (2,) + rows.shape)], a...]
    ppermute x3 -> x6, waiting for transfers between devices: 8.35 us -> 7.9 us  [from_ahead(): return lax.ppermute(x, 'dp', [((i + s) % n_dp, i) for i in range(n_dp)])]
    unnamed x10 -> x16, local copies, waits for them, and re-layouts: 4.93 us -> 4.94 us
  transfers between devices with their start and end apart: 6 -> 9, of which waited for: 3 -> 4; matrix products, arithmetic and copies ran while one was open for 0% -> 0% of each run, Pallas kernels for 12% -> 30%
where the time goes in v3:
time: 57.8 us; the launch traced here: 57.5 us
  Pallas kernels  23.2 us (40%)
  starting transfers between devices  17.1 us (30%)
  waiting for transfers between devices  10.7 us (19%)
  local copies, waits for them, and re-layouts  4.94 us (9%)
  between operations  0.73 us (1%)
  other arithmetic  0.72 us (1%)
    pallas_call x4, Pallas kernels, near_grads(): pl.pallas_call(lambda *refs: group_kernel(turn, dims, refs), out_shape=[j...  23.2 us
    ppermute x6, starting transfers between devices, from_ahead(): return lax.ppermute(x, 'dp', [((i + s) % n_dp, i) for i in range(n_dp)])  11.1 us
    ppermute x6, waiting for transfers between devices, from_ahead(): return lax.ppermute(x, 'dp', [((i + s) % n_dp, i) for i in range(n_dp)])  7.9 us
    ppermute x3, starting transfers between devices, shards(): lax.ppermute(grads, 'dp', [(i, (i + turn) % n_dp) for i in range(n_dp)])  5.98 us
    unnamed x16, local copies, waits for them, and re-layouts  4.94 us
    ppermute x3, waiting for transfers between devices, shards(): lax.ppermute(grads, 'dp', [(i, (i + turn) % n_dp) for i in range(n_dp)])  2.84 us
  transfers between devices with their start and end apart: 9, of which 4 were waited for; matrix products, arithmetic and copies ran while one was open for 0% of the time, Pallas kernels for 30%

profile of v3, /device:TPU:0, one launch (start us, length us, event | category | flops | bytes accessed | tf_op | source)
XLA Modules:
  0.0 57.5 jit_solution(17865520072498320578)
XLA Ops:
  0.6 5.1 %collective-permute-start.5 = (bf16[2,128,256]{2,1,0:T(8,128)(2,1)}, bf16[2,128,256]{2,1,0:T(8,128)(2,1)S(1)}, u32[]{:S(2)}, u32[]{:S(2)}) collective-permute-start(bf16[2,128,256]{2,1,0:T(8,128)(2,1)} %refs_6_.1), channel_id=1, source_target_pairs={{4,0},{8,4},{12,8},{0,12},{5,1},{9,5},{13,9},{1,13},{6,2},{10,6},{... | collective-permute-start | bytes 393224 | tf_op jit(solution)/shard_map/ppermute | solution.py:445
  5.7 0.0 collective-permute-start.4
  5.7 1.0 %collective-permute-start.3 = (bf16[2,128,256]{2,1,0:T(8,128)(2,1)}, bf16[2,128,256]{2,1,0:T(8,128)(2,1)S(1)}, u32[]{:S(2)}, u32[]{:S(2)}) collective-permute-start(bf16[2,128,256]{2,1,0:T(8,128)(2,1)} %refs_6_.1), channel_id=1, source_target_pairs={{12,0},{0,4},{4,8},{8,12},{13,1},{1,5},{5,9},{9,13},{14,2},{2,6},{... | collective-permute-start | bytes 393224 | tf_op jit(solution)/shard_map/ppermute | solution.py:445
  6.7 2.5 %collective-permute-start.2 = (f32[16]{0:T(128)}, f32[16]{0:T(128)S(1)}, u32[]{:S(2)}, u32[]{:S(2)}) collective-permute-start(f32[16]{0:T(128)} %refs_2_.7), channel_id=1, source_target_pairs={{12,0},{0,4},{4,8},{8,12},{13,1},{1,5},{5,9},{9,13},{14,2},{2,6},{... | collective-permute-start | bytes 200 | tf_op jit(solution)/shard_map/ppermute | solution.py:445
  9.2 0.9 %collective-permute-start.1 = (f32[16]{0:T(128)}, f32[16]{0:T(128)S(1)}, u32[]{:S(2)}, u32[]{:S(2)}) collective-permute-start(f32[16]{0:T(128)} %refs_2_.7), channel_id=1, source_target_pairs={{8,0},{12,4},{0,8},{4,12},{9,1},{13,5},{1,9},{5,13},{10,2},{14,6},... | collective-permute-start | bytes 200 | tf_op jit(solution)/shard_map/ppermute | solution.py:445
  10.1 5.3 %collective-permute-done.2.refs_5_ = f32[16]{0:T(128)S(1)} collective-permute-done((f32[16]{0:T(128)}, f32[16]{0:T(128)S(1)}, u32[]{:S(2)}, u32[]{:S(2)}) %collective-permute-start.2) | collective-permute-done | bytes 96 | tf_op jit(solution)/shard_map/ppermute | solution.py:445
  15.4 1.6 %collective-permute-start = (f32[16]{0:T(128)}, f32[16]{0:T(128)S(1)}, u32[]{:S(2)}, u32[]{:S(2)}) collective-permute-start(f32[16]{0:T(128)} %refs_2_.7), channel_id=1, source_target_pairs={{4,0},{8,4},{12,8},{0,12},{5,1},{9,5},{13,9},{1,13},{6,2},{10,6},{... | collective-permute-start | bytes 200 | tf_op jit(solution)/shard_map/ppermute | solution.py:445
  17.0 0.2 collective-permute-done.1.refs_4_
  17.2 2.4 %collective-permute-done.refs_3_ = f32[16]{0:T(128)S(1)} collective-permute-done((f32[16]{0:T(128)}, f32[16]{0:T(128)S(1)}, u32[]{:S(2)}, u32[]{:S(2)}) %collective-permute-start) | collective-permute-done | bytes 96 | tf_op jit(solution)/shard_map/ppermute | solution.py:445
  19.6 0.0 collective-permute-done.5.refs_6_
  19.6 1.7 %copy-done = bf16[1024,1280]{1,0:T(8,128)(2,1)S(1)} copy-done((bf16[1024,1280]{1,0:T(8,128)(2,1)S(1)}, bf16[1024,1280]{1,0:T(8,128)(2,1)}, u32[]{:S(2)}) %copy-start) | copy-done | bytes 2621464
  21.4 1.2 %copy-done.2 = bf16[2,1024,256]{2,1,0:T(8,128)(2,1)S(1)} copy-done((bf16[2,1024,256]{2,1,0:T(8,128)(2,1)S(1)}, bf16[2,1024,256]{2,1,0:T(8,128)(2,1)}, u32[]{:S(2)}) %copy-start.2) | copy-done | bytes 1048600
  22.6 0.7 %copy-done.5 = s32[64]{0:T(128)S(1)} copy-done((s32[64]{0:T(128)S(1)}, s32[64]{0:T(128)}, u32[]{:S(2)}) %copy-start.5) | copy-done | bytes 280
  23.3 0.7 %copy-done.6 = s32[16]{0:T(128)S(1)} copy-done((s32[16]{0:T(128)S(1)}, s32[16]{0:T(128)}, u32[]{:S(2)}) %copy-start.6) | copy-done | bytes 88
  23.9 0.7 %copy-done.7 = f32[16]{0:T(128)S(1)} copy-done((f32[16]{0:T(128)S(1)}, f32[16]{0:T(128)}, u32[]{:S(2)}) %copy-start.7) | copy-done | bytes 88
  24.6 5.8 %group_grads.4 = (bf16[1024,1280]{1,0:T(8,128)(2,1)}, bf16[2,1024,256]{2,1,0:T(8,128)(2,1)}, bf16[2,128,256]{2,1,0:T(8,128)(2,1)S(1)}) custom-call(s32[64]{0:T(128)S(1)} %copy-done.5, s32[16]{0:T(128)S(1)} %copy-done.6, f32[16]{0:T(128)S(1)} %copy-done.7, f32[16]{0:T(128)S(1)} %collective-permute-done.refs_3_, f32[16]{0:T(128)S(1)} %collective-permute-done.1.refs_4_, ...), custom_call_target="tpu_custom_call" | custom-call | flops 629145600 | bytes 2490368 | tf_op jit(solution)/shard_map/group_grads/pallas_call | solution.py:241
  30.4 0.0 collective-permute-done.4.refs_6_
  30.4 0.0 copy-done.1
  30.4 0.0 copy-done.3
  30.4 5.8 %group_grads.5 = (bf16[1024,1280]{1,0:T(8,128)(2,1)}, bf16[2,1024,256]{2,1,0:T(8,128)(2,1)}, bf16[2,128,256]{2,1,0:T(8,128)(2,1)S(1)}) custom-call(s32[64]{0:T(128)S(1)} %copy-done.5, s32[16]{0:T(128)S(1)} %copy-done.6, f32[16]{0:T(128)S(1)} %copy-done.7, f32[16]{0:T(128)S(1)} %collective-permute-done.refs_3_, ...), custom_call_target="tpu_custom_call", output_to_operand_aliasing={{0}: (10, {}), {1}: (11, {})} | custom-call | flops 629145600 | bytes 2490368 | tf_op jit(solution)/shard_map/group_grads/pallas_call | solution.py:241
  36.3 0.0 collective-permute-done.3.refs_6_
  36.3 0.0 copy-start.4
  36.3 5.8 %group_grads.6 = (bf16[1024,1280]{1,0:T(8,128)(2,1)}, bf16[2,1024,256]{2,1,0:T(8,128)(2,1)}, bf16[2,128,256]{2,1,0:T(8,128)(2,1)S(1)}) custom-call(s32[64]{0:T(128)S(1)} %copy-done.5, s32[16]{0:T(128)S(1)} %copy-done.6, f32[16]{0:T(128)S(1)} %copy-done.7, f32[16]{0:T(128)S(1)} %collective-permute-done.refs_3_, ...), custom_call_target="tpu_custom_call", output_to_operand_aliasing={{0}: (10, {}), {1}: (11, {})} | custom-call | flops 629145600 | bytes 2490368 | tf_op jit(solution)/shard_map/group_grads/pallas_call | solution.py:241
  42.1 3.2 %collective-permute-start.8 = (bf16[2,128,256]{2,1,0:T(8,128)(2,1)S(1)}, bf16[2,128,256]{2,1,0:T(8,128)(2,1)S(1)}, u32[]{:S(2)}, u32[]{:S(2)}) collective-permute-start(bf16[2,128,256]{2,1,0:T(8,128)(2,1)S(1)} %get-tuple-element.25), channel_id=1, source_target_pairs={{0,12},{4,0},{8,4},{12,8},{1,13},{5,1},{9,5},{13,9},{2,14},{6,2},{... | collective-permute-start | bytes 393224 | tf_op jit(solution)/shard_map/ppermute | solution.py:456
  45.3 0.9 %collective-permute-start.7 = (bf16[2,128,256]{2,1,0:T(8,128)(2,1)S(1)}, bf16[2,128,256]{2,1,0:T(8,128)(2,1)S(1)}, u32[]{:S(2)}, u32[]{:S(2)}) collective-permute-start(bf16[2,128,256]{2,1,0:T(8,128)(2,1)S(1)} %get-tuple-element.24), channel_id=1, source_target_pairs={{0,8},{4,12},{8,0},{12,4},{1,9},{5,13},{9,1},{13,5},{2,10},{6,14},... | collective-permute-start | bytes 393224 | tf_op jit(solution)/shard_map/ppermute | solution.py:456
  46.1 1.9 %collective-permute-start.6 = (bf16[2,128,256]{2,1,0:T(8,128)(2,1)S(1)}, bf16[2,128,256]{2,1,0:T(8,128)(2,1)S(1)}, u32[]{:S(2)}, u32[]{:S(2)}) collective-permute-start(bf16[2,128,256]{2,1,0:T(8,128)(2,1)S(1)} %get-tuple-element.23), channel_id=1, source_target_pairs={{0,4},{4,8},{8,12},{12,0},{1,5},{5,9},{9,13},{13,1},{2,6},{6,10},{... | collective-permute-start | bytes 393224 | tf_op jit(solution)/shard_map/ppermute | solution.py:456
  48.1 0.0 copy-done.4
  48.1 5.8 %group_grads.7 = (bf16[1024,1280]{1,0:T(8,128)(2,1)}, bf16[2,1024,256]{2,1,0:T(8,128)(2,1)}, bf16[2,128,256]{2,1,0:T(8,128)(2,1)S(1)}) custom-call(s32[64]{0:T(128)S(1)} %copy-done.5, s32[16]{0:T(128)S(1)} %copy-done.6, f32[16]{0:T(128)S(1)} %copy-done.7, f32[16]{0:T(128)S(1)} %collective-permute-done.refs_3_, ...), custom_call_target="tpu_custom_call", output_to_operand_aliasing={{0}: (10, {}), {1}: (11, {})} | custom-call | flops 629145600 | bytes 2490368 | tf_op jit(solution)/shard_map/group_grads/pallas_call | solution.py:241
  53.9 0.0 collective-permute-done.8
  53.9 2.8 %collective-permute-done.7 = bf16[2,128,256]{2,1,0:T(8,128)(2,1)S(1)} collective-permute-done((bf16[2,128,256]{2,1,0:T(8,128)(2,1)S(1)}, bf16[2,128,256]{2,1,0:T(8,128)(2,1)S(1)}, u32[]{:S(2)}, u32[]{:S(2)}) %collective-permute-start.7) | collective-permute-done | bytes 131104 | tf_op jit(solution)/shard_map/ppermute | solution.py:456
  56.7 0.0 collective-permute-done.6
  56.7 0.7 %add_convert_fusion = bf16[2,128,256]{2,1,0:T(8,128)(2,1)} fusion(bf16[2,128,256]{2,1,0:T(8,128)(2,1)S(1)} %get-tuple-element.26, bf16[2,128,256]{2,1,0:T(8,128)(2,1)S(1)} %collective-permute-done.8, bf16[2,128,256]{2,1,0:T(8,128)(2,1)S(1)} %collective-permute-done.7, bf16[2,128,256]{2,1,0:T(8,128)(2,1)S(1)} %collective-permute-done.6), kind=kLoop, calls=%fused_computation | loop fusion | flops 524288 | bytes 655360 | tf_op jit(solution)/shard_map/convert_element_type | solution.py:458
  (7 shorter events, 0.0 us)
Async XLA Ops:
  0.6 19.0 %collective-permute-start.5 = (bf16[2,128,256]{2,1,0:T(8,128)(2,1)}, bf16[2,128,256]{2,1,0:T(8,128)(2,1)S(1)}, u32[]{:S(2)}, u32[]{:S(2)}) collective-permute-start(bf16[2,128,256]{2,1,0:T(8,128)(2,1)} %refs_6_.1), channel_id=1, source_target_pairs={{4,0},{8,4},{12,8},{0,12},{5,1},{9,5},{13,9},{1,13},{6,2},{10,6},{... | collective-permute-start | bytes 393224 | tf_op jit(solution)/shard_map/ppermute | solution.py:445
  5.7 24.7 %collective-permute-start.4 = (bf16[2,128,256]{2,1,0:T(8,128)(2,1)}, bf16[2,128,256]{2,1,0:T(8,128)(2,1)S(1)}, u32[]{:S(2)}, u32[]{:S(2)}) collective-permute-start(bf16[2,128,256]{2,1,0:T(8,128)(2,1)} %refs_6_.1), channel_id=1, source_target_pairs={{8,0},{12,4},{0,8},{4,12},{9,1},{13,5},{1,9},{5,13},{10,2},{14,6},... | collective-permute-start | bytes 393224 | tf_op jit(solution)/shard_map/ppermute | solution.py:445
  5.7 30.5 %collective-permute-start.3 = (bf16[2,128,256]{2,1,0:T(8,128)(2,1)}, bf16[2,128,256]{2,1,0:T(8,128)(2,1)S(1)}, u32[]{:S(2)}, u32[]{:S(2)}) collective-permute-start(bf16[2,128,256]{2,1,0:T(8,128)(2,1)} %refs_6_.1), channel_id=1, source_target_pairs={{12,0},{0,4},{4,8},{8,12},{13,1},{1,5},{5,9},{9,13},{14,2},{2,6},{... | collective-permute-start | bytes 393224 | tf_op jit(solution)/shard_map/ppermute | solution.py:445
  6.7 8.6 %collective-permute-start.2 = (f32[16]{0:T(128)}, f32[16]{0:T(128)S(1)}, u32[]{:S(2)}, u32[]{:S(2)}) collective-permute-start(f32[16]{0:T(128)} %refs_2_.7), channel_id=1, source_target_pairs={{12,0},{0,4},{4,8},{8,12},{13,1},{1,5},{5,9},{9,13},{14,2},{2,6},{... | collective-permute-start | bytes 200 | tf_op jit(solution)/shard_map/ppermute | solution.py:445
  9.2 8.0 %collective-permute-start.1 = (f32[16]{0:T(128)}, f32[16]{0:T(128)S(1)}, u32[]{:S(2)}, u32[]{:S(2)}) collective-permute-start(f32[16]{0:T(128)} %refs_2_.7), channel_id=1, source_target_pairs={{8,0},{12,4},{0,8},{4,12},{9,1},{13,5},{1,9},{5,13},{10,2},{14,6},... | collective-permute-start | bytes 200 | tf_op jit(solution)/shard_map/ppermute | solution.py:445
  15.4 4.2 %collective-permute-start = (f32[16]{0:T(128)}, f32[16]{0:T(128)S(1)}, u32[]{:S(2)}, u32[]{:S(2)}) collective-permute-start(f32[16]{0:T(128)} %refs_2_.7), channel_id=1, source_target_pairs={{4,0},{8,4},{12,8},{0,12},{5,1},{9,5},{13,9},{1,13},{6,2},{10,6},{... | collective-permute-start | bytes 200 | tf_op jit(solution)/shard_map/ppermute | solution.py:445
  19.6 1.7 %copy-start = (bf16[1024,1280]{1,0:T(8,128)(2,1)S(1)}, bf16[1024,1280]{1,0:T(8,128)(2,1)}, u32[]{:S(2)}) copy-start(bf16[1024,1280]{1,0:T(8,128)(2,1)} %refs_7_.7) | copy-start | bytes 7864324
  21.4 1.2 %copy-start.2 = (bf16[2,1024,256]{2,1,0:T(8,128)(2,1)S(1)}, bf16[2,1024,256]{2,1,0:T(8,128)(2,1)}, u32[]{:S(2)}) copy-start(bf16[2,1024,256]{2,1,0:T(8,128)(2,1)} %refs_9_.7) | copy-start | bytes 3145732
  22.6 0.7 %copy-start.5 = (s32[64]{0:T(128)S(1)}, s32[64]{0:T(128)}, u32[]{:S(2)}) copy-start(s32[64]{0:T(128)} %refs_0_.7) | copy-start | bytes 772
  23.3 0.7 %copy-start.6 = (s32[16]{0:T(128)S(1)}, s32[16]{0:T(128)}, u32[]{:S(2)}) copy-start(s32[16]{0:T(128)} %refs_1_.7) | copy-start | bytes 196
  23.9 0.7 %copy-start.7 = (f32[16]{0:T(128)S(1)}, f32[16]{0:T(128)}, u32[]{:S(2)}) copy-start(f32[16]{0:T(128)} %refs_2_.7) | copy-start | bytes 196
  24.6 5.8 %copy-start.1 = (bf16[1024,1280]{1,0:T(8,128)(2,1)S(1)}, bf16[1024,1280]{1,0:T(8,128)(2,1)}, u32[]{:S(2)}) copy-start(bf16[1024,1280]{1,0:T(8,128)(2,1)} %refs_7_.7) | copy-start | bytes 7864324
  24.6 5.8 %copy-start.3 = (bf16[2,1024,256]{2,1,0:T(8,128)(2,1)S(1)}, bf16[2,1024,256]{2,1,0:T(8,128)(2,1)}, u32[]{:S(2)}) copy-start(bf16[2,1024,256]{2,1,0:T(8,128)(2,1)} %refs_9_.7) | copy-start | bytes 3145732
  36.3 11.8 %copy-start.4 = (bf16[2,128,256]{2,1,0:T(8,128)(2,1)S(1)}, bf16[2,128,256]{2,1,0:T(8,128)(2,1)}, u32[]{:S(2)}) copy-start(bf16[2,128,256]{2,1,0:T(8,128)(2,1)} %refs_6_.1) | copy-start | bytes 393220
  42.1 11.8 %collective-permute-start.8 = (bf16[2,128,256]{2,1,0:T(8,128)(2,1)S(1)}, bf16[2,128,256]{2,1,0:T(8,128)(2,1)S(1)}, u32[]{:S(2)}, u32[]{:S(2)}) collective-permute-start(bf16[2,128,256]{2,1,0:T(8,128)(2,1)S(1)} %get-tuple-element.25), channel_id=1, source_target_pairs={{0,12},{4,0},{8,4},{12,8},{1,13},{5,1},{9,5},{13,9},{2,14},{6,2},{... | collective-permute-start | bytes 393224 | tf_op jit(solution)/shard_map/ppermute | solution.py:456
  45.3 11.5 %collective-permute-start.7 = (bf16[2,128,256]{2,1,0:T(8,128)(2,1)S(1)}, bf16[2,128,256]{2,1,0:T(8,128)(2,1)S(1)}, u32[]{:S(2)}, u32[]{:S(2)}) collective-permute-start(bf16[2,128,256]{2,1,0:T(8,128)(2,1)S(1)} %get-tuple-element.24), channel_id=1, source_target_pairs={{0,8},{4,12},{8,0},{12,4},{1,9},{5,13},{9,1},{13,5},{2,10},{6,14},... | collective-permute-start | bytes 393224 | tf_op jit(solution)/shard_map/ppermute | solution.py:456
  46.1 10.6 %collective-permute-start.6 = (bf16[2,128,256]{2,1,0:T(8,128)(2,1)S(1)}, bf16[2,128,256]{2,1,0:T(8,128)(2,1)S(1)}, u32[]{:S(2)}, u32[]{:S(2)}) collective-permute-start(bf16[2,128,256]{2,1,0:T(8,128)(2,1)S(1)} %get-tuple-element.23), channel_id=1, source_target_pairs={{0,4},{4,8},{8,12},{12,0},{1,5},{5,9},{9,13},{13,1},{2,6},{6,10},{... | collective-permute-start | bytes 393224 | tf_op jit(solution)/shard_map/ppermute | solution.py:456

commit v4 on v0

v4 whole, which is shorter than its diff:
```python
import functools
import math
from typing import NamedTuple

import jax
import jax.numpy as jnp
from jax import lax
from jax.experimental import pallas as pl
from jax.experimental.pallas import tpu as pltpu
from jax.sharding import PartitionSpec as P

HD = 128
NEG = -1e30
TAIL = 16
F32 = jnp.float32
BF16 = jnp.bfloat16
VMEM_BYTES = 63 * 1024 * 1024
ANYWHERE = pl.BlockSpec(memory_space=pl.ANY)


class Sizes(NamedTuple):
    n_dp: int
    count: int
    slots: int
    kv_heads: int
    group_size: int
    tokens: int
    prefix_len: int

    @property
    def width(self):
        return self.kv_heads * HD

    @property
    def lanes(self):
        return self.kv_heads * self.group_size * HD


def dot(a, b, dims):
    return lax.dot_general(a, b, (dims, ((), ())), preferred_element_type=F32)


NN = ((1,), (0,))
NT = ((1,), (1,))


class Bag:
    pass


def attend_pair(z, at, q, og, kv, prefix, lens, factors, out, own_out, sink, apart):
    tokens, prefix_len, group_size = z.tokens, z.prefix_len, z.group_size
    scale = 1.0 / math.sqrt(HD)
    log_scale = scale * math.log2(math.e)
    whole = group_size - group_size % 2
    single = len(at) == 1
    members = range(len(at))
    sides = (0, 0) if single else (0, 1)
    most = max(whole, 2) * tokens
    assert tokens & (tokens - 1) == 0
    token = lax.broadcasted_iota(jnp.int32, (1, most), 1) & (tokens - 1)
    key = lax.broadcasted_iota(jnp.int32, (tokens, most), 0)
    causal = key <= (lax.broadcasted_iota(jnp.int32, (tokens, most), 1) & (tokens - 1))
    left = lax.broadcasted_iota(jnp.int32, (1, 2 * tokens), 1) < tokens

    def head(k, h):
        start = (k * group_size + h) * HD
        return slice(start, start + HD)

    def rows(ref, k, blocks):
        return jnp.concatenate([ref[at[n], :, head(k, h)] for n, h in blocks], axis=0)

    def halves(part):
        none = jnp.zeros_like(part)
        return [jnp.where(left, part, none), jnp.where(left, none, part)]

    chunks = []
    for k in range(z.kv_heads):
        t = Bag()
        t.cols = slice(k * HD, (k + 1) * HD)
        t.key_p, t.value_p = prefix[0, :, t.cols], prefix[1, :, t.cols]
        t.keys = [kv[at[n], 0, :, t.cols] for n in sides]
        t.values = [kv[at[n], 1, :, t.cols] for n in sides]
        t.key_pair = jnp.concatenate(t.keys, axis=0)
        t.value_pair = jnp.concatenate(t.values, axis=0)
        t.key_t = jnp.concatenate([t.key_p.T, t.key_pair.T], axis=1)
        t.prefix_sums = {n: [] for n in members}
        t.self_sums = {n: [] for n in members}
        mine = []
        for n in members:
            c = Bag()
            c.k, c.t, c.side, c.blocks = k, t, n, [(n, h) for h in range(whole)]
            mine.append(c)
        if group_size % 2:
            c = Bag()
            c.k, c.t, c.side, c.blocks = k, t, None, [(n, group_size - 1) for n in sides]
            mine.append(c)
        t.left_over = len(mine)
        chunks += mine

    def products(c):
        t = c.t
        c.q_rows, c.g_rows = rows(q, c.k, c.blocks), rows(og, c.k, c.blocks)
        if c.side is None:
            key_s, value_s = t.key_pair, t.value_pair
        else:
            key_s, value_s = t.keys[c.side], t.values[c.side]
        c.scores = dot(jnp.concatenate([t.key_p, key_s], axis=0), c.q_rows, NT)
        c.gw = dot(jnp.concatenate([t.value_p, value_s], axis=0), c.g_rows, NT)

    def weigh(c):
        lanes = len(c.blocks) * tokens
        scores_p, scores_s = c.scores[:prefix_len], c.scores[prefix_len:]
        c.gw_p, c.gw_s = c.gw[:prefix_len], c.gw[prefix_len:]
        if c.side is None:
            scores_s = jnp.where(left, scores_s[:tokens], scores_s[tokens:])
            c.gw_s = jnp.where(left, c.gw_s[:tokens], c.gw_s[tokens:])
        scores_s = jnp.where(causal[:, :lanes], scores_s, NEG)
        top = jnp.maximum(
            jnp.max(scores_p, axis=0, keepdims=True), jnp.max(scores_s, axis=0, keepdims=True)
        )
        c.e_p = jnp.exp2((scores_p - top) * log_scale)
        c.e_s = jnp.exp2((scores_s - top) * log_scale)
        total = jnp.sum(c.e_p, axis=0, keepdims=True) + jnp.sum(c.e_s, axis=0, keepdims=True)
        weighted = jnp.sum(c.e_p * c.gw_p, axis=0, keepdims=True) + jnp.sum(
            c.e_s * c.gw_s, axis=0, keepdims=True
        )
        if c.side is None:
            length = jnp.where(left, lens[0], 0 if single else lens[1])
            gain = jnp.where(left, factors[0], factors[-1])
        else:
            length, gain = lens[c.side], factors[c.side]
        inverse = 1.0 / total
        c.delta = weighted * inverse
        c.gain = inverse * jnp.where(token[:, :lanes] < length, gain, 0.0)

    def gradients(c):
        w_p, w_s = c.e_p * c.gain, c.e_s * c.gain
        d_p = (w_p * (c.gw_p - c.delta)).astype(BF16)
        d_s = (w_s * (c.gw_s - c.delta)).astype(BF16)
        w_p, w_s = w_p.astype(BF16), w_s.astype(BF16)
        if c.side is None:
            d_s, w_s = halves(d_s), halves(w_s)
            c.d_wide = jnp.concatenate([d_p, *d_s], axis=0)
            c.d_all = jnp.concatenate([*halves(d_p), *d_s], axis=0) if apart else c.d_wide
            c.w_all = jnp.concatenate([*(halves(w_p) if apart else [w_p]), *w_s], axis=0)
        else:
            empty = jnp.zeros_like(d_s)
            c.d_wide = jnp.concatenate([d_p, empty, d_s] if c.side else [d_p, d_s, empty], axis=0)
            c.d_all = jnp.concatenate([d_p, d_s], axis=0)
            c.w_all = jnp.concatenate([w_p, w_s], axis=0)

    def outgoing(c):
        t = c.t
        q_grad = (dot(t.key_t, c.d_wide, NN) * scale).astype(BF16).T
        kg = dot(c.d_all, c.q_rows, NN)
        vg = dot(c.w_all, c.g_rows, NN)
        targets = members if c.side is None else [c.side]
        for place, (n, h) in enumerate(c.blocks):
            if c.side is not None or place < len(targets):
                out[at[n], :, head(c.k, h)] = q_grad[place * tokens : (place + 1) * tokens]
        many = 2 if c.side is None and apart else 1
        for place, n in enumerate(targets):
            if place < many:
                rows_p = slice(place * prefix_len, (place + 1) * prefix_len)
                t.prefix_sums[n if apart else 0].append((kg[rows_p], vg[rows_p]))
            start = many * prefix_len + place * tokens
            rows_s = slice(start, start + tokens)
            t.self_sums[n].append((kg[rows_s], vg[rows_s]))
        t.left_over -= 1
        if t.left_over == 0:
            for n in members:
                keys, values = zip(*t.self_sums[n])
                own_out[at[n], 0, :, t.cols] = (sum(keys) * scale).astype(BF16)
                own_out[at[n], 1, :, t.cols] = sum(values).astype(BF16)
                if apart or n == 0:
                    keys, values = zip(*t.prefix_sums[n])
                    sink(n, t.cols, sum(keys) * scale, sum(values))

    stages = (products, weigh, gradients, outgoing)
    for step in range(len(chunks) + len(stages) - 1):
        for late, stage in enumerate(stages):
            if 0 <= step - late < len(chunks):
                stage(chunks[step - late])


def token_rows(z, i):
    return pl.ds(pl.multiple_of(i * z.tokens, z.tokens), z.tokens)


def find_responses(z, me, turns, resp_prompt, order):
    for t, turn in enumerate(turns):
        prompt = lax.rem(me + turn, z.n_dp)
        found = t * z.slots
        for i in range(z.count):
            order[found] = i
            found = found + (resp_prompt[me * z.count + i] == prompt).astype(jnp.int32)


def prompt_total(z, prompt, tails):
    sums = jnp.zeros((1, tails.shape[2]), F32)
    for s in range(z.n_dp):
        tail = tails[s].astype(F32)
        sums += tail[0:1] + tail[1:2] + tail[2:3]
    lane = lax.broadcasted_iota(jnp.int32, sums.shape, 1)
    return jnp.sum(jnp.where(lane == prompt, sums, 0.0))


def reward_factor(z, reward, total, length):
    return (reward - total / z.count) * (z.tokens / length.astype(F32))


def pack_kernel(z, prompt_hbm, rewards_hbm, resp_prompt_hbm, payload, rewards, resp_prompt, tail, sems):
    me = lax.axis_index("dp")
    small = [
        pltpu.make_async_copy(rewards_hbm, rewards, sems.at[0]),
        pltpu.make_async_copy(resp_prompt_hbm, resp_prompt, sems.at[1]),
    ]
    large = [
        pltpu.make_async_copy(
            prompt_hbm.at[n], payload.at[pl.ds(n * z.prefix_len, z.prefix_len)], sems.at[2 + n]
        )
        for n in range(2)
    ]
    for copy in small + large:
        copy.start()
    for copy in small:
        copy.wait()
    lane = lax.broadcasted_iota(jnp.int32, (1, z.width), 1)
    sums = jnp.zeros((1, z.width), F32)
    for i in range(z.count):
        sums += jnp.where(lane == resp_prompt[me * z.count + i], rewards[i], 0.0)
    high = sums.astype(BF16).astype(F32)
    middle = (sums - high).astype(BF16).astype(F32)
    low = sums - high - middle
    row = lax.broadcasted_iota(jnp.int32, (TAIL, z.width), 0)
    pieces = jnp.where(row == 0, high, jnp.where(row == 1, middle, jnp.where(row == 2, low, 0.0)))
    tail[...] = pieces.astype(BF16)
    last = pltpu.make_async_copy(tail, payload.at[pl.ds(2 * z.prefix_len, TAIL)], sems.at[0])
    last.start()
    for copy in large + [last]:
        copy.wait()


def tail_copies(z, payloads, tails, sems):
    return [
        pltpu.make_async_copy(payloads[s].at[pl.ds(2 * z.prefix_len, TAIL)], tails.at[s], sems.at[s])
        for s in range(z.n_dp)
    ]


def near_kernel(z, turns, raw, aliased, *refs):
    refs = list(refs)
    small_hbm = refs[:3]
    q_hbm, og_hbm, kv_hbm = refs[3:6]
    n_payloads = 1 if raw else z.n_dp
    payloads = refs[6 : 6 + n_payloads]
    refs = refs[6 + n_payloads + aliased :]
    n_grads = 1 if raw else len(turns)
    q_out, self_out = refs[:2]
    grads_out = refs[2 : 2 + n_grads]
    (resp_prompt, resp_len, rewards, order, lens, factors, q, og, kv, prefix, tails, acc, out, own, grads,
     sem_small, sem_prefix, sem_in, sem_out, sem_grads) = refs[2 + n_grads :]
    me = lax.axis_index("dp")
    n_slots = len(turns) * z.slots
    per_unit = 2 - z.slots % 2
    units = n_slots // per_unit

    small = [
        pltpu.make_async_copy(src, dst, sem_small.at[n])
        for n, (src, dst) in enumerate(zip(small_hbm, (resp_prompt, resp_len, rewards)))
    ]
    for copy in small:
        copy.start()
    prefix_copies = [
        pltpu.make_async_copy(
            payloads[0 if raw else turn].at[pl.ds(n * z.prefix_len, z.prefix_len)],
            prefix.at[t, n],
            sem_prefix.at[t, n],
        )
        for t, turn in enumerate(turns)
        for n in range(2)
    ]
    late = [] if raw else tail_copies(z, payloads, tails, sem_grads)
    for copy in prefix_copies + late:
        copy.start()
    small[0].wait()
    find_responses(z, me, turns, resp_prompt, order)

    def copies_in(slot):
        rows = token_rows(z, order[slot])
        return (
            pltpu.make_async_copy(q_hbm.at[rows], q.at[slot], sem_in.at[slot, 0]),
            pltpu.make_async_copy(og_hbm.at[rows], og.at[slot], sem_in.at[slot, 1]),
            pltpu.make_async_copy(kv_hbm.at[0, rows], kv.at[slot, 0], sem_in.at[slot, 2]),
            pltpu.make_async_copy(kv_hbm.at[1, rows], kv.at[slot, 1], sem_in.at[slot, 3]),
        )

    def copies_out(slot):
        rows = token_rows(z, order[slot])
        return (
            pltpu.make_async_copy(out.at[slot], q_out.at[rows], sem_out.at[slot, 0]),
            pltpu.make_async_copy(own.at[slot, 0], self_out.at[0, rows], sem_out.at[slot, 1]),
            pltpu.make_async_copy(own.at[slot, 1], self_out.at[1, rows], sem_out.at[slot, 2]),
        )

    for slot in range(n_slots):
        for copy in copies_in(slot):
            copy.start()
    for copy in small[1:] + late:
        copy.wait()
    for t, turn in enumerate(turns):
        total = None if raw else prompt_total(z, lax.rem(me + turn, z.n_dp), tails)
        for slot in range(t * z.slots, (t + 1) * z.slots):
            i = order[slot]
            lens[slot] = resp_len[i]
            factors[slot] = 1.0 if raw else reward_factor(z, rewards[i], total, resp_len[i])
    if not raw:
        acc[...] = jnp.zeros(acc.shape, F32)
    for copy in prefix_copies:
        copy.wait()

    def unit(u, _):
        at = [u * per_unit + n for n in range(per_unit)]
        t = u // (z.slots // per_unit)
        for slot in at:
            for copy in copies_in(slot):
                copy.wait()

        def sink(n, cols, key_grad, value_grad):
            if raw:
                grads[at[n], 0, :, cols] = key_grad.astype(BF16)
                grads[at[n], 1, :, cols] = value_grad.astype(BF16)
            else:
                acc[t, 0, :, cols] += key_grad
                acc[t, 1, :, cols] += value_grad

        attend_pair(
            z, at, q, og, kv, prefix.at[t], [lens[n] for n in at], [factors[n] for n in at], out, own, sink, raw
        )
        for slot in at:
            for copy in copies_out(slot):
                copy.start()
        return 0

    lax.fori_loop(0, units, unit, 0)
    if raw:
        last = [pltpu.make_async_copy(grads, grads_out[0], sem_grads.at[0])]
    else:
        grads[...] = acc[...].astype(BF16)
        last = [
            pltpu.make_async_copy(grads.at[t], grads_out[t], sem_grads.at[t]) for t in range(len(turns))
        ]
    for copy in last:
        copy.start()
    for slot in range(n_slots):
        for copy in copies_out(slot):
            copy.wait()
    for copy in last:
        copy.wait()


def near_grads(z, turns, raw, small, resp_q, out_grad, resp_kv, payloads, earlier):
    n_slots = len(turns) * z.slots
    operands = [*small, resp_q, out_grad, resp_kv, *payloads, *earlier]
    one = (2, z.prefix_len, z.width)
    grads_shapes = [(z.slots,) + one] if raw else [one] * len(turns)
    return pl.pallas_call(
        functools.partial(near_kernel, z, turns, raw, len(earlier)),
        out_shape=[
            jax.ShapeDtypeStruct(resp_q.shape, BF16),
            jax.ShapeDtypeStruct(resp_kv.shape, BF16),
            *[jax.ShapeDtypeStruct(shape, BF16) for shape in grads_shapes],
        ],
        in_specs=[ANYWHERE] * len(operands),
        out_specs=[ANYWHERE] * (2 + len(grads_shapes)),
        input_output_aliases={len(operands) - 2: 0, len(operands) - 1: 1} if earlier else {},
        scratch_shapes=[
            *[pltpu.SMEM(x.shape, x.dtype) for x in small],
            pltpu.SMEM((n_slots + 1,), jnp.int32),
            pltpu.SMEM((n_slots,), jnp.int32),
            pltpu.SMEM((n_slots,), F32),
            pltpu.VMEM((n_slots, z.tokens, z.lanes), BF16),
            pltpu.VMEM((n_slots, z.tokens, z.lanes), BF16),
            pltpu.VMEM((n_slots, 2, z.tokens, z.width), BF16),
            pltpu.VMEM((len(turns),) + one, BF16),
            pltpu.VMEM((z.n_dp, TAIL, z.width), BF16),
            pltpu.VMEM((len(turns),) + one, F32),
            pltpu.VMEM((n_slots, z.tokens, z.lanes), BF16),
            pltpu.VMEM((n_slots, 2, z.tokens, z.width), BF16),
            pltpu.VMEM(grads_shapes[0] if raw else (len(turns),) + one, BF16),
            pltpu.SemaphoreType.DMA((len(small),)),
            pltpu.SemaphoreType.DMA((len(turns), 2)),
            pltpu.SemaphoreType.DMA((n_slots, 4)),
            pltpu.SemaphoreType.DMA((n_slots, 3)),
            pltpu.SemaphoreType.DMA((z.n_dp,)),
        ],
        compiler_params=pltpu.CompilerParams(vmem_limit_bytes=VMEM_BYTES),
        cost_estimate=pl.CostEstimate(flops=0, bytes_accessed=0, transcendentals=0),
        name="raw_grads" if raw else "group_grads",
    )(*operands)


def finish_kernel(z, *refs):
    refs = list(refs)
    small_hbm, payloads = refs[:3], refs[3 : 3 + z.n_dp]
    per_resp_hbm = refs[3 + z.n_dp]
    q_out, self_out, grads_out = refs[6 + z.n_dp : 9 + z.n_dp]
    (resp_prompt, resp_len, rewards, order, tails, q, own, per_resp, grads, sem_small, sem_in, sem_out) = refs[
        9 + z.n_dp :
    ]
    me = lax.axis_index("dp")
    small = [
        pltpu.make_async_copy(src, dst, sem_small.at[n])
        for n, (src, dst) in enumerate(zip(small_hbm, (resp_prompt, resp_len, rewards)))
    ]
    late = tail_copies(z, payloads, tails, sem_small.at[pl.ds(3, z.n_dp)])
    late.append(pltpu.make_async_copy(per_resp_hbm, per_resp, sem_small.at[3 + z.n_dp]))
    for copy in small + late:
        copy.start()
    small[0].wait()
    find_responses(z, me, (0,), resp_prompt, order)

    def moves(slot, back):
        rows = token_rows(z, order[slot])
        ends = [(q_out.at[rows], q.at[slot])]
        ends += [(self_out.at[n, rows], own.at[slot, n]) for n in range(2)]
        sems = sem_out if back else sem_in
        return [
            pltpu.make_async_copy(*(reversed(pair) if back else pair), sems.at[slot, n])
            for n, pair in enumerate(ends)
        ]

    for slot in range(z.slots):
        for copy in moves(slot, False):
            copy.start()
    for copy in small[1:] + late:
        copy.wait()
    total = prompt_total(z, me, tails)
    factors = [
        reward_factor(z, rewards[order[slot]], total, resp_len[order[slot]]) for slot in range(z.slots)
    ]
    summed = per_resp[0].astype(F32) * factors[0]
    for slot in range(1, z.slots):
        summed += per_resp[slot].astype(F32) * factors[slot]
    grads[...] = summed.astype(BF16)
    last = pltpu.make_async_copy(grads, grads_out, sem_small.at[0])
    last.start()
    for slot in range(z.slots):
        for copy in moves(slot, False):
            copy.wait()
        q[slot] = (q[slot].astype(F32) * factors[slot]).astype(BF16)
        own[slot] = (own[slot].astype(F32) * factors[slot]).astype(BF16)
        for copy in moves(slot, True):
            copy.start()
    for slot in range(z.slots):
        for copy in moves(slot, True):
            copy.wait()
    last.wait()


def finish(z, small, payloads, per_resp, q_out, self_out):
    operands = [*small, *payloads, per_resp, q_out, self_out]
    one = (2, z.prefix_len, z.width)
    return pl.pallas_call(
        functools.partial(finish_kernel, z),
        out_shape=[
            jax.ShapeDtypeStruct(q_out.shape, BF16),
            jax.ShapeDtypeStruct(self_out.shape, BF16),
            jax.ShapeDtypeStruct(one, BF16),
        ],
        in_specs=[ANYWHERE] * len(operands),
        out_specs=[ANYWHERE] * 3,
        input_output_aliases={len(operands) - 2: 0, len(operands) - 1: 1},
        scratch_shapes=[
            *[pltpu.SMEM(x.shape, x.dtype) for x in small],
            pltpu.SMEM((z.slots + 1,), jnp.int32),
            pltpu.VMEM((z.n_dp, TAIL, z.width), BF16),
            pltpu.VMEM((z.slots, z.tokens, z.lanes), BF16),
            pltpu.VMEM((z.slots, 2, z.tokens, z.width), BF16),
            pltpu.VMEM((z.slots,) + one, BF16),
            pltpu.VMEM(one, BF16),
            pltpu.SemaphoreType.DMA((len(small) + z.n_dp + 1,)),
            pltpu.SemaphoreType.DMA((z.slots, 3)),
            pltpu.SemaphoreType.DMA((z.slots, 3)),
        ],
        compiler_params=pltpu.CompilerParams(vmem_limit_bytes=VMEM_BYTES),
        cost_estimate=pl.CostEstimate(flops=0, bytes_accessed=0, transcendentals=0),
        name="finish_own",
    )(*operands)


def near_shards(z, prompt_kv, resp_q, resp_kv, out_grad, rewards, resp_prompt, resp_len):
    n_dp = z.n_dp
    small = (resp_prompt, resp_len, rewards)
    payload = pl.pallas_call(
        functools.partial(pack_kernel, z),
        out_shape=jax.ShapeDtypeStruct((2 * z.prefix_len + TAIL, z.width), BF16),
        in_specs=[ANYWHERE] * 3,
        out_specs=ANYWHERE,
        scratch_shapes=[
            pltpu.SMEM(rewards.shape, F32),
            pltpu.SMEM(resp_prompt.shape, jnp.int32),
            pltpu.VMEM((TAIL, z.width), BF16),
            pltpu.SemaphoreType.DMA((4,)),
        ],
        compiler_params=pltpu.CompilerParams(vmem_limit_bytes=VMEM_BYTES),
        name="pack",
    )(prompt_kv, rewards, resp_prompt)

    away = sorted(range(1, n_dp), key=lambda s: -min(s, n_dp - s))
    payloads = {0: payload}
    for s in away:
        payloads[s] = lax.ppermute(payload, "dp", [((i + s) % n_dp, i) for i in range(n_dp)])
    everyone = [payloads[s] for s in range(n_dp)]

    *written, per_resp = near_grads(z, (0,), True, small, resp_q, out_grad, resp_kv, [payload], ())
    first = len(away) // 2
    arrived = []
    for turns in (tuple(away[:first]), tuple(away[first:])):
        if not turns:
            continue
        results = near_grads(z, turns, False, small, resp_q, out_grad, resp_kv, everyone, written)
        written = results[:2]
        for turn, grads in zip(turns, results[2:]):
            arrived.append(lax.ppermute(grads, "dp", [(i, (i + turn) % n_dp) for i in range(n_dp)]))
    q_out, self_out, own_grads = finish(z, small, everyone, per_resp, *written)
    prefix_out = sum(part.astype(F32) for part in [own_grads, *arrived]).astype(BF16)
    return (q_out, self_out, prefix_out)


def far_kernel(z, *refs):
    (resp_prompt, resp_len, rewards, q_hbm, og_hbm, kv_hbm, prompts, q_out, self_out, prefix_outs,
     totals, lens, factors, q, og, kv, prefix, out, own, grads, sem_in, sem_prefix, sem_out) = refs
    me = lax.axis_index("dp")

    for p in range(z.n_dp):
        totals[p] = 0.0

    def copies_in(slot):
        rows = token_rows(z, slot)
        prompt = resp_prompt[me * z.count + slot]
        return (
            pltpu.make_async_copy(q_hbm.at[rows], q.at[slot], sem_in.at[slot, 0]),
            pltpu.make_async_copy(og_hbm.at[rows], og.at[slot], sem_in.at[slot, 1]),
            pltpu.make_async_copy(kv_hbm.at[0, rows], kv.at[slot, 0], sem_in.at[slot, 2]),
            pltpu.make_async_copy(kv_hbm.at[1, rows], kv.at[slot, 1], sem_in.at[slot, 3]),
            pltpu.make_async_copy(prompts.at[prompt], prefix.at[slot], sem_prefix.at[slot]),
        )

    def copies_out(slot):
        rows = token_rows(z, slot)
        return (
            pltpu.make_async_copy(out.at[slot], q_out.at[rows], sem_out.at[slot, 0]),
            pltpu.make_async_copy(own.at[slot, 0], self_out.at[0, rows], sem_out.at[slot, 1]),
            pltpu.make_async_copy(own.at[slot, 1], self_out.at[1, rows], sem_out.at[slot, 2]),
            pltpu.make_async_copy(grads.at[slot], prefix_outs.at[slot], sem_out.at[slot, 3]),
        )

    def start(slot, _):
        for copy in copies_in(slot):
            copy.start()
        return 0

    lax.fori_loop(0, z.count, start, 0)

    def add(i, _):
        prompt = resp_prompt[i]
        totals[prompt] = totals[prompt] + rewards[i]
        return 0

    lax.fori_loop(0, z.n_dp * z.count, add, 0)

    def find_factor(slot, _):
        place = me * z.count + slot
        lens[slot] = resp_len[slot]
        factors[slot] = reward_factor(z, rewards[place], totals[resp_prompt[place]], resp_len[slot])
        return 0

    lax.fori_loop(0, z.count, find_factor, 0)

    def unit(slot, _):
        for copy in copies_in(slot):
            copy.wait()

        def sink(_, cols, key_grad, value_grad):
            grads[slot, 0, :, cols] = key_grad.astype(BF16)
            grads[slot, 1, :, cols] = value_grad.astype(BF16)

        attend_pair(
            z, [slot], q, og, kv, prefix.at[slot], [lens[slot]], [factors[slot]], out, own, sink, True
        )
        for copy in copies_out(slot):
            copy.start()
        return 0

    lax.fori_loop(0, z.count, unit, 0)

    def end(slot, _):
        for copy in copies_out(slot):
            copy.wait()
        return 0

    lax.fori_loop(0, z.count, end, 0)


def far_shards(z, prompt_kv, resp_q, resp_kv, out_grad, rewards, resp_prompt, resp_len):
    assert z.slots == 1
    count, n_dp = z.count, z.n_dp
    one = (2, z.prefix_len, z.width)
    smem = pl.BlockSpec(memory_space=pltpu.SMEM)
    q_out, self_out, per_resp = pl.pallas_call(
        functools.partial(far_kernel, z),
        out_shape=[
            jax.ShapeDtypeStruct(resp_q.shape, BF16),
            jax.ShapeDtypeStruct(resp_kv.shape, BF16),
            jax.ShapeDtypeStruct((count,) + one, BF16),
        ],
        in_specs=[smem] * 3 + [ANYWHERE] * 4,
        out_specs=[ANYWHERE] * 3,
        scratch_shapes=[
            pltpu.SMEM((n_dp,), F32),
            pltpu.SMEM((count,), jnp.int32),
            pltpu.SMEM((count,), F32),
            pltpu.VMEM((count, z.tokens, z.lanes), BF16),
            pltpu.VMEM((count, z.tokens, z.lanes), BF16),
            pltpu.VMEM((count, 2, z.tokens, z.width), BF16),
            pltpu.VMEM((count,) + one, BF16),
            pltpu.VMEM((count, z.tokens, z.lanes), BF16),
            pltpu.VMEM((count, 2, z.tokens, z.width), BF16),
            pltpu.VMEM((count,) + one, BF16),
            pltpu.SemaphoreType.DMA((count, 4)),
            pltpu.SemaphoreType.DMA((count,)),
            pltpu.SemaphoreType.DMA((count, 4)),
        ],
        compiler_params=pltpu.CompilerParams(vmem_limit_bytes=VMEM_BYTES),
        name="far_grads",
    )(
        resp_prompt,
        resp_len,
        lax.all_gather(rewards, "dp", axis=0, tiled=True),
        resp_q,
        out_grad,
        resp_kv,
        lax.all_gather(prompt_kv, "dp", axis=0),
    )
    my_prompts = lax.dynamic_slice_in_dim(resp_prompt, lax.axis_index("dp") * count, count)
    route = (jnp.arange(n_dp, dtype=jnp.int32)[:, None] == my_prompts[None, :]).astype(BF16)
    outgoing = jnp.dot(route, per_resp.reshape(count, -1), preferred_element_type=F32).astype(BF16)
    outgoing = outgoing.reshape((n_dp,) + one)
    incoming = lax.all_to_all(outgoing, "dp", split_axis=0, concat_axis=0, tiled=True)
    prefix_out = jnp.sum(incoming, axis=0, dtype=F32).astype(BF16)
    return (q_out, self_out, prefix_out)


def shards(prompt_kv, resp_q, resp_kv, out_grad, rewards, resp_prompt, resp_len):
    n_dp = lax.axis_size("dp")
    count = rewards.shape[0]
    prefix_len, width = prompt_kv.shape[1:]
    slots = (count + n_dp - 1) // n_dp
    z = Sizes(
        n_dp, count, slots, width // HD, resp_q.shape[1] // width, resp_q.shape[0] // count, prefix_len
    )
    part = near_shards if count // slots == n_dp else far_shards
    return part(z, prompt_kv, resp_q, resp_kv, out_grad, rewards, resp_prompt, resp_len)


def solution(mesh):
    in_specs = (
        P(None, ("groups", "dp"), "tensor"),
        P(("groups", "dp"), "tensor"),
        P(None, ("groups", "dp"), "tensor"),
        P(("groups", "dp"), "tensor"),
        P(("groups", "dp")),
        P("groups"),
        P(("groups", "dp")),
    )
    out_specs = (
        P(("groups", "dp"), "tensor"),
        P(None, ("groups", "dp"), "tensor"),
        P(None, ("groups", "dp"), "tensor"),
    )
    return jax.shard_map(shards, mesh=mesh, in_specs=in_specs, out_specs=out_specs, check_vma=False)
```

time: 168 us -> 48.4 us (0.29)
  local copies, waits for them, and re-layouts: 56.2 us -> 0.69 us
  other arithmetic: 34.2 us -> 1.63 us
  blocking collectives: 28.5 us -> 0 us
  Pallas kernels: 0 us -> 26.1 us
  matrix products: 25.7 us -> 0 us
  waiting for transfers between devices: 16.9 us -> 5.42 us
  starting transfers between devices: 4.68 us -> 13.5 us
    pallas_call x0 -> x5, Pallas kernels: none -> 26.1 us  [the longest x3 18.1 us: near_grads(): pl.pallas_call(functools.partial(near_kernel, z, turns, raw, len(earlier)...]
    dot_general x7 -> x0, matrix products: 25.7 us -> none  [the longest x1 8.58 us: local_attention(): jnp.einsum('rtkgd,rskd->rkgts', scaled, all_values, preferred_element_typ...]
    reshape x5 -> x0, local copies, waits for them, and re-layouts: 19.6 us -> none  [the longest x1 7.12 us: shards(): q_out = query_grad.reshape(resp_count * resp_tokens, -1)]
    all_to_all x1 -> x0, waiting for transfers between devices: 16.9 us -> none  [shards(): lax.all_to_all(outgoing_grads, 'dp', split_axis=0, concat_axis=0, tiled=T...]
    all_gather x1 -> x0, blocking collectives: 15.1 us -> none  [shards(): gathered = lax.all_gather(prompt_kv, 'dp', axis=1, tiled=True)]
    sub x2 -> x0, other arithmetic: 14.7 us -> none  [the longest x1 14.7 us: local_attention(): exp_scores = jnp.exp(scores - row_max)]
    ppermute x0 -> x6, starting transfers between devices: none -> 13.5 us  [the longest x3 7.01 us: near_shards(): lax.ppermute(payload, 'dp', [((i + s) % n_dp, i) for i in range(n_dp)])]
    psum x1 -> x0, blocking collectives: 13.5 us -> none  [shards(): totals = lax.psum(partial_sums, 'dp')]
  transfers between devices with their start and end apart: 1 -> 6, of which waited for: 1 -> 3; matrix products, arithmetic and copies ran while one was open for 16% -> 0% of each run, Pallas kernels for 0% -> 33%
where the time goes in v4:
time: 48.4 us; the launch traced here: 48 us
  Pallas kernels  26.1 us (54%)
  starting transfers between devices  13.5 us (28%)
  waiting for transfers between devices  5.42 us (11%)
  other arithmetic  1.63 us (3%)
  between operations  0.7 us (1%)
  local copies, waits for them, and re-layouts  0.69 us (1%)
    pallas_call x3, Pallas kernels, near_grads(): pl.pallas_call(functools.partial(near_kernel, z, turns, raw, len(earlier)...  18.1 us
    ppermute x3, starting transfers between devices, near_shards(): lax.ppermute(payload, 'dp', [((i + s) % n_dp, i) for i in range(n_dp)])  7.01 us
    ppermute x3, starting transfers between devices, near_shards(): lax.ppermute(grads, 'dp', [(i, (i + turn) % n_dp) for i in range(n_dp)])  6.45 us
    pallas_call x1, Pallas kernels, near_shards(): pl.pallas_call(functools.partial(pack_kernel, z), out_shape=jax.ShapeDtyp...  5.11 us
    pallas_call x1, Pallas kernels, finish(): pl.pallas_call(functools.partial(finish_kernel, z), out_shape=[jax.ShapeD...  2.9 us
    ppermute x3, waiting for transfers between devices, near_shards(): lax.ppermute(payload, 'dp', [((i + s) % n_dp, i) for i in range(n_dp)])  2.76 us
    ppermute x3, waiting for transfers between devices, near_shards(): lax.ppermute(grads, 'dp', [(i, (i + turn) % n_dp) for i in range(n_dp)])  2.66 us
    convert_element_type x1, other arithmetic, near_shards(): sum((part.astype(F32) for part in [own_grads, *arrived])).astype(BF16)  1.63 us
  transfers between devices with their start and end apart: 6, of which 3 were waited for; matrix products, arithmetic and copies ran while one was open for 0% of the time, Pallas kernels for 33%

profile of v4, /device:TPU:0, one launch (start us, length us, event | category | flops | bytes accessed | tf_op | source)
XLA Modules:
  0.0 48.0 jit_solution(2369324565156695400)
XLA Ops:
  0.6 5.1 %pack.1.refs_6_.refs_3_ = bf16[272,256]{1,0:T(8,128)(2,1)} custom-call(bf16[2,128,256]{2,1,0:T(8,128)(2,1)} %prompt_hbm.1, f32[16]{0:T(128)} %refs_2_.7, s32[64]{0:T(128)} %refs_0_.7), custom_call_target="tpu_custom_call" | custom-call | tf_op jit(solution)/shard_map/pack/pallas_call | solution.py:496
  5.8 3.1 %collective-permute-start.2 = (bf16[272,256]{1,0:T(8,128)(2,1)}, bf16[272,256]{1,0:T(8,128)(2,1)S(1)}, u32[]{:S(2)}, u32[]{:S(2)}) collective-permute-start(bf16[272,256]{1,0:T(8,128)(2,1)} %pack.1.refs_6_.refs_3_), channel_id=1, source_target_pairs={{12,0},{0,4},{4,8},{8,12},{13,1},{1,5},{5,9},{9,13},{14,2},{2,6},{... | collective-permute-start | bytes 417800 | tf_op jit(solution)/shard_map/ppermute | solution.py:514
  8.8 2.6 %collective-permute-start.1 = (bf16[272,256]{1,0:T(8,128)(2,1)}, bf16[272,256]{1,0:T(8,128)(2,1)S(1)}, u32[]{:S(2)}, u32[]{:S(2)}) collective-permute-start(bf16[272,256]{1,0:T(8,128)(2,1)} %pack.1.refs_6_.refs_3_), channel_id=1, source_target_pairs={{8,0},{12,4},{0,8},{4,12},{9,1},{13,5},{1,9},{5,13},{10,2},{14,6},... | collective-permute-start | bytes 417800 | tf_op jit(solution)/shard_map/ppermute | solution.py:514
  11.4 1.3 %collective-permute-start = (bf16[272,256]{1,0:T(8,128)(2,1)}, bf16[272,256]{1,0:T(8,128)(2,1)S(1)}, u32[]{:S(2)}, u32[]{:S(2)}) collective-permute-start(bf16[272,256]{1,0:T(8,128)(2,1)} %pack.1.refs_6_.refs_3_), channel_id=1, source_target_pairs={{4,0},{8,4},{12,8},{0,12},{5,1},{9,5},{13,9},{1,13},{6,2},{10,6},{... | collective-permute-start | bytes 417800 | tf_op jit(solution)/shard_map/ppermute | solution.py:514
  12.8 5.2 %raw_grads.1 = (bf16[1024,1280]{1,0:T(8,128)(2,1)}, bf16[2,1024,256]{2,1,0:T(8,128)(2,1)}, bf16[4,2,128,256]{3,2,1,0:T(8,128)(2,1)}) custom-call(s32[64]{0:T(128)} %refs_0_.7, s32[16]{0:T(128)} %refs_1_.7, f32[16]{0:T(128)} %refs_2_.7, bf16[1024,1280]{1,0:T(8,128)(2,1)} %refs_3_.5, bf16[1024,1280]{1,0:T(8,128)(2,1)} %refs_4_.5, ...), custom_call_target="tpu_custom_call" | custom-call | tf_op jit(solution)/shard_map/raw_grads/pallas_call | solution.py:368
  18.0 0.0 collective-permute-done.2.refs_9_.refs_6_
  18.0 0.0 copy-start
  18.0 2.8 %collective-permute-done.1.refs_8_.refs_5_ = bf16[272,256]{1,0:T(8,128)(2,1)S(1)} collective-permute-done((bf16[272,256]{1,0:T(8,128)(2,1)}, bf16[272,256]{1,0:T(8,128)(2,1)S(1)}, u32[]{:S(2)}, u32[]{:S(2)}) %collective-permute-start.1) | collective-permute-done | bytes 139296 | tf_op jit(solution)/shard_map/ppermute | solution.py:514
  20.8 0.0 copy-start.1
  20.8 0.0 collective-permute-done.refs_7_.refs_4_
  20.8 0.0 copy-start.2
  20.8 0.0 copy-done
  20.8 0.6 %copy-done.1 = bf16[272,256]{1,0:T(8,128)(2,1)} copy-done((bf16[272,256]{1,0:T(8,128)(2,1)}, bf16[272,256]{1,0:T(8,128)(2,1)S(1)}, u32[]{:S(2)}) %copy-start.1) | copy-done | bytes 139288
  21.4 0.1 copy-done.2
  21.5 5.2 %group_grads.2 = (bf16[1024,1280]{1,0:T(8,128)(2,1)}, bf16[2,1024,256]{2,1,0:T(8,128)(2,1)}, bf16[2,128,256]{2,1,0:T(8,128)(2,1)}) custom-call(s32[64]{0:T(128)} %refs_0_.7, s32[16]{0:T(128)} %refs_1_.7, f32[16]{0:T(128)} %refs_2_.7, bf16[1024,1280]{1,0:T(8,128)(2,1)} %refs_3_.5, ...), custom_call_target="tpu_custom_call", output_to_operand_aliasing={{0}: (10, {}), {1}: (11, {})} | custom-call | tf_op jit(solution)/shard_map/group_grads/pallas_call | solution.py:368
  26.7 2.6 %collective-permute-start.3 = (bf16[2,128,256]{2,1,0:T(8,128)(2,1)}, bf16[2,128,256]{2,1,0:T(8,128)(2,1)S(1)}, u32[]{:S(2)}, u32[]{:S(2)}) collective-permute-start(bf16[2,128,256]{2,1,0:T(8,128)(2,1)} %get-tuple-element.26), channel_id=1, source_target_pairs={{0,8},{4,12},{8,0},{12,4},{1,9},{5,13},{9,1},{13,5},{2,10},{6,14},... | collective-permute-start | bytes 393224 | tf_op jit(solution)/shard_map/ppermute | solution.py:526
  29.3 7.7 %group_grads.3 = (bf16[1024,1280]{1,0:T(8,128)(2,1)}, bf16[2,1024,256]{2,1,0:T(8,128)(2,1)}, bf16[2,128,256]{2,1,0:T(8,128)(2,1)}, bf16[2,128,256]{2,1,0:T(8,128)(2,1)}) custom-call(s32[64]{0:T(128)} %refs_0_.7, s32[16]{0:T(128)} %refs_1_.7, f32[16]{0:T(128)} %refs_2_.7, bf16[1024,1280]{1,0:T(8,128)(2,1)} %refs_3_.5, ...), custom_call_target="tpu_custom_call", output_to_operand_aliasing={{0}: (10, {}), {1}: (11, {})} | custom-call | tf_op jit(solution)/shard_map/group_grads/pallas_call | solution.py:368
  37.0 2.6 %collective-permute-start.4 = (bf16[2,128,256]{2,1,0:T(8,128)(2,1)}, bf16[2,128,256]{2,1,0:T(8,128)(2,1)S(1)}, u32[]{:S(2)}, u32[]{:S(2)}) collective-permute-start(bf16[2,128,256]{2,1,0:T(8,128)(2,1)} %get-tuple-element.27), channel_id=1, source_target_pairs={{0,4},{4,8},{8,12},{12,0},{1,5},{5,9},{9,13},{13,1},{2,6},{6,10},{... | collective-permute-start | bytes 393224 | tf_op jit(solution)/shard_map/ppermute | solution.py:526
  39.6 1.2 %collective-permute-start.5 = (bf16[2,128,256]{2,1,0:T(8,128)(2,1)}, bf16[2,128,256]{2,1,0:T(8,128)(2,1)S(1)}, u32[]{:S(2)}, u32[]{:S(2)}) collective-permute-start(bf16[2,128,256]{2,1,0:T(8,128)(2,1)} %get-tuple-element.28), channel_id=1, source_target_pairs={{0,12},{4,0},{8,4},{12,8},{1,13},{5,1},{9,5},{13,9},{2,14},{6,2},{... | collective-permute-start | bytes 393224 | tf_op jit(solution)/shard_map/ppermute | solution.py:526
  40.8 2.9 %finish_own.1 = (bf16[1024,1280]{1,0:T(8,128)(2,1)}, bf16[2,1024,256]{2,1,0:T(8,128)(2,1)}, bf16[2,128,256]{2,1,0:T(8,128)(2,1)}) custom-call(s32[64]{0:T(128)} %refs_0_.7, s32[16]{0:T(128)} %refs_1_.7, f32[16]{0:T(128)} %refs_2_.7, bf16[272,256]{1,0:T(8,128)(2,1)} %pack.1.refs_6_.refs_3_, ...), custom_call_target="tpu_custom_call", output_to_operand_aliasing={{0}: (8, {}), {1}: (9, {})} | custom-call | tf_op jit(solution)/shard_map/finish_own/pallas_call | solution.py:465
  43.7 0.0 collective-permute-done.3
  43.7 1.7 %collective-permute-done.4 = bf16[2,128,256]{2,1,0:T(8,128)(2,1)S(1)} collective-permute-done((bf16[2,128,256]{2,1,0:T(8,128)(2,1)}, bf16[2,128,256]{2,1,0:T(8,128)(2,1)S(1)}, u32[]{:S(2)}, u32[]{:S(2)}) %collective-permute-start.4) | collective-permute-done | bytes 131104 | tf_op jit(solution)/shard_map/ppermute | solution.py:526
  45.4 1.0 %collective-permute-done.5 = bf16[2,128,256]{2,1,0:T(8,128)(2,1)S(1)} collective-permute-done((bf16[2,128,256]{2,1,0:T(8,128)(2,1)}, bf16[2,128,256]{2,1,0:T(8,128)(2,1)S(1)}, u32[]{:S(2)}, u32[]{:S(2)}) %collective-permute-start.5) | collective-permute-done | bytes 131104 | tf_op jit(solution)/shard_map/ppermute | solution.py:526
  46.4 1.6 %add_convert_fusion = bf16[2,128,256]{2,1,0:T(8,128)(2,1)} fusion(bf16[2,128,256]{2,1,0:T(8,128)(2,1)S(1)} %collective-permute-done.5, bf16[2,128,256]{2,1,0:T(8,128)(2,1)S(1)} %collective-permute-done.4, bf16[2,128,256]{2,1,0:T(8,128)(2,1)S(1)} %collective-permute-done.3, bf16[2,128,256]{2,1,0:T(8,128)(2,1)} %get-tuple-element.25), kind=kLoop, calls=%fused_computation | loop fusion | flops 524288 | bytes 655360 | tf_op jit(solution)/shard_map/convert_element_type | solution.py:528
Async XLA Ops:
  5.8 12.3 %collective-permute-start.2 = (bf16[272,256]{1,0:T(8,128)(2,1)}, bf16[272,256]{1,0:T(8,128)(2,1)S(1)}, u32[]{:S(2)}, u32[]{:S(2)}) collective-permute-start(bf16[272,256]{1,0:T(8,128)(2,1)} %pack.1.refs_6_.refs_3_), channel_id=1, source_target_pairs={{12,0},{0,4},{4,8},{8,12},{13,1},{1,5},{5,9},{9,13},{14,2},{2,6},{... | collective-permute-start | bytes 417800 | tf_op jit(solution)/shard_map/ppermute | solution.py:514
  8.8 12.0 %collective-permute-start.1 = (bf16[272,256]{1,0:T(8,128)(2,1)}, bf16[272,256]{1,0:T(8,128)(2,1)S(1)}, u32[]{:S(2)}, u32[]{:S(2)}) collective-permute-start(bf16[272,256]{1,0:T(8,128)(2,1)} %pack.1.refs_6_.refs_3_), channel_id=1, source_target_pairs={{8,0},{12,4},{0,8},{4,12},{9,1},{13,5},{1,9},{5,13},{10,2},{14,6},... | collective-permute-start | bytes 417800 | tf_op jit(solution)/shard_map/ppermute | solution.py:514
  11.4 9.4 %collective-permute-start = (bf16[272,256]{1,0:T(8,128)(2,1)}, bf16[272,256]{1,0:T(8,128)(2,1)S(1)}, u32[]{:S(2)}, u32[]{:S(2)}) collective-permute-start(bf16[272,256]{1,0:T(8,128)(2,1)} %pack.1.refs_6_.refs_3_), channel_id=1, source_target_pairs={{4,0},{8,4},{12,8},{0,12},{5,1},{9,5},{13,9},{1,13},{6,2},{10,6},{... | collective-permute-start | bytes 417800 | tf_op jit(solution)/shard_map/ppermute | solution.py:514
  18.0 2.8 %copy-start = (bf16[272,256]{1,0:T(8,128)(2,1)}, bf16[272,256]{1,0:T(8,128)(2,1)S(1)}, u32[]{:S(2)}) copy-start(bf16[272,256]{1,0:T(8,128)(2,1)S(1)} %collective-permute-done.2.refs_9_.refs_6_) | copy-start | bytes 417796
  20.8 0.6 %copy-start.1 = (bf16[272,256]{1,0:T(8,128)(2,1)}, bf16[272,256]{1,0:T(8,128)(2,1)S(1)}, u32[]{:S(2)}) copy-start(bf16[272,256]{1,0:T(8,128)(2,1)S(1)} %collective-permute-done.1.refs_8_.refs_5_) | copy-start | bytes 417796
  20.8 0.7 %copy-start.2 = (bf16[272,256]{1,0:T(8,128)(2,1)}, bf16[272,256]{1,0:T(8,128)(2,1)S(1)}, u32[]{:S(2)}) copy-start(bf16[272,256]{1,0:T(8,128)(2,1)S(1)} %collective-permute-done.refs_7_.refs_4_) | copy-start | bytes 417796
  26.7 17.0 %collective-permute-start.3 = (bf16[2,128,256]{2,1,0:T(8,128)(2,1)}, bf16[2,128,256]{2,1,0:T(8,128)(2,1)S(1)}, u32[]{:S(2)}, u32[]{:S(2)}) collective-permute-start(bf16[2,128,256]{2,1,0:T(8,128)(2,1)} %get-tuple-element.26), channel_id=1, source_target_pairs={{0,8},{4,12},{8,0},{12,4},{1,9},{5,13},{9,1},{13,5},{2,10},{6,14},... | collective-permute-start | bytes 393224 | tf_op jit(solution)/shard_map/ppermute | solution.py:526
  37.0 8.5 %collective-permute-start.4 = (bf16[2,128,256]{2,1,0:T(8,128)(2,1)}, bf16[2,128,256]{2,1,0:T(8,128)(2,1)S(1)}, u32[]{:S(2)}, u32[]{:S(2)}) collective-permute-start(bf16[2,128,256]{2,1,0:T(8,128)(2,1)} %get-tuple-element.27), channel_id=1, source_target_pairs={{0,4},{4,8},{8,12},{12,0},{1,5},{5,9},{9,13},{13,1},{2,6},{6,10},{... | collective-permute-start | bytes 393224 | tf_op jit(solution)/shard_map/ppermute | solution.py:526
  39.6 6.8 %collective-permute-start.5 = (bf16[2,128,256]{2,1,0:T(8,128)(2,1)}, bf16[2,128,256]{2,1,0:T(8,128)(2,1)S(1)}, u32[]{:S(2)}, u32[]{:S(2)}) collective-permute-start(bf16[2,128,256]{2,1,0:T(8,128)(2,1)} %get-tuple-element.28), channel_id=1, source_target_pairs={{0,12},{4,0},{8,4},{12,8},{1,13},{5,1},{9,5},{13,9},{2,14},{6,2},{... | collective-permute-start | bytes 393224 | tf_op jit(solution)/shard_map/ppermute | solution.py:526

commit v5 on v4

v5 whole, which is shorter than its diff:
```python
import functools
import math
from typing import NamedTuple

import jax
import jax.numpy as jnp
from jax import lax
from jax.experimental import pallas as pl
from jax.experimental.pallas import tpu as pltpu
from jax.sharding import PartitionSpec as P

HD = 128
NEG = -1e30
TAIL = 16
F32 = jnp.float32
BF16 = jnp.bfloat16
PAIR = 2
VMEM_BYTES = 63 * 1024 * 1024
ANYWHERE = pl.BlockSpec(memory_space=pl.ANY)
IN_SMEM = pl.BlockSpec(memory_space=pltpu.SMEM)


class Sizes(NamedTuple):
    n_dp: int
    count: int
    slots: int
    kv_heads: int
    group_size: int
    tokens: int
    prefix_len: int

    @property
    def width(self):
        return self.kv_heads * HD

    @property
    def lanes(self):
        return self.kv_heads * self.group_size * HD


def dot(a, b, dims):
    return lax.dot_general(a, b, (dims, ((), ())), preferred_element_type=F32)


NN = ((1,), (0,))
NT = ((1,), (1,))


class Bag:
    pass


def attend_pair(z, at, places, q, og, kv, prefix, lens, factors, out, own_out, sink, apart):
    tokens, prefix_len, group_size = z.tokens, z.prefix_len, z.group_size
    scale = 1.0 / math.sqrt(HD)
    log_scale = scale * math.log2(math.e)
    whole = group_size - group_size % 2
    single = len(at) == 1
    members = range(len(at))
    sides = (0, 0) if single else (0, 1)
    two = 2 * tokens
    assert tokens & (tokens - 1) == 0
    token = lax.broadcasted_iota(jnp.int32, (1, two), 1) & (tokens - 1)
    key = lax.broadcasted_iota(jnp.int32, (tokens, two), 0)
    causal = key <= (lax.broadcasted_iota(jnp.int32, (tokens, two), 1) & (tokens - 1))
    left = lax.broadcasted_iota(jnp.int32, (1, two), 1) < tokens

    def head(k, h):
        start = (k * group_size + h) * HD
        return slice(start, start + HD)

    def rows(ref, k, blocks):
        return jnp.concatenate([ref[at[n], head(k, h)] for n, h in blocks], axis=0)

    def halves(part):
        none = jnp.zeros_like(part)
        return [jnp.where(left, part, none), jnp.where(left, none, part)]

    chunks = []
    for k in range(z.kv_heads):
        t = Bag()
        t.cols = slice(k * HD, (k + 1) * HD)
        t.key_p, t.value_p = prefix[0, :, t.cols], prefix[1, :, t.cols]
        t.keys = [kv[0, at[n], t.cols] for n in sides]
        t.values = [kv[1, at[n], t.cols] for n in sides]
        t.key_pair = jnp.concatenate(t.keys, axis=0)
        t.value_pair = jnp.concatenate(t.values, axis=0)
        t.key_t = jnp.concatenate([t.key_p.T, t.key_pair.T], axis=1)
        t.prefix_sums = {n: [] for n in members}
        t.self_sums = {n: [] for n in members}
        mine = []
        for n in members:
            c = Bag()
            c.k, c.t, c.side, c.blocks = k, t, n, [(n, h) for h in range(whole)]
            mine.append(c)
        if group_size % 2:
            c = Bag()
            c.k, c.t, c.side, c.blocks = k, t, None, [(n, group_size - 1) for n in sides]
            mine.append(c)
        t.left_over = len(mine)
        chunks += mine

    def products(c):
        t = c.t
        c.q_rows, c.g_rows = rows(q, c.k, c.blocks), rows(og, c.k, c.blocks)
        if c.side is None:
            key_s, value_s = t.key_pair, t.value_pair
        else:
            key_s, value_s = t.keys[c.side], t.values[c.side]
        c.scores = dot(jnp.concatenate([t.key_p, key_s], axis=0), c.q_rows, NT)
        c.gw = dot(jnp.concatenate([t.value_p, value_s], axis=0), c.g_rows, NT)

    def weigh(c, scores, gw, keep):
        scores_p, scores_s = scores[:prefix_len], scores[prefix_len:]
        gw_p, gw_s = gw[:prefix_len], gw[prefix_len:]
        if c.side is None:
            scores_s = jnp.where(left, scores_s[:tokens], scores_s[tokens:])
            gw_s = jnp.where(left, gw_s[:tokens], gw_s[tokens:])
        scores_s = jnp.where(causal, scores_s, NEG)
        top = jnp.maximum(
            jnp.max(scores_p, axis=0, keepdims=True), jnp.max(scores_s, axis=0, keepdims=True)
        )
        e_p = jnp.exp2((scores_p - top) * log_scale)
        e_s = jnp.exp2((scores_s - top) * log_scale)
        total = jnp.sum(e_p, axis=0, keepdims=True) + jnp.sum(e_s, axis=0, keepdims=True)
        weighted = jnp.sum(e_p * gw_p, axis=0, keepdims=True) + jnp.sum(
            e_s * gw_s, axis=0, keepdims=True
        )
        inverse = 1.0 / total
        delta = weighted * inverse
        gain = inverse * keep
        w_p, w_s = e_p * gain, e_s * gain
        d_p = (w_p * (gw_p - delta)).astype(BF16)
        d_s = (w_s * (gw_s - delta)).astype(BF16)
        return w_p.astype(BF16), w_s.astype(BF16), d_p, d_s

    def gradients(c):
        if c.side is None:
            length = jnp.where(left, lens[0], 0 if single else lens[1])
            gain = jnp.where(left, factors[0], factors[-1])
        else:
            length, gain = lens[c.side], factors[c.side]
        keep = jnp.where(token < length, gain, 0.0)
        parts = []
        for n in range(0, len(c.blocks), 2):
            at_lanes = slice(n * tokens, (n + 2) * tokens)
            parts.append(weigh(c, c.scores[:, at_lanes], c.gw[:, at_lanes], keep))
        w_p, w_s, d_p, d_s = (jnp.concatenate(part, axis=1) for part in zip(*parts))
        if c.side is None:
            d_s, w_s = halves(d_s), halves(w_s)
            c.d_wide = jnp.concatenate([d_p, *d_s], axis=0)
            c.d_all = jnp.concatenate([*halves(d_p), *d_s], axis=0) if apart else c.d_wide
            c.w_all = jnp.concatenate([*(halves(w_p) if apart else [w_p]), *w_s], axis=0)
        else:
            empty = jnp.zeros_like(d_s)
            c.d_wide = jnp.concatenate([d_p, empty, d_s] if c.side else [d_p, d_s, empty], axis=0)
            c.d_all = jnp.concatenate([d_p, d_s], axis=0)
            c.w_all = jnp.concatenate([w_p, w_s], axis=0)

    def outgoing(c):
        t = c.t
        q_grad = (dot(t.key_t, c.d_wide, NN) * scale).astype(BF16).T
        kg = dot(c.d_all, c.q_rows, NN)
        vg = dot(c.w_all, c.g_rows, NN)
        targets = members if c.side is None else [c.side]
        for place, (n, h) in enumerate(c.blocks):
            if c.side is not None or place < len(targets):
                out[places[n], :, head(c.k, h)] = q_grad[place * tokens : (place + 1) * tokens]
        many = 2 if c.side is None and apart else 1
        for place, n in enumerate(targets):
            if place < many:
                rows_p = slice(place * prefix_len, (place + 1) * prefix_len)
                t.prefix_sums[n if apart else 0].append((kg[rows_p], vg[rows_p]))
            start = many * prefix_len + place * tokens
            rows_s = slice(start, start + tokens)
            t.self_sums[n].append((kg[rows_s], vg[rows_s]))
        t.left_over -= 1
        if t.left_over == 0:
            for n in members:
                keys, values = zip(*t.self_sums[n])
                own_out[places[n], 0, :, t.cols] = (sum(keys) * scale).astype(BF16)
                own_out[places[n], 1, :, t.cols] = sum(values).astype(BF16)
                if apart or n == 0:
                    keys, values = zip(*t.prefix_sums[n])
                    sink(n, t.cols, sum(keys) * scale, sum(values))

    stages = (products, gradients, outgoing)
    for step in range(len(chunks) + len(stages) - 1):
        for late, stage in enumerate(stages):
            if 0 <= step - late < len(chunks):
                stage(chunks[step - late])


def token_rows(z, i):
    return pl.ds(pl.multiple_of(i * z.tokens, z.tokens), z.tokens)


def make_plan(z, me, resp_prompt, resp_len, rewards, places, order, lens, gains):
    for t in range(z.n_dp):
        places[t] = t * z.slots
    for i in range(z.count):
        turn = lax.rem(resp_prompt[me * z.count + i] - me + z.n_dp, z.n_dp)
        slot = places[turn]
        places[turn] = slot + 1
        order[slot] = i
        lens[slot] = resp_len[i]
        gains[slot] = rewards[i]


def prompt_total(z, prompt, tails):
    sums = jnp.zeros((1, tails.shape[2]), F32)
    for s in range(z.n_dp):
        tail = tails[s].astype(F32)
        sums += tail[0:1] + tail[1:2] + tail[2:3]
    lane = lax.broadcasted_iota(jnp.int32, sums.shape, 1)
    return jnp.sum(jnp.where(lane == prompt, sums, 0.0))


def reward_factor(z, reward, total, length):
    return (reward - total / z.count) * (z.tokens / length.astype(F32))


def pack_kernel(z, prompt_hbm, rewards_hbm, resp_prompt_hbm, payload, rewards, resp_prompt, staged, sems):
    me = lax.axis_index("dp")
    small = [
        pltpu.make_async_copy(rewards_hbm, rewards, sems.at[0]),
        pltpu.make_async_copy(resp_prompt_hbm, resp_prompt, sems.at[1]),
    ]
    large = [
        pltpu.make_async_copy(
            prompt_hbm.at[n], staged.at[pl.ds(n * z.prefix_len, z.prefix_len)], sems.at[2 + n]
        )
        for n in range(2)
    ]
    for copy in small + large:
        copy.start()
    for copy in small:
        copy.wait()
    lane = lax.broadcasted_iota(jnp.int32, (1, z.width), 1)
    sums = jnp.zeros((1, z.width), F32)
    for i in range(z.count):
        sums += jnp.where(lane == resp_prompt[me * z.count + i], rewards[i], 0.0)
    high = sums.astype(BF16).astype(F32)
    middle = (sums - high).astype(BF16).astype(F32)
    low = sums - high - middle
    row = lax.broadcasted_iota(jnp.int32, (TAIL, z.width), 0)
    pieces = jnp.where(row == 0, high, jnp.where(row == 1, middle, jnp.where(row == 2, low, 0.0)))
    staged[2 * z.prefix_len :, :] = pieces.astype(BF16)
    for copy in large:
        copy.wait()
    last = pltpu.make_async_copy(staged, payload, sems.at[0])
    last.start()
    last.wait()


def tail_copies(z, payloads, tails, sems):
    return [
        pltpu.make_async_copy(payloads[s].at[pl.ds(2 * z.prefix_len, TAIL)], tails.at[s], sems.at[s])
        for s in range(z.n_dp)
    ]


def row_copies(z, here, there, at_here, at_there, sems):
    (q0, og0, kv0), (q1, og1, kv1) = here, there
    return (
        pltpu.make_async_copy(q0.at[at_here], q1.at[at_there], sems.at[0]),
        pltpu.make_async_copy(og0.at[at_here], og1.at[at_there], sems.at[1]),
        pltpu.make_async_copy(kv0.at[0, at_here], kv1.at[0, at_there], sems.at[2]),
        pltpu.make_async_copy(kv0.at[1, at_here], kv1.at[1, at_there], sems.at[3]),
    )


def result_copies(z, out, own, q_out, self_out, place, at, sems):
    return (
        pltpu.make_async_copy(out.at[place], q_out.at[at], sems.at[place, 0]),
        pltpu.make_async_copy(own.at[place, 0], self_out.at[0, at], sems.at[place, 1]),
        pltpu.make_async_copy(own.at[place, 1], self_out.at[1, at], sems.at[place, 2]),
    )


def raw_kernel(z, *refs):
    small_hbm, given, payload = refs[:3], refs[3:6], refs[6]
    plan, sorted_out, (q_out, self_out, grads_out) = refs[7:10], refs[10:13], refs[13:16]
    (resp_prompt, resp_len, rewards, places, q, og, kv, prefix, out, own, grads,
     sem_small, sem_in, sem_sorted, sem_out) = refs[16:]
    order, lens, gains = plan
    held = (q, og, kv)
    me = lax.axis_index("dp")
    small = [
        pltpu.make_async_copy(src, dst, sem_small.at[n])
        for n, (src, dst) in enumerate(zip(small_hbm, (resp_prompt, resp_len, rewards)))
    ]
    small += [
        pltpu.make_async_copy(payload.at[pl.ds(n * z.prefix_len, z.prefix_len)], prefix.at[n], sem_small.at[3 + n])
        for n in range(2)
    ]
    for copy in small:
        copy.start()
    for copy in small[:3]:
        copy.wait()
    make_plan(z, me, resp_prompt, resp_len, rewards, places, order, lens, gains)

    def copies_in(slot):
        return row_copies(
            z, given, held, token_rows(z, order[slot]), token_rows(z, slot), sem_in.at[slot]
        )

    def copies_sorted(slot):
        return row_copies(
            z, held, sorted_out, token_rows(z, slot), token_rows(z, slot - z.slots), sem_sorted.at[slot - z.slots]
        )

    def start_in(slot, _):
        for copy in copies_in(slot):
            copy.start()
        return 0

    lax.fori_loop(0, z.count, start_in, 0)
    for copy in small[3:]:
        copy.wait()

    def unit(u, _):
        at = [u * PAIR + n for n in range(PAIR)]
        for slot in at:
            for copy in copies_in(slot):
                copy.wait()

        def sink(n, cols, key_grad, value_grad):
            grads[at[n], 0, :, cols] = key_grad.astype(BF16)
            grads[at[n], 1, :, cols] = value_grad.astype(BF16)

        attend_pair(
            z, [token_rows(z, n) for n in at], at, q, og, kv, prefix, [lens[n] for n in at], [1.0] * PAIR, out, own,
            sink, True,
        )
        return 0

    lax.fori_loop(0, z.slots // PAIR, unit, 0)
    last = [
        pltpu.make_async_copy(src, dst, sem_out.at[n])
        for n, (src, dst) in enumerate([(out, q_out), (own, self_out), (grads, grads_out)])
    ]
    for copy in last:
        copy.start()

    def start_sorted(slot, _):
        for copy in copies_in(slot):
            copy.wait()
        for copy in copies_sorted(slot):
            copy.start()
        return 0

    def end_sorted(slot, _):
        for copy in copies_sorted(slot):
            copy.wait()
        return 0

    lax.fori_loop(z.slots, z.count, start_sorted, 0)
    lax.fori_loop(z.slots, z.count, end_sorted, 0)
    for copy in last:
        copy.wait()


def group_kernel(z, turns, aliased, *refs):
    plan_hbm, given, payloads = refs[:3], refs[3:6], refs[6 : 6 + z.n_dp]
    refs = refs[6 + z.n_dp + aliased :]
    (q_out, self_out), grads_out = refs[:2], refs[2 : 2 + len(turns)]
    (order, lens, gains, factors, q, og, kv, prefix, tails, acc, out, own, grads,
     sem_plan, sem_prefix, sem_in, sem_out, sem_grads) = refs[2 + len(turns) :]
    me = lax.axis_index("dp")
    n_slots = len(turns) * z.slots
    starts = [(turn - 1) * z.slots * z.tokens for turn in turns]
    span = z.slots * z.tokens

    first = [pltpu.make_async_copy(src, dst, sem_plan.at[n]) for n, (src, dst) in enumerate(zip(plan_hbm, (order, lens, gains)))]
    first += tail_copies(z, payloads, tails, sem_grads)
    second = [
        [
            pltpu.make_async_copy(
                payloads[turn].at[pl.ds(n * z.prefix_len, z.prefix_len)], prefix.at[t, n], sem_prefix.at[t, n]
            )
            for n in range(2)
        ]
        + list(
            row_copies(z, given, (q, og, kv), pl.ds(starts[t], span), pl.ds(t * span, span), sem_in.at[t])
        )
        for t, turn in enumerate(turns)
    ]
    for copy in [*first, *sum(second, [])]:
        copy.start()
    for copy in first:
        copy.wait()
    slots = [turn * z.slots + n for turn in turns for n in range(z.slots)]
    for t, turn in enumerate(turns):
        total = prompt_total(z, lax.rem(me + turn, z.n_dp), tails)
        for place in range(t * z.slots, (t + 1) * z.slots):
            slot = slots[place]
            factors[place] = reward_factor(z, gains[slot], total, lens[slot])
    order_of, lens_of = [order[slot] for slot in slots], [lens[slot] for slot in slots]
    for place in range(n_slots):
        order[place] = order_of[place]
        lens[place] = lens_of[place]
    acc[...] = jnp.zeros(acc.shape, F32)
    for copy in sum(second, []):
        copy.wait()

    def copies_out(place):
        return result_copies(z, out, own, q_out, self_out, place, token_rows(z, order[place]), sem_out)

    def unit(u, _):
        at = [u * PAIR + n for n in range(PAIR)]
        t = u // (z.slots // PAIR)

        def sink(_, cols, key_grad, value_grad):
            acc[t, 0, :, cols] += key_grad
            acc[t, 1, :, cols] += value_grad

        attend_pair(
            z, [token_rows(z, n) for n in at], at, q, og, kv, prefix.at[t], [lens[n] for n in at],
            [factors[n] for n in at], out, own, sink, False,
        )
        for place in at:
            for copy in copies_out(place):
                copy.start()
        return 0

    lax.fori_loop(0, n_slots // PAIR, unit, 0)
    grads[...] = acc[...].astype(BF16)
    last = [pltpu.make_async_copy(grads.at[t], grads_out[t], sem_grads.at[t]) for t in range(len(turns))]
    for copy in last:
        copy.start()
    for place in range(n_slots):
        for copy in copies_out(place):
            copy.wait()
    for copy in last:
        copy.wait()


def finish_kernel(z, *refs):
    plan_hbm, payloads, raw_hbm = refs[:3], refs[3 : 3 + z.n_dp], refs[3 + z.n_dp : 7 + z.n_dp]
    q_out, self_out, grads_out = refs[9 + z.n_dp : 12 + z.n_dp]
    order, lens, gains, tails, out, own, per_resp, come, grads, sem_small, sem_tails, sem_out = refs[12 + z.n_dp :]
    copies = [
        pltpu.make_async_copy(src, dst, sem_small.at[n])
        for n, (src, dst) in enumerate(zip([*plan_hbm, *raw_hbm], (order, lens, gains, out, own, per_resp, come)))
    ]
    copies += tail_copies(z, payloads, tails, sem_tails)
    for copy in copies:
        copy.start()
    for copy in copies:
        copy.wait()
    total = prompt_total(z, lax.axis_index("dp"), tails)
    results = []
    summed = come[...].astype(F32)
    for slot in range(z.slots):
        factor = reward_factor(z, gains[slot], total, lens[slot])
        out[slot] = (out[slot].astype(F32) * factor).astype(BF16)
        own[slot] = (own[slot].astype(F32) * factor).astype(BF16)
        results.append(result_copies(z, out, own, q_out, self_out, slot, token_rows(z, order[slot]), sem_out))
        for copy in results[-1]:
            copy.start()
        summed += per_resp[slot].astype(F32) * factor
    grads[...] = summed
    last = pltpu.make_async_copy(grads, grads_out, sem_small.at[0])
    last.start()
    for copy in sum(results, ()):
        copy.wait()
    last.wait()


def near_shards(z, prompt_kv, resp_q, resp_kv, out_grad, rewards, resp_prompt, resp_len):
    n_dp = z.n_dp
    assert z.slots % PAIR == 0
    shape = jax.ShapeDtypeStruct
    one = (2, z.prefix_len, z.width)
    params = pltpu.CompilerParams(vmem_limit_bytes=VMEM_BYTES)
    cost = pl.CostEstimate(flops=0, bytes_accessed=0, transcendentals=0)
    small = (resp_prompt, resp_len, rewards)
    payload = pl.pallas_call(
        functools.partial(pack_kernel, z),
        out_shape=jax.ShapeDtypeStruct((2 * z.prefix_len + TAIL, z.width), BF16),
        in_specs=[ANYWHERE] * 3,
        out_specs=ANYWHERE,
        scratch_shapes=[
            pltpu.SMEM(rewards.shape, F32),
            pltpu.SMEM(resp_prompt.shape, jnp.int32),
            pltpu.VMEM((2 * z.prefix_len + TAIL, z.width), BF16),
            pltpu.SemaphoreType.DMA((4,)),
        ],
        compiler_params=pltpu.CompilerParams(vmem_limit_bytes=VMEM_BYTES),
        name="pack",
    )(prompt_kv, rewards, resp_prompt)

    away = sorted(range(1, n_dp), key=lambda s: -min(s, n_dp - s))
    payloads = {0: payload}
    for s in away:
        payloads[s] = lax.ppermute(payload, "dp", [((i + s) % n_dp, i) for i in range(n_dp)])
    everyone = [payloads[s] for s in range(n_dp)]

    given = (resp_q, out_grad, resp_kv)
    slots, count, rest = z.slots, z.count, (z.count - z.slots) * z.tokens
    plan_smem = [pltpu.SMEM((count,), kind) for kind in (jnp.int32, jnp.int32, F32)]
    results = pl.pallas_call(
        functools.partial(raw_kernel, z),
        out_shape=[
            shape((count,), jnp.int32),
            shape((count,), jnp.int32),
            shape((count,), F32),
            shape((rest, z.lanes), BF16),
            shape((rest, z.lanes), BF16),
            shape((2, rest, z.width), BF16),
            shape((slots, z.tokens, z.lanes), BF16),
            shape((slots, 2, z.tokens, z.width), BF16),
            shape((slots,) + one, BF16),
        ],
        in_specs=[ANYWHERE] * 7,
        out_specs=[IN_SMEM] * 3 + [ANYWHERE] * 6,
        scratch_shapes=[
            *[pltpu.SMEM(x.shape, x.dtype) for x in small],
            pltpu.SMEM((n_dp,), jnp.int32),
            pltpu.VMEM(resp_q.shape, BF16),
            pltpu.VMEM(resp_q.shape, BF16),
            pltpu.VMEM(resp_kv.shape, BF16),
            pltpu.VMEM(one, BF16),
            pltpu.VMEM((slots, z.tokens, z.lanes), BF16),
            pltpu.VMEM((slots, 2, z.tokens, z.width), BF16),
            pltpu.VMEM((slots,) + one, BF16),
            pltpu.SemaphoreType.DMA((5,)),
            pltpu.SemaphoreType.DMA((count, 4)),
            pltpu.SemaphoreType.DMA((count - slots, 4)),
            pltpu.SemaphoreType.DMA((3,)),
        ],
        compiler_params=params,
        cost_estimate=cost,
        name="raw_grads",
    )(*small, *given, payload)
    plan, in_order, raw = results[:3], results[3:6], results[6:]

    first = len(away) // 2
    written = ()
    arrived = []
    for turns in (tuple(away[:first]), tuple(away[first:])):
        if not turns:
            continue
        n_slots = len(turns) * slots
        operands = [*plan, *in_order, *everyone, *written]
        results = pl.pallas_call(
            functools.partial(group_kernel, z, turns, len(written)),
            out_shape=[shape(resp_q.shape, BF16), shape(resp_kv.shape, BF16)] + [shape(one, BF16)] * len(turns),
            in_specs=[ANYWHERE] * len(operands),
            out_specs=[ANYWHERE] * (2 + len(turns)),
            input_output_aliases={len(operands) - 2: 0, len(operands) - 1: 1} if written else {},
            scratch_shapes=[
                *plan_smem,
                pltpu.SMEM((n_slots,), F32),
                pltpu.VMEM((n_slots * z.tokens, z.lanes), BF16),
                pltpu.VMEM((n_slots * z.tokens, z.lanes), BF16),
                pltpu.VMEM((2, n_slots * z.tokens, z.width), BF16),
                pltpu.VMEM((len(turns),) + one, BF16),
                pltpu.VMEM((n_dp, TAIL, z.width), BF16),
                pltpu.VMEM((len(turns),) + one, F32),
                pltpu.VMEM((n_slots, z.tokens, z.lanes), BF16),
                pltpu.VMEM((n_slots, 2, z.tokens, z.width), BF16),
                pltpu.VMEM((len(turns),) + one, BF16),
                pltpu.SemaphoreType.DMA((3,)),
                pltpu.SemaphoreType.DMA((len(turns), 2)),
                pltpu.SemaphoreType.DMA((len(turns), 4)),
                pltpu.SemaphoreType.DMA((n_slots, 3)),
                pltpu.SemaphoreType.DMA((n_dp,)),
            ],
            compiler_params=params,
            cost_estimate=cost,
            name="group_grads",
        )(*operands)
        written = results[:2]
        for turn, grads in zip(turns, results[2:]):
            arrived.append(lax.ppermute(grads, "dp", [(i, (i + turn) % n_dp) for i in range(n_dp)]))
    operands = [*plan, *everyone, *raw, arrived[0], *written]
    q_out, self_out, own_grads = pl.pallas_call(
        functools.partial(finish_kernel, z),
        out_shape=[shape(resp_q.shape, BF16), shape(resp_kv.shape, BF16), shape(one, F32)],
        in_specs=[ANYWHERE] * len(operands),
        out_specs=[ANYWHERE] * 3,
        input_output_aliases={len(operands) - 2: 0, len(operands) - 1: 1},
        scratch_shapes=[
            *plan_smem,
            pltpu.VMEM((n_dp, TAIL, z.width), BF16),
            pltpu.VMEM((slots, z.tokens, z.lanes), BF16),
            pltpu.VMEM((slots, 2, z.tokens, z.width), BF16),
            pltpu.VMEM((slots,) + one, BF16),
            pltpu.VMEM(one, BF16),
            pltpu.VMEM(one, F32),
            pltpu.SemaphoreType.DMA((7,)),
            pltpu.SemaphoreType.DMA((n_dp,)),
            pltpu.SemaphoreType.DMA((slots, 3)),
        ],
        compiler_params=params,
        cost_estimate=cost,
        name="finish_own",
    )(*operands)
    prefix_out = sum(part.astype(F32) for part in [own_grads, *arrived[1:]]).astype(BF16)
    return (q_out, self_out, prefix_out)


def far_kernel(z, *refs):
    (resp_prompt, resp_len, rewards, q_hbm, og_hbm, kv_hbm, prompts, q_out, self_out, prefix_outs,
     totals, lens, factors, q, og, kv, prefix, out, own, grads, sem_in, sem_prefix, sem_out) = refs
    me = lax.axis_index("dp")

    for p in range(z.n_dp):
        totals[p] = 0.0

    def copies_in(slot):
        rows = token_rows(z, slot)
        prompt = resp_prompt[me * z.count + slot]
        return (
            *row_copies(z, (q_hbm, og_hbm, kv_hbm), (q, og, kv), rows, rows, sem_in.at[slot]),
            pltpu.make_async_copy(prompts.at[prompt], prefix.at[slot], sem_prefix.at[slot]),
        )

    def copies_out(slot):
        rows = token_rows(z, slot)
        return (
            *result_copies(z, out, own, q_out, self_out, slot, rows, sem_out),
            pltpu.make_async_copy(grads.at[slot], prefix_outs.at[slot], sem_out.at[slot, 3]),
        )

    def start(slot, _):
        for copy in copies_in(slot):
            copy.start()
        return 0

    lax.fori_loop(0, z.count, start, 0)

    def add(i, _):
        prompt = resp_prompt[i]
        totals[prompt] = totals[prompt] + rewards[i]
        return 0

    lax.fori_loop(0, z.n_dp * z.count, add, 0)

    def find_factor(slot, _):
        place = me * z.count + slot
        lens[slot] = resp_len[slot]
        factors[slot] = reward_factor(z, rewards[place], totals[resp_prompt[place]], resp_len[slot])
        return 0

    lax.fori_loop(0, z.count, find_factor, 0)

    def unit(slot, _):
        for copy in copies_in(slot):
            copy.wait()

        def sink(_, cols, key_grad, value_grad):
            grads[slot, 0, :, cols] = key_grad.astype(BF16)
            grads[slot, 1, :, cols] = value_grad.astype(BF16)

        attend_pair(
            z, [token_rows(z, slot)], [slot], q, og, kv, prefix.at[slot], [lens[slot]], [factors[slot]], out, own, sink, True
        )
        for copy in copies_out(slot):
            copy.start()
        return 0

    lax.fori_loop(0, z.count, unit, 0)

    def end(slot, _):
        for copy in copies_out(slot):
            copy.wait()
        return 0

    lax.fori_loop(0, z.count, end, 0)


def far_shards(z, prompt_kv, resp_q, resp_kv, out_grad, rewards, resp_prompt, resp_len):
    assert z.slots == 1
    count, n_dp = z.count, z.n_dp
    one = (2, z.prefix_len, z.width)
    smem = pl.BlockSpec(memory_space=pltpu.SMEM)
    q_out, self_out, per_resp = pl.pallas_call(
        functools.partial(far_kernel, z),
        out_shape=[
            jax.ShapeDtypeStruct(resp_q.shape, BF16),
            jax.ShapeDtypeStruct(resp_kv.shape, BF16),
            jax.ShapeDtypeStruct((count,) + one, BF16),
        ],
        in_specs=[smem] * 3 + [ANYWHERE] * 4,
        out_specs=[ANYWHERE] * 3,
        scratch_shapes=[
            pltpu.SMEM((n_dp,), F32),
            pltpu.SMEM((count,), jnp.int32),
            pltpu.SMEM((count,), F32),
            pltpu.VMEM(resp_q.shape, BF16),
            pltpu.VMEM(resp_q.shape, BF16),
            pltpu.VMEM(resp_kv.shape, BF16),
            pltpu.VMEM((count,) + one, BF16),
            pltpu.VMEM((count, z.tokens, z.lanes), BF16),
            pltpu.VMEM((count, 2, z.tokens, z.width), BF16),
            pltpu.VMEM((count,) + one, BF16),
            pltpu.SemaphoreType.DMA((count, 4)),
            pltpu.SemaphoreType.DMA((count,)),
            pltpu.SemaphoreType.DMA((count, 4)),
        ],
        compiler_params=pltpu.CompilerParams(vmem_limit_bytes=VMEM_BYTES),
        name="far_grads",
    )(
        resp_prompt,
        resp_len,
        lax.all_gather(rewards, "dp", axis=0, tiled=True),
        resp_q,
        out_grad,
        resp_kv,
        lax.all_gather(prompt_kv, "dp", axis=0),
    )
    my_prompts = lax.dynamic_slice_in_dim(resp_prompt, lax.axis_index("dp") * count, count)
    route = (jnp.arange(n_dp, dtype=jnp.int32)[:, None] == my_prompts[None, :]).astype(BF16)
    outgoing = jnp.dot(route, per_resp.reshape(count, -1), preferred_element_type=F32).astype(BF16)
    outgoing = outgoing.reshape((n_dp,) + one)
    incoming = lax.all_to_all(outgoing, "dp", split_axis=0, concat_axis=0, tiled=True)
    prefix_out = jnp.sum(incoming, axis=0, dtype=F32).astype(BF16)
    return (q_out, self_out, prefix_out)


def shards(prompt_kv, resp_q, resp_kv, out_grad, rewards, resp_prompt, resp_len):
    n_dp = lax.axis_size("dp")
    count = rewards.shape[0]
    prefix_len, width = prompt_kv.shape[1:]
    slots = (count + n_dp - 1) // n_dp
    z = Sizes(
        n_dp, count, slots, width // HD, resp_q.shape[1] // width, resp_q.shape[0] // count, prefix_len
    )
    part = near_shards if count // slots == n_dp else far_shards
    return part(z, prompt_kv, resp_q, resp_kv, out_grad, rewards, resp_prompt, resp_len)


def solution(mesh):
    in_specs = (
        P(None, ("groups", "dp"), "tensor"),
        P(("groups", "dp"), "tensor"),
        P(None, ("groups", "dp"), "tensor"),
        P(("groups", "dp"), "tensor"),
        P(("groups", "dp")),
        P("groups"),
        P(("groups", "dp")),
    )
    out_specs = (
        P(("groups", "dp"), "tensor"),
        P(None, ("groups", "dp"), "tensor"),
        P(None, ("groups", "dp"), "tensor"),
    )
    return jax.shard_map(shards, mesh=mesh, in_specs=in_specs, out_specs=out_specs, check_vma=False)
```

time: 48.4 us -> 45.2 us (0.934)
  starting transfers between devices: 13.5 us -> 10.9 us
  Pallas kernels: 26.1 us -> 25.1 us
  local copies, waits for them, and re-layouts: 0.69 us -> 1.36 us
    pallas_call x1, Pallas kernels: 5.11 us -> 1.58 us  [near_shards(): pl.pallas_call(functools.partial(pack_kernel, z), out_shape=jax.ShapeDtyp...]
    pallas_call x4, Pallas kernels: 21 us -> 23.5 us  [the longest x2 12.4 us: near_shards(): pl.pallas_call(functools.partial(group_kernel, z, turns, len(written)), o...]
    ppermute x3, starting transfers between devices: 6.45 us -> 4.83 us  [near_shards(): lax.ppermute(grads, 'dp', [(i, (i + turn) % n_dp) for i in range(n_dp)])]
    ppermute x3, starting transfers between devices: 7.01 us -> 6.11 us  [near_shards(): lax.ppermute(payload, 'dp', [((i + s) % n_dp, i) for i in range(n_dp)])]
    unnamed x6 -> x8, local copies, waits for them, and re-layouts: 0.69 us -> 1.36 us
  transfers between devices with their start and end apart: 6 -> 6, of which waited for: 3 -> 2; matrix products, arithmetic and copies ran while one was open for 0% -> 0% of each run, Pallas kernels for 33% -> 42%
where the time goes in v5:
time: 45.2 us; the launch traced here: 44.9 us
  Pallas kernels  25.1 us (56%)
  starting transfers between devices  10.9 us (24%)
  waiting for transfers between devices  5.15 us (11%)
  other arithmetic  1.65 us (4%)
  local copies, waits for them, and re-layouts  1.36 us (3%)
  between operations  0.7 us (2%)
    pallas_call x2, Pallas kernels, near_shards(): pl.pallas_call(functools.partial(group_kernel, z, turns, len(written)), o...  12.4 us
    pallas_call x1, Pallas kernels, near_shards(): pl.pallas_call(functools.partial(raw_kernel, z), out_shape=[shape((count,...  8.38 us
    ppermute x3, starting transfers between devices, near_shards(): lax.ppermute(payload, 'dp', [((i + s) % n_dp, i) for i in range(n_dp)])  6.11 us
    ppermute x3, starting transfers between devices, near_shards(): lax.ppermute(grads, 'dp', [(i, (i + turn) % n_dp) for i in range(n_dp)])  4.83 us
    pallas_call x1, Pallas kernels, near_shards(): pl.pallas_call(functools.partial(finish_kernel, z), out_shape=[shape(resp...  2.76 us
    ppermute x3, waiting for transfers between devices, near_shards(): lax.ppermute(payload, 'dp', [((i + s) % n_dp, i) for i in range(n_dp)])  2.61 us
    ppermute x3, waiting for transfers between devices, near_shards(): lax.ppermute(grads, 'dp', [(i, (i + turn) % n_dp) for i in range(n_dp)])  2.54 us
    convert_element_type x1, other arithmetic, near_shards(): sum((part.astype(F32) for part in [own_grads, *arrived[1:]])).astype(BF16)  1.65 us
  transfers between devices with their start and end apart: 6, of which 2 were waited for; matrix products, arithmetic and copies ran while one was open for 0% of the time, Pallas kernels for 42%

profile of v5, /device:TPU:0, one launch (start us, length us, event | category | flops | bytes accessed | tf_op | source)
XLA Modules:
  0.0 44.9 jit_solution(12927760503652045929)
XLA Ops:
  0.6 1.6 %pack.1.refs_6_.refs_3_ = bf16[272,256]{1,0:T(8,128)(2,1)} custom-call(bf16[2,128,256]{2,1,0:T(8,128)(2,1)} %prompt_hbm.1, f32[16]{0:T(128)} %refs_2_.1, s32[64]{0:T(128)} %refs_0_.1), custom_call_target="tpu_custom_call" | custom-call | tf_op jit(solution)/shard_map/pack/pallas_call | solution.py:479
  2.2 5.1 %collective-permute-start = (bf16[272,256]{1,0:T(8,128)(2,1)}, bf16[272,256]{1,0:T(8,128)(2,1)S(1)}, u32[]{:S(2)}, u32[]{:S(2)}) collective-permute-start(bf16[272,256]{1,0:T(8,128)(2,1)} %pack.1.refs_6_.refs_3_), channel_id=1, source_target_pairs={{4,0},{8,4},{12,8},{0,12},{5,1},{9,5},{13,9},{1,13},{6,2},{10,6},{... | collective-permute-start | bytes 417800 | tf_op jit(solution)/shard_map/ppermute | solution.py:497
  7.3 0.0 collective-permute-start.1
  7.3 1.0 %collective-permute-start.2 = (bf16[272,256]{1,0:T(8,128)(2,1)}, bf16[272,256]{1,0:T(8,128)(2,1)S(1)}, u32[]{:S(2)}, u32[]{:S(2)}) collective-permute-start(bf16[272,256]{1,0:T(8,128)(2,1)} %pack.1.refs_6_.refs_3_), channel_id=1, source_target_pairs={{12,0},{0,4},{4,8},{8,12},{13,1},{1,5},{5,9},{9,13},{14,2},{2,6},{... | collective-permute-start | bytes 417800 | tf_op jit(solution)/shard_map/ppermute | solution.py:497
  8.3 8.4 %raw_grads.1 = (s32[16]{0:T(128)}, s32[16]{0:T(128)}, f32[16]{0:T(128)}, bf16[768,1280]{1,0:T(8,128)(2,1)}, bf16[768,1280]{1,0:T(8,128)(2,1)}, /*index=5*/bf16[2...) custom-call(s32[64]{0:T(128)} %refs_0_.1, ...), custom_call_target="tpu_custom_call" | custom-call | tf_op jit(solution)/shard_map/raw_grads/pallas_call | solution.py:503
  16.7 0.0 collective-permute-done.refs_7_.refs_4_
  16.7 0.0 copy-start
  16.7 2.6 %collective-permute-done.1.refs_8_.refs_5_ = bf16[272,256]{1,0:T(8,128)(2,1)S(1)} collective-permute-done((bf16[272,256]{1,0:T(8,128)(2,1)}, bf16[272,256]{1,0:T(8,128)(2,1)S(1)}, u32[]{:S(2)}, u32[]{:S(2)}) %collective-permute-start.1) | collective-permute-done | bytes 139296 | tf_op jit(solution)/shard_map/ppermute | solution.py:497
  19.3 0.0 copy-start.1
  19.4 0.0 collective-permute-done.2.refs_9_.refs_6_
  19.4 0.0 copy-start.2
  19.4 0.0 copy-done
  19.4 0.6 %copy-done.1 = bf16[272,256]{1,0:T(8,128)(2,1)} copy-done((bf16[272,256]{1,0:T(8,128)(2,1)}, bf16[272,256]{1,0:T(8,128)(2,1)S(1)}, u32[]{:S(2)}) %copy-start.1) | copy-done | bytes 139288
  20.0 0.0 copy-done.2
  20.1 4.7 %group_grads.2 = (bf16[1024,1280]{1,0:T(8,128)(2,1)}, bf16[2,1024,256]{2,1,0:T(8,128)(2,1)}, bf16[2,128,256]{2,1,0:T(8,128)(2,1)}) custom-call(s32[16]{0:T(128)} %get-tuple-element.22.refs_0_, s32[16]{0:T(128)} %get-tuple-element.23.refs_1_, f32[16]{0:T(128)} %get-tuple-element.24.refs_2_, bf16[768,1280]{1,0:T(8,128)(2,1)} %get-tuple-element.28.refs_3_, ...), custom_call_target="tpu_custom_call" | custom-call | tf_op jit(solution)/shard_map/group_grads/pallas_call | solution.py:547
  24.8 2.7 %collective-permute-start.3 = (bf16[2,128,256]{2,1,0:T(8,128)(2,1)}, bf16[2,128,256]{2,1,0:T(8,128)(2,1)S(1)}, u32[]{:S(2)}, u32[]{:S(2)}) collective-permute-start(bf16[2,128,256]{2,1,0:T(8,128)(2,1)} %get-tuple-element.31), channel_id=1, source_target_pairs={{0,8},{4,12},{8,0},{12,4},{1,9},{5,13},{9,1},{13,5},{2,10},{6,14},... | collective-permute-start | bytes 393224 | tf_op jit(solution)/shard_map/ppermute | solution.py:577
  27.5 7.7 %group_grads.3 = (bf16[1024,1280]{1,0:T(8,128)(2,1)}, bf16[2,1024,256]{2,1,0:T(8,128)(2,1)}, bf16[2,128,256]{2,1,0:T(8,128)(2,1)}, bf16[2,128,256]{2,1,0:T(8,128)(2,1)}) custom-call(s32[16]{0:T(128)} %get-tuple-element.22.refs_0_, s32[16]{0:T(128)} %get-tuple-element.23.refs_1_, ...), custom_call_target="tpu_custom_call", output_to_operand_aliasing={{0}: (10, {}), {1}: (11, {})} | custom-call | tf_op jit(solution)/shard_map/group_grads/pallas_call | solution.py:547
  35.2 0.6 %collective-permute-start.5 = (bf16[2,128,256]{2,1,0:T(8,128)(2,1)}, bf16[2,128,256]{2,1,0:T(8,128)(2,1)S(1)}, u32[]{:S(2)}, u32[]{:S(2)}) collective-permute-start(bf16[2,128,256]{2,1,0:T(8,128)(2,1)} %get-tuple-element.40), channel_id=1, source_target_pairs={{0,12},{4,0},{8,4},{12,8},{1,13},{5,1},{9,5},{13,9},{2,14},{6,2},{... | collective-permute-start | bytes 393224 | tf_op jit(solution)/shard_map/ppermute | solution.py:577
  35.8 1.5 %collective-permute-start.4 = (bf16[2,128,256]{2,1,0:T(8,128)(2,1)}, bf16[2,128,256]{2,1,0:T(8,128)(2,1)S(1)}, u32[]{:S(2)}, u32[]{:S(2)}) collective-permute-start(bf16[2,128,256]{2,1,0:T(8,128)(2,1)} %get-tuple-element.39), channel_id=1, source_target_pairs={{0,4},{4,8},{8,12},{12,0},{1,5},{5,9},{9,13},{13,1},{2,6},{6,10},{... | collective-permute-start | bytes 393224 | tf_op jit(solution)/shard_map/ppermute | solution.py:577
  37.3 0.0 collective-permute-done.3.refs_10_
  37.3 0.0 copy-start.3
  37.3 0.7 %copy-done.3 = bf16[2,128,256]{2,1,0:T(8,128)(2,1)} copy-done((bf16[2,128,256]{2,1,0:T(8,128)(2,1)}, bf16[2,128,256]{2,1,0:T(8,128)(2,1)S(1)}, u32[]{:S(2)}) %copy-start.3) | copy-done | bytes 131096
  38.0 2.8 %finish_own.1 = (bf16[1024,1280]{1,0:T(8,128)(2,1)}, bf16[2,1024,256]{2,1,0:T(8,128)(2,1)}, f32[2,128,256]{2,1,0:T(8,128)}) custom-call(s32[16]{0:T(128)} %get-tuple-element.22.refs_0_, s32[16]{0:T(128)} %get-tuple-element.23.refs_1_, f32[16]{0:T(128)} %get-tuple-element.24.refs_2_, ...), custom_call_target="tpu_custom_call", output_to_operand_aliasing={{0}: (11, {}), {1}: (12, {})} | custom-call | tf_op jit(solution)/shard_map/finish_own/pallas_call | solution.py:579
  40.7 2.5 %collective-permute-done.5 = bf16[2,128,256]{2,1,0:T(8,128)(2,1)S(1)} collective-permute-done((bf16[2,128,256]{2,1,0:T(8,128)(2,1)}, bf16[2,128,256]{2,1,0:T(8,128)(2,1)S(1)}, u32[]{:S(2)}, u32[]{:S(2)}) %collective-permute-start.5) | collective-permute-done | bytes 131104 | tf_op jit(solution)/shard_map/ppermute | solution.py:577
  43.3 0.0 collective-permute-done.4
  43.3 1.6 %add_convert_fusion = bf16[2,128,256]{2,1,0:T(8,128)(2,1)} fusion(bf16[2,128,256]{2,1,0:T(8,128)(2,1)S(1)} %collective-permute-done.5, f32[2,128,256]{2,1,0:T(8,128)} %get-tuple-element.38, bf16[2,128,256]{2,1,0:T(8,128)(2,1)S(1)} %collective-permute-done.4), kind=kLoop, calls=%fused_computation | loop fusion | flops 327680 | bytes 655360 | tf_op jit(solution)/shard_map/convert_element_type | solution.py:601
Async XLA Ops:
  2.2 14.5 %collective-permute-start = (bf16[272,256]{1,0:T(8,128)(2,1)}, bf16[272,256]{1,0:T(8,128)(2,1)S(1)}, u32[]{:S(2)}, u32[]{:S(2)}) collective-permute-start(bf16[272,256]{1,0:T(8,128)(2,1)} %pack.1.refs_6_.refs_3_), channel_id=1, source_target_pairs={{4,0},{8,4},{12,8},{0,12},{5,1},{9,5},{13,9},{1,13},{6,2},{10,6},{... | collective-permute-start | bytes 417800 | tf_op jit(solution)/shard_map/ppermute | solution.py:497
  7.3 12.0 %collective-permute-start.1 = (bf16[272,256]{1,0:T(8,128)(2,1)}, bf16[272,256]{1,0:T(8,128)(2,1)S(1)}, u32[]{:S(2)}, u32[]{:S(2)}) collective-permute-start(bf16[272,256]{1,0:T(8,128)(2,1)} %pack.1.refs_6_.refs_3_), channel_id=1, source_target_pairs={{8,0},{12,4},{0,8},{4,12},{9,1},{13,5},{1,9},{5,13},{10,2},{14,6},... | collective-permute-start | bytes 417800 | tf_op jit(solution)/shard_map/ppermute | solution.py:497
  7.3 12.0 %collective-permute-start.2 = (bf16[272,256]{1,0:T(8,128)(2,1)}, bf16[272,256]{1,0:T(8,128)(2,1)S(1)}, u32[]{:S(2)}, u32[]{:S(2)}) collective-permute-start(bf16[272,256]{1,0:T(8,128)(2,1)} %pack.1.refs_6_.refs_3_), channel_id=1, source_target_pairs={{12,0},{0,4},{4,8},{8,12},{13,1},{1,5},{5,9},{9,13},{14,2},{2,6},{... | collective-permute-start | bytes 417800 | tf_op jit(solution)/shard_map/ppermute | solution.py:497
  16.7 2.6 %copy-start = (bf16[272,256]{1,0:T(8,128)(2,1)}, bf16[272,256]{1,0:T(8,128)(2,1)S(1)}, u32[]{:S(2)}) copy-start(bf16[272,256]{1,0:T(8,128)(2,1)S(1)} %collective-permute-done.refs_7_.refs_4_) | copy-start | bytes 417796
  19.3 0.7 %copy-start.1 = (bf16[272,256]{1,0:T(8,128)(2,1)}, bf16[272,256]{1,0:T(8,128)(2,1)S(1)}, u32[]{:S(2)}) copy-start(bf16[272,256]{1,0:T(8,128)(2,1)S(1)} %collective-permute-done.1.refs_8_.refs_5_) | copy-start | bytes 417796
  19.4 0.7 %copy-start.2 = (bf16[272,256]{1,0:T(8,128)(2,1)}, bf16[272,256]{1,0:T(8,128)(2,1)S(1)}, u32[]{:S(2)}) copy-start(bf16[272,256]{1,0:T(8,128)(2,1)S(1)} %collective-permute-done.2.refs_9_.refs_6_) | copy-start | bytes 417796
  24.8 12.5 %collective-permute-start.3 = (bf16[2,128,256]{2,1,0:T(8,128)(2,1)}, bf16[2,128,256]{2,1,0:T(8,128)(2,1)S(1)}, u32[]{:S(2)}, u32[]{:S(2)}) collective-permute-start(bf16[2,128,256]{2,1,0:T(8,128)(2,1)} %get-tuple-element.31), channel_id=1, source_target_pairs={{0,8},{4,12},{8,0},{12,4},{1,9},{5,13},{9,1},{13,5},{2,10},{6,14},... | collective-permute-start | bytes 393224 | tf_op jit(solution)/shard_map/ppermute | solution.py:577
  35.2 8.0 %collective-permute-start.5 = (bf16[2,128,256]{2,1,0:T(8,128)(2,1)}, bf16[2,128,256]{2,1,0:T(8,128)(2,1)S(1)}, u32[]{:S(2)}, u32[]{:S(2)}) collective-permute-start(bf16[2,128,256]{2,1,0:T(8,128)(2,1)} %get-tuple-element.40), channel_id=1, source_target_pairs={{0,12},{4,0},{8,4},{12,8},{1,13},{5,1},{9,5},{13,9},{2,14},{6,2},{... | collective-permute-start | bytes 393224 | tf_op jit(solution)/shard_map/ppermute | solution.py:577
  35.8 7.4 %collective-permute-start.4 = (bf16[2,128,256]{2,1,0:T(8,128)(2,1)}, bf16[2,128,256]{2,1,0:T(8,128)(2,1)S(1)}, u32[]{:S(2)}, u32[]{:S(2)}) collective-permute-start(bf16[2,128,256]{2,1,0:T(8,128)(2,1)} %get-tuple-element.39), channel_id=1, source_target_pairs={{0,4},{4,8},{8,12},{12,0},{1,5},{5,9},{9,13},{13,1},{2,6},{6,10},{... | collective-permute-start | bytes 393224 | tf_op jit(solution)/shard_map/ppermute | solution.py:577
  37.3 0.7 %copy-start.3 = (bf16[2,128,256]{2,1,0:T(8,128)(2,1)}, bf16[2,128,256]{2,1,0:T(8,128)(2,1)S(1)}, u32[]{:S(2)}) copy-start(bf16[2,128,256]{2,1,0:T(8,128)(2,1)S(1)} %collective-permute-done.3.refs_10_) | copy-start | bytes 393220

commit v6 on v4

v6 whole, which is shorter than its diff:
```python
import functools
import math
from typing import NamedTuple

import jax
import jax.numpy as jnp
from jax import lax
from jax.experimental import pallas as pl
from jax.experimental.pallas import tpu as pltpu
from jax.sharding import PartitionSpec as P

HD = 128
NEG = -1e30
TAIL = 16
F32 = jnp.float32
BF16 = jnp.bfloat16
PAIR = 2
FAR = 3
VMEM_BYTES = 63 * 1024 * 1024
ANYWHERE = pl.BlockSpec(memory_space=pl.ANY)


class Sizes(NamedTuple):
    n_dp: int
    count: int
    slots: int
    kv_heads: int
    group_size: int
    tokens: int
    prefix_len: int

    @property
    def width(self):
        return self.kv_heads * HD

    @property
    def lanes(self):
        return self.kv_heads * self.group_size * HD


def dot(a, b, dims):
    return lax.dot_general(a, b, (dims, ((), ())), preferred_element_type=F32)


NN = ((1,), (0,))
NT = ((1,), (1,))


class Bag:
    pass


def attend_pair(z, at, places, q, og, kv, prefix, lens, factors, out, own_out, sink, apart):
    tokens, prefix_len, group_size = z.tokens, z.prefix_len, z.group_size
    scale = 1.0 / math.sqrt(HD)
    log_scale = scale * math.log2(math.e)
    whole = group_size - group_size % 2
    single = len(at) == 1
    members = range(len(at))
    sides = (0, 0) if single else (0, 1)
    most = max(whole, 2) * tokens
    assert tokens & (tokens - 1) == 0
    token = lax.broadcasted_iota(jnp.int32, (1, most), 1) & (tokens - 1)
    key = lax.broadcasted_iota(jnp.int32, (tokens, most), 0)
    causal = key <= (lax.broadcasted_iota(jnp.int32, (tokens, most), 1) & (tokens - 1))
    left = lax.broadcasted_iota(jnp.int32, (1, 2 * tokens), 1) < tokens

    def head(k, h):
        start = (k * group_size + h) * HD
        return slice(start, start + HD)

    def rows(ref, k, blocks):
        return jnp.concatenate([ref[at[n], head(k, h)] for n, h in blocks], axis=0)

    def halves(part):
        none = jnp.zeros_like(part)
        return [jnp.where(left, part, none), jnp.where(left, none, part)]

    def own_half(both):
        return jnp.where(left, both[:tokens], both[tokens:])

    def rounded(*parts):
        return jnp.concatenate([part.astype(BF16) for part in parts], axis=0)

    chunks = []
    for k in range(z.kv_heads):
        t = Bag()
        t.cols = slice(k * HD, (k + 1) * HD)
        t.key_p, t.value_p = prefix[0, :, t.cols], prefix[1, :, t.cols]
        t.keys = [kv[0, at[n], t.cols] for n in sides]
        t.values = [kv[1, at[n], t.cols] for n in sides]
        t.key_pair = jnp.concatenate(t.keys, axis=0)
        t.value_pair = jnp.concatenate(t.values, axis=0)
        t.key_t = jnp.concatenate([t.key_p.T, t.key_pair.T], axis=1)
        t.prefix_sums = {n: [] for n in members}
        t.self_sums = {n: [] for n in members}
        mine = []
        for n in members:
            c = Bag()
            c.k, c.t, c.side, c.blocks = k, t, n, [(n, h) for h in range(whole)]
            mine.append(c)
        if group_size % 2:
            c = Bag()
            c.k, c.t, c.side, c.blocks = k, t, None, [(n, group_size - 1) for n in sides]
            mine.append(c)
        t.left_over = len(mine)
        chunks += mine

    def products(c):
        t = c.t
        c.q_rows, c.g_rows = rows(q, c.k, c.blocks), rows(og, c.k, c.blocks)
        if c.side is None:
            key_s, value_s = t.key_pair, t.value_pair
        else:
            key_s, value_s = t.keys[c.side], t.values[c.side]
        c.scores = dot(jnp.concatenate([t.key_p, key_s], axis=0), c.q_rows, NT)
        c.gw = dot(jnp.concatenate([t.value_p, value_s], axis=0), c.g_rows, NT)

    def weigh(c):
        scores_p, scores_s = c.scores[:prefix_len], c.scores[prefix_len:]
        c.gw_p, c.gw_s = c.gw[:prefix_len], c.gw[prefix_len:]
        if c.side is None:
            scores_s, c.gw_s = own_half(scores_s), own_half(c.gw_s)
        scores_s = jnp.where(causal[:, : scores_s.shape[1]], scores_s, NEG)
        top = jnp.maximum(
            jnp.max(scores_p, axis=0, keepdims=True), jnp.max(scores_s, axis=0, keepdims=True)
        )
        c.e_p = jnp.exp2((scores_p - top) * log_scale)
        c.e_s = jnp.exp2((scores_s - top) * log_scale)
        total = jnp.sum(c.e_p, axis=0, keepdims=True) + jnp.sum(c.e_s, axis=0, keepdims=True)
        weighted = jnp.sum(c.e_p * c.gw_p, axis=0, keepdims=True) + jnp.sum(
            c.e_s * c.gw_s, axis=0, keepdims=True
        )
        if c.side is None:
            length = jnp.where(left, lens[0], 0 if single else lens[1])
            gain = jnp.where(left, factors[0], factors[-1])
        else:
            length, gain = lens[c.side], factors[c.side]
        inverse = 1.0 / total
        c.delta = weighted * inverse
        c.gain = inverse * jnp.where(token[:, : total.shape[1]] < length, gain, 0.0)

    def gradients(c):
        w_p, w_s = c.e_p * c.gain, c.e_s * c.gain
        d_p, d_s = w_p * (c.gw_p - c.delta), w_s * (c.gw_s - c.delta)
        if c.side is None:
            d_s, w_s = halves(d_s), halves(w_s)
            c.d_wide = rounded(d_p, *d_s)
            c.d_all = rounded(*halves(d_p), *d_s) if apart else c.d_wide
            c.w_all = rounded(*(halves(w_p) if apart else [w_p]), *w_s)
        else:
            empty = jnp.zeros_like(d_s)
            c.d_wide = rounded(*([d_p, empty, d_s] if c.side else [d_p, d_s, empty]))
            c.d_all = rounded(d_p, d_s)
            c.w_all = rounded(w_p, w_s)

    def outgoing(c):
        t = c.t
        q_grad = (dot(t.key_t, c.d_wide, NN) * scale).astype(BF16).T
        kg = dot(c.d_all, c.q_rows, NN)
        vg = dot(c.w_all, c.g_rows, NN)
        targets = members if c.side is None else [c.side]
        for place, (n, h) in enumerate(c.blocks):
            if c.side is not None or place < len(targets):
                out[places[n], :, head(c.k, h)] = q_grad[place * tokens : (place + 1) * tokens]
        many = 2 if c.side is None and apart else 1
        for place, n in enumerate(targets):
            if place < many:
                rows_p = slice(place * prefix_len, (place + 1) * prefix_len)
                t.prefix_sums[n if apart else 0].append((kg[rows_p], vg[rows_p]))
            start = many * prefix_len + place * tokens
            rows_s = slice(start, start + tokens)
            t.self_sums[n].append((kg[rows_s], vg[rows_s]))
        t.left_over -= 1
        if t.left_over == 0:
            for n in members:
                keys, values = zip(*t.self_sums[n])
                own_out[places[n], 0, :, t.cols] = (sum(keys) * scale).astype(BF16)
                own_out[places[n], 1, :, t.cols] = sum(values).astype(BF16)
                if apart or n == 0:
                    keys, values = zip(*t.prefix_sums[n])
                    sink(n, t.cols, sum(keys) * scale, sum(values))

    stages = (products, weigh, gradients, outgoing)
    for step in range(len(chunks) + len(stages) - 1):
        for late, stage in enumerate(stages):
            if 0 <= step - late < len(chunks):
                stage(chunks[step - late])


def token_rows(z, i):
    return pl.ds(pl.multiple_of(i * z.tokens, z.tokens), z.tokens)


def find_responses(z, me, turns, resp_prompt, order):
    for t, turn in enumerate(turns):
        prompt = me ^ turn
        found = t * z.slots
        for i in range(z.count):
            order[found] = i
            found = found + (resp_prompt[me * z.count + i] == prompt).astype(jnp.int32)


def prompt_total(z, me, prompt, resp_prompt, tails, far_rewards):
    sums = jnp.zeros((1, z.width), F32)
    for s in range(tails.shape[0]):
        tail = tails[s].astype(F32)
        sums += tail[0:1] + tail[1:2] + tail[2:3]
    lane = lax.broadcasted_iota(jnp.int32, sums.shape, 1)
    total = jnp.sum(jnp.where(lane == prompt, sums, 0.0))
    for i in range(z.count):
        total += jnp.where(resp_prompt[(me ^ FAR) * z.count + i] == prompt, far_rewards[i], 0.0)
    return total


def reward_factor(z, reward, total, length):
    return (reward - total / z.count) * (z.tokens / length.astype(F32))


def pack_kernel(z, prompt_hbm, rewards_hbm, resp_prompt_hbm, payload, rewards, resp_prompt, staged, sems):
    me = lax.axis_index("dp")
    small = [
        pltpu.make_async_copy(rewards_hbm, rewards, sems.at[0]),
        pltpu.make_async_copy(resp_prompt_hbm, resp_prompt, sems.at[1]),
    ]
    large = [
        pltpu.make_async_copy(
            prompt_hbm.at[n], staged.at[pl.ds(n * z.prefix_len, z.prefix_len)], sems.at[2 + n]
        )
        for n in range(2)
    ]
    for copy in small + large:
        copy.start()
    for copy in small:
        copy.wait()
    lane = lax.broadcasted_iota(jnp.int32, (1, z.width), 1)
    sums = jnp.zeros((1, z.width), F32)
    for i in range(z.count):
        sums += jnp.where(lane == resp_prompt[me * z.count + i], rewards[i], 0.0)
    high = sums.astype(BF16).astype(F32)
    middle = (sums - high).astype(BF16).astype(F32)
    low = sums - high - middle
    row = lax.broadcasted_iota(jnp.int32, (TAIL, z.width), 0)
    pieces = jnp.where(row == 0, high, jnp.where(row == 1, middle, jnp.where(row == 2, low, 0.0)))
    staged[2 * z.prefix_len :, :] = pieces.astype(BF16)
    for copy in large:
        copy.wait()
    last = pltpu.make_async_copy(staged, payload, sems.at[0])
    last.start()
    last.wait()


def tail_copies(z, payloads, tails, sems):
    return [
        pltpu.make_async_copy(payload.at[pl.ds(2 * z.prefix_len, TAIL)], tails.at[n], sems.at[n])
        for n, payload in enumerate(payloads)
    ]


def row_copies(here, there, at_here, at_there, sems):
    (q0, og0, kv0), (q1, og1, kv1) = here, there
    return (
        pltpu.make_async_copy(q0.at[at_here], q1.at[at_there], sems.at[0]),
        pltpu.make_async_copy(og0.at[at_here], og1.at[at_there], sems.at[1]),
        pltpu.make_async_copy(kv0.at[0, at_here], kv1.at[0, at_there], sems.at[2]),
        pltpu.make_async_copy(kv0.at[1, at_here], kv1.at[1, at_there], sems.at[3]),
    )


def result_copies(out, own, q_out, self_out, place, at, sems, back=False):
    pairs = [
        (out.at[place], q_out.at[at]),
        (own.at[place, 0], self_out.at[0, at]),
        (own.at[place, 1], self_out.at[1, at]),
    ]
    return [
        pltpu.make_async_copy(*(reversed(pair) if back else pair), sems.at[place, n])
        for n, pair in enumerate(pairs)
    ]


def group_kernel(z, turns, raw, n_tails, aliased, *refs):
    small_hbm, given = refs[:4], refs[4:7]
    tail_hbm, prompts = refs[7 : 7 + n_tails], refs[7 + n_tails : 7 + n_tails + len(turns)]
    refs = refs[7 + n_tails + len(turns) + aliased :]
    (q_out, self_out), grads_out = refs[:2], refs[2 : 2 + len(turns)]
    (resp_prompt, resp_len, rewards, far_rewards, order, lens, factors, q, og, kv, prefix, tails, acc, out, own, grads,
     sem_small, sem_tails, sem_prefix, sem_in, sem_out, sem_grads) = refs[2 + len(turns) :]
    me = lax.axis_index("dp")
    n_slots = len(turns) * z.slots

    small = [
        pltpu.make_async_copy(src, dst, sem_small.at[n])
        for n, (src, dst) in enumerate(zip(small_hbm, (resp_prompt, resp_len, rewards, far_rewards)))
    ]
    prefix_copies = [
        pltpu.make_async_copy(
            prompts[t].at[pl.ds(n * z.prefix_len, z.prefix_len)], prefix.at[t, n], sem_prefix.at[t, n]
        )
        for t in range(len(turns))
        for n in range(2)
    ]
    late = tail_copies(z, tail_hbm, tails, sem_tails)
    for copy in small + prefix_copies + late:
        copy.start()
    small[0].wait()
    find_responses(z, me, turns, resp_prompt, order)

    def copies_in(slot):
        return row_copies(
            given, (q, og, kv), token_rows(z, order[slot]), token_rows(z, slot), sem_in.at[slot]
        )

    def copies_out(slot):
        return result_copies(out, own, q_out, self_out, slot, token_rows(z, order[slot]), sem_out)

    for slot in range(n_slots):
        for copy in copies_in(slot):
            copy.start()
    for copy in small[1:] + late:
        copy.wait()
    for t, turn in enumerate(turns):
        total = None if raw else prompt_total(z, me, me ^ turn, resp_prompt, tails, far_rewards)
        for slot in range(t * z.slots, (t + 1) * z.slots):
            i = order[slot]
            lens[slot] = resp_len[i]
            factors[slot] = 1.0 if raw else reward_factor(z, rewards[i], total, resp_len[i])
    if not raw:
        acc[...] = jnp.zeros(acc.shape, F32)
    for copy in prefix_copies:
        copy.wait()

    def unit(u, _):
        at = [u * PAIR + n for n in range(PAIR)]
        t = u // (z.slots // PAIR)
        for slot in at:
            for copy in copies_in(slot):
                copy.wait()

        def sink(n, cols, key_grad, value_grad):
            if raw:
                grads[at[n], 0, :, cols] = key_grad.astype(BF16)
                grads[at[n], 1, :, cols] = value_grad.astype(BF16)
            else:
                acc[t, 0, :, cols] += key_grad
                acc[t, 1, :, cols] += value_grad

        attend_pair(
            z, [token_rows(z, n) for n in at], at, q, og, kv, prefix.at[t], [lens[n] for n in at],
            [factors[n] for n in at], out, own, sink, raw,
        )
        for slot in at:
            for copy in copies_out(slot):
                copy.start()
        return 0

    lax.fori_loop(0, n_slots // PAIR, unit, 0)
    if raw:
        last = [pltpu.make_async_copy(grads, grads_out[0], sem_grads.at[0])]
    else:
        grads[...] = acc[...].astype(BF16)
        last = [
            pltpu.make_async_copy(grads.at[t], grads_out[t], sem_grads.at[t]) for t in range(len(turns))
        ]
    for copy in last:
        copy.start()
    for slot in range(n_slots):
        for copy in copies_out(slot):
            copy.wait()
    for copy in last:
        copy.wait()


def finish_kernel(z, n_tails, n_come, *refs):
    small_hbm, tail_hbm = refs[:4], refs[4 : 4 + n_tails]
    per_resp_hbm, come_hbm = refs[4 + n_tails], refs[5 + n_tails : 5 + n_tails + n_come]
    q_out, self_out, grads_out = refs[7 + n_tails + n_come : 10 + n_tails + n_come]
    (resp_prompt, resp_len, rewards, far_rewards, order, tails, out, own, per_resp, come, grads,
     sem_small, sem_tails, sem_come, sem_in, sem_out) = refs[10 + n_tails + n_come :]
    me = lax.axis_index("dp")
    small = [
        pltpu.make_async_copy(src, dst, sem_small.at[n])
        for n, (src, dst) in enumerate(zip(small_hbm, (resp_prompt, resp_len, rewards, far_rewards)))
    ]
    late = tail_copies(z, tail_hbm, tails, sem_tails)
    late += [pltpu.make_async_copy(src, come.at[n], sem_come.at[n]) for n, src in enumerate(come_hbm)]
    late += [pltpu.make_async_copy(per_resp_hbm, per_resp, sem_come.at[n_come])]
    for copy in small + late:
        copy.start()
    small[0].wait()
    find_responses(z, me, (0,), resp_prompt, order)

    def moves(slot, back):
        sems = sem_in if back else sem_out
        return result_copies(out, own, q_out, self_out, slot, token_rows(z, order[slot]), sems, back)

    for slot in range(z.slots):
        for copy in moves(slot, True):
            copy.start()
    for copy in small[1:] + late:
        copy.wait()
    total = prompt_total(z, me, me, resp_prompt, tails, far_rewards)
    summed = come[0].astype(F32)
    for n in range(1, n_come):
        summed += come[n].astype(F32)
    factors = [reward_factor(z, rewards[order[n]], total, resp_len[order[n]]) for n in range(z.slots)]
    for slot in range(z.slots):
        summed += per_resp[slot].astype(F32) * factors[slot]
    grads[...] = summed
    last = pltpu.make_async_copy(grads, grads_out, sem_small.at[0])
    last.start()
    for slot in range(z.slots):
        for copy in moves(slot, True):
            copy.wait()
        out[slot] = (out[slot].astype(F32) * factors[slot]).astype(BF16)
        own[slot] = (own[slot].astype(F32) * factors[slot]).astype(BF16)
        for copy in moves(slot, False):
            copy.start()
    for slot in range(z.slots):
        for copy in moves(slot, False):
            copy.wait()
    last.wait()


def near_shards(z, prompt_kv, resp_q, resp_kv, out_grad, rewards, resp_prompt, resp_len):
    n_dp = z.n_dp
    assert z.slots % PAIR == 0
    shape = jax.ShapeDtypeStruct
    one = (2, z.prefix_len, z.width)
    params = pltpu.CompilerParams(vmem_limit_bytes=VMEM_BYTES)
    cost = pl.CostEstimate(flops=0, bytes_accessed=0, transcendentals=0)
    payload = pl.pallas_call(
        functools.partial(pack_kernel, z),
        out_shape=jax.ShapeDtypeStruct((2 * z.prefix_len + TAIL, z.width), BF16),
        in_specs=[ANYWHERE] * 3,
        out_specs=ANYWHERE,
        scratch_shapes=[
            pltpu.SMEM(rewards.shape, F32),
            pltpu.SMEM(resp_prompt.shape, jnp.int32),
            pltpu.VMEM((2 * z.prefix_len + TAIL, z.width), BF16),
            pltpu.SemaphoreType.DMA((4,)),
        ],
        compiler_params=pltpu.CompilerParams(vmem_limit_bytes=VMEM_BYTES),
        name="pack",
    )(prompt_kv, rewards, resp_prompt)

    assert n_dp == FAR + 1

    def swap(x, s):
        return lax.ppermute(x, "dp", [(i, i ^ s) for i in range(n_dp)])

    payloads = {0: payload, 2: swap(payload, 2), 1: swap(payload, 1)}
    tails = [payloads[s] for s in range(FAR)]
    small = (resp_prompt, resp_len, rewards)
    far_rewards = swap(rewards, FAR)
    smem = [pltpu.SMEM(x.shape, x.dtype) for x in (*small, rewards)]
    slots = z.slots

    def grads_of(turns, raw, written):
        n_slots, n_turns = len(turns) * slots, len(turns)
        used_tails = [] if raw else tails
        used_small = (*small, rewards if raw else far_rewards)
        prompts = [payloads[turn] for turn in turns]
        operands = [*used_small, resp_q, out_grad, resp_kv, *used_tails, *prompts, *written]
        grads_shapes = [(slots,) + one] if raw else [one] * n_turns
        return pl.pallas_call(
            functools.partial(group_kernel, z, turns, raw, len(used_tails), len(written)),
            out_shape=[shape(resp_q.shape, BF16), shape(resp_kv.shape, BF16)]
            + [shape(x, BF16) for x in grads_shapes],
            in_specs=[ANYWHERE] * len(operands),
            out_specs=[ANYWHERE] * (2 + len(grads_shapes)),
            input_output_aliases={len(operands) - 2: 0, len(operands) - 1: 1} if written else {},
            scratch_shapes=[
                *smem,
                pltpu.SMEM((n_slots + 1,), jnp.int32),
                pltpu.SMEM((n_slots,), jnp.int32),
                pltpu.SMEM((n_slots,), F32),
                pltpu.VMEM((n_slots * z.tokens, z.lanes), BF16),
                pltpu.VMEM((n_slots * z.tokens, z.lanes), BF16),
                pltpu.VMEM((2, n_slots * z.tokens, z.width), BF16),
                pltpu.VMEM((n_turns,) + one, BF16),
                pltpu.VMEM((FAR, TAIL, z.width), BF16),
                pltpu.VMEM((n_turns,) + one, F32),
                pltpu.VMEM((n_slots, z.tokens, z.lanes), BF16),
                pltpu.VMEM((n_slots, 2, z.tokens, z.width), BF16),
                pltpu.VMEM(grads_shapes[0] if raw else (n_turns,) + one, BF16),
                pltpu.SemaphoreType.DMA((len(smem),)),
                pltpu.SemaphoreType.DMA((FAR,)),
                pltpu.SemaphoreType.DMA((n_turns, 2)),
                pltpu.SemaphoreType.DMA((n_slots, 4)),
                pltpu.SemaphoreType.DMA((n_slots, 3)),
                pltpu.SemaphoreType.DMA((n_turns,)),
            ],
            compiler_params=params,
            cost_estimate=cost,
            name="raw_grads" if raw else "group_grads",
        )(*operands)

    *written, per_resp = grads_of((0,), True, ())
    onward, per_resp, far_rewards = lax.optimization_barrier((payloads[2], per_resp, far_rewards))
    payloads[FAR] = swap(onward, 1)
    *written, for_2, for_1 = grads_of((2, 1), False, written)
    come = [swap(for_2, 2), swap(for_1, 1)]
    *written, for_far = grads_of((FAR,), False, written)
    last = swap(for_far, FAR)
    operands = [*small, far_rewards, *tails, per_resp, *come, *written]
    q_out, self_out, own_grads = pl.pallas_call(
        functools.partial(finish_kernel, z, len(tails), len(come)),
        out_shape=[shape(resp_q.shape, BF16), shape(resp_kv.shape, BF16), shape(one, F32)],
        in_specs=[ANYWHERE] * len(operands),
        out_specs=[ANYWHERE] * 3,
        input_output_aliases={len(operands) - 2: 0, len(operands) - 1: 1},
        scratch_shapes=[
            *smem,
            pltpu.SMEM((slots + 1,), jnp.int32),
            pltpu.VMEM((FAR, TAIL, z.width), BF16),
            pltpu.VMEM((slots, z.tokens, z.lanes), BF16),
            pltpu.VMEM((slots, 2, z.tokens, z.width), BF16),
            pltpu.VMEM((slots,) + one, BF16),
            pltpu.VMEM((len(come),) + one, BF16),
            pltpu.VMEM(one, F32),
            pltpu.SemaphoreType.DMA((len(smem),)),
            pltpu.SemaphoreType.DMA((FAR,)),
            pltpu.SemaphoreType.DMA((len(come) + 1,)),
            pltpu.SemaphoreType.DMA((slots, 3)),
            pltpu.SemaphoreType.DMA((slots, 3)),
        ],
        compiler_params=params,
        cost_estimate=cost,
        name="finish_own",
    )(*operands)
    prefix_out = (own_grads + last.astype(F32)).astype(BF16)
    return (q_out, self_out, prefix_out)


def far_kernel(z, *refs):
    (resp_prompt, resp_len, rewards, q_hbm, og_hbm, kv_hbm, prompts, q_out, self_out, prefix_outs,
     totals, lens, factors, q, og, kv, prefix, out, own, grads, sem_in, sem_prefix, sem_out) = refs
    me = lax.axis_index("dp")

    for p in range(z.n_dp):
        totals[p] = 0.0

    def copies_in(slot):
        rows = token_rows(z, slot)
        prompt = resp_prompt[me * z.count + slot]
        return (
            *row_copies((q_hbm, og_hbm, kv_hbm), (q, og, kv), rows, rows, sem_in.at[slot]),
            pltpu.make_async_copy(prompts.at[prompt], prefix.at[slot], sem_prefix.at[slot]),
        )

    def copies_out(slot):
        rows = token_rows(z, slot)
        return (
            *result_copies(out, own, q_out, self_out, slot, rows, sem_out),
            pltpu.make_async_copy(grads.at[slot], prefix_outs.at[slot], sem_out.at[slot, 3]),
        )

    def start(slot, _):
        for copy in copies_in(slot):
            copy.start()
        return 0

    lax.fori_loop(0, z.count, start, 0)

    def add(i, _):
        prompt = resp_prompt[i]
        totals[prompt] = totals[prompt] + rewards[i]
        return 0

    lax.fori_loop(0, z.n_dp * z.count, add, 0)

    def find_factor(slot, _):
        place = me * z.count + slot
        lens[slot] = resp_len[slot]
        factors[slot] = reward_factor(z, rewards[place], totals[resp_prompt[place]], resp_len[slot])
        return 0

    lax.fori_loop(0, z.count, find_factor, 0)

    def unit(slot, _):
        for copy in copies_in(slot):
            copy.wait()

        def sink(_, cols, key_grad, value_grad):
            grads[slot, 0, :, cols] = key_grad.astype(BF16)
            grads[slot, 1, :, cols] = value_grad.astype(BF16)

        attend_pair(
            z, [token_rows(z, slot)], [slot], q, og, kv, prefix.at[slot], [lens[slot]], [factors[slot]], out, own, sink, True
        )
        for copy in copies_out(slot):
            copy.start()
        return 0

    lax.fori_loop(0, z.count, unit, 0)

    def end(slot, _):
        for copy in copies_out(slot):
            copy.wait()
        return 0

    lax.fori_loop(0, z.count, end, 0)


def far_shards(z, prompt_kv, resp_q, resp_kv, out_grad, rewards, resp_prompt, resp_len):
    assert z.slots == 1
    count, n_dp = z.count, z.n_dp
    one = (2, z.prefix_len, z.width)
    smem = pl.BlockSpec(memory_space=pltpu.SMEM)
    q_out, self_out, per_resp = pl.pallas_call(
        functools.partial(far_kernel, z),
        out_shape=[
            jax.ShapeDtypeStruct(resp_q.shape, BF16),
            jax.ShapeDtypeStruct(resp_kv.shape, BF16),
            jax.ShapeDtypeStruct((count,) + one, BF16),
        ],
        in_specs=[smem] * 3 + [ANYWHERE] * 4,
        out_specs=[ANYWHERE] * 3,
        scratch_shapes=[
            pltpu.SMEM((n_dp,), F32),
            pltpu.SMEM((count,), jnp.int32),
            pltpu.SMEM((count,), F32),
            pltpu.VMEM(resp_q.shape, BF16),
            pltpu.VMEM(resp_q.shape, BF16),
            pltpu.VMEM(resp_kv.shape, BF16),
            pltpu.VMEM((count,) + one, BF16),
            pltpu.VMEM((count, z.tokens, z.lanes), BF16),
            pltpu.VMEM((count, 2, z.tokens, z.width), BF16),
            pltpu.VMEM((count,) + one, BF16),
            pltpu.SemaphoreType.DMA((count, 4)),
            pltpu.SemaphoreType.DMA((count,)),
            pltpu.SemaphoreType.DMA((count, 4)),
        ],
        compiler_params=pltpu.CompilerParams(vmem_limit_bytes=VMEM_BYTES),
        name="far_grads",
    )(
        resp_prompt,
        resp_len,
        lax.all_gather(rewards, "dp", axis=0, tiled=True),
        resp_q,
        out_grad,
        resp_kv,
        lax.all_gather(prompt_kv, "dp", axis=0),
    )
    my_prompts = lax.dynamic_slice_in_dim(resp_prompt, lax.axis_index("dp") * count, count)
    route = (jnp.arange(n_dp, dtype=jnp.int32)[:, None] == my_prompts[None, :]).astype(BF16)
    outgoing = jnp.dot(route, per_resp.reshape(count, -1), preferred_element_type=F32).astype(BF16)
    outgoing = outgoing.reshape((n_dp,) + one)
    incoming = lax.all_to_all(outgoing, "dp", split_axis=0, concat_axis=0, tiled=True)
    prefix_out = jnp.sum(incoming, axis=0, dtype=F32).astype(BF16)
    return (q_out, self_out, prefix_out)


def shards(prompt_kv, resp_q, resp_kv, out_grad, rewards, resp_prompt, resp_len):
    n_dp = lax.axis_size("dp")
    count = rewards.shape[0]
    prefix_len, width = prompt_kv.shape[1:]
    slots = (count + n_dp - 1) // n_dp
    z = Sizes(
        n_dp, count, slots, width // HD, resp_q.shape[1] // width, resp_q.shape[0] // count, prefix_len
    )
    part = near_shards if count // slots == n_dp else far_shards
    return part(z, prompt_kv, resp_q, resp_kv, out_grad, rewards, resp_prompt, resp_len)


def solution(mesh):
    in_specs = (
        P(None, ("groups", "dp"), "tensor"),
        P(("groups", "dp"), "tensor"),
        P(None, ("groups", "dp"), "tensor"),
        P(("groups", "dp"), "tensor"),
        P(("groups", "dp")),
        P("groups"),
        P(("groups", "dp")),
    )
    out_specs = (
        P(("groups", "dp"), "tensor"),
        P(None, ("groups", "dp"), "tensor"),
        P(None, ("groups", "dp"), "tensor"),
    )
    return jax.shard_map(shards, mesh=mesh, in_specs=in_specs, out_specs=out_specs, check_vma=False)
```

time: 48.4 us -> 42 us (0.87)
  Pallas kernels: 26.1 us -> 22.5 us
  waiting for transfers between devices: 5.42 us -> 2.77 us
  starting transfers between devices: 13.5 us -> 12 us
  local copies, waits for them, and re-layouts: 0.69 us -> 2 us
    pallas_call x1, Pallas kernels: 5.11 us -> 1.56 us  [near_shards(): pl.pallas_call(functools.partial(pack_kernel, z), out_shape=jax.ShapeDtyp...]
    ppermute x6 -> x7, waiting for transfers between devices: 5.42 us -> 2.77 us  [swap(): return lax.ppermute(x, 'dp', [(i, i ^ s) for i in range(n_dp)])]
    ppermute x6 -> x7, starting transfers between devices: 13.5 us -> 12 us  [swap(): return lax.ppermute(x, 'dp', [(i, i ^ s) for i in range(n_dp)])]
    unnamed x6 -> x12, local copies, waits for them, and re-layouts: 0.69 us -> 2 us
  transfers between devices with their start and end apart: 6 -> 7, of which waited for: 3 -> 2; matrix products, arithmetic and copies ran while one was open for 0% -> 0% of each run, Pallas kernels for 33% -> 50%
where the time goes in v6:
time: 42 us; the launch traced here: 41.6 us
  Pallas kernels  22.5 us (54%)
  starting transfers between devices  12 us (29%)
  waiting for transfers between devices  2.77 us (7%)
  local copies, waits for them, and re-layouts  2 us (5%)
  other arithmetic  1.63 us (4%)
  between operations  0.71 us (2%)
    pallas_call x3, Pallas kernels, grads_of(): pl.pallas_call(functools.partial(group_kernel, z, turns, raw, len(used_ta...  18 us
    ppermute x7, starting transfers between devices, swap(): return lax.ppermute(x, 'dp', [(i, i ^ s) for i in range(n_dp)])  12 us
    pallas_call x1, Pallas kernels, near_shards(): pl.pallas_call(functools.partial(finish_kernel, z, len(tails), len(come))...  2.94 us
    ppermute x7, waiting for transfers between devices, swap(): return lax.ppermute(x, 'dp', [(i, i ^ s) for i in range(n_dp)])  2.77 us
    unnamed x12, local copies, waits for them, and re-layouts  2 us
    convert_element_type x1, other arithmetic, near_shards(): prefix_out = (own_grads + last.astype(F32)).astype(BF16)  1.63 us
    pallas_call x1, Pallas kernels, near_shards(): pl.pallas_call(functools.partial(pack_kernel, z), out_shape=jax.ShapeDtyp...  1.56 us
  transfers between devices with their start and end apart: 7, of which 2 were waited for; matrix products, arithmetic and copies ran while one was open for 0% of the time, Pallas kernels for 50%

profile of v6, /device:TPU:0, one launch (start us, length us, event | category | flops | bytes accessed | tf_op | source)
XLA Modules:
  0.0 41.6 jit_solution(14710207377997154868)
XLA Ops:
  0.6 1.6 %pack.1.refs_7_.refs_4_ = bf16[272,256]{1,0:T(8,128)(2,1)} custom-call(bf16[2,128,256]{2,1,0:T(8,128)(2,1)} %prompt_hbm.1, f32[16]{0:T(128)} %refs_2_.7, s32[64]{0:T(128)} %refs_0_.7), custom_call_target="tpu_custom_call" | custom-call | tf_op jit(solution)/shard_map/pack/pallas_call | solution.py:432
  2.2 4.1 %collective-permute-start = (bf16[272,256]{1,0:T(8,128)(2,1)}, bf16[272,256]{1,0:T(8,128)(2,1)S(1)}, u32[]{:S(2)}, u32[]{:S(2)}) collective-permute-start(bf16[272,256]{1,0:T(8,128)(2,1)} %pack.1.refs_7_.refs_4_), channel_id=1, source_target_pairs={{0,8},{4,12},{8,0},{12,4},{1,9},{5,13},{9,1},{13,5},{2,10},{6,14},... | collective-permute-start | bytes 417800 | tf_op jit(solution)/shard_map/ppermute | solution.py:450
  6.3 1.3 %collective-permute-start.1 = (f32[16]{0:T(128)}, f32[16]{0:T(128)S(1)}, u32[]{:S(2)}, u32[]{:S(2)}) collective-permute-start(f32[16]{0:T(128)} %refs_2_.7), channel_id=1, source_target_pairs={{0,12},{4,8},{8,4},{12,0},{1,13},{5,9},{9,5},{13,1},{2,14},{6,10},... | collective-permute-start | bytes 200 | tf_op jit(solution)/shard_map/ppermute | solution.py:450
  7.7 0.2 collective-permute-start.2
  7.9 5.3 %raw_grads.1 = (bf16[1024,1280]{1,0:T(8,128)(2,1)}, bf16[2,1024,256]{2,1,0:T(8,128)(2,1)}, bf16[4,2,128,256]{3,2,1,0:T(8,128)(2,1)}) custom-call(s32[64]{0:T(128)} %refs_0_.7, s32[16]{0:T(128)} %refs_1_.7, f32[16]{0:T(128)} %refs_2_.7, f32[16]{0:T(128)} %refs_2_.7, bf16[1024,1280]{1,0:T(8,128)(2,1)} %refs_4_.5, bf16[1024,1280]{1,0:T(8,128)(2,1)} %refs_5_.5, ...), custom_call_target="tpu_custom_call" | custom-call | tf_op jit(solution)/shard_map/raw_grads/pallas_call | solution.py:466
  13.2 0.0 collective-permute-done.1.refs_3_
  13.2 0.0 copy-start.5
  13.2 0.1 collective-permute-done.refs_9_.refs_10_.refs_6_
  13.3 0.0 copy-start
  13.3 1.8 %collective-permute-start.5 = (bf16[272,256]{1,0:T(8,128)(2,1)S(1)}, bf16[272,256]{1,0:T(8,128)(2,1)S(1)}, u32[]{:S(2)}, u32[]{:S(2)}) collective-permute-start(bf16[272,256]{1,0:T(8,128)(2,1)S(1)} %collective-permute-done.refs_9_.refs_10_.refs_6_), channel_id=1, source_target_pairs={{0,4},{4,0},{8,12},{12,8},{1,5},{5,1},{9,13},{13,9},{2,6},{6,2},{1... | collective-permute-start | bytes 417800 | tf_op jit(solution)/shard_map/ppermute | solution.py:450
  15.1 0.0 collective-permute-done.2.refs_8_.refs_11_.refs_5_
  15.1 0.0 copy-start.1
  15.1 0.0 copy-done.5
  15.1 0.0 copy-done
  15.1 0.6 %copy-done.1 = bf16[272,256]{1,0:T(8,128)(2,1)} copy-done((bf16[272,256]{1,0:T(8,128)(2,1)}, bf16[272,256]{1,0:T(8,128)(2,1)S(1)}, u32[]{:S(2)}) %copy-start.1) | copy-done | bytes 139288
  15.7 7.6 %group_grads.2 = (bf16[1024,1280]{1,0:T(8,128)(2,1)}, bf16[2,1024,256]{2,1,0:T(8,128)(2,1)}, bf16[2,128,256]{2,1,0:T(8,128)(2,1)}, bf16[2,128,256]{2,1,0:T(8,128)(2,1)}) custom-call(s32[64]{0:T(128)} %refs_0_.7, s32[16]{0:T(128)} %refs_1_.7, f32[16]{0:T(128)} %refs_2_.7, f32[16]{0:T(128)} %copy-done.5, ...), custom_call_target="tpu_custom_call", output_to_operand_aliasing={{0}: (12, {}), {1}: (13, {})} | custom-call | tf_op jit(solution)/shard_map/group_grads/pallas_call | solution.py:466
  23.4 2.4 %collective-permute-start.3 = (bf16[2,128,256]{2,1,0:T(8,128)(2,1)}, bf16[2,128,256]{2,1,0:T(8,128)(2,1)S(1)}, u32[]{:S(2)}, u32[]{:S(2)}) collective-permute-start(bf16[2,128,256]{2,1,0:T(8,128)(2,1)} %get-tuple-element.24), channel_id=1, source_target_pairs={{0,8},{4,12},{8,0},{12,4},{1,9},{5,13},{9,1},{13,5},{2,10},{6,14},... | collective-permute-start | bytes 393224 | tf_op jit(solution)/shard_map/ppermute | solution.py:450
  25.8 1.3 %collective-permute-start.4 = (bf16[2,128,256]{2,1,0:T(8,128)(2,1)}, bf16[2,128,256]{2,1,0:T(8,128)(2,1)S(1)}, u32[]{:S(2)}, u32[]{:S(2)}) collective-permute-start(bf16[2,128,256]{2,1,0:T(8,128)(2,1)} %get-tuple-element.25), channel_id=1, source_target_pairs={{0,4},{4,0},{8,12},{12,8},{1,5},{5,1},{9,13},{13,9},{2,6},{6,2},{1... | collective-permute-start | bytes 393224 | tf_op jit(solution)/shard_map/ppermute | solution.py:450
  27.0 0.0 collective-permute-done.5.refs_10_
  27.0 0.0 copy-start.2
  27.0 0.7 %copy-done.2 = bf16[272,256]{1,0:T(8,128)(2,1)} copy-done((bf16[272,256]{1,0:T(8,128)(2,1)}, bf16[272,256]{1,0:T(8,128)(2,1)S(1)}, u32[]{:S(2)}) %copy-start.2) | copy-done | bytes 139288
  27.7 5.1 %group_grads.3 = (bf16[1024,1280]{1,0:T(8,128)(2,1)}, bf16[2,1024,256]{2,1,0:T(8,128)(2,1)}, bf16[2,128,256]{2,1,0:T(8,128)(2,1)}) custom-call(s32[64]{0:T(128)} %refs_0_.7, s32[16]{0:T(128)} %refs_1_.7, f32[16]{0:T(128)} %refs_2_.7, f32[16]{0:T(128)} %copy-done.5, bf16[1024,1280]{1,0:T(8,128)(2,1)} %refs_4_.5, ...), custom_call_target="tpu_custom_call", output_to_operand_aliasing={{0}: (11, {}), {1}: (12, {})} | custom-call | tf_op jit(solution)/shard_map/group_grads/pallas_call | solution.py:466
  32.8 0.9 %collective-permute-start.6 = (bf16[2,128,256]{2,1,0:T(8,128)(2,1)}, bf16[2,128,256]{2,1,0:T(8,128)(2,1)S(1)}, u32[]{:S(2)}, u32[]{:S(2)}) collective-permute-start(bf16[2,128,256]{2,1,0:T(8,128)(2,1)} %get-tuple-element.34), channel_id=1, source_target_pairs={{0,12},{4,8},{8,4},{12,0},{1,13},{5,9},{9,5},{13,1},{2,14},{6,10},... | collective-permute-start | bytes 393224 | tf_op jit(solution)/shard_map/ppermute | solution.py:450
  33.6 0.0 collective-permute-done.3.refs_8_
  33.6 0.0 copy-start.3
  33.6 0.0 collective-permute-done.4.refs_9_
  33.7 0.0 copy-start.4
  33.7 0.6 %copy-done.3 = bf16[2,128,256]{2,1,0:T(8,128)(2,1)} copy-done((bf16[2,128,256]{2,1,0:T(8,128)(2,1)}, bf16[2,128,256]{2,1,0:T(8,128)(2,1)S(1)}, u32[]{:S(2)}) %copy-start.3) | copy-done | bytes 131096
  34.3 0.0 copy-done.4
  34.3 2.9 %finish_own.1 = (bf16[1024,1280]{1,0:T(8,128)(2,1)}, bf16[2,1024,256]{2,1,0:T(8,128)(2,1)}, f32[2,128,256]{2,1,0:T(8,128)}) custom-call(s32[64]{0:T(128)} %refs_0_.7, s32[16]{0:T(128)} %refs_1_.7, f32[16]{0:T(128)} %refs_2_.7, f32[16]{0:T(128)} %copy-done.5, bf16[272,256]{1,0:T(8,128)(2,1)} %pack.1.refs_7_.refs_4_, ...), custom_call_target="tpu_custom_call", output_to_operand_aliasing={{0}: (10, {}), {1}: (11, {})} | custom-call | tf_op jit(solution)/shard_map/finish_own/pallas_call | solution.py:507
  37.3 2.6 %collective-permute-done.6 = bf16[2,128,256]{2,1,0:T(8,128)(2,1)S(1)} collective-permute-done((bf16[2,128,256]{2,1,0:T(8,128)(2,1)}, bf16[2,128,256]{2,1,0:T(8,128)(2,1)S(1)}, u32[]{:S(2)}, u32[]{:S(2)}) %collective-permute-start.6) | collective-permute-done | bytes 131104 | tf_op jit(solution)/shard_map/ppermute | solution.py:450
  39.9 1.6 %add_convert_fusion = bf16[2,128,256]{2,1,0:T(8,128)(2,1)} fusion(f32[2,128,256]{2,1,0:T(8,128)} %get-tuple-element.33, bf16[2,128,256]{2,1,0:T(8,128)(2,1)S(1)} %collective-permute-done.6), kind=kLoop, calls=%fused_computation | loop fusion | flops 196608 | bytes 524288 | tf_op jit(solution)/shard_map/convert_element_type | solution.py:532
Async XLA Ops:
  2.2 11.1 %collective-permute-start = (bf16[272,256]{1,0:T(8,128)(2,1)}, bf16[272,256]{1,0:T(8,128)(2,1)S(1)}, u32[]{:S(2)}, u32[]{:S(2)}) collective-permute-start(bf16[272,256]{1,0:T(8,128)(2,1)} %pack.1.refs_7_.refs_4_), channel_id=1, source_target_pairs={{0,8},{4,12},{8,0},{12,4},{1,9},{5,13},{9,1},{13,5},{2,10},{6,14},... | collective-permute-start | bytes 417800 | tf_op jit(solution)/shard_map/ppermute | solution.py:450
  6.3 6.9 %collective-permute-start.1 = (f32[16]{0:T(128)}, f32[16]{0:T(128)S(1)}, u32[]{:S(2)}, u32[]{:S(2)}) collective-permute-start(f32[16]{0:T(128)} %refs_2_.7), channel_id=1, source_target_pairs={{0,12},{4,8},{8,4},{12,0},{1,13},{5,9},{9,5},{13,1},{2,14},{6,10},... | collective-permute-start | bytes 200 | tf_op jit(solution)/shard_map/ppermute | solution.py:450
  7.7 7.4 %collective-permute-start.2 = (bf16[272,256]{1,0:T(8,128)(2,1)}, bf16[272,256]{1,0:T(8,128)(2,1)S(1)}, u32[]{:S(2)}, u32[]{:S(2)}) collective-permute-start(bf16[272,256]{1,0:T(8,128)(2,1)} %pack.1.refs_7_.refs_4_), channel_id=1, source_target_pairs={{0,4},{4,0},{8,12},{12,8},{1,5},{5,1},{9,13},{13,9},{2,6},{6,2},{1... | collective-permute-start | bytes 417800 | tf_op jit(solution)/shard_map/ppermute | solution.py:450
  13.2 1.9 %copy-start.5 = (f32[16]{0:T(128)}, f32[16]{0:T(128)S(1)}, u32[]{:S(2)}) copy-start(f32[16]{0:T(128)S(1)} %collective-permute-done.1.refs_3_) | copy-start | bytes 196
  13.3 1.8 %copy-start = (bf16[272,256]{1,0:T(8,128)(2,1)}, bf16[272,256]{1,0:T(8,128)(2,1)S(1)}, u32[]{:S(2)}) copy-start(bf16[272,256]{1,0:T(8,128)(2,1)S(1)} %collective-permute-done.refs_9_.refs_10_.refs_6_) | copy-start | bytes 417796
  13.3 13.7 %collective-permute-start.5 = (bf16[272,256]{1,0:T(8,128)(2,1)S(1)}, bf16[272,256]{1,0:T(8,128)(2,1)S(1)}, u32[]{:S(2)}, u32[]{:S(2)}) collective-permute-start(bf16[272,256]{1,0:T(8,128)(2,1)S(1)} %collective-permute-done.refs_9_.refs_10_.refs_6_), channel_id=1, source_target_pairs={{0,4},{4,0},{8,12},{12,8},{1,5},{5,1},{9,13},{13,9},{2,6},{6,2},{1... | collective-permute-start | bytes 417800 | tf_op jit(solution)/shard_map/ppermute | solution.py:450
  15.1 0.7 %copy-start.1 = (bf16[272,256]{1,0:T(8,128)(2,1)}, bf16[272,256]{1,0:T(8,128)(2,1)S(1)}, u32[]{:S(2)}) copy-start(bf16[272,256]{1,0:T(8,128)(2,1)S(1)} %collective-permute-done.2.refs_8_.refs_11_.refs_5_) | copy-start | bytes 417796
  23.4 10.3 %collective-permute-start.3 = (bf16[2,128,256]{2,1,0:T(8,128)(2,1)}, bf16[2,128,256]{2,1,0:T(8,128)(2,1)S(1)}, u32[]{:S(2)}, u32[]{:S(2)}) collective-permute-start(bf16[2,128,256]{2,1,0:T(8,128)(2,1)} %get-tuple-element.24), channel_id=1, source_target_pairs={{0,8},{4,12},{8,0},{12,4},{1,9},{5,13},{9,1},{13,5},{2,10},{6,14},... | collective-permute-start | bytes 393224 | tf_op jit(solution)/shard_map/ppermute | solution.py:450
  25.8 7.9 %collective-permute-start.4 = (bf16[2,128,256]{2,1,0:T(8,128)(2,1)}, bf16[2,128,256]{2,1,0:T(8,128)(2,1)S(1)}, u32[]{:S(2)}, u32[]{:S(2)}) collective-permute-start(bf16[2,128,256]{2,1,0:T(8,128)(2,1)} %get-tuple-element.25), channel_id=1, source_target_pairs={{0,4},{4,0},{8,12},{12,8},{1,5},{5,1},{9,13},{13,9},{2,6},{6,2},{1... | collective-permute-start | bytes 393224 | tf_op jit(solution)/shard_map/ppermute | solution.py:450
  27.0 0.7 %copy-start.2 = (bf16[272,256]{1,0:T(8,128)(2,1)}, bf16[272,256]{1,0:T(8,128)(2,1)S(1)}, u32[]{:S(2)}) copy-start(bf16[272,256]{1,0:T(8,128)(2,1)S(1)} %collective-permute-done.5.refs_10_) | copy-start | bytes 417796
  32.8 7.1 %collective-permute-start.6 = (bf16[2,128,256]{2,1,0:T(8,128)(2,1)}, bf16[2,128,256]{2,1,0:T(8,128)(2,1)S(1)}, u32[]{:S(2)}, u32[]{:S(2)}) collective-permute-start(bf16[2,128,256]{2,1,0:T(8,128)(2,1)} %get-tuple-element.34), channel_id=1, source_target_pairs={{0,12},{4,8},{8,4},{12,0},{1,13},{5,9},{9,5},{13,1},{2,14},{6,10},... | collective-permute-start | bytes 393224 | tf_op jit(solution)/shard_map/ppermute | solution.py:450
  33.6 0.7 %copy-start.3 = (bf16[2,128,256]{2,1,0:T(8,128)(2,1)}, bf16[2,128,256]{2,1,0:T(8,128)(2,1)S(1)}, u32[]{:S(2)}) copy-start(bf16[2,128,256]{2,1,0:T(8,128)(2,1)S(1)} %collective-permute-done.3.refs_8_) | copy-start | bytes 393220
  33.7 0.7 %copy-start.4 = (bf16[2,128,256]{2,1,0:T(8,128)(2,1)}, bf16[2,128,256]{2,1,0:T(8,128)(2,1)S(1)}, u32[]{:S(2)}) copy-start(bf16[2,128,256]{2,1,0:T(8,128)(2,1)S(1)} %collective-permute-done.4.refs_9_) | copy-start | bytes 393220

commit v7 on v6

--- a/solution.py
+++ b/solution.py
@@ -17,6 +17,8 @@
 PAIR = 2
 FAR = 3
 VMEM_BYTES = 63 * 1024 * 1024
+GROUP_BYTES = 53 * 1024 * 1024
+FINISH_BYTES = 24 * 1024 * 1024
 ANYWHERE = pl.BlockSpec(memory_space=pl.ANY)
 
 
@@ -183,7 +185,7 @@
 
     stages = (products, weigh, gradients, outgoing)
     for step in range(len(chunks) + len(stages) - 1):
-        for late, stage in enumerate(stages):
+        for late, stage in reversed(list(enumerate(stages))):
             if 0 <= step - late < len(chunks):
                 stage(chunks[step - late])
 
@@ -262,16 +264,14 @@
     return (
         pltpu.make_async_copy(q0.at[at_here], q1.at[at_there], sems.at[0]),
         pltpu.make_async_copy(og0.at[at_here], og1.at[at_there], sems.at[1]),
-        pltpu.make_async_copy(kv0.at[0, at_here], kv1.at[0, at_there], sems.at[2]),
-        pltpu.make_async_copy(kv0.at[1, at_here], kv1.at[1, at_there], sems.at[3]),
+        pltpu.make_async_copy(kv0.at[:, at_here], kv1.at[:, at_there], sems.at[2]),
     )
 
 
 def result_copies(out, own, q_out, self_out, place, at, sems, back=False):
     pairs = [
         (out.at[place], q_out.at[at]),
-        (own.at[place, 0], self_out.at[0, at]),
-        (own.at[place, 1], self_out.at[1, at]),
+        (own.at[place], self_out.at[:, at]),
     ]
     return [
         pltpu.make_async_copy(*(reversed(pair) if back else pair), sems.at[place, n])
@@ -491,7 +491,7 @@
                 pltpu.SemaphoreType.DMA((n_slots, 3)),
                 pltpu.SemaphoreType.DMA((n_turns,)),
             ],
-            compiler_params=params,
+            compiler_params=params if raw else pltpu.CompilerParams(vmem_limit_bytes=GROUP_BYTES),
             cost_estimate=cost,
             name="raw_grads" if raw else "group_grads",
         )(*operands)
@@ -500,9 +500,10 @@
     onward, per_resp, far_rewards = lax.optimization_barrier((payloads[2], per_resp, far_rewards))
     payloads[FAR] = swap(onward, 1)
     *written, for_2, for_1 = grads_of((2, 1), False, written)
-    come = [swap(for_2, 2), swap(for_1, 1)]
+    come = [swap(for_2, 2)]
     *written, for_far = grads_of((FAR,), False, written)
-    last = swap(for_far, FAR)
+    for_far, for_1 = lax.optimization_barrier((for_far, for_1))
+    last = [swap(for_far, FAR), swap(for_1, 1)]
     operands = [*small, far_rewards, *tails, per_resp, *come, *written]
     q_out, self_out, own_grads = pl.pallas_call(
         functools.partial(finish_kernel, z, len(tails), len(come)),
@@ -525,11 +526,11 @@
             pltpu.SemaphoreType.DMA((slots, 3)),
             pltpu.SemaphoreType.DMA((slots, 3)),
         ],
-        compiler_params=params,
+        compiler_params=pltpu.CompilerParams(vmem_limit_bytes=FINISH_BYTES),
         cost_estimate=cost,
         name="finish_own",
     )(*operands)
-    prefix_out = (own_grads + last.astype(F32)).astype(BF16)
+    prefix_out = (own_grads + sum(part.astype(F32) for part in last)).astype(BF16)
     return (q_out, self_out, prefix_out)
 
 

time: 42 us -> 39.5 us (0.940)
  local copies, waits for them, and re-layouts: 2 us -> 0.03 us
  waiting for transfers between devices: 2.77 us -> 3.84 us
  other arithmetic: 1.63 us -> 0.7 us
  starting transfers between devices: 12 us -> 11.2 us
    unnamed x12 -> x10, local copies, waits for them, and re-layouts: 2 us -> 0.03 us
    ppermute x7, waiting for transfers between devices: 2.77 us -> 3.84 us  [swap(): return lax.ppermute(x, 'dp', [(i, i ^ s) for i in range(n_dp)])]
    convert_element_type x1, other arithmetic: 1.63 us -> 0.7 us  [near_shards(): (own_grads + sum((part.astype(F32) for part in last))).astype(BF16)]
    ppermute x7, starting transfers between devices: 12 us -> 11.2 us  [swap(): return lax.ppermute(x, 'dp', [(i, i ^ s) for i in range(n_dp)])]
  transfers between devices with their start and end apart: 7 -> 7, of which waited for: 2 -> 1; matrix products, arithmetic and copies ran while one was open for 0% -> 0% of each run, Pallas kernels for 50% -> 54%
where the time goes in v7:
time: 39.5 us; the launch traced here: 39.2 us
  Pallas kernels  22.7 us (57%)
  starting transfers between devices  11.2 us (28%)
  waiting for transfers between devices  3.84 us (10%)
  between operations  0.74 us (2%)
  other arithmetic  0.7 us (2%)
    pallas_call x3, Pallas kernels, grads_of(): pl.pallas_call(functools.partial(group_kernel, z, turns, raw, len(used_ta...  18.3 us
    ppermute x7, starting transfers between devices, swap(): return lax.ppermute(x, 'dp', [(i, i ^ s) for i in range(n_dp)])  11.2 us
    ppermute x7, waiting for transfers between devices, swap(): return lax.ppermute(x, 'dp', [(i, i ^ s) for i in range(n_dp)])  3.84 us
    pallas_call x1, Pallas kernels, near_shards(): pl.pallas_call(functools.partial(finish_kernel, z, len(tails), len(come))...  2.83 us
    pallas_call x1, Pallas kernels, near_shards(): pl.pallas_call(functools.partial(pack_kernel, z), out_shape=jax.ShapeDtyp...  1.57 us
  transfers between devices with their start and end apart: 7, of which 1 were waited for; matrix products, arithmetic and copies ran while one was open for 0% of the time, Pallas kernels for 54%

profile of v7, /device:TPU:0, one launch (start us, length us, event | category | flops | bytes accessed | tf_op | source)
XLA Modules:
  0.0 39.2 jit_solution(14407208921432815539)
XLA Ops:
  0.6 1.6 %pack.1.refs_7_.refs_4_ = bf16[272,256]{1,0:T(8,128)(2,1)} custom-call(bf16[2,128,256]{2,1,0:T(8,128)(2,1)} %prompt_hbm.1, f32[16]{0:T(128)} %refs_2_.7, s32[64]{0:T(128)} %refs_0_.7), custom_call_target="tpu_custom_call" | custom-call | tf_op jit(solution)/shard_map/pack/pallas_call | solution.py:432
  2.2 0.0 copy-start
  2.2 0.0 copy-start.2
  2.2 0.0 copy-start.3
  2.2 0.0 copy-start.4
  2.3 4.1 %collective-permute-start = (bf16[272,256]{1,0:T(8,128)(2,1)}, bf16[272,256]{1,0:T(8,128)(2,1)S(1)}, u32[]{:S(2)}, u32[]{:S(2)}) collective-permute-start(bf16[272,256]{1,0:T(8,128)(2,1)} %pack.1.refs_7_.refs_4_), channel_id=1, source_target_pairs={{0,8},{4,12},{8,0},{12,4},{1,9},{5,13},{9,1},{13,5},{2,10},{6,14},... | collective-permute-start | bytes 417800 | tf_op jit(solution)/shard_map/ppermute | solution.py:450
  6.4 1.3 %collective-permute-start.1 = (f32[16]{0:T(128)}, f32[16]{0:T(128)S(1)}, u32[]{:S(2)}, u32[]{:S(2)}) collective-permute-start(f32[16]{0:T(128)} %refs_2_.7), channel_id=1, source_target_pairs={{0,12},{4,8},{8,4},{12,0},{1,13},{5,9},{9,5},{13,1},{2,14},{6,10},... | collective-permute-start | bytes 200 | tf_op jit(solution)/shard_map/ppermute | solution.py:450
  7.7 0.2 collective-permute-start.2
  7.9 5.4 %raw_grads.1 = (bf16[1024,1280]{1,0:T(8,128)(2,1)}, bf16[2,1024,256]{2,1,0:T(8,128)(2,1)}, bf16[4,2,128,256]{3,2,1,0:T(8,128)(2,1)}) custom-call(s32[64]{0:T(128)} %refs_0_.7, s32[16]{0:T(128)} %refs_1_.7, f32[16]{0:T(128)} %refs_2_.7, f32[16]{0:T(128)} %refs_2_.7, bf16[1024,1280]{1,0:T(8,128)(2,1)} %refs_4_.5, bf16[1024,1280]{1,0:T(8,128)(2,1)} %refs_5_.5, ...), custom_call_target="tpu_custom_call" | custom-call | tf_op jit(solution)/shard_map/raw_grads/pallas_call | solution.py:466
  13.4 0.0 collective-permute-done.1.refs_3_
  13.4 0.0 collective-permute-done.refs_9_.refs_10_.refs_6_
  13.4 1.9 %collective-permute-start.4 = (bf16[272,256]{1,0:T(8,128)(2,1)S(1)}, bf16[272,256]{1,0:T(8,128)(2,1)S(1)}, u32[]{:S(2)}, u32[]{:S(2)}) collective-permute-start(bf16[272,256]{1,0:T(8,128)(2,1)S(1)} %collective-permute-done.refs_9_.refs_10_.refs_6_), channel_id=1, source_target_pairs={{0,4},{4,0},{8,12},{12,8},{1,5},{5,1},{9,13},{13,9},{2,6},{6,2},{1... | collective-permute-start | bytes 417800 | tf_op jit(solution)/shard_map/ppermute | solution.py:450
  15.2 0.0 collective-permute-done.2.refs_8_.refs_11_.refs_5_
  15.2 0.0 copy-done
  15.2 0.0 copy-done.2
  15.2 0.0 copy-done.3
  15.3 0.0 copy-done.4
  15.3 7.8 %group_grads.2 = (bf16[1024,1280]{1,0:T(8,128)(2,1)}, bf16[2,1024,256]{2,1,0:T(8,128)(2,1)}, bf16[2,128,256]{2,1,0:T(8,128)(2,1)S(1)}, bf16[2,128,256]{2,1,0:T(8,128)(2,1)S(1)}) custom-call(s32[64]{0:T(128)S(1)} %copy-done.3, s32[16]{0:T(128)S(1)} %copy-done.4, f32[16]{0:T(128)S(1)} %copy-done.2, ...), custom_call_target="tpu_custom_call", output_to_operand_aliasing={{0}: (12, {}), {1}: (13, {})} | custom-call | tf_op jit(solution)/shard_map/group_grads/pallas_call | solution.py:466
  23.0 2.3 %collective-permute-start.3 = (bf16[2,128,256]{2,1,0:T(8,128)(2,1)S(1)}, bf16[2,128,256]{2,1,0:T(8,128)(2,1)S(1)}, u32[]{:S(2)}, u32[]{:S(2)}) collective-permute-start(bf16[2,128,256]{2,1,0:T(8,128)(2,1)S(1)} %get-tuple-element.26), channel_id=1, source_target_pairs={{0,8},{4,12},{8,0},{12,4},{1,9},{5,13},{9,1},{13,5},{2,10},{6,14},... | collective-permute-start | bytes 393224 | tf_op jit(solution)/shard_map/ppermute | solution.py:450
  25.3 0.0 collective-permute-done.4.refs_10_
  25.3 0.0 copy-start.1
  25.3 5.1 %group_grads.3 = (bf16[1024,1280]{1,0:T(8,128)(2,1)}, bf16[2,1024,256]{2,1,0:T(8,128)(2,1)}, bf16[2,128,256]{2,1,0:T(8,128)(2,1)S(1)}) custom-call(s32[64]{0:T(128)S(1)} %copy-done.3, s32[16]{0:T(128)S(1)} %copy-done.4, f32[16]{0:T(128)S(1)} %copy-done.2, f32[16]{0:T(128)S(1)} %collective-permute-done.1.refs_3_, ...), custom_call_target="tpu_custom_call", output_to_operand_aliasing={{0}: (11, {}), {1}: (12, {})} | custom-call | tf_op jit(solution)/shard_map/group_grads/pallas_call | solution.py:466
  30.4 0.8 %collective-permute-start.5 = (bf16[2,128,256]{2,1,0:T(8,128)(2,1)S(1)}, bf16[2,128,256]{2,1,0:T(8,128)(2,1)S(1)}, u32[]{:S(2)}, u32[]{:S(2)}) collective-permute-start(bf16[2,128,256]{2,1,0:T(8,128)(2,1)S(1)} %get-tuple-element.37), channel_id=1, source_target_pairs={{0,12},{4,8},{8,4},{12,0},{1,13},{5,9},{9,5},{13,1},{2,14},{6,10},... | collective-permute-start | bytes 393224 | tf_op jit(solution)/shard_map/ppermute | solution.py:450
  31.2 0.6 %collective-permute-start.6 = (bf16[2,128,256]{2,1,0:T(8,128)(2,1)S(1)}, bf16[2,128,256]{2,1,0:T(8,128)(2,1)S(1)}, u32[]{:S(2)}, u32[]{:S(2)}) collective-permute-start(bf16[2,128,256]{2,1,0:T(8,128)(2,1)S(1)} %get-tuple-element.38), channel_id=1, source_target_pairs={{0,4},{4,0},{8,12},{12,8},{1,5},{5,1},{9,13},{13,9},{2,6},{6,2},{1... | collective-permute-start | bytes 393224 | tf_op jit(solution)/shard_map/ppermute | solution.py:450
  31.8 0.0 collective-permute-done.3.refs_8_
  31.8 0.0 copy-done.1
  31.8 2.8 %finish_own.1 = (bf16[1024,1280]{1,0:T(8,128)(2,1)}, bf16[2,1024,256]{2,1,0:T(8,128)(2,1)}, f32[2,128,256]{2,1,0:T(8,128)S(1)}) custom-call(s32[64]{0:T(128)S(1)} %copy-done.3, s32[16]{0:T(128)S(1)} %copy-done.4, f32[16]{0:T(128)S(1)} %copy-done.2, f32[16]{0:T(128)S(1)} %collective-permute-done.1.refs_3_, ...), custom_call_target="tpu_custom_call", output_to_operand_aliasing={{0}: (9, {}), {1}: (10, {})} | custom-call | tf_op jit(solution)/shard_map/finish_own/pallas_call | solution.py:508
  34.7 3.8 %collective-permute-done.5 = bf16[2,128,256]{2,1,0:T(8,128)(2,1)S(1)} collective-permute-done((bf16[2,128,256]{2,1,0:T(8,128)(2,1)S(1)}, bf16[2,128,256]{2,1,0:T(8,128)(2,1)S(1)}, u32[]{:S(2)}, u32[]{:S(2)}) %collective-permute-start.5) | collective-permute-done | bytes 131104 | tf_op jit(solution)/shard_map/ppermute | solution.py:450
  38.5 0.0 collective-permute-done.6
  38.5 0.7 %add_convert_fusion = bf16[2,128,256]{2,1,0:T(8,128)(2,1)} fusion(f32[2,128,256]{2,1,0:T(8,128)S(1)} %get-tuple-element.34, bf16[2,128,256]{2,1,0:T(8,128)(2,1)S(1)} %collective-permute-done.6, bf16[2,128,256]{2,1,0:T(8,128)(2,1)S(1)} %collective-permute-done.5), kind=kLoop, calls=%fused_computation | loop fusion | flops 327680 | bytes 655360 | tf_op jit(solution)/shard_map/convert_element_type | solution.py:533
Async XLA Ops:
  2.2 13.0 %copy-start = (bf16[272,256]{1,0:T(8,128)(2,1)S(1)}, bf16[272,256]{1,0:T(8,128)(2,1)}, u32[]{:S(2)}) copy-start(bf16[272,256]{1,0:T(8,128)(2,1)} %pack.1.refs_7_.refs_4_) | copy-start | bytes 417796
  2.2 13.0 %copy-start.2 = (f32[16]{0:T(128)S(1)}, f32[16]{0:T(128)}, u32[]{:S(2)}) copy-start(f32[16]{0:T(128)} %refs_2_.7) | copy-start | bytes 196
  2.2 13.0 %copy-start.3 = (s32[64]{0:T(128)S(1)}, s32[64]{0:T(128)}, u32[]{:S(2)}) copy-start(s32[64]{0:T(128)} %refs_0_.7) | copy-start | bytes 772
  2.2 13.0 %copy-start.4 = (s32[16]{0:T(128)S(1)}, s32[16]{0:T(128)}, u32[]{:S(2)}) copy-start(s32[16]{0:T(128)} %refs_1_.7) | copy-start | bytes 196
  2.3 11.1 %collective-permute-start = (bf16[272,256]{1,0:T(8,128)(2,1)}, bf16[272,256]{1,0:T(8,128)(2,1)S(1)}, u32[]{:S(2)}, u32[]{:S(2)}) collective-permute-start(bf16[272,256]{1,0:T(8,128)(2,1)} %pack.1.refs_7_.refs_4_), channel_id=1, source_target_pairs={{0,8},{4,12},{8,0},{12,4},{1,9},{5,13},{9,1},{13,5},{2,10},{6,14},... | collective-permute-start | bytes 417800 | tf_op jit(solution)/shard_map/ppermute | solution.py:450
  6.4 7.0 %collective-permute-start.1 = (f32[16]{0:T(128)}, f32[16]{0:T(128)S(1)}, u32[]{:S(2)}, u32[]{:S(2)}) collective-permute-start(f32[16]{0:T(128)} %refs_2_.7), channel_id=1, source_target_pairs={{0,12},{4,8},{8,4},{12,0},{1,13},{5,9},{9,5},{13,1},{2,14},{6,10},... | collective-permute-start | bytes 200 | tf_op jit(solution)/shard_map/ppermute | solution.py:450
  7.7 7.5 %collective-permute-start.2 = (bf16[272,256]{1,0:T(8,128)(2,1)}, bf16[272,256]{1,0:T(8,128)(2,1)S(1)}, u32[]{:S(2)}, u32[]{:S(2)}) collective-permute-start(bf16[272,256]{1,0:T(8,128)(2,1)} %pack.1.refs_7_.refs_4_), channel_id=1, source_target_pairs={{0,4},{4,0},{8,12},{12,8},{1,5},{5,1},{9,13},{13,9},{2,6},{6,2},{1... | collective-permute-start | bytes 417800 | tf_op jit(solution)/shard_map/ppermute | solution.py:450
  13.4 11.9 %collective-permute-start.4 = (bf16[272,256]{1,0:T(8,128)(2,1)S(1)}, bf16[272,256]{1,0:T(8,128)(2,1)S(1)}, u32[]{:S(2)}, u32[]{:S(2)}) collective-permute-start(bf16[272,256]{1,0:T(8,128)(2,1)S(1)} %collective-permute-done.refs_9_.refs_10_.refs_6_), channel_id=1, source_target_pairs={{0,4},{4,0},{8,12},{12,8},{1,5},{5,1},{9,13},{13,9},{2,6},{6,2},{1... | collective-permute-start | bytes 417800 | tf_op jit(solution)/shard_map/ppermute | solution.py:450
  23.0 8.8 %collective-permute-start.3 = (bf16[2,128,256]{2,1,0:T(8,128)(2,1)S(1)}, bf16[2,128,256]{2,1,0:T(8,128)(2,1)S(1)}, u32[]{:S(2)}, u32[]{:S(2)}) collective-permute-start(bf16[2,128,256]{2,1,0:T(8,128)(2,1)S(1)} %get-tuple-element.26), channel_id=1, source_target_pairs={{0,8},{4,12},{8,0},{12,4},{1,9},{5,13},{9,1},{13,5},{2,10},{6,14},... | collective-permute-start | bytes 393224 | tf_op jit(solution)/shard_map/ppermute | solution.py:450
  25.3 6.5 %copy-start.1 = (bf16[4,2,128,256]{3,2,1,0:T(8,128)(2,1)S(1)}, bf16[4,2,128,256]{3,2,1,0:T(8,128)(2,1)}, u32[]{:S(2)}) copy-start(bf16[4,2,128,256]{3,2,1,0:T(8,128)(2,1)} %get-tuple-element.23.refs_7_) | copy-start | bytes 1572868
  30.4 8.1 %collective-permute-start.5 = (bf16[2,128,256]{2,1,0:T(8,128)(2,1)S(1)}, bf16[2,128,256]{2,1,0:T(8,128)(2,1)S(1)}, u32[]{:S(2)}, u32[]{:S(2)}) collective-permute-start(bf16[2,128,256]{2,1,0:T(8,128)(2,1)S(1)} %get-tuple-element.37), channel_id=1, source_target_pairs={{0,12},{4,8},{8,4},{12,0},{1,13},{5,9},{9,5},{13,1},{2,14},{6,10},... | collective-permute-start | bytes 393224 | tf_op jit(solution)/shard_map/ppermute | solution.py:450
  31.2 7.3 %collective-permute-start.6 = (bf16[2,128,256]{2,1,0:T(8,128)(2,1)S(1)}, bf16[2,128,256]{2,1,0:T(8,128)(2,1)S(1)}, u32[]{:S(2)}, u32[]{:S(2)}) collective-permute-start(bf16[2,128,256]{2,1,0:T(8,128)(2,1)S(1)} %get-tuple-element.38), channel_id=1, source_target_pairs={{0,4},{4,0},{8,12},{12,8},{1,5},{5,1},{9,13},{13,9},{2,6},{6,2},{1... | collective-permute-start | bytes 393224 | tf_op jit(solution)/shard_map/ppermute | solution.py:450

commit v8 on v7

--- a/solution.py
+++ b/solution.py
@@ -77,6 +77,11 @@
     def halves(part):
         none = jnp.zeros_like(part)
         return [jnp.where(left, part, none), jnp.where(left, none, part)]
+
+    def over_keys(combine, *parts):
+        reduce = jnp.max if combine is jnp.maximum else jnp.sum
+        eights = [reduce(part.reshape(-1, 8, part.shape[1]), axis=0) for part in parts]
+        return reduce(functools.reduce(combine, eights), axis=0, keepdims=True)
 
     def own_half(both):
         return jnp.where(left, both[:tokens], both[tokens:])
@@ -124,15 +129,11 @@
         if c.side is None:
             scores_s, c.gw_s = own_half(scores_s), own_half(c.gw_s)
         scores_s = jnp.where(causal[:, : scores_s.shape[1]], scores_s, NEG)
-        top = jnp.maximum(
-            jnp.max(scores_p, axis=0, keepdims=True), jnp.max(scores_s, axis=0, keepdims=True)
-        )
+        top = over_keys(jnp.maximum, scores_p, scores_s)
         c.e_p = jnp.exp2((scores_p - top) * log_scale)
         c.e_s = jnp.exp2((scores_s - top) * log_scale)
-        total = jnp.sum(c.e_p, axis=0, keepdims=True) + jnp.sum(c.e_s, axis=0, keepdims=True)
-        weighted = jnp.sum(c.e_p * c.gw_p, axis=0, keepdims=True) + jnp.sum(
-            c.e_s * c.gw_s, axis=0, keepdims=True
-        )
+        total = over_keys(jnp.add, c.e_p, c.e_s)
+        weighted = over_keys(jnp.add, c.e_p * c.gw_p, c.e_s * c.gw_s)
         if c.side is None:
             length = jnp.where(left, lens[0], 0 if single else lens[1])
             gain = jnp.where(left, factors[0], factors[-1])
@@ -185,7 +186,7 @@
 
     stages = (products, weigh, gradients, outgoing)
     for step in range(len(chunks) + len(stages) - 1):
-        for late, stage in reversed(list(enumerate(stages))):
+        for late, stage in enumerate(stages):
             if 0 <= step - late < len(chunks):
                 stage(chunks[step - late])
 

time: 39.5 us -> 38.8 us (0.982)
  Pallas kernels: 22.7 us -> 21.8 us
    pallas_call x3, Pallas kernels: 18.3 us -> 17.4 us  [grads_of(): pl.pallas_call(functools.partial(group_kernel, z, turns, raw, len(used_ta...]
  transfers between devices with their start and end apart: 7 -> 7, of which waited for: 1 -> 2; matrix products, arithmetic and copies ran while one was open for 0% -> 0% of each run, Pallas kernels for 54% -> 52%
where the time goes in v8:
time: 38.8 us; the launch traced here: 38.6 us
  Pallas kernels  21.8 us (56%)
  starting transfers between devices  11.2 us (29%)
  waiting for transfers between devices  4.03 us (10%)
  between operations  0.74 us (2%)
  other arithmetic  0.7 us (2%)
    pallas_call x3, Pallas kernels, grads_of(): pl.pallas_call(functools.partial(group_kernel, z, turns, raw, len(used_ta...  17.4 us
    ppermute x7, starting transfers between devices, swap(): return lax.ppermute(x, 'dp', [(i, i ^ s) for i in range(n_dp)])  11.2 us
    ppermute x7, waiting for transfers between devices, swap(): return lax.ppermute(x, 'dp', [(i, i ^ s) for i in range(n_dp)])  4.03 us
    pallas_call x1, Pallas kernels, near_shards(): pl.pallas_call(functools.partial(finish_kernel, z, len(tails), len(come))...  2.83 us
    pallas_call x1, Pallas kernels, near_shards(): pl.pallas_call(functools.partial(pack_kernel, z), out_shape=jax.ShapeDtyp...  1.57 us
  transfers between devices with their start and end apart: 7, of which 2 were waited for; matrix products, arithmetic and copies ran while one was open for 0% of the time, Pallas kernels for 52%

profile of v8, /device:TPU:0, one launch (start us, length us, event | category | flops | bytes accessed | tf_op | source)
XLA Modules:
  0.0 38.6 jit_solution(14510951691625115523)
XLA Ops:
  0.6 1.6 %pack.1.refs_7_.refs_4_ = bf16[272,256]{1,0:T(8,128)(2,1)} custom-call(bf16[2,128,256]{2,1,0:T(8,128)(2,1)} %prompt_hbm.1, f32[16]{0:T(128)} %refs_2_.7, s32[64]{0:T(128)} %refs_0_.7), custom_call_target="tpu_custom_call" | custom-call | tf_op jit(solution)/shard_map/pack/pallas_call | solution.py:433
  2.2 0.0 copy-start
  2.2 0.0 copy-start.2
  2.2 0.0 copy-start.3
  2.2 0.0 copy-start.4
  2.3 4.1 %collective-permute-start = (bf16[272,256]{1,0:T(8,128)(2,1)}, bf16[272,256]{1,0:T(8,128)(2,1)S(1)}, u32[]{:S(2)}, u32[]{:S(2)}) collective-permute-start(bf16[272,256]{1,0:T(8,128)(2,1)} %pack.1.refs_7_.refs_4_), channel_id=1, source_target_pairs={{0,8},{4,12},{8,0},{12,4},{1,9},{5,13},{9,1},{13,5},{2,10},{6,14},... | collective-permute-start | bytes 417800 | tf_op jit(solution)/shard_map/ppermute | solution.py:451
  6.4 1.3 %collective-permute-start.1 = (f32[16]{0:T(128)}, f32[16]{0:T(128)S(1)}, u32[]{:S(2)}, u32[]{:S(2)}) collective-permute-start(f32[16]{0:T(128)} %refs_2_.7), channel_id=1, source_target_pairs={{0,12},{4,8},{8,4},{12,0},{1,13},{5,9},{9,5},{13,1},{2,14},{6,10},... | collective-permute-start | bytes 200 | tf_op jit(solution)/shard_map/ppermute | solution.py:451
  7.7 0.2 collective-permute-start.2
  7.9 5.2 %raw_grads.1 = (bf16[1024,1280]{1,0:T(8,128)(2,1)}, bf16[2,1024,256]{2,1,0:T(8,128)(2,1)}, bf16[4,2,128,256]{3,2,1,0:T(8,128)(2,1)}) custom-call(s32[64]{0:T(128)} %refs_0_.7, s32[16]{0:T(128)} %refs_1_.7, f32[16]{0:T(128)} %refs_2_.7, f32[16]{0:T(128)} %refs_2_.7, bf16[1024,1280]{1,0:T(8,128)(2,1)} %refs_4_.5, bf16[1024,1280]{1,0:T(8,128)(2,1)} %refs_5_.5, ...), custom_call_target="tpu_custom_call" | custom-call | tf_op jit(solution)/shard_map/raw_grads/pallas_call | solution.py:467
  13.1 0.0 collective-permute-done.1.refs_3_
  13.1 0.2 collective-permute-done.refs_9_.refs_10_.refs_6_
  13.3 1.7 %collective-permute-start.4 = (bf16[272,256]{1,0:T(8,128)(2,1)S(1)}, bf16[272,256]{1,0:T(8,128)(2,1)S(1)}, u32[]{:S(2)}, u32[]{:S(2)}) collective-permute-start(bf16[272,256]{1,0:T(8,128)(2,1)S(1)} %collective-permute-done.refs_9_.refs_10_.refs_6_), channel_id=1, source_target_pairs={{0,4},{4,0},{8,12},{12,8},{1,5},{5,1},{9,13},{13,9},{2,6},{6,2},{1... | collective-permute-start | bytes 417800 | tf_op jit(solution)/shard_map/ppermute | solution.py:451
  15.0 0.0 collective-permute-done.2.refs_8_.refs_11_.refs_5_
  15.0 0.0 copy-done
  15.0 0.0 copy-done.2
  15.0 0.0 copy-done.3
  15.0 0.0 copy-done.4
  15.1 7.3 %group_grads.2 = (bf16[1024,1280]{1,0:T(8,128)(2,1)}, bf16[2,1024,256]{2,1,0:T(8,128)(2,1)}, bf16[2,128,256]{2,1,0:T(8,128)(2,1)S(1)}, bf16[2,128,256]{2,1,0:T(8,128)(2,1)S(1)}) custom-call(s32[64]{0:T(128)S(1)} %copy-done.3, s32[16]{0:T(128)S(1)} %copy-done.4, f32[16]{0:T(128)S(1)} %copy-done.2, ...), custom_call_target="tpu_custom_call", output_to_operand_aliasing={{0}: (12, {}), {1}: (13, {})} | custom-call | tf_op jit(solution)/shard_map/group_grads/pallas_call | solution.py:467
  22.4 2.5 %collective-permute-start.3 = (bf16[2,128,256]{2,1,0:T(8,128)(2,1)S(1)}, bf16[2,128,256]{2,1,0:T(8,128)(2,1)S(1)}, u32[]{:S(2)}, u32[]{:S(2)}) collective-permute-start(bf16[2,128,256]{2,1,0:T(8,128)(2,1)S(1)} %get-tuple-element.26), channel_id=1, source_target_pairs={{0,8},{4,12},{8,0},{12,4},{1,9},{5,13},{9,1},{13,5},{2,10},{6,14},... | collective-permute-start | bytes 393224 | tf_op jit(solution)/shard_map/ppermute | solution.py:451
  24.9 0.0 collective-permute-done.4.refs_10_
  24.9 0.0 copy-start.1
  24.9 4.9 %group_grads.3 = (bf16[1024,1280]{1,0:T(8,128)(2,1)}, bf16[2,1024,256]{2,1,0:T(8,128)(2,1)}, bf16[2,128,256]{2,1,0:T(8,128)(2,1)S(1)}) custom-call(s32[64]{0:T(128)S(1)} %copy-done.3, s32[16]{0:T(128)S(1)} %copy-done.4, f32[16]{0:T(128)S(1)} %copy-done.2, f32[16]{0:T(128)S(1)} %collective-permute-done.1.refs_3_, ...), custom_call_target="tpu_custom_call", output_to_operand_aliasing={{0}: (11, {}), {1}: (12, {})} | custom-call | tf_op jit(solution)/shard_map/group_grads/pallas_call | solution.py:467
  29.8 0.8 %collective-permute-start.5 = (bf16[2,128,256]{2,1,0:T(8,128)(2,1)S(1)}, bf16[2,128,256]{2,1,0:T(8,128)(2,1)S(1)}, u32[]{:S(2)}, u32[]{:S(2)}) collective-permute-start(bf16[2,128,256]{2,1,0:T(8,128)(2,1)S(1)} %get-tuple-element.37), channel_id=1, source_target_pairs={{0,12},{4,8},{8,4},{12,0},{1,13},{5,9},{9,5},{13,1},{2,14},{6,10},... | collective-permute-start | bytes 393224 | tf_op jit(solution)/shard_map/ppermute | solution.py:451
  30.6 0.6 %collective-permute-start.6 = (bf16[2,128,256]{2,1,0:T(8,128)(2,1)S(1)}, bf16[2,128,256]{2,1,0:T(8,128)(2,1)S(1)}, u32[]{:S(2)}, u32[]{:S(2)}) collective-permute-start(bf16[2,128,256]{2,1,0:T(8,128)(2,1)S(1)} %get-tuple-element.38), channel_id=1, source_target_pairs={{0,4},{4,0},{8,12},{12,8},{1,5},{5,1},{9,13},{13,9},{2,6},{6,2},{1... | collective-permute-start | bytes 393224 | tf_op jit(solution)/shard_map/ppermute | solution.py:451
  31.2 0.0 collective-permute-done.3.refs_8_
  31.2 0.0 copy-done.1
  31.2 2.8 %finish_own.1 = (bf16[1024,1280]{1,0:T(8,128)(2,1)}, bf16[2,1024,256]{2,1,0:T(8,128)(2,1)}, f32[2,128,256]{2,1,0:T(8,128)S(1)}) custom-call(s32[64]{0:T(128)S(1)} %copy-done.3, s32[16]{0:T(128)S(1)} %copy-done.4, f32[16]{0:T(128)S(1)} %copy-done.2, f32[16]{0:T(128)S(1)} %collective-permute-done.1.refs_3_, ...), custom_call_target="tpu_custom_call", output_to_operand_aliasing={{0}: (9, {}), {1}: (10, {})} | custom-call | tf_op jit(solution)/shard_map/finish_own/pallas_call | solution.py:509
  34.0 3.8 %collective-permute-done.5 = bf16[2,128,256]{2,1,0:T(8,128)(2,1)S(1)} collective-permute-done((bf16[2,128,256]{2,1,0:T(8,128)(2,1)S(1)}, bf16[2,128,256]{2,1,0:T(8,128)(2,1)S(1)}, u32[]{:S(2)}, u32[]{:S(2)}) %collective-permute-start.5) | collective-permute-done | bytes 131104 | tf_op jit(solution)/shard_map/ppermute | solution.py:451
  37.9 0.0 collective-permute-done.6
  37.9 0.7 %add_convert_fusion = bf16[2,128,256]{2,1,0:T(8,128)(2,1)} fusion(f32[2,128,256]{2,1,0:T(8,128)S(1)} %get-tuple-element.34, bf16[2,128,256]{2,1,0:T(8,128)(2,1)S(1)} %collective-permute-done.6, bf16[2,128,256]{2,1,0:T(8,128)(2,1)S(1)} %collective-permute-done.5), kind=kLoop, calls=%fused_computation | loop fusion | flops 327680 | bytes 655360 | tf_op jit(solution)/shard_map/convert_element_type | solution.py:534
Async XLA Ops:
  2.2 12.8 %copy-start = (bf16[272,256]{1,0:T(8,128)(2,1)S(1)}, bf16[272,256]{1,0:T(8,128)(2,1)}, u32[]{:S(2)}) copy-start(bf16[272,256]{1,0:T(8,128)(2,1)} %pack.1.refs_7_.refs_4_) | copy-start | bytes 417796
  2.2 12.8 %copy-start.2 = (f32[16]{0:T(128)S(1)}, f32[16]{0:T(128)}, u32[]{:S(2)}) copy-start(f32[16]{0:T(128)} %refs_2_.7) | copy-start | bytes 196
  2.2 12.8 %copy-start.3 = (s32[64]{0:T(128)S(1)}, s32[64]{0:T(128)}, u32[]{:S(2)}) copy-start(s32[64]{0:T(128)} %refs_0_.7) | copy-start | bytes 772
  2.2 12.8 %copy-start.4 = (s32[16]{0:T(128)S(1)}, s32[16]{0:T(128)}, u32[]{:S(2)}) copy-start(s32[16]{0:T(128)} %refs_1_.7) | copy-start | bytes 196
  2.3 11.1 %collective-permute-start = (bf16[272,256]{1,0:T(8,128)(2,1)}, bf16[272,256]{1,0:T(8,128)(2,1)S(1)}, u32[]{:S(2)}, u32[]{:S(2)}) collective-permute-start(bf16[272,256]{1,0:T(8,128)(2,1)} %pack.1.refs_7_.refs_4_), channel_id=1, source_target_pairs={{0,8},{4,12},{8,0},{12,4},{1,9},{5,13},{9,1},{13,5},{2,10},{6,14},... | collective-permute-start | bytes 417800 | tf_op jit(solution)/shard_map/ppermute | solution.py:451
  6.4 6.8 %collective-permute-start.1 = (f32[16]{0:T(128)}, f32[16]{0:T(128)S(1)}, u32[]{:S(2)}, u32[]{:S(2)}) collective-permute-start(f32[16]{0:T(128)} %refs_2_.7), channel_id=1, source_target_pairs={{0,12},{4,8},{8,4},{12,0},{1,13},{5,9},{9,5},{13,1},{2,14},{6,10},... | collective-permute-start | bytes 200 | tf_op jit(solution)/shard_map/ppermute | solution.py:451
  7.7 7.3 %collective-permute-start.2 = (bf16[272,256]{1,0:T(8,128)(2,1)}, bf16[272,256]{1,0:T(8,128)(2,1)S(1)}, u32[]{:S(2)}, u32[]{:S(2)}) collective-permute-start(bf16[272,256]{1,0:T(8,128)(2,1)} %pack.1.refs_7_.refs_4_), channel_id=1, source_target_pairs={{0,4},{4,0},{8,12},{12,8},{1,5},{5,1},{9,13},{13,9},{2,6},{6,2},{1... | collective-permute-start | bytes 417800 | tf_op jit(solution)/shard_map/ppermute | solution.py:451
  13.3 11.5 %collective-permute-start.4 = (bf16[272,256]{1,0:T(8,128)(2,1)S(1)}, bf16[272,256]{1,0:T(8,128)(2,1)S(1)}, u32[]{:S(2)}, u32[]{:S(2)}) collective-permute-start(bf16[272,256]{1,0:T(8,128)(2,1)S(1)} %collective-permute-done.refs_9_.refs_10_.refs_6_), channel_id=1, source_target_pairs={{0,4},{4,0},{8,12},{12,8},{1,5},{5,1},{9,13},{13,9},{2,6},{6,2},{1... | collective-permute-start | bytes 417800 | tf_op jit(solution)/shard_map/ppermute | solution.py:451
  22.4 8.8 %collective-permute-start.3 = (bf16[2,128,256]{2,1,0:T(8,128)(2,1)S(1)}, bf16[2,128,256]{2,1,0:T(8,128)(2,1)S(1)}, u32[]{:S(2)}, u32[]{:S(2)}) collective-permute-start(bf16[2,128,256]{2,1,0:T(8,128)(2,1)S(1)} %get-tuple-element.26), channel_id=1, source_target_pairs={{0,8},{4,12},{8,0},{12,4},{1,9},{5,13},{9,1},{13,5},{2,10},{6,14},... | collective-permute-start | bytes 393224 | tf_op jit(solution)/shard_map/ppermute | solution.py:451
  24.9 6.3 %copy-start.1 = (bf16[4,2,128,256]{3,2,1,0:T(8,128)(2,1)S(1)}, bf16[4,2,128,256]{3,2,1,0:T(8,128)(2,1)}, u32[]{:S(2)}) copy-start(bf16[4,2,128,256]{3,2,1,0:T(8,128)(2,1)} %get-tuple-element.23.refs_7_) | copy-start | bytes 1572868
  29.8 8.1 %collective-permute-start.5 = (bf16[2,128,256]{2,1,0:T(8,128)(2,1)S(1)}, bf16[2,128,256]{2,1,0:T(8,128)(2,1)S(1)}, u32[]{:S(2)}, u32[]{:S(2)}) collective-permute-start(bf16[2,128,256]{2,1,0:T(8,128)(2,1)S(1)} %get-tuple-element.37), channel_id=1, source_target_pairs={{0,12},{4,8},{8,4},{12,0},{1,13},{5,9},{9,5},{13,1},{2,14},{6,10},... | collective-permute-start | bytes 393224 | tf_op jit(solution)/shard_map/ppermute | solution.py:451
  30.6 7.3 %collective-permute-start.6 = (bf16[2,128,256]{2,1,0:T(8,128)(2,1)S(1)}, bf16[2,128,256]{2,1,0:T(8,128)(2,1)S(1)}, u32[]{:S(2)}, u32[]{:S(2)}) collective-permute-start(bf16[2,128,256]{2,1,0:T(8,128)(2,1)S(1)} %get-tuple-element.38), channel_id=1, source_target_pairs={{0,4},{4,0},{8,12},{12,8},{1,5},{5,1},{9,13},{13,9},{2,6},{6,2},{1... | collective-permute-start | bytes 393224 | tf_op jit(solution)/shard_map/ppermute | solution.py:451

commit v9 on v8

--- a/solution.py
+++ b/solution.py
@@ -52,14 +52,19 @@
     pass
 
 
-def attend_pair(z, at, places, q, og, kv, prefix, lens, factors, out, own_out, sink, apart):
+class Unit(NamedTuple):
+    at: list
+    places: list
+    k: object
+    lens: list
+    factors: list
+
+
+def attend(z, units, q, og, kv, prefix, out, own_out, sink, apart):
     tokens, prefix_len, group_size = z.tokens, z.prefix_len, z.group_size
     scale = 1.0 / math.sqrt(HD)
     log_scale = scale * math.log2(math.e)
     whole = group_size - group_size % 2
-    single = len(at) == 1
-    members = range(len(at))
-    sides = (0, 0) if single else (0, 1)
     most = max(whole, 2) * tokens
     assert tokens & (tokens - 1) == 0
     token = lax.broadcasted_iota(jnp.int32, (1, most), 1) & (tokens - 1)
@@ -67,12 +72,16 @@
     causal = key <= (lax.broadcasted_iota(jnp.int32, (tokens, most), 1) & (tokens - 1))
     left = lax.broadcasted_iota(jnp.int32, (1, 2 * tokens), 1) < tokens
 
+    def columns(index):
+        if isinstance(index, int):
+            return slice(index * HD, (index + 1) * HD)
+        return pl.ds(pl.multiple_of(index * HD, HD), HD)
+
     def head(k, h):
-        start = (k * group_size + h) * HD
-        return slice(start, start + HD)
-
-    def rows(ref, k, blocks):
-        return jnp.concatenate([ref[at[n], head(k, h)] for n, h in blocks], axis=0)
+        return columns(k * group_size + h)
+
+    def rows(ref, c):
+        return jnp.concatenate([ref[c.t.at[n], head(c.t.k, h)] for n, h in c.blocks], axis=0)
 
     def halves(part):
         none = jnp.zeros_like(part)
@@ -90,32 +99,36 @@
         return jnp.concatenate([part.astype(BF16) for part in parts], axis=0)
 
     chunks = []
-    for k in range(z.kv_heads):
+    for unit in units:
         t = Bag()
-        t.cols = slice(k * HD, (k + 1) * HD)
+        t.at, t.places, t.k, t.lens, t.factors = unit
+        t.single = len(t.at) == 1
+        t.members = range(len(t.at))
+        sides = (0, 0) if t.single else (0, 1)
+        t.cols = columns(t.k)
         t.key_p, t.value_p = prefix[0, :, t.cols], prefix[1, :, t.cols]
-        t.keys = [kv[0, at[n], t.cols] for n in sides]
-        t.values = [kv[1, at[n], t.cols] for n in sides]
+        t.keys = [kv[0, t.at[n], t.cols] for n in sides]
+        t.values = [kv[1, t.at[n], t.cols] for n in sides]
         t.key_pair = jnp.concatenate(t.keys, axis=0)
         t.value_pair = jnp.concatenate(t.values, axis=0)
         t.key_t = jnp.concatenate([t.key_p.T, t.key_pair.T], axis=1)
-        t.prefix_sums = {n: [] for n in members}
-        t.self_sums = {n: [] for n in members}
+        t.prefix_sums = {n: [] for n in t.members}
+        t.self_sums = {n: [] for n in t.members}
         mine = []
-        for n in members:
+        for n in t.members:
             c = Bag()
-            c.k, c.t, c.side, c.blocks = k, t, n, [(n, h) for h in range(whole)]
+            c.t, c.side, c.blocks = t, n, [(n, h) for h in range(whole)]
             mine.append(c)
         if group_size % 2:
             c = Bag()
-            c.k, c.t, c.side, c.blocks = k, t, None, [(n, group_size - 1) for n in sides]
+            c.t, c.side, c.blocks = t, None, [(n, group_size - 1) for n in sides]
             mine.append(c)
         t.left_over = len(mine)
         chunks += mine
 
     def products(c):
         t = c.t
-        c.q_rows, c.g_rows = rows(q, c.k, c.blocks), rows(og, c.k, c.blocks)
+        c.q_rows, c.g_rows = rows(q, c), rows(og, c)
         if c.side is None:
             key_s, value_s = t.key_pair, t.value_pair
         else:
@@ -135,10 +148,10 @@
         total = over_keys(jnp.add, c.e_p, c.e_s)
         weighted = over_keys(jnp.add, c.e_p * c.gw_p, c.e_s * c.gw_s)
         if c.side is None:
-            length = jnp.where(left, lens[0], 0 if single else lens[1])
-            gain = jnp.where(left, factors[0], factors[-1])
+            length = jnp.where(left, c.t.lens[0], 0 if c.t.single else c.t.lens[1])
+            gain = jnp.where(left, c.t.factors[0], c.t.factors[-1])
         else:
-            length, gain = lens[c.side], factors[c.side]
+            length, gain = c.t.lens[c.side], c.t.factors[c.side]
         inverse = 1.0 / total
         c.delta = weighted * inverse
         c.gain = inverse * jnp.where(token[:, : total.shape[1]] < length, gain, 0.0)
@@ -162,10 +175,10 @@
         q_grad = (dot(t.key_t, c.d_wide, NN) * scale).astype(BF16).T
         kg = dot(c.d_all, c.q_rows, NN)
         vg = dot(c.w_all, c.g_rows, NN)
-        targets = members if c.side is None else [c.side]
+        targets = t.members if c.side is None else [c.side]
         for place, (n, h) in enumerate(c.blocks):
             if c.side is not None or place < len(targets):
-                out[places[n], :, head(c.k, h)] = q_grad[place * tokens : (place + 1) * tokens]
+                out[t.places[n], :, head(t.k, h)] = q_grad[place * tokens : (place + 1) * tokens]
         many = 2 if c.side is None and apart else 1
         for place, n in enumerate(targets):
             if place < many:
@@ -176,13 +189,13 @@
             t.self_sums[n].append((kg[rows_s], vg[rows_s]))
         t.left_over -= 1
         if t.left_over == 0:
-            for n in members:
+            for n in t.members:
                 keys, values = zip(*t.self_sums[n])
-                own_out[places[n], 0, :, t.cols] = (sum(keys) * scale).astype(BF16)
-                own_out[places[n], 1, :, t.cols] = sum(values).astype(BF16)
+                own_out[t.places[n], 0, :, t.cols] = (sum(keys) * scale).astype(BF16)
+                own_out[t.places[n], 1, :, t.cols] = sum(values).astype(BF16)
                 if apart or n == 0:
                     keys, values = zip(*t.prefix_sums[n])
-                    sink(n, t.cols, sum(keys) * scale, sum(values))
+                    sink(t.places[n], t.cols, sum(keys) * scale, sum(values))
 
     stages = (products, weigh, gradients, outgoing)
     for step in range(len(chunks) + len(stages) - 1):
@@ -280,7 +293,7 @@
     ]
 
 
-def group_kernel(z, turns, raw, n_tails, aliased, *refs):
+def group_kernel(z, turns, raw, body, n_tails, aliased, *refs):
     small_hbm, given = refs[:4], refs[4:7]
     tail_hbm, prompts = refs[7 : 7 + n_tails], refs[7 + n_tails : 7 + n_tails + len(turns)]
     refs = refs[7 + n_tails + len(turns) + aliased :]
@@ -331,31 +344,57 @@
     for copy in prefix_copies:
         copy.wait()
 
-    def unit(u, _):
-        at = [u * PAIR + n for n in range(PAIR)]
-        t = u // (z.slots // PAIR)
-        for slot in at:
-            for copy in copies_in(slot):
-                copy.wait()
-
-        def sink(n, cols, key_grad, value_grad):
+    pairs_per_turn = z.slots // PAIR
+    pairs_in_body, heads_in_body = body
+    head_steps = z.kv_heads // heads_in_body
+    pair_steps = pairs_per_turn // pairs_in_body
+
+    def step(u, _):
+        k_step = lax.rem(u, head_steps) if head_steps > 1 else 0
+        pair_step = u // head_steps
+        t = pair_step // pair_steps
+        first = pair_step * pairs_in_body * PAIR
+        mine = range(pairs_in_body * PAIR)
+
+        def moves(starting):
+            for n in mine:
+                for copy in copies_out(first + n) if starting else copies_in(first + n):
+                    copy.start() if starting else copy.wait()
+
+        if head_steps > 1:
+            pl.when(k_step == 0)(lambda: moves(False))
+        else:
+            moves(False)
+
+        def sink(place, cols, key_grad, value_grad):
             if raw:
-                grads[at[n], 0, :, cols] = key_grad.astype(BF16)
-                grads[at[n], 1, :, cols] = value_grad.astype(BF16)
+                grads[place, 0, :, cols] = key_grad.astype(BF16)
+                grads[place, 1, :, cols] = value_grad.astype(BF16)
             else:
                 acc[t, 0, :, cols] += key_grad
                 acc[t, 1, :, cols] += value_grad
 
-        attend_pair(
-            z, [token_rows(z, n) for n in at], at, q, og, kv, prefix.at[t], [lens[n] for n in at],
-            [factors[n] for n in at], out, own, sink, raw,
-        )
-        for slot in at:
-            for copy in copies_out(slot):
-                copy.start()
+        units = []
+        for pair in range(pairs_in_body):
+            places = [first + pair * PAIR + n for n in range(PAIR)]
+            for k in range(heads_in_body):
+                units.append(
+                    Unit(
+                        [token_rows(z, n) for n in places],
+                        places,
+                        k_step * heads_in_body + k if head_steps > 1 else k,
+                        [lens[n] for n in places],
+                        [factors[n] for n in places],
+                    )
+                )
+        attend(z, units, q, og, kv, prefix.at[t], out, own, sink, raw)
+        if head_steps > 1:
+            pl.when(k_step == head_steps - 1)(lambda: moves(True))
+        else:
+            moves(True)
         return 0
 
-    lax.fori_loop(0, n_slots // PAIR, unit, 0)
+    lax.fori_loop(0, len(turns) * pair_steps * head_steps, step, 0)
     if raw:
         last = [pltpu.make_async_copy(grads, grads_out[0], sem_grads.at[0])]
     else:
@@ -457,7 +496,7 @@
     smem = [pltpu.SMEM(x.shape, x.dtype) for x in (*small, rewards)]
     slots = z.slots
 
-    def grads_of(turns, raw, written):
+    def grads_of(turns, raw, written, body):
         n_slots, n_turns = len(turns) * slots, len(turns)
         used_tails = [] if raw else tails
         used_small = (*small, rewards if raw else far_rewards)
@@ -465,7 +504,7 @@
         operands = [*used_small, resp_q, out_grad, resp_kv, *used_tails, *prompts, *written]
         grads_shapes = [(slots,) + one] if raw else [one] * n_turns
         return pl.pallas_call(
-            functools.partial(group_kernel, z, turns, raw, len(used_tails), len(written)),
+            functools.partial(group_kernel, z, turns, raw, body, len(used_tails), len(written)),
             out_shape=[shape(resp_q.shape, BF16), shape(resp_kv.shape, BF16)]
             + [shape(x, BF16) for x in grads_shapes],
             in_specs=[ANYWHERE] * len(operands),
@@ -497,12 +536,12 @@
             name="raw_grads" if raw else "group_grads",
         )(*operands)
 
-    *written, per_resp = grads_of((0,), True, ())
+    *written, per_resp = grads_of((0,), True, (), (1, z.kv_heads))
     onward, per_resp, far_rewards = lax.optimization_barrier((payloads[2], per_resp, far_rewards))
     payloads[FAR] = swap(onward, 1)
-    *written, for_2, for_1 = grads_of((2, 1), False, written)
+    *written, for_2, for_1 = grads_of((2, 1), False, written, (slots // PAIR, z.kv_heads))
     come = [swap(for_2, 2)]
-    *written, for_far = grads_of((FAR,), False, written)
+    *written, for_far = grads_of((FAR,), False, written, (1, 1))
     for_far, for_1 = lax.optimization_barrier((for_far, for_1))
     last = [swap(for_far, FAR), swap(for_1, 1)]
     operands = [*small, far_rewards, *tails, per_resp, *come, *written]
@@ -588,9 +627,10 @@
             grads[slot, 0, :, cols] = key_grad.astype(BF16)
             grads[slot, 1, :, cols] = value_grad.astype(BF16)
 
-        attend_pair(
-            z, [token_rows(z, slot)], [slot], q, og, kv, prefix.at[slot], [lens[slot]], [factors[slot]], out, own, sink, True
-        )
+        units = [
+            Unit([token_rows(z, slot)], [slot], k, [lens[slot]], [factors[slot]]) for k in range(z.kv_heads)
+        ]
+        attend(z, units, q, og, kv, prefix.at[slot], out, own, sink, True)
         for copy in copies_out(slot):
             copy.start()
         return 0

time: 38.8 us -> 39.5 us (1.018)
  Pallas kernels: 21.8 us -> 22.5 us
    pallas_call x3, Pallas kernels: 17.4 us -> 18.1 us  [grads_of(): pl.pallas_call(functools.partial(group_kernel, z, turns, raw, body, len(u...]
  transfers between devices with their start and end apart: 7 -> 7, of which waited for: 2 -> 2; matrix products, arithmetic and copies ran while one was open for 0% -> 0% of each run, Pallas kernels for 52% -> 53%
where the time goes in v9:
time: 39.5 us; the launch traced here: 39.2 us
  Pallas kernels  22.5 us (57%)
  starting transfers between devices  11.2 us (28%)
  waiting for transfers between devices  4.01 us (10%)
  between operations  0.74 us (2%)
  other arithmetic  0.7 us (2%)
    pallas_call x3, Pallas kernels, grads_of(): pl.pallas_call(functools.partial(group_kernel, z, turns, raw, body, len(u...  18.1 us
    ppermute x7, starting transfers between devices, swap(): return lax.ppermute(x, 'dp', [(i, i ^ s) for i in range(n_dp)])  11.2 us
    ppermute x7, waiting for transfers between devices, swap(): return lax.ppermute(x, 'dp', [(i, i ^ s) for i in range(n_dp)])  4.01 us
    pallas_call x1, Pallas kernels, near_shards(): pl.pallas_call(functools.partial(finish_kernel, z, len(tails), len(come))...  2.83 us
    pallas_call x1, Pallas kernels, near_shards(): pl.pallas_call(functools.partial(pack_kernel, z), out_shape=jax.ShapeDtyp...  1.57 us
  transfers between devices with their start and end apart: 7, of which 2 were waited for; matrix products, arithmetic and copies ran while one was open for 0% of the time, Pallas kernels for 53%

profile of v9, /device:TPU:0, one launch (start us, length us, event | category | flops | bytes accessed | tf_op | source)
XLA Modules:
  0.0 39.2 jit_solution(13044252727756243604)
XLA Ops:
  0.6 1.6 %pack.1.refs_7_.refs_4_ = bf16[272,256]{1,0:T(8,128)(2,1)} custom-call(bf16[2,128,256]{2,1,0:T(8,128)(2,1)} %prompt_hbm.1, f32[16]{0:T(128)} %refs_2_.7, s32[64]{0:T(128)} %refs_0_.7), custom_call_target="tpu_custom_call" | custom-call | tf_op jit(solution)/shard_map/pack/pallas_call | solution.py:472
  2.2 0.0 copy-start
  2.2 0.0 copy-start.2
  2.2 0.0 copy-start.3
  2.2 0.0 copy-start.4
  2.3 4.1 %collective-permute-start = (bf16[272,256]{1,0:T(8,128)(2,1)}, bf16[272,256]{1,0:T(8,128)(2,1)S(1)}, u32[]{:S(2)}, u32[]{:S(2)}) collective-permute-start(bf16[272,256]{1,0:T(8,128)(2,1)} %pack.1.refs_7_.refs_4_), channel_id=1, source_target_pairs={{0,8},{4,12},{8,0},{12,4},{1,9},{5,13},{9,1},{13,5},{2,10},{6,14},... | collective-permute-start | bytes 417800 | tf_op jit(solution)/shard_map/ppermute | solution.py:490
  6.4 1.3 %collective-permute-start.1 = (f32[16]{0:T(128)}, f32[16]{0:T(128)S(1)}, u32[]{:S(2)}, u32[]{:S(2)}) collective-permute-start(f32[16]{0:T(128)} %refs_2_.7), channel_id=1, source_target_pairs={{0,12},{4,8},{8,4},{12,0},{1,13},{5,9},{9,5},{13,1},{2,14},{6,10},... | collective-permute-start | bytes 200 | tf_op jit(solution)/shard_map/ppermute | solution.py:490
  7.7 0.2 collective-permute-start.2
  7.9 5.2 %raw_grads.1 = (bf16[1024,1280]{1,0:T(8,128)(2,1)}, bf16[2,1024,256]{2,1,0:T(8,128)(2,1)}, bf16[4,2,128,256]{3,2,1,0:T(8,128)(2,1)}) custom-call(s32[64]{0:T(128)} %refs_0_.7, s32[16]{0:T(128)} %refs_1_.7, f32[16]{0:T(128)} %refs_2_.7, f32[16]{0:T(128)} %refs_2_.7, bf16[1024,1280]{1,0:T(8,128)(2,1)} %refs_4_.5, bf16[1024,1280]{1,0:T(8,128)(2,1)} %refs_5_.5, ...), custom_call_target="tpu_custom_call" | custom-call | tf_op jit(solution)/shard_map/raw_grads/pallas_call | solution.py:506
  13.1 0.0 collective-permute-done.1.refs_3_
  13.1 0.2 collective-permute-done.refs_9_.refs_10_.refs_6_
  13.3 1.7 %collective-permute-start.4 = (bf16[272,256]{1,0:T(8,128)(2,1)S(1)}, bf16[272,256]{1,0:T(8,128)(2,1)S(1)}, u32[]{:S(2)}, u32[]{:S(2)}) collective-permute-start(bf16[272,256]{1,0:T(8,128)(2,1)S(1)} %collective-permute-done.refs_9_.refs_10_.refs_6_), channel_id=1, source_target_pairs={{0,4},{4,0},{8,12},{12,8},{1,5},{5,1},{9,13},{13,9},{2,6},{6,2},{1... | collective-permute-start | bytes 417800 | tf_op jit(solution)/shard_map/ppermute | solution.py:490
  15.0 0.0 collective-permute-done.2.refs_8_.refs_11_.refs_5_
  15.0 0.0 copy-done
  15.0 0.0 copy-done.2
  15.0 0.0 copy-done.3
  15.0 0.0 copy-done.4
  15.1 7.1 %group_grads.2 = (bf16[1024,1280]{1,0:T(8,128)(2,1)}, bf16[2,1024,256]{2,1,0:T(8,128)(2,1)}, bf16[2,128,256]{2,1,0:T(8,128)(2,1)S(1)}, bf16[2,128,256]{2,1,0:T(8,128)(2,1)S(1)}) custom-call(s32[64]{0:T(128)S(1)} %copy-done.3, s32[16]{0:T(128)S(1)} %copy-done.4, f32[16]{0:T(128)S(1)} %copy-done.2, ...), custom_call_target="tpu_custom_call", output_to_operand_aliasing={{0}: (12, {}), {1}: (13, {})} | custom-call | tf_op jit(solution)/shard_map/group_grads/pallas_call | solution.py:506
  22.1 2.5 %collective-permute-start.3 = (bf16[2,128,256]{2,1,0:T(8,128)(2,1)S(1)}, bf16[2,128,256]{2,1,0:T(8,128)(2,1)S(1)}, u32[]{:S(2)}, u32[]{:S(2)}) collective-permute-start(bf16[2,128,256]{2,1,0:T(8,128)(2,1)S(1)} %get-tuple-element.26), channel_id=1, source_target_pairs={{0,8},{4,12},{8,0},{12,4},{1,9},{5,13},{9,1},{13,5},{2,10},{6,14},... | collective-permute-start | bytes 393224 | tf_op jit(solution)/shard_map/ppermute | solution.py:490
  24.6 0.0 collective-permute-done.4.refs_10_
  24.6 0.0 copy-start.1
  24.6 5.8 %group_grads.3 = (bf16[1024,1280]{1,0:T(8,128)(2,1)}, bf16[2,1024,256]{2,1,0:T(8,128)(2,1)}, bf16[2,128,256]{2,1,0:T(8,128)(2,1)S(1)}) custom-call(s32[64]{0:T(128)S(1)} %copy-done.3, s32[16]{0:T(128)S(1)} %copy-done.4, f32[16]{0:T(128)S(1)} %copy-done.2, f32[16]{0:T(128)S(1)} %collective-permute-done.1.refs_3_, ...), custom_call_target="tpu_custom_call", output_to_operand_aliasing={{0}: (11, {}), {1}: (12, {})} | custom-call | tf_op jit(solution)/shard_map/group_grads/pallas_call | solution.py:506
  30.5 0.8 %collective-permute-start.5 = (bf16[2,128,256]{2,1,0:T(8,128)(2,1)S(1)}, bf16[2,128,256]{2,1,0:T(8,128)(2,1)S(1)}, u32[]{:S(2)}, u32[]{:S(2)}) collective-permute-start(bf16[2,128,256]{2,1,0:T(8,128)(2,1)S(1)} %get-tuple-element.37), channel_id=1, source_target_pairs={{0,12},{4,8},{8,4},{12,0},{1,13},{5,9},{9,5},{13,1},{2,14},{6,10},... | collective-permute-start | bytes 393224 | tf_op jit(solution)/shard_map/ppermute | solution.py:490
  31.2 0.6 %collective-permute-start.6 = (bf16[2,128,256]{2,1,0:T(8,128)(2,1)S(1)}, bf16[2,128,256]{2,1,0:T(8,128)(2,1)S(1)}, u32[]{:S(2)}, u32[]{:S(2)}) collective-permute-start(bf16[2,128,256]{2,1,0:T(8,128)(2,1)S(1)} %get-tuple-element.38), channel_id=1, source_target_pairs={{0,4},{4,0},{8,12},{12,8},{1,5},{5,1},{9,13},{13,9},{2,6},{6,2},{1... | collective-permute-start | bytes 393224 | tf_op jit(solution)/shard_map/ppermute | solution.py:490
  31.8 0.0 collective-permute-done.3.refs_8_
  31.8 0.0 copy-done.1
  31.9 2.8 %finish_own.1 = (bf16[1024,1280]{1,0:T(8,128)(2,1)}, bf16[2,1024,256]{2,1,0:T(8,128)(2,1)}, f32[2,128,256]{2,1,0:T(8,128)S(1)}) custom-call(s32[64]{0:T(128)S(1)} %copy-done.3, s32[16]{0:T(128)S(1)} %copy-done.4, f32[16]{0:T(128)S(1)} %copy-done.2, f32[16]{0:T(128)S(1)} %collective-permute-done.1.refs_3_, ...), custom_call_target="tpu_custom_call", output_to_operand_aliasing={{0}: (9, {}), {1}: (10, {})} | custom-call | tf_op jit(solution)/shard_map/finish_own/pallas_call | solution.py:548
  34.7 3.8 %collective-permute-done.5 = bf16[2,128,256]{2,1,0:T(8,128)(2,1)S(1)} collective-permute-done((bf16[2,128,256]{2,1,0:T(8,128)(2,1)S(1)}, bf16[2,128,256]{2,1,0:T(8,128)(2,1)S(1)}, u32[]{:S(2)}, u32[]{:S(2)}) %collective-permute-start.5) | collective-permute-done | bytes 131104 | tf_op jit(solution)/shard_map/ppermute | solution.py:490
  38.5 0.0 collective-permute-done.6
  38.5 0.7 %add_convert_fusion = bf16[2,128,256]{2,1,0:T(8,128)(2,1)} fusion(f32[2,128,256]{2,1,0:T(8,128)S(1)} %get-tuple-element.34, bf16[2,128,256]{2,1,0:T(8,128)(2,1)S(1)} %collective-permute-done.6, bf16[2,128,256]{2,1,0:T(8,128)(2,1)S(1)} %collective-permute-done.5), kind=kLoop, calls=%fused_computation | loop fusion | flops 327680 | bytes 655360 | tf_op jit(solution)/shard_map/convert_element_type | solution.py:573
Async XLA Ops:
  2.2 12.8 %copy-start = (bf16[272,256]{1,0:T(8,128)(2,1)S(1)}, bf16[272,256]{1,0:T(8,128)(2,1)}, u32[]{:S(2)}) copy-start(bf16[272,256]{1,0:T(8,128)(2,1)} %pack.1.refs_7_.refs_4_) | copy-start | bytes 417796
  2.2 12.8 %copy-start.2 = (f32[16]{0:T(128)S(1)}, f32[16]{0:T(128)}, u32[]{:S(2)}) copy-start(f32[16]{0:T(128)} %refs_2_.7) | copy-start | bytes 196
  2.2 12.8 %copy-start.3 = (s32[64]{0:T(128)S(1)}, s32[64]{0:T(128)}, u32[]{:S(2)}) copy-start(s32[64]{0:T(128)} %refs_0_.7) | copy-start | bytes 772
  2.2 12.8 %copy-start.4 = (s32[16]{0:T(128)S(1)}, s32[16]{0:T(128)}, u32[]{:S(2)}) copy-start(s32[16]{0:T(128)} %refs_1_.7) | copy-start | bytes 196
  2.3 11.1 %collective-permute-start = (bf16[272,256]{1,0:T(8,128)(2,1)}, bf16[272,256]{1,0:T(8,128)(2,1)S(1)}, u32[]{:S(2)}, u32[]{:S(2)}) collective-permute-start(bf16[272,256]{1,0:T(8,128)(2,1)} %pack.1.refs_7_.refs_4_), channel_id=1, source_target_pairs={{0,8},{4,12},{8,0},{12,4},{1,9},{5,13},{9,1},{13,5},{2,10},{6,14},... | collective-permute-start | bytes 417800 | tf_op jit(solution)/shard_map/ppermute | solution.py:490
  6.4 6.8 %collective-permute-start.1 = (f32[16]{0:T(128)}, f32[16]{0:T(128)S(1)}, u32[]{:S(2)}, u32[]{:S(2)}) collective-permute-start(f32[16]{0:T(128)} %refs_2_.7), channel_id=1, source_target_pairs={{0,12},{4,8},{8,4},{12,0},{1,13},{5,9},{9,5},{13,1},{2,14},{6,10},... | collective-permute-start | bytes 200 | tf_op jit(solution)/shard_map/ppermute | solution.py:490
  7.7 7.3 %collective-permute-start.2 = (bf16[272,256]{1,0:T(8,128)(2,1)}, bf16[272,256]{1,0:T(8,128)(2,1)S(1)}, u32[]{:S(2)}, u32[]{:S(2)}) collective-permute-start(bf16[272,256]{1,0:T(8,128)(2,1)} %pack.1.refs_7_.refs_4_), channel_id=1, source_target_pairs={{0,4},{4,0},{8,12},{12,8},{1,5},{5,1},{9,13},{13,9},{2,6},{6,2},{1... | collective-permute-start | bytes 417800 | tf_op jit(solution)/shard_map/ppermute | solution.py:490
  13.3 11.3 %collective-permute-start.4 = (bf16[272,256]{1,0:T(8,128)(2,1)S(1)}, bf16[272,256]{1,0:T(8,128)(2,1)S(1)}, u32[]{:S(2)}, u32[]{:S(2)}) collective-permute-start(bf16[272,256]{1,0:T(8,128)(2,1)S(1)} %collective-permute-done.refs_9_.refs_10_.refs_6_), channel_id=1, source_target_pairs={{0,4},{4,0},{8,12},{12,8},{1,5},{5,1},{9,13},{13,9},{2,6},{6,2},{1... | collective-permute-start | bytes 417800 | tf_op jit(solution)/shard_map/ppermute | solution.py:490
  22.1 9.7 %collective-permute-start.3 = (bf16[2,128,256]{2,1,0:T(8,128)(2,1)S(1)}, bf16[2,128,256]{2,1,0:T(8,128)(2,1)S(1)}, u32[]{:S(2)}, u32[]{:S(2)}) collective-permute-start(bf16[2,128,256]{2,1,0:T(8,128)(2,1)S(1)} %get-tuple-element.26), channel_id=1, source_target_pairs={{0,8},{4,12},{8,0},{12,4},{1,9},{5,13},{9,1},{13,5},{2,10},{6,14},... | collective-permute-start | bytes 393224 | tf_op jit(solution)/shard_map/ppermute | solution.py:490
  24.6 7.2 %copy-start.1 = (bf16[4,2,128,256]{3,2,1,0:T(8,128)(2,1)S(1)}, bf16[4,2,128,256]{3,2,1,0:T(8,128)(2,1)}, u32[]{:S(2)}) copy-start(bf16[4,2,128,256]{3,2,1,0:T(8,128)(2,1)} %get-tuple-element.23.refs_7_) | copy-start | bytes 1572868
  30.5 8.1 %collective-permute-start.5 = (bf16[2,128,256]{2,1,0:T(8,128)(2,1)S(1)}, bf16[2,128,256]{2,1,0:T(8,128)(2,1)S(1)}, u32[]{:S(2)}, u32[]{:S(2)}) collective-permute-start(bf16[2,128,256]{2,1,0:T(8,128)(2,1)S(1)} %get-tuple-element.37), channel_id=1, source_target_pairs={{0,12},{4,8},{8,4},{12,0},{1,13},{5,9},{9,5},{13,1},{2,14},{6,10},... | collective-permute-start | bytes 393224 | tf_op jit(solution)/shard_map/ppermute | solution.py:490
  31.2 7.3 %collective-permute-start.6 = (bf16[2,128,256]{2,1,0:T(8,128)(2,1)S(1)}, bf16[2,128,256]{2,1,0:T(8,128)(2,1)S(1)}, u32[]{:S(2)}, u32[]{:S(2)}) collective-permute-start(bf16[2,128,256]{2,1,0:T(8,128)(2,1)S(1)} %get-tuple-element.38), channel_id=1, source_target_pairs={{0,4},{4,0},{8,12},{12,8},{1,5},{5,1},{9,13},{13,9},{2,6},{6,2},{1... | collective-permute-start | bytes 393224 | tf_op jit(solution)/shard_map/ppermute | solution.py:490

commit v10 on v9

--- a/solution.py
+++ b/solution.py
@@ -293,15 +293,21 @@
     ]
 
 
-def group_kernel(z, turns, raw, body, n_tails, aliased, *refs):
+def group_kernel(z, turns, raw, body, ahead, n_tails, aliased, *refs):
     small_hbm, given = refs[:4], refs[4:7]
     tail_hbm, prompts = refs[7 : 7 + n_tails], refs[7 + n_tails : 7 + n_tails + len(turns)]
-    refs = refs[7 + n_tails + len(turns) + aliased :]
-    (q_out, self_out), grads_out = refs[:2], refs[2 : 2 + len(turns)]
+    refs = refs[7 + n_tails + len(turns) :]
+    if raw:
+        (q_out, self_out), grads_out, in_order, refs = refs[:2], refs[2:3], refs[3:5], refs[5:]
+    else:
+        in_order, refs = refs[:2], refs[2 + aliased :]
+        (q_out, self_out), grads_out, refs = refs[:2], refs[2 : 2 + len(turns)], refs[2 + len(turns) :]
+    in_order = (in_order[0].at[0], in_order[0].at[1], in_order[1])
     (resp_prompt, resp_len, rewards, far_rewards, order, lens, factors, q, og, kv, prefix, tails, acc, out, own, grads,
-     sem_small, sem_tails, sem_prefix, sem_in, sem_out, sem_grads) = refs[2 + len(turns) :]
+     sem_small, sem_tails, sem_prefix, sem_in, sem_out, sem_grads, sem_order) = refs
     me = lax.axis_index("dp")
     n_slots = len(turns) * z.slots
+    span = z.slots * z.tokens
 
     small = [
         pltpu.make_async_copy(src, dst, sem_small.at[n])
@@ -315,10 +321,14 @@
         for n in range(2)
     ]
     late = tail_copies(z, tail_hbm, tails, sem_tails)
-    for copy in small + prefix_copies + late:
+    first_rows = []
+    if not raw:
+        first_rows = row_copies(in_order, (q, og, kv), pl.ds(ahead * span, span), pl.ds(0, span), sem_order.at[0])
+    for copy in [*small, *first_rows, *prefix_copies, *late]:
         copy.start()
     small[0].wait()
-    find_responses(z, me, turns, resp_prompt, order)
+    ordered = [*turns, *ahead] if raw else turns
+    find_responses(z, me, ordered, resp_prompt, order)
 
     def copies_in(slot):
         return row_copies(
@@ -328,7 +338,11 @@
     def copies_out(slot):
         return result_copies(out, own, q_out, self_out, slot, token_rows(z, order[slot]), sem_out)
 
-    for slot in range(n_slots):
+    def copies_ordered(slot):
+        rows = token_rows(z, slot - n_slots)
+        return row_copies((q, og, kv), in_order, token_rows(z, slot), rows, sem_order.at[slot - n_slots])
+
+    for slot in range(0 if raw else z.slots, len(ordered) * z.slots):
         for copy in copies_in(slot):
             copy.start()
     for copy in small[1:] + late:
@@ -344,27 +358,30 @@
     for copy in prefix_copies:
         copy.wait()
 
-    pairs_per_turn = z.slots // PAIR
-    pairs_in_body, heads_in_body = body
-    head_steps = z.kv_heads // heads_in_body
-    pair_steps = pairs_per_turn // pairs_in_body
+    pairs_in_body = body
+    steps_per_turn = z.slots // PAIR // pairs_in_body
 
     def step(u, _):
-        k_step = lax.rem(u, head_steps) if head_steps > 1 else 0
-        pair_step = u // head_steps
-        t = pair_step // pair_steps
-        first = pair_step * pairs_in_body * PAIR
+        t = u // steps_per_turn
+        first = u * pairs_in_body * PAIR
         mine = range(pairs_in_body * PAIR)
 
-        def moves(starting):
+        def wait_for_slots():
             for n in mine:
-                for copy in copies_out(first + n) if starting else copies_in(first + n):
-                    copy.start() if starting else copy.wait()
-
-        if head_steps > 1:
-            pl.when(k_step == 0)(lambda: moves(False))
+                for copy in copies_in(first + n):
+                    copy.wait()
+
+        if raw:
+            wait_for_slots()
         else:
-            moves(False)
+
+            @pl.when(u == 0)
+            def _():
+                for copy in first_rows:
+                    copy.wait()
+
+            if len(turns) > 1:
+                pl.when(u >= steps_per_turn)(wait_for_slots)
 
         def sink(place, cols, key_grad, value_grad):
             if raw:
@@ -377,24 +394,29 @@
         units = []
         for pair in range(pairs_in_body):
             places = [first + pair * PAIR + n for n in range(PAIR)]
-            for k in range(heads_in_body):
-                units.append(
-                    Unit(
-                        [token_rows(z, n) for n in places],
-                        places,
-                        k_step * heads_in_body + k if head_steps > 1 else k,
-                        [lens[n] for n in places],
-                        [factors[n] for n in places],
-                    )
-                )
+            at = [token_rows(z, n) for n in places]
+            for k in range(z.kv_heads):
+                units.append(Unit(at, places, k, [lens[n] for n in places], [factors[n] for n in places]))
         attend(z, units, q, og, kv, prefix.at[t], out, own, sink, raw)
-        if head_steps > 1:
-            pl.when(k_step == head_steps - 1)(lambda: moves(True))
-        else:
-            moves(True)
+        for n in mine:
+            for copy in copies_out(first + n):
+                copy.start()
+        if raw:
+
+            @pl.when(u == 0)
+            def _():
+                def pass_on(slot, _):
+                    for copy in copies_in(slot):
+                        copy.wait()
+                    for copy in copies_ordered(slot):
+                        copy.start()
+                    return 0
+
+                lax.fori_loop(n_slots, len(ordered) * z.slots, pass_on, 0)
+
         return 0
 
-    lax.fori_loop(0, len(turns) * pair_steps * head_steps, step, 0)
+    lax.fori_loop(0, len(turns) * steps_per_turn, step, 0)
     if raw:
         last = [pltpu.make_async_copy(grads, grads_out[0], sem_grads.at[0])]
     else:
@@ -407,6 +429,10 @@
     for slot in range(n_slots):
         for copy in copies_out(slot):
             copy.wait()
+    if raw:
+        for slot in range(n_slots, len(ordered) * z.slots):
+            for copy in copies_ordered(slot):
+                copy.wait()
     for copy in last:
         copy.wait()
 
@@ -496,28 +522,31 @@
     smem = [pltpu.SMEM(x.shape, x.dtype) for x in (*small, rewards)]
     slots = z.slots
 
-    def grads_of(turns, raw, written, body):
+    def grads_of(turns, raw, body, ahead, in_order=(), written=()):
         n_slots, n_turns = len(turns) * slots, len(turns)
+        n_ahead = len(ahead) * slots if raw else 0
+        n_held = n_slots + n_ahead
         used_tails = [] if raw else tails
         used_small = (*small, rewards if raw else far_rewards)
         prompts = [payloads[turn] for turn in turns]
-        operands = [*used_small, resp_q, out_grad, resp_kv, *used_tails, *prompts, *written]
+        operands = [*used_small, resp_q, out_grad, resp_kv, *used_tails, *prompts, *in_order, *written]
         grads_shapes = [(slots,) + one] if raw else [one] * n_turns
+        ordered_shapes = [(2, n_ahead * z.tokens, z.lanes), (2, n_ahead * z.tokens, z.width)] if raw else []
         return pl.pallas_call(
-            functools.partial(group_kernel, z, turns, raw, body, len(used_tails), len(written)),
+            functools.partial(group_kernel, z, turns, raw, body, ahead, len(used_tails), len(written)),
             out_shape=[shape(resp_q.shape, BF16), shape(resp_kv.shape, BF16)]
-            + [shape(x, BF16) for x in grads_shapes],
+            + [shape(x, BF16) for x in grads_shapes + ordered_shapes],
             in_specs=[ANYWHERE] * len(operands),
-            out_specs=[ANYWHERE] * (2 + len(grads_shapes)),
+            out_specs=[ANYWHERE] * (2 + len(grads_shapes) + len(ordered_shapes)),
             input_output_aliases={len(operands) - 2: 0, len(operands) - 1: 1} if written else {},
             scratch_shapes=[
                 *smem,
-                pltpu.SMEM((n_slots + 1,), jnp.int32),
+                pltpu.SMEM((n_held + 1,), jnp.int32),
                 pltpu.SMEM((n_slots,), jnp.int32),
                 pltpu.SMEM((n_slots,), F32),
-                pltpu.VMEM((n_slots * z.tokens, z.lanes), BF16),
-                pltpu.VMEM((n_slots * z.tokens, z.lanes), BF16),
-                pltpu.VMEM((2, n_slots * z.tokens, z.width), BF16),
+                pltpu.VMEM((n_held * z.tokens, z.lanes), BF16),
+                pltpu.VMEM((n_held * z.tokens, z.lanes), BF16),
+                pltpu.VMEM((2, n_held * z.tokens, z.width), BF16),
                 pltpu.VMEM((n_turns,) + one, BF16),
                 pltpu.VMEM((FAR, TAIL, z.width), BF16),
                 pltpu.VMEM((n_turns,) + one, F32),
@@ -527,21 +556,23 @@
                 pltpu.SemaphoreType.DMA((len(smem),)),
                 pltpu.SemaphoreType.DMA((FAR,)),
                 pltpu.SemaphoreType.DMA((n_turns, 2)),
-                pltpu.SemaphoreType.DMA((n_slots, 4)),
-                pltpu.SemaphoreType.DMA((n_slots, 3)),
+                pltpu.SemaphoreType.DMA((n_held, 3)),
+                pltpu.SemaphoreType.DMA((n_slots, 2)),
                 pltpu.SemaphoreType.DMA((n_turns,)),
+                pltpu.SemaphoreType.DMA((max(n_ahead, 1), 3)),
             ],
             compiler_params=params if raw else pltpu.CompilerParams(vmem_limit_bytes=GROUP_BYTES),
             cost_estimate=cost,
             name="raw_grads" if raw else "group_grads",
         )(*operands)
 
-    *written, per_resp = grads_of((0,), True, (), (1, z.kv_heads))
+    *written, per_resp, rows_ahead, kv_ahead = grads_of((0,), True, 1, (2, FAR))
+    in_order = (rows_ahead, kv_ahead)
     onward, per_resp, far_rewards = lax.optimization_barrier((payloads[2], per_resp, far_rewards))
     payloads[FAR] = swap(onward, 1)
-    *written, for_2, for_1 = grads_of((2, 1), False, written, (slots // PAIR, z.kv_heads))
+    *written, for_2, for_1 = grads_of((2, 1), False, slots // PAIR, 0, in_order, written)
     come = [swap(for_2, 2)]
-    *written, for_far = grads_of((FAR,), False, written, (1, 1))
+    *written, for_far = grads_of((FAR,), False, slots // PAIR, 1, in_order, written)
     for_far, for_1 = lax.optimization_barrier((for_far, for_1))
     last = [swap(for_far, FAR), swap(for_1, 1)]
     operands = [*small, far_rewards, *tails, per_resp, *come, *written]

time: 39.5 us -> 37.2 us (0.942)
  Pallas kernels: 22.5 us -> 20.8 us
  waiting for transfers between devices: 4.01 us -> 3.48 us
    pallas_call x3, Pallas kernels: 18.1 us -> 16.5 us  [grads_of(): pl.pallas_call(functools.partial(group_kernel, z, turns, raw, body, ahead...]
    ppermute x7, waiting for transfers between devices: 4.01 us -> 3.48 us  [swap(): return lax.ppermute(x, 'dp', [(i, i ^ s) for i in range(n_dp)])]
  transfers between devices with their start and end apart: 7 -> 7, of which waited for: 2 -> 1; matrix products, arithmetic and copies ran while one was open for 0% -> 0% of each run, Pallas kernels for 53% -> 52%
where the time goes in v10:
time: 37.2 us; the launch traced here: 37 us
  Pallas kernels  20.8 us (56%)
  starting transfers between devices  11.2 us (30%)
  waiting for transfers between devices  3.48 us (9%)
  between operations  0.74 us (2%)
  other arithmetic  0.7 us (2%)
    pallas_call x3, Pallas kernels, grads_of(): pl.pallas_call(functools.partial(group_kernel, z, turns, raw, body, ahead...  16.5 us
    ppermute x7, starting transfers between devices, swap(): return lax.ppermute(x, 'dp', [(i, i ^ s) for i in range(n_dp)])  11.2 us
    ppermute x7, waiting for transfers between devices, swap(): return lax.ppermute(x, 'dp', [(i, i ^ s) for i in range(n_dp)])  3.48 us
    pallas_call x1, Pallas kernels, near_shards(): pl.pallas_call(functools.partial(finish_kernel, z, len(tails), len(come))...  2.83 us
    pallas_call x1, Pallas kernels, near_shards(): pl.pallas_call(functools.partial(pack_kernel, z), out_shape=jax.ShapeDtyp...  1.56 us
  transfers between devices with their start and end apart: 7, of which 1 were waited for; matrix products, arithmetic and copies ran while one was open for 0% of the time, Pallas kernels for 52%

profile of v10, /device:TPU:0, one launch (start us, length us, event | category | flops | bytes accessed | tf_op | source)
XLA Modules:
  0.0 37.0 jit_solution(4727166414108672942)
XLA Ops:
  0.6 1.6 %pack.1.refs_7_.refs_4_ = bf16[272,256]{1,0:T(8,128)(2,1)} custom-call(bf16[2,128,256]{2,1,0:T(8,128)(2,1)} %prompt_hbm.1, f32[16]{0:T(128)} %refs_2_.7, s32[64]{0:T(128)} %refs_0_.7), custom_call_target="tpu_custom_call" | custom-call | tf_op jit(solution)/shard_map/pack/pallas_call | solution.py:498
  2.2 0.0 copy-start
  2.2 0.0 copy-start.2
  2.2 0.0 copy-start.3
  2.2 0.0 copy-start.4
  2.2 4.1 %collective-permute-start = (bf16[272,256]{1,0:T(8,128)(2,1)}, bf16[272,256]{1,0:T(8,128)(2,1)S(1)}, u32[]{:S(2)}, u32[]{:S(2)}) collective-permute-start(bf16[272,256]{1,0:T(8,128)(2,1)} %pack.1.refs_7_.refs_4_), channel_id=1, source_target_pairs={{0,8},{4,12},{8,0},{12,4},{1,9},{5,13},{9,1},{13,5},{2,10},{6,14},... | collective-permute-start | bytes 417800 | tf_op jit(solution)/shard_map/ppermute | solution.py:516
  6.3 1.3 %collective-permute-start.1 = (f32[16]{0:T(128)}, f32[16]{0:T(128)S(1)}, u32[]{:S(2)}, u32[]{:S(2)}) collective-permute-start(f32[16]{0:T(128)} %refs_2_.7), channel_id=1, source_target_pairs={{0,12},{4,8},{8,4},{12,0},{1,13},{5,9},{9,5},{13,1},{2,14},{6,10},... | collective-permute-start | bytes 200 | tf_op jit(solution)/shard_map/ppermute | solution.py:516
  7.7 0.2 collective-permute-start.2
  7.9 5.8 %raw_grads.1 = (bf16[1024,1280]{1,0:T(8,128)(2,1)}, bf16[2,1024,256]{2,1,0:T(8,128)(2,1)}, bf16[4,2,128,256]{3,2,1,0:T(8,128)(2,1)}, bf16[2,512,1280]{2,1,0:T(8,128)(2,1)}, bf16[2,512,256]{2,1,0:T(8,128)(2,1)}) custom-call(s32[64]{0:T(128)} %refs_0_.7, s32[16]{0:T(128)} %refs_1_.7, f32[16]{0:T(128)} %refs_2_.7, f32[16]{0:T(128)} %refs_2_.7, ...), custom_call_target="tpu_custom_call" | custom-call | tf_op jit(solution)/shard_map/raw_grads/pallas_call | solution.py:535
  13.8 0.0 collective-permute-done.1.refs_3_
  13.8 0.0 collective-permute-done.refs_9_.refs_10_.refs_6_
  13.8 1.9 %collective-permute-start.4 = (bf16[272,256]{1,0:T(8,128)(2,1)S(1)}, bf16[272,256]{1,0:T(8,128)(2,1)S(1)}, u32[]{:S(2)}, u32[]{:S(2)}) collective-permute-start(bf16[272,256]{1,0:T(8,128)(2,1)S(1)} %collective-permute-done.refs_9_.refs_10_.refs_6_), channel_id=1, source_target_pairs={{0,4},{4,0},{8,12},{12,8},{1,5},{5,1},{9,13},{13,9},{2,6},{6,2},{1... | collective-permute-start | bytes 417800 | tf_op jit(solution)/shard_map/ppermute | solution.py:516
  15.6 0.0 collective-permute-done.2.refs_8_.refs_11_.refs_5_
  15.7 0.0 copy-done
  15.7 0.0 copy-done.2
  15.7 0.0 copy-done.3
  15.7 0.0 copy-done.4
  15.7 6.3 %group_grads.2 = (bf16[1024,1280]{1,0:T(8,128)(2,1)}, bf16[2,1024,256]{2,1,0:T(8,128)(2,1)}, bf16[2,128,256]{2,1,0:T(8,128)(2,1)S(1)}, bf16[2,128,256]{2,1,0:T(8,128)(2,1)S(1)}) custom-call(s32[64]{0:T(128)S(1)} %copy-done.3, s32[16]{0:T(128)S(1)} %copy-done.4, f32[16]{0:T(128)S(1)} %copy-done.2, ...), custom_call_target="tpu_custom_call", output_to_operand_aliasing={{0}: (14, {}), {1}: (15, {})} | custom-call | tf_op jit(solution)/shard_map/group_grads/pallas_call | solution.py:535
  22.0 1.9 %collective-permute-start.3 = (bf16[2,128,256]{2,1,0:T(8,128)(2,1)S(1)}, bf16[2,128,256]{2,1,0:T(8,128)(2,1)S(1)}, u32[]{:S(2)}, u32[]{:S(2)}) collective-permute-start(bf16[2,128,256]{2,1,0:T(8,128)(2,1)S(1)} %get-tuple-element.30), channel_id=1, source_target_pairs={{0,8},{4,12},{8,0},{12,4},{1,9},{5,13},{9,1},{13,5},{2,10},{6,14},... | collective-permute-start | bytes 393224 | tf_op jit(solution)/shard_map/ppermute | solution.py:516
  23.8 0.0 collective-permute-done.4.refs_10_
  23.8 0.0 copy-start.1
  23.8 4.3 %group_grads.3 = (bf16[1024,1280]{1,0:T(8,128)(2,1)}, bf16[2,1024,256]{2,1,0:T(8,128)(2,1)}, bf16[2,128,256]{2,1,0:T(8,128)(2,1)S(1)}) custom-call(s32[64]{0:T(128)S(1)} %copy-done.3, s32[16]{0:T(128)S(1)} %copy-done.4, f32[16]{0:T(128)S(1)} %copy-done.2, f32[16]{0:T(128)S(1)} %collective-permute-done.1.refs_3_, ...), custom_call_target="tpu_custom_call", output_to_operand_aliasing={{0}: (13, {}), {1}: (14, {})} | custom-call | tf_op jit(solution)/shard_map/group_grads/pallas_call | solution.py:535
  28.2 0.9 %collective-permute-start.5 = (bf16[2,128,256]{2,1,0:T(8,128)(2,1)S(1)}, bf16[2,128,256]{2,1,0:T(8,128)(2,1)S(1)}, u32[]{:S(2)}, u32[]{:S(2)}) collective-permute-start(bf16[2,128,256]{2,1,0:T(8,128)(2,1)S(1)} %get-tuple-element.41), channel_id=1, source_target_pairs={{0,12},{4,8},{8,4},{12,0},{1,13},{5,9},{9,5},{13,1},{2,14},{6,10},... | collective-permute-start | bytes 393224 | tf_op jit(solution)/shard_map/ppermute | solution.py:516
  29.0 0.9 %collective-permute-start.6 = (bf16[2,128,256]{2,1,0:T(8,128)(2,1)S(1)}, bf16[2,128,256]{2,1,0:T(8,128)(2,1)S(1)}, u32[]{:S(2)}, u32[]{:S(2)}) collective-permute-start(bf16[2,128,256]{2,1,0:T(8,128)(2,1)S(1)} %get-tuple-element.42), channel_id=1, source_target_pairs={{0,4},{4,0},{8,12},{12,8},{1,5},{5,1},{9,13},{13,9},{2,6},{6,2},{1... | collective-permute-start | bytes 393224 | tf_op jit(solution)/shard_map/ppermute | solution.py:516
  29.9 0.0 collective-permute-done.3.refs_8_
  29.9 0.0 copy-done.1
  29.9 2.8 %finish_own.1 = (bf16[1024,1280]{1,0:T(8,128)(2,1)}, bf16[2,1024,256]{2,1,0:T(8,128)(2,1)}, f32[2,128,256]{2,1,0:T(8,128)S(1)}) custom-call(s32[64]{0:T(128)S(1)} %copy-done.3, s32[16]{0:T(128)S(1)} %copy-done.4, f32[16]{0:T(128)S(1)} %copy-done.2, f32[16]{0:T(128)S(1)} %collective-permute-done.1.refs_3_, ...), custom_call_target="tpu_custom_call", output_to_operand_aliasing={{0}: (9, {}), {1}: (10, {})} | custom-call | tf_op jit(solution)/shard_map/finish_own/pallas_call | solution.py:579
  32.8 3.5 %collective-permute-done.5 = bf16[2,128,256]{2,1,0:T(8,128)(2,1)S(1)} collective-permute-done((bf16[2,128,256]{2,1,0:T(8,128)(2,1)S(1)}, bf16[2,128,256]{2,1,0:T(8,128)(2,1)S(1)}, u32[]{:S(2)}, u32[]{:S(2)}) %collective-permute-start.5) | collective-permute-done | bytes 131104 | tf_op jit(solution)/shard_map/ppermute | solution.py:516
  36.3 0.0 collective-permute-done.6
  36.3 0.7 %add_convert_fusion = bf16[2,128,256]{2,1,0:T(8,128)(2,1)} fusion(f32[2,128,256]{2,1,0:T(8,128)S(1)} %get-tuple-element.38, bf16[2,128,256]{2,1,0:T(8,128)(2,1)S(1)} %collective-permute-done.6, bf16[2,128,256]{2,1,0:T(8,128)(2,1)S(1)} %collective-permute-done.5), kind=kLoop, calls=%fused_computation | loop fusion | flops 327680 | bytes 655360 | tf_op jit(solution)/shard_map/convert_element_type | solution.py:604
Async XLA Ops:
  2.2 13.5 %copy-start = (bf16[272,256]{1,0:T(8,128)(2,1)S(1)}, bf16[272,256]{1,0:T(8,128)(2,1)}, u32[]{:S(2)}) copy-start(bf16[272,256]{1,0:T(8,128)(2,1)} %pack.1.refs_7_.refs_4_) | copy-start | bytes 417796
  2.2 13.4 %copy-start.2 = (f32[16]{0:T(128)S(1)}, f32[16]{0:T(128)}, u32[]{:S(2)}) copy-start(f32[16]{0:T(128)} %refs_2_.7) | copy-start | bytes 196
  2.2 13.4 %copy-start.3 = (s32[64]{0:T(128)S(1)}, s32[64]{0:T(128)}, u32[]{:S(2)}) copy-start(s32[64]{0:T(128)} %refs_0_.7) | copy-start | bytes 772
  2.2 13.4 %copy-start.4 = (s32[16]{0:T(128)S(1)}, s32[16]{0:T(128)}, u32[]{:S(2)}) copy-start(s32[16]{0:T(128)} %refs_1_.7) | copy-start | bytes 196
  2.2 11.5 %collective-permute-start = (bf16[272,256]{1,0:T(8,128)(2,1)}, bf16[272,256]{1,0:T(8,128)(2,1)S(1)}, u32[]{:S(2)}, u32[]{:S(2)}) collective-permute-start(bf16[272,256]{1,0:T(8,128)(2,1)} %pack.1.refs_7_.refs_4_), channel_id=1, source_target_pairs={{0,8},{4,12},{8,0},{12,4},{1,9},{5,13},{9,1},{13,5},{2,10},{6,14},... | collective-permute-start | bytes 417800 | tf_op jit(solution)/shard_map/ppermute | solution.py:516
  6.3 7.4 %collective-permute-start.1 = (f32[16]{0:T(128)}, f32[16]{0:T(128)S(1)}, u32[]{:S(2)}, u32[]{:S(2)}) collective-permute-start(f32[16]{0:T(128)} %refs_2_.7), channel_id=1, source_target_pairs={{0,12},{4,8},{8,4},{12,0},{1,13},{5,9},{9,5},{13,1},{2,14},{6,10},... | collective-permute-start | bytes 200 | tf_op jit(solution)/shard_map/ppermute | solution.py:516
  7.7 8.0 %collective-permute-start.2 = (bf16[272,256]{1,0:T(8,128)(2,1)}, bf16[272,256]{1,0:T(8,128)(2,1)S(1)}, u32[]{:S(2)}, u32[]{:S(2)}) collective-permute-start(bf16[272,256]{1,0:T(8,128)(2,1)} %pack.1.refs_7_.refs_4_), channel_id=1, source_target_pairs={{0,4},{4,0},{8,12},{12,8},{1,5},{5,1},{9,13},{13,9},{2,6},{6,2},{1... | collective-permute-start | bytes 417800 | tf_op jit(solution)/shard_map/ppermute | solution.py:516
  13.8 10.0 %collective-permute-start.4 = (bf16[272,256]{1,0:T(8,128)(2,1)S(1)}, bf16[272,256]{1,0:T(8,128)(2,1)S(1)}, u32[]{:S(2)}, u32[]{:S(2)}) collective-permute-start(bf16[272,256]{1,0:T(8,128)(2,1)S(1)} %collective-permute-done.refs_9_.refs_10_.refs_6_), channel_id=1, source_target_pairs={{0,4},{4,0},{8,12},{12,8},{1,5},{5,1},{9,13},{13,9},{2,6},{6,2},{1... | collective-permute-start | bytes 417800 | tf_op jit(solution)/shard_map/ppermute | solution.py:516
  22.0 8.0 %collective-permute-start.3 = (bf16[2,128,256]{2,1,0:T(8,128)(2,1)S(1)}, bf16[2,128,256]{2,1,0:T(8,128)(2,1)S(1)}, u32[]{:S(2)}, u32[]{:S(2)}) collective-permute-start(bf16[2,128,256]{2,1,0:T(8,128)(2,1)S(1)} %get-tuple-element.30), channel_id=1, source_target_pairs={{0,8},{4,12},{8,0},{12,4},{1,9},{5,13},{9,1},{13,5},{2,10},{6,14},... | collective-permute-start | bytes 393224 | tf_op jit(solution)/shard_map/ppermute | solution.py:516
  23.8 6.1 %copy-start.1 = (bf16[4,2,128,256]{3,2,1,0:T(8,128)(2,1)S(1)}, bf16[4,2,128,256]{3,2,1,0:T(8,128)(2,1)}, u32[]{:S(2)}) copy-start(bf16[4,2,128,256]{3,2,1,0:T(8,128)(2,1)} %get-tuple-element.25.refs_7_) | copy-start | bytes 1572868
  28.2 8.1 %collective-permute-start.5 = (bf16[2,128,256]{2,1,0:T(8,128)(2,1)S(1)}, bf16[2,128,256]{2,1,0:T(8,128)(2,1)S(1)}, u32[]{:S(2)}, u32[]{:S(2)}) collective-permute-start(bf16[2,128,256]{2,1,0:T(8,128)(2,1)S(1)} %get-tuple-element.41), channel_id=1, source_target_pairs={{0,12},{4,8},{8,4},{12,0},{1,13},{5,9},{9,5},{13,1},{2,14},{6,10},... | collective-permute-start | bytes 393224 | tf_op jit(solution)/shard_map/ppermute | solution.py:516
  29.0 7.2 %collective-permute-start.6 = (bf16[2,128,256]{2,1,0:T(8,128)(2,1)S(1)}, bf16[2,128,256]{2,1,0:T(8,128)(2,1)S(1)}, u32[]{:S(2)}, u32[]{:S(2)}) collective-permute-start(bf16[2,128,256]{2,1,0:T(8,128)(2,1)S(1)} %get-tuple-element.42), channel_id=1, source_target_pairs={{0,4},{4,0},{8,12},{12,8},{1,5},{5,1},{9,13},{13,9},{2,6},{6,2},{1... | collective-permute-start | bytes 393224 | tf_op jit(solution)/shard_map/ppermute | solution.py:516

commit v11 on v10

--- a/solution.py
+++ b/solution.py
@@ -570,10 +570,9 @@
     in_order = (rows_ahead, kv_ahead)
     onward, per_resp, far_rewards = lax.optimization_barrier((payloads[2], per_resp, far_rewards))
     payloads[FAR] = swap(onward, 1)
-    *written, for_2, for_1 = grads_of((2, 1), False, slots // PAIR, 0, in_order, written)
+    *written, for_2 = grads_of((2,), False, slots // PAIR, 0, in_order, written)
     come = [swap(for_2, 2)]
-    *written, for_far = grads_of((FAR,), False, slots // PAIR, 1, in_order, written)
-    for_far, for_1 = lax.optimization_barrier((for_far, for_1))
+    *written, for_far, for_1 = grads_of((FAR, 1), False, slots // PAIR, 1, in_order, written)
     last = [swap(for_far, FAR), swap(for_1, 1)]
     operands = [*small, far_rewards, *tails, per_resp, *come, *written]
     q_out, self_out, own_grads = pl.pallas_call(

time: 37.2 us -> 37.2 us (level)
  no operation moved by 1% of the time
where the time goes in v11:
time: 37.2 us; the launch traced here: 37 us
  Pallas kernels  20.8 us (56%)
  starting transfers between devices  11.2 us (30%)
  waiting for transfers between devices  3.47 us (9%)
  between operations  0.74 us (2%)
  other arithmetic  0.7 us (2%)
    pallas_call x3, Pallas kernels, grads_of(): pl.pallas_call(functools.partial(group_kernel, z, turns, raw, body, ahead...  16.5 us
    ppermute x7, starting transfers between devices, swap(): return lax.ppermute(x, 'dp', [(i, i ^ s) for i in range(n_dp)])  11.2 us
    ppermute x7, waiting for transfers between devices, swap(): return lax.ppermute(x, 'dp', [(i, i ^ s) for i in range(n_dp)])  3.47 us
    pallas_call x1, Pallas kernels, near_shards(): pl.pallas_call(functools.partial(finish_kernel, z, len(tails), len(come))...  2.83 us
    pallas_call x1, Pallas kernels, near_shards(): pl.pallas_call(functools.partial(pack_kernel, z), out_shape=jax.ShapeDtyp...  1.56 us
  transfers between devices with their start and end apart: 7, of which 1 were waited for; matrix products, arithmetic and copies ran while one was open for 0% of the time, Pallas kernels for 52%

profile of v11, /device:TPU:0, one launch (start us, length us, event | category | flops | bytes accessed | tf_op | source)
XLA Modules:
  0.0 37.0 jit_solution(1938099000552628217)
XLA Ops:
  0.6 1.6 %pack.1.refs_7_.refs_4_ = bf16[272,256]{1,0:T(8,128)(2,1)} custom-call(bf16[2,128,256]{2,1,0:T(8,128)(2,1)} %prompt_hbm.1, f32[16]{0:T(128)} %refs_2_.7, s32[64]{0:T(128)} %refs_0_.7), custom_call_target="tpu_custom_call" | custom-call | tf_op jit(solution)/shard_map/pack/pallas_call | solution.py:498
  2.2 0.0 copy-start
  2.2 0.0 copy-start.2
  2.2 0.0 copy-start.3
  2.2 0.0 copy-start.4
  2.2 4.1 %collective-permute-start = (bf16[272,256]{1,0:T(8,128)(2,1)}, bf16[272,256]{1,0:T(8,128)(2,1)S(1)}, u32[]{:S(2)}, u32[]{:S(2)}) collective-permute-start(bf16[272,256]{1,0:T(8,128)(2,1)} %pack.1.refs_7_.refs_4_), channel_id=1, source_target_pairs={{0,8},{4,12},{8,0},{12,4},{1,9},{5,13},{9,1},{13,5},{2,10},{6,14},... | collective-permute-start | bytes 417800 | tf_op jit(solution)/shard_map/ppermute | solution.py:516
  6.3 1.3 %collective-permute-start.1 = (f32[16]{0:T(128)}, f32[16]{0:T(128)S(1)}, u32[]{:S(2)}, u32[]{:S(2)}) collective-permute-start(f32[16]{0:T(128)} %refs_2_.7), channel_id=1, source_target_pairs={{0,12},{4,8},{8,4},{12,0},{1,13},{5,9},{9,5},{13,1},{2,14},{6,10},... | collective-permute-start | bytes 200 | tf_op jit(solution)/shard_map/ppermute | solution.py:516
  7.7 0.2 collective-permute-start.2
  7.9 5.8 %raw_grads.1 = (bf16[1024,1280]{1,0:T(8,128)(2,1)}, bf16[2,1024,256]{2,1,0:T(8,128)(2,1)}, bf16[4,2,128,256]{3,2,1,0:T(8,128)(2,1)}, bf16[2,512,1280]{2,1,0:T(8,128)(2,1)}, bf16[2,512,256]{2,1,0:T(8,128)(2,1)}) custom-call(s32[64]{0:T(128)} %refs_0_.7, s32[16]{0:T(128)} %refs_1_.7, f32[16]{0:T(128)} %refs_2_.7, f32[16]{0:T(128)} %refs_2_.7, ...), custom_call_target="tpu_custom_call" | custom-call | tf_op jit(solution)/shard_map/raw_grads/pallas_call | solution.py:535
  13.8 0.0 collective-permute-done.1.refs_3_
  13.8 0.0 collective-permute-done.refs_9_.refs_10_.refs_6_
  13.8 1.9 %collective-permute-start.4 = (bf16[272,256]{1,0:T(8,128)(2,1)S(1)}, bf16[272,256]{1,0:T(8,128)(2,1)S(1)}, u32[]{:S(2)}, u32[]{:S(2)}) collective-permute-start(bf16[272,256]{1,0:T(8,128)(2,1)S(1)} %collective-permute-done.refs_9_.refs_10_.refs_6_), channel_id=1, source_target_pairs={{0,4},{4,0},{8,12},{12,8},{1,5},{5,1},{9,13},{13,9},{2,6},{6,2},{1... | collective-permute-start | bytes 417800 | tf_op jit(solution)/shard_map/ppermute | solution.py:516
  15.6 0.0 collective-permute-done.2.refs_8_.refs_11_.refs_5_
  15.7 0.0 copy-done
  15.7 0.0 copy-done.2
  15.7 0.0 copy-done.3
  15.7 0.0 copy-done.4
  15.7 4.3 %group_grads.2 = (bf16[1024,1280]{1,0:T(8,128)(2,1)}, bf16[2,1024,256]{2,1,0:T(8,128)(2,1)}, bf16[2,128,256]{2,1,0:T(8,128)(2,1)S(1)}) custom-call(s32[64]{0:T(128)S(1)} %copy-done.3, s32[16]{0:T(128)S(1)} %copy-done.4, f32[16]{0:T(128)S(1)} %copy-done.2, f32[16]{0:T(128)S(1)} %collective-permute-done.1.refs_3_, ...), custom_call_target="tpu_custom_call", output_to_operand_aliasing={{0}: (13, {}), {1}: (14, {})} | custom-call | tf_op jit(solution)/shard_map/group_grads/pallas_call | solution.py:535
  20.0 1.8 %collective-permute-start.3 = (bf16[2,128,256]{2,1,0:T(8,128)(2,1)S(1)}, bf16[2,128,256]{2,1,0:T(8,128)(2,1)S(1)}, u32[]{:S(2)}, u32[]{:S(2)}) collective-permute-start(bf16[2,128,256]{2,1,0:T(8,128)(2,1)S(1)} %get-tuple-element.28), channel_id=1, source_target_pairs={{0,8},{4,12},{8,0},{12,4},{1,9},{5,13},{9,1},{13,5},{2,10},{6,14},... | collective-permute-start | bytes 393224 | tf_op jit(solution)/shard_map/ppermute | solution.py:516
  21.8 0.0 collective-permute-done.4.refs_10_
  21.8 0.0 copy-start.1
  21.8 6.3 %group_grads.3 = (bf16[1024,1280]{1,0:T(8,128)(2,1)}, bf16[2,1024,256]{2,1,0:T(8,128)(2,1)}, bf16[2,128,256]{2,1,0:T(8,128)(2,1)S(1)}, bf16[2,128,256]{2,1,0:T(8,128)(2,1)S(1)}) custom-call(s32[64]{0:T(128)S(1)} %copy-done.3, s32[16]{0:T(128)S(1)} %copy-done.4, f32[16]{0:T(128)S(1)} %copy-done.2, ...), custom_call_target="tpu_custom_call", output_to_operand_aliasing={{0}: (14, {}), {1}: (15, {})} | custom-call | tf_op jit(solution)/shard_map/group_grads/pallas_call | solution.py:535
  28.2 0.9 %collective-permute-start.5 = (bf16[2,128,256]{2,1,0:T(8,128)(2,1)S(1)}, bf16[2,128,256]{2,1,0:T(8,128)(2,1)S(1)}, u32[]{:S(2)}, u32[]{:S(2)}) collective-permute-start(bf16[2,128,256]{2,1,0:T(8,128)(2,1)S(1)} %get-tuple-element.37), channel_id=1, source_target_pairs={{0,12},{4,8},{8,4},{12,0},{1,13},{5,9},{9,5},{13,1},{2,14},{6,10},... | collective-permute-start | bytes 393224 | tf_op jit(solution)/shard_map/ppermute | solution.py:516
  29.0 0.9 %collective-permute-start.6 = (bf16[2,128,256]{2,1,0:T(8,128)(2,1)S(1)}, bf16[2,128,256]{2,1,0:T(8,128)(2,1)S(1)}, u32[]{:S(2)}, u32[]{:S(2)}) collective-permute-start(bf16[2,128,256]{2,1,0:T(8,128)(2,1)S(1)} %get-tuple-element.38), channel_id=1, source_target_pairs={{0,4},{4,0},{8,12},{12,8},{1,5},{5,1},{9,13},{13,9},{2,6},{6,2},{1... | collective-permute-start | bytes 393224 | tf_op jit(solution)/shard_map/ppermute | solution.py:516
  29.9 0.0 collective-permute-done.3.refs_8_
  29.9 0.0 copy-done.1
  30.0 2.8 %finish_own.1 = (bf16[1024,1280]{1,0:T(8,128)(2,1)}, bf16[2,1024,256]{2,1,0:T(8,128)(2,1)}, f32[2,128,256]{2,1,0:T(8,128)S(1)}) custom-call(s32[64]{0:T(128)S(1)} %copy-done.3, s32[16]{0:T(128)S(1)} %copy-done.4, f32[16]{0:T(128)S(1)} %copy-done.2, f32[16]{0:T(128)S(1)} %collective-permute-done.1.refs_3_, ...), custom_call_target="tpu_custom_call", output_to_operand_aliasing={{0}: (9, {}), {1}: (10, {})} | custom-call | tf_op jit(solution)/shard_map/finish_own/pallas_call | solution.py:578
  32.8 3.5 %collective-permute-done.5 = bf16[2,128,256]{2,1,0:T(8,128)(2,1)S(1)} collective-permute-done((bf16[2,128,256]{2,1,0:T(8,128)(2,1)S(1)}, bf16[2,128,256]{2,1,0:T(8,128)(2,1)S(1)}, u32[]{:S(2)}, u32[]{:S(2)}) %collective-permute-start.5) | collective-permute-done | bytes 131104 | tf_op jit(solution)/shard_map/ppermute | solution.py:516
  36.2 0.0 collective-permute-done.6
  36.3 0.7 %add_convert_fusion = bf16[2,128,256]{2,1,0:T(8,128)(2,1)} fusion(f32[2,128,256]{2,1,0:T(8,128)S(1)} %get-tuple-element.36, bf16[2,128,256]{2,1,0:T(8,128)(2,1)S(1)} %collective-permute-done.6, bf16[2,128,256]{2,1,0:T(8,128)(2,1)S(1)} %collective-permute-done.5), kind=kLoop, calls=%fused_computation | loop fusion | flops 327680 | bytes 655360 | tf_op jit(solution)/shard_map/convert_element_type | solution.py:603
Async XLA Ops:
  2.2 13.5 %copy-start = (bf16[272,256]{1,0:T(8,128)(2,1)S(1)}, bf16[272,256]{1,0:T(8,128)(2,1)}, u32[]{:S(2)}) copy-start(bf16[272,256]{1,0:T(8,128)(2,1)} %pack.1.refs_7_.refs_4_) | copy-start | bytes 417796
  2.2 13.4 %copy-start.2 = (f32[16]{0:T(128)S(1)}, f32[16]{0:T(128)}, u32[]{:S(2)}) copy-start(f32[16]{0:T(128)} %refs_2_.7) | copy-start | bytes 196
  2.2 13.4 %copy-start.3 = (s32[64]{0:T(128)S(1)}, s32[64]{0:T(128)}, u32[]{:S(2)}) copy-start(s32[64]{0:T(128)} %refs_0_.7) | copy-start | bytes 772
  2.2 13.4 %copy-start.4 = (s32[16]{0:T(128)S(1)}, s32[16]{0:T(128)}, u32[]{:S(2)}) copy-start(s32[16]{0:T(128)} %refs_1_.7) | copy-start | bytes 196
  2.2 11.5 %collective-permute-start = (bf16[272,256]{1,0:T(8,128)(2,1)}, bf16[272,256]{1,0:T(8,128)(2,1)S(1)}, u32[]{:S(2)}, u32[]{:S(2)}) collective-permute-start(bf16[272,256]{1,0:T(8,128)(2,1)} %pack.1.refs_7_.refs_4_), channel_id=1, source_target_pairs={{0,8},{4,12},{8,0},{12,4},{1,9},{5,13},{9,1},{13,5},{2,10},{6,14},... | collective-permute-start | bytes 417800 | tf_op jit(solution)/shard_map/ppermute | solution.py:516
  6.3 7.4 %collective-permute-start.1 = (f32[16]{0:T(128)}, f32[16]{0:T(128)S(1)}, u32[]{:S(2)}, u32[]{:S(2)}) collective-permute-start(f32[16]{0:T(128)} %refs_2_.7), channel_id=1, source_target_pairs={{0,12},{4,8},{8,4},{12,0},{1,13},{5,9},{9,5},{13,1},{2,14},{6,10},... | collective-permute-start | bytes 200 | tf_op jit(solution)/shard_map/ppermute | solution.py:516
  7.7 8.0 %collective-permute-start.2 = (bf16[272,256]{1,0:T(8,128)(2,1)}, bf16[272,256]{1,0:T(8,128)(2,1)S(1)}, u32[]{:S(2)}, u32[]{:S(2)}) collective-permute-start(bf16[272,256]{1,0:T(8,128)(2,1)} %pack.1.refs_7_.refs_4_), channel_id=1, source_target_pairs={{0,4},{4,0},{8,12},{12,8},{1,5},{5,1},{9,13},{13,9},{2,6},{6,2},{1... | collective-permute-start | bytes 417800 | tf_op jit(solution)/shard_map/ppermute | solution.py:516
  13.8 8.0 %collective-permute-start.4 = (bf16[272,256]{1,0:T(8,128)(2,1)S(1)}, bf16[272,256]{1,0:T(8,128)(2,1)S(1)}, u32[]{:S(2)}, u32[]{:S(2)}) collective-permute-start(bf16[272,256]{1,0:T(8,128)(2,1)S(1)} %collective-permute-done.refs_9_.refs_10_.refs_6_), channel_id=1, source_target_pairs={{0,4},{4,0},{8,12},{12,8},{1,5},{5,1},{9,13},{13,9},{2,6},{6,2},{1... | collective-permute-start | bytes 417800 | tf_op jit(solution)/shard_map/ppermute | solution.py:516
  20.0 10.0 %collective-permute-start.3 = (bf16[2,128,256]{2,1,0:T(8,128)(2,1)S(1)}, bf16[2,128,256]{2,1,0:T(8,128)(2,1)S(1)}, u32[]{:S(2)}, u32[]{:S(2)}) collective-permute-start(bf16[2,128,256]{2,1,0:T(8,128)(2,1)S(1)} %get-tuple-element.28), channel_id=1, source_target_pairs={{0,8},{4,12},{8,0},{12,4},{1,9},{5,13},{9,1},{13,5},{2,10},{6,14},... | collective-permute-start | bytes 393224 | tf_op jit(solution)/shard_map/ppermute | solution.py:516
  21.8 8.1 %copy-start.1 = (bf16[4,2,128,256]{3,2,1,0:T(8,128)(2,1)S(1)}, bf16[4,2,128,256]{3,2,1,0:T(8,128)(2,1)}, u32[]{:S(2)}) copy-start(bf16[4,2,128,256]{3,2,1,0:T(8,128)(2,1)} %get-tuple-element.23.refs_7_) | copy-start | bytes 1572868
  28.2 8.1 %collective-permute-start.5 = (bf16[2,128,256]{2,1,0:T(8,128)(2,1)S(1)}, bf16[2,128,256]{2,1,0:T(8,128)(2,1)S(1)}, u32[]{:S(2)}, u32[]{:S(2)}) collective-permute-start(bf16[2,128,256]{2,1,0:T(8,128)(2,1)S(1)} %get-tuple-element.37), channel_id=1, source_target_pairs={{0,12},{4,8},{8,4},{12,0},{1,13},{5,9},{9,5},{13,1},{2,14},{6,10},... | collective-permute-start | bytes 393224 | tf_op jit(solution)/shard_map/ppermute | solution.py:516
  29.0 7.2 %collective-permute-start.6 = (bf16[2,128,256]{2,1,0:T(8,128)(2,1)S(1)}, bf16[2,128,256]{2,1,0:T(8,128)(2,1)S(1)}, u32[]{:S(2)}, u32[]{:S(2)}) collective-permute-start(bf16[2,128,256]{2,1,0:T(8,128)(2,1)S(1)} %get-tuple-element.38), channel_id=1, source_target_pairs={{0,4},{4,0},{8,12},{12,8},{1,5},{5,1},{9,13},{13,9},{2,6},{6,2},{1... | collective-permute-start | bytes 393224 | tf_op jit(solution)/shard_map/ppermute | solution.py:516

commit v12 on v9

--- a/solution.py
+++ b/solution.py
@@ -18,7 +18,6 @@
 FAR = 3
 VMEM_BYTES = 63 * 1024 * 1024
 GROUP_BYTES = 53 * 1024 * 1024
-FINISH_BYTES = 24 * 1024 * 1024
 ANYWHERE = pl.BlockSpec(memory_space=pl.ANY)
 
 
@@ -293,20 +292,62 @@
     ]
 
 
-def group_kernel(z, turns, raw, body, n_tails, aliased, *refs):
-    small_hbm, given = refs[:4], refs[4:7]
-    tail_hbm, prompts = refs[7 : 7 + n_tails], refs[7 + n_tails : 7 + n_tails + len(turns)]
-    refs = refs[7 + n_tails + len(turns) + aliased :]
-    (q_out, self_out), grads_out = refs[:2], refs[2 : 2 + len(turns)]
-    (resp_prompt, resp_len, rewards, far_rewards, order, lens, factors, q, og, kv, prefix, tails, acc, out, own, grads,
-     sem_small, sem_tails, sem_prefix, sem_in, sem_out, sem_grads) = refs[2 + len(turns) :]
+def sort_kernel(z, ahead, resp_prompt_hbm, q_hbm, og_hbm, kv_hbm, both_out, kv_out, *scratch):
+    resp_prompt, order, q, og, kv, sem_small, sem_in, sem_out = scratch
+    me = lax.axis_index("dp")
+    small = pltpu.make_async_copy(resp_prompt_hbm, resp_prompt, sem_small)
+    small.start()
+    small.wait()
+    find_responses(z, me, ahead, resp_prompt, order)
+    held, in_order = (q, og, kv), (both_out.at[0], both_out.at[1], kv_out)
+    slots = range(len(ahead) * z.slots)
+
+    def copies_in(slot):
+        return row_copies(
+            (q_hbm, og_hbm, kv_hbm), held, token_rows(z, order[slot]), token_rows(z, slot), sem_in.at[slot]
+        )
+
+    def copies_out(slot):
+        rows = token_rows(z, slot)
+        return row_copies(held, in_order, rows, rows, sem_out.at[slot])
+
+    for slot in slots:
+        for copy in copies_in(slot):
+            copy.start()
+    for slot in slots:
+        for copy in copies_in(slot):
+            copy.wait()
+        for copy in copies_out(slot):
+            copy.start()
+    for slot in slots:
+        for copy in copies_out(slot):
+            copy.wait()
+
+
+def group_kernel(z, turns, ahead, n_come, aliased, *refs):
+    small_hbm, given, tail_hbm = refs[:4], refs[4:7], refs[7 : 7 + FAR]
+    refs = refs[7 + FAR :]
+    prompts, refs = refs[: len(turns)], refs[len(turns) :]
+    come_hbm, refs = refs[:n_come], refs[n_come:]
+    if ahead is not None:
+        (both, kv_ordered), refs = refs[:2], refs[2:]
+    (q_out, self_out), refs = refs[aliased : aliased + 2], refs[aliased + 2 :]
+    grads_out, refs = refs[: len(turns)], refs[len(turns) :]
+    (resp_prompt, resp_len, rewards, far_rewards, order, lens, factors, q, og, kv, prefix, tails, come, acc, out, own,
+     grads, sem_small, sem_tails, sem_prefix, sem_in, sem_out, sem_grads, sem_first) = refs
     me = lax.axis_index("dp")
     n_slots = len(turns) * z.slots
+    span = z.slots * z.tokens
 
     small = [
         pltpu.make_async_copy(src, dst, sem_small.at[n])
         for n, (src, dst) in enumerate(zip(small_hbm, (resp_prompt, resp_len, rewards, far_rewards)))
     ]
+    first_rows = ()
+    if ahead is not None:
+        first_rows = row_copies(
+            (both.at[0], both.at[1], kv_ordered), (q, og, kv), pl.ds(ahead * span, span), pl.ds(0, span), sem_first
+        )
     prefix_copies = [
         pltpu.make_async_copy(
             prompts[t].at[pl.ds(n * z.prefix_len, z.prefix_len)], prefix.at[t, n], sem_prefix.at[t, n]
@@ -315,7 +356,8 @@
         for n in range(2)
     ]
     late = tail_copies(z, tail_hbm, tails, sem_tails)
-    for copy in small + prefix_copies + late:
+    late += [pltpu.make_async_copy(src, come, sem_grads.at[0]) for src in come_hbm]
+    for copy in [*small, *first_rows, *prefix_copies, *late]:
         copy.start()
     small[0].wait()
     find_responses(z, me, turns, resp_prompt, order)
@@ -328,80 +370,63 @@
     def copies_out(slot):
         return result_copies(out, own, q_out, self_out, slot, token_rows(z, order[slot]), sem_out)
 
-    for slot in range(n_slots):
+    for slot in range(0 if ahead is None else z.slots, n_slots):
         for copy in copies_in(slot):
             copy.start()
     for copy in small[1:] + late:
         copy.wait()
     for t, turn in enumerate(turns):
-        total = None if raw else prompt_total(z, me, me ^ turn, resp_prompt, tails, far_rewards)
+        total = prompt_total(z, me, me ^ turn, resp_prompt, tails, far_rewards)
         for slot in range(t * z.slots, (t + 1) * z.slots):
             i = order[slot]
             lens[slot] = resp_len[i]
-            factors[slot] = 1.0 if raw else reward_factor(z, rewards[i], total, resp_len[i])
-    if not raw:
+            factors[slot] = reward_factor(z, rewards[i], total, resp_len[i])
+    if n_come:
+        acc[0] = come[...].astype(F32)
+    else:
         acc[...] = jnp.zeros(acc.shape, F32)
     for copy in prefix_copies:
         copy.wait()
 
-    pairs_per_turn = z.slots // PAIR
-    pairs_in_body, heads_in_body = body
-    head_steps = z.kv_heads // heads_in_body
-    pair_steps = pairs_per_turn // pairs_in_body
-
-    def step(u, _):
-        k_step = lax.rem(u, head_steps) if head_steps > 1 else 0
-        pair_step = u // head_steps
-        t = pair_step // pair_steps
-        first = pair_step * pairs_in_body * PAIR
-        mine = range(pairs_in_body * PAIR)
-
-        def moves(starting):
-            for n in mine:
-                for copy in copies_out(first + n) if starting else copies_in(first + n):
-                    copy.start() if starting else copy.wait()
-
-        if head_steps > 1:
-            pl.when(k_step == 0)(lambda: moves(False))
+    def step(t, _):
+        slots = [t * z.slots + n for n in range(z.slots)]
+
+        def wait_for_slots():
+            for slot in slots:
+                for copy in copies_in(slot):
+                    copy.wait()
+
+        if ahead is None:
+            wait_for_slots()
         else:
-            moves(False)
-
-        def sink(place, cols, key_grad, value_grad):
-            if raw:
-                grads[place, 0, :, cols] = key_grad.astype(BF16)
-                grads[place, 1, :, cols] = value_grad.astype(BF16)
-            else:
-                acc[t, 0, :, cols] += key_grad
-                acc[t, 1, :, cols] += value_grad
+
+            @pl.when(t == 0)
+            def _():
+                for copy in first_rows:
+                    copy.wait()
+
+            if len(turns) > 1:
+                pl.when(t > 0)(wait_for_slots)
+
+        def sink(_, cols, key_grad, value_grad):
+            acc[t, 0, :, cols] += key_grad
+            acc[t, 1, :, cols] += value_grad
 
         units = []
-        for pair in range(pairs_in_body):
-            places = [first + pair * PAIR + n for n in range(PAIR)]
-            for k in range(heads_in_body):
-                units.append(
-                    Unit(
-                        [token_rows(z, n) for n in places],
-                        places,
-                        k_step * heads_in_body + k if head_steps > 1 else k,
-                        [lens[n] for n in places],
-                        [factors[n] for n in places],
-                    )
-                )
-        attend(z, units, q, og, kv, prefix.at[t], out, own, sink, raw)
-        if head_steps > 1:
-            pl.when(k_step == head_steps - 1)(lambda: moves(True))
-        else:
-            moves(True)
+        for pair in range(0, z.slots, PAIR):
+            places = slots[pair : pair + PAIR]
+            at = [token_rows(z, n) for n in places]
+            for k in range(z.kv_heads):
+                units.append(Unit(at, places, k, [lens[n] for n in places], [factors[n] for n in places]))
+        attend(z, units, q, og, kv, prefix.at[t], out, own, sink, False)
+        for slot in slots:
+            for copy in copies_out(slot):
+                copy.start()
         return 0
 
-    lax.fori_loop(0, len(turns) * pair_steps * head_steps, step, 0)
-    if raw:
-        last = [pltpu.make_async_copy(grads, grads_out[0], sem_grads.at[0])]
-    else:
-        grads[...] = acc[...].astype(BF16)
-        last = [
-            pltpu.make_async_copy(grads.at[t], grads_out[t], sem_grads.at[t]) for t in range(len(turns))
-        ]
+    lax.fori_loop(0, len(turns), step, 0)
+    grads[...] = acc[...].astype(grads.dtype)
+    last = [pltpu.make_async_copy(grads.at[t], grads_out[t], sem_grads.at[t]) for t in range(len(turns))]
     for copy in last:
         copy.start()
     for slot in range(n_slots):
@@ -409,57 +434,6 @@
             copy.wait()
     for copy in last:
         copy.wait()
-
-
-def finish_kernel(z, n_tails, n_come, *refs):
-    small_hbm, tail_hbm = refs[:4], refs[4 : 4 + n_tails]
-    per_resp_hbm, come_hbm = refs[4 + n_tails], refs[5 + n_tails : 5 + n_tails + n_come]
-    q_out, self_out, grads_out = refs[7 + n_tails + n_come : 10 + n_tails + n_come]
-    (resp_prompt, resp_len, rewards, far_rewards, order, tails, out, own, per_resp, come, grads,
-     sem_small, sem_tails, sem_come, sem_in, sem_out) = refs[10 + n_tails + n_come :]
-    me = lax.axis_index("dp")
-    small = [
-        pltpu.make_async_copy(src, dst, sem_small.at[n])
-        for n, (src, dst) in enumerate(zip(small_hbm, (resp_prompt, resp_len, rewards, far_rewards)))
-    ]
-    late = tail_copies(z, tail_hbm, tails, sem_tails)
-    late += [pltpu.make_async_copy(src, come.at[n], sem_come.at[n]) for n, src in enumerate(come_hbm)]
-    late += [pltpu.make_async_copy(per_resp_hbm, per_resp, sem_come.at[n_come])]
-    for copy in small + late:
-        copy.start()
-    small[0].wait()
-    find_responses(z, me, (0,), resp_prompt, order)
-
-    def moves(slot, back):
-        sems = sem_in if back else sem_out
-        return result_copies(out, own, q_out, self_out, slot, token_rows(z, order[slot]), sems, back)
-
-    for slot in range(z.slots):
-        for copy in moves(slot, True):
-            copy.start()
-    for copy in small[1:] + late:
-        copy.wait()
-    total = prompt_total(z, me, me, resp_prompt, tails, far_rewards)
-    summed = come[0].astype(F32)
-    for n in range(1, n_come):
-        summed += come[n].astype(F32)
-    factors = [reward_factor(z, rewards[order[n]], total, resp_len[order[n]]) for n in range(z.slots)]
-    for slot in range(z.slots):
-        summed += per_resp[slot].astype(F32) * factors[slot]
-    grads[...] = summed
-    last = pltpu.make_async_copy(grads, grads_out, sem_small.at[0])
-    last.start()
-    for slot in range(z.slots):
-        for copy in moves(slot, True):
-            copy.wait()
-        out[slot] = (out[slot].astype(F32) * factors[slot]).astype(BF16)
-        own[slot] = (own[slot].astype(F32) * factors[slot]).astype(BF16)
-        for copy in moves(slot, False):
-            copy.start()
-    for slot in range(z.slots):
-        for copy in moves(slot, False):
-            copy.wait()
-    last.wait()
 
 
 def near_shards(z, prompt_kv, resp_q, resp_kv, out_grad, rewards, resp_prompt, resp_len):
@@ -496,19 +470,40 @@
     smem = [pltpu.SMEM(x.shape, x.dtype) for x in (*small, rewards)]
     slots = z.slots
 
-    def grads_of(turns, raw, written, body):
+    given = (resp_q, out_grad, resp_kv)
+    n_ahead = 2 * slots * z.tokens
+    in_order = pl.pallas_call(
+        functools.partial(sort_kernel, z, (2, FAR)),
+        out_shape=[shape((2, n_ahead, z.lanes), BF16), shape((2, n_ahead, z.width), BF16)],
+        in_specs=[ANYWHERE] * 4,
+        out_specs=[ANYWHERE] * 2,
+        scratch_shapes=[
+            smem[0],
+            pltpu.SMEM((2 * slots + 1,), jnp.int32),
+            pltpu.VMEM((n_ahead, z.lanes), BF16),
+            pltpu.VMEM((n_ahead, z.lanes), BF16),
+            pltpu.VMEM((2, n_ahead, z.width), BF16),
+            pltpu.SemaphoreType.DMA,
+            pltpu.SemaphoreType.DMA((2 * slots, 3)),
+            pltpu.SemaphoreType.DMA((2 * slots, 3)),
+        ],
+        compiler_params=params,
+        cost_estimate=cost,
+        name="sort_rows",
+    )(resp_prompt, *given)
+    onward, far_rewards, *in_order = lax.optimization_barrier((payloads[2], far_rewards, *in_order))
+    payloads[FAR] = swap(onward, 1)
+
+    def grads_of(turns, ahead, written, come=(), kind=BF16):
         n_slots, n_turns = len(turns) * slots, len(turns)
-        used_tails = [] if raw else tails
-        used_small = (*small, rewards if raw else far_rewards)
+        rows = () if ahead is None else in_order
         prompts = [payloads[turn] for turn in turns]
-        operands = [*used_small, resp_q, out_grad, resp_kv, *used_tails, *prompts, *written]
-        grads_shapes = [(slots,) + one] if raw else [one] * n_turns
+        operands = [*small, far_rewards, *given, *tails, *prompts, *come, *rows, *written]
         return pl.pallas_call(
-            functools.partial(group_kernel, z, turns, raw, body, len(used_tails), len(written)),
-            out_shape=[shape(resp_q.shape, BF16), shape(resp_kv.shape, BF16)]
-            + [shape(x, BF16) for x in grads_shapes],
+            functools.partial(group_kernel, z, turns, ahead, len(come), len(written)),
+            out_shape=[shape(resp_q.shape, BF16), shape(resp_kv.shape, BF16)] + [shape(one, kind)] * n_turns,
             in_specs=[ANYWHERE] * len(operands),
-            out_specs=[ANYWHERE] * (2 + len(grads_shapes)),
+            out_specs=[ANYWHERE] * (2 + n_turns),
             input_output_aliases={len(operands) - 2: 0, len(operands) - 1: 1} if written else {},
             scratch_shapes=[
                 *smem,
@@ -520,57 +515,30 @@
                 pltpu.VMEM((2, n_slots * z.tokens, z.width), BF16),
                 pltpu.VMEM((n_turns,) + one, BF16),
                 pltpu.VMEM((FAR, TAIL, z.width), BF16),
+                pltpu.VMEM(one, BF16),
                 pltpu.VMEM((n_turns,) + one, F32),
                 pltpu.VMEM((n_slots, z.tokens, z.lanes), BF16),
                 pltpu.VMEM((n_slots, 2, z.tokens, z.width), BF16),
-                pltpu.VMEM(grads_shapes[0] if raw else (n_turns,) + one, BF16),
+                pltpu.VMEM((n_turns,) + one, kind),
                 pltpu.SemaphoreType.DMA((len(smem),)),
                 pltpu.SemaphoreType.DMA((FAR,)),
                 pltpu.SemaphoreType.DMA((n_turns, 2)),
-                pltpu.SemaphoreType.DMA((n_slots, 4)),
                 pltpu.SemaphoreType.DMA((n_slots, 3)),
+                pltpu.SemaphoreType.DMA((n_slots, 2)),
                 pltpu.SemaphoreType.DMA((n_turns,)),
+                pltpu.SemaphoreType.DMA((3,)),
             ],
-            compiler_params=params if raw else pltpu.CompilerParams(vmem_limit_bytes=GROUP_BYTES),
+            compiler_params=pltpu.CompilerParams(vmem_limit_bytes=GROUP_BYTES),
             cost_estimate=cost,
-            name="raw_grads" if raw else "group_grads",
+            name="group_grads" if turns[0] else "own_grads",
         )(*operands)
 
-    *written, per_resp = grads_of((0,), True, (), (1, z.kv_heads))
-    onward, per_resp, far_rewards = lax.optimization_barrier((payloads[2], per_resp, far_rewards))
-    payloads[FAR] = swap(onward, 1)
-    *written, for_2, for_1 = grads_of((2, 1), False, written, (slots // PAIR, z.kv_heads))
+    *written, for_2 = grads_of((2,), 0, ())
     come = [swap(for_2, 2)]
-    *written, for_far = grads_of((FAR,), False, written, (1, 1))
-    for_far, for_1 = lax.optimization_barrier((for_far, for_1))
+    *written, for_far, for_1 = grads_of((FAR, 1), 1, written)
     last = [swap(for_far, FAR), swap(for_1, 1)]
-    operands = [*small, far_rewards, *tails, per_resp, *come, *written]
-    q_out, self_out, own_grads = pl.pallas_call(
-        functools.partial(finish_kernel, z, len(tails), len(come)),
-        out_shape=[shape(resp_q.shape, BF16), shape(resp_kv.shape, BF16), shape(one, F32)],
-        in_specs=[ANYWHERE] * len(operands),
-        out_specs=[ANYWHERE] * 3,
-        input_output_aliases={len(operands) - 2: 0, len(operands) - 1: 1},
-        scratch_shapes=[
-            *smem,
-            pltpu.SMEM((slots + 1,), jnp.int32),
-            pltpu.VMEM((FAR, TAIL, z.width), BF16),
-            pltpu.VMEM((slots, z.tokens, z.lanes), BF16),
-            pltpu.VMEM((slots, 2, z.tokens, z.width), BF16),
-            pltpu.VMEM((slots,) + one, BF16),
-            pltpu.VMEM((len(come),) + one, BF16),
-            pltpu.VMEM(one, F32),
-            pltpu.SemaphoreType.DMA((len(smem),)),
-            pltpu.SemaphoreType.DMA((FAR,)),
-            pltpu.SemaphoreType.DMA((len(come) + 1,)),
-            pltpu.SemaphoreType.DMA((slots, 3)),
-            pltpu.SemaphoreType.DMA((slots, 3)),
-        ],
-        compiler_params=pltpu.CompilerParams(vmem_limit_bytes=FINISH_BYTES),
-        cost_estimate=cost,
-        name="finish_own",
-    )(*operands)
-    prefix_out = (own_grads + sum(part.astype(F32) for part in last)).astype(BF16)
+    q_out, self_out, summed = grads_of((0,), None, written, come, F32)
+    prefix_out = (summed + sum(part.astype(F32) for part in last)).astype(BF16)
     return (q_out, self_out, prefix_out)
 
 

time: 39.5 us -> 37.1 us (0.939)
  Pallas kernels: 22.5 us -> 21 us
  starting transfers between devices: 11.2 us -> 10.8 us
    pallas_call x4, Pallas kernels: 20.9 us -> 19.4 us  [the longest x3 15.5 us: grads_of(): pl.pallas_call(functools.partial(group_kernel, z, turns, ahead, len(come)...]
    ppermute x7, starting transfers between devices: 11.2 us -> 10.8 us  [swap(): return lax.ppermute(x, 'dp', [(i, i ^ s) for i in range(n_dp)])]
  transfers between devices with their start and end apart: 7 -> 7, of which waited for: 2 -> 4; matrix products, arithmetic and copies ran while one was open for 0% -> 0% of each run, Pallas kernels for 53% -> 53%
where the time goes in v12:
time: 37.1 us; the launch traced here: 36.9 us
  Pallas kernels  21 us (57%)
  starting transfers between devices  10.8 us (29%)
  waiting for transfers between devices  3.72 us (10%)
  between operations  0.72 us (2%)
  other arithmetic  0.7 us (2%)
    pallas_call x3, Pallas kernels, grads_of(): pl.pallas_call(functools.partial(group_kernel, z, turns, ahead, len(come)...  15.5 us
    ppermute x7, starting transfers between devices, swap(): return lax.ppermute(x, 'dp', [(i, i ^ s) for i in range(n_dp)])  10.8 us
    pallas_call x1, Pallas kernels, near_shards(): pl.pallas_call(functools.partial(sort_kernel, z, (2, FAR)), out_shape=[sh...  3.9 us
    ppermute x7, waiting for transfers between devices, swap(): return lax.ppermute(x, 'dp', [(i, i ^ s) for i in range(n_dp)])  3.72 us
    pallas_call x1, Pallas kernels, near_shards(): pl.pallas_call(functools.partial(pack_kernel, z), out_shape=jax.ShapeDtyp...  1.57 us
  transfers between devices with their start and end apart: 7, of which 4 were waited for; matrix products, arithmetic and copies ran while one was open for 0% of the time, Pallas kernels for 53%

profile of v12, /device:TPU:0, one launch (start us, length us, event | category | flops | bytes accessed | tf_op | source)
XLA Modules:
  0.0 36.9 jit_solution(16102476797439466310)
XLA Ops:
  0.6 1.6 %pack.1.refs_7_.refs_10_ = bf16[272,256]{1,0:T(8,128)(2,1)} custom-call(bf16[2,128,256]{2,1,0:T(8,128)(2,1)} %prompt_hbm.1, f32[16]{0:T(128)} %refs_2_.5, s32[64]{0:T(128)} %refs_0_.5), custom_call_target="tpu_custom_call" | custom-call | tf_op jit(solution)/shard_map/pack/pallas_call | solution.py:446
  2.2 0.0 copy-start
  2.2 0.0 copy-start.1
  2.2 0.0 copy-start.2
  2.2 0.0 copy-start.3
  2.3 4.1 %collective-permute-start = (bf16[272,256]{1,0:T(8,128)(2,1)}, bf16[272,256]{1,0:T(8,128)(2,1)S(1)}, u32[]{:S(2)}, u32[]{:S(2)}) collective-permute-start(bf16[272,256]{1,0:T(8,128)(2,1)} %pack.1.refs_7_.refs_10_), channel_id=1, source_target_pairs={{0,8},{4,12},{8,0},{12,4},{1,9},{5,13},{9,1},{13,5},{2,10},{6,14},... | collective-permute-start | bytes 417800 | tf_op jit(solution)/shard_map/ppermute | solution.py:464
  6.4 1.3 %collective-permute-start.1 = (f32[16]{0:T(128)}, f32[16]{0:T(128)S(1)}, u32[]{:S(2)}, u32[]{:S(2)}) collective-permute-start(f32[16]{0:T(128)} %refs_2_.5), channel_id=1, source_target_pairs={{0,12},{4,8},{8,4},{12,0},{1,13},{5,9},{9,5},{13,1},{2,14},{6,10},... | collective-permute-start | bytes 200 | tf_op jit(solution)/shard_map/ppermute | solution.py:464
  7.7 0.2 collective-permute-start.2
  7.9 3.9 %sort_rows.1 = (bf16[2,512,1280]{2,1,0:T(8,128)(2,1)}, bf16[2,512,256]{2,1,0:T(8,128)(2,1)}) custom-call(s32[64]{0:T(128)} %refs_0_.5, bf16[1024,1280]{1,0:T(8,128)(2,1)} %refs_4_.5, bf16[1024,1280]{1,0:T(8,128)(2,1)} %refs_5_.5, bf16[2,1024,256]{2,1,0:T(8,128)(2,1)} %refs_6_.5), custom_call_target="tpu_custom_call" | custom-call | tf_op jit(solution)/shard_map/sort_rows/pallas_call | solution.py:475
  11.8 0.1 collective-permute-done.1.refs_3_
  11.9 1.4 %collective-permute-done.refs_9_.refs_10_ = bf16[272,256]{1,0:T(8,128)(2,1)S(1)} collective-permute-done((bf16[272,256]{1,0:T(8,128)(2,1)}, bf16[272,256]{1,0:T(8,128)(2,1)S(1)}, u32[]{:S(2)}, u32[]{:S(2)}) %collective-permute-start) | collective-permute-done | bytes 139296 | tf_op jit(solution)/shard_map/ppermute | solution.py:464
  13.3 0.8 %collective-permute-start.4 = (bf16[272,256]{1,0:T(8,128)(2,1)S(1)}, bf16[272,256]{1,0:T(8,128)(2,1)S(1)}, u32[]{:S(2)}, u32[]{:S(2)}) collective-permute-start(bf16[272,256]{1,0:T(8,128)(2,1)S(1)} %collective-permute-done.refs_9_.refs_10_), channel_id=1, source_target_pairs={{0,4},{4,0},{8,12},{12,8},{1,5},{5,1},{9,13},{13,9},{2,6},{6,2},{1... | collective-permute-start | bytes 417800 | tf_op jit(solution)/shard_map/ppermute | solution.py:464
  14.1 0.5 %collective-permute-done.2.refs_8_.refs_11_ = bf16[272,256]{1,0:T(8,128)(2,1)S(1)} collective-permute-done((bf16[272,256]{1,0:T(8,128)(2,1)}, bf16[272,256]{1,0:T(8,128)(2,1)S(1)}, u32[]{:S(2)}, u32[]{:S(2)}) %collective-permute-start.2) | collective-permute-done | bytes 139296 | tf_op jit(solution)/shard_map/ppermute | solution.py:464
  14.6 0.0 copy-done
  14.6 0.0 copy-done.1
  14.6 0.0 copy-done.2
  14.6 0.0 copy-done.3
  14.6 4.3 %group_grads.2 = (bf16[1024,1280]{1,0:T(8,128)(2,1)}, bf16[2,1024,256]{2,1,0:T(8,128)(2,1)}, bf16[2,128,256]{2,1,0:T(8,128)(2,1)S(1)}) custom-call(s32[64]{0:T(128)S(1)} %copy-done.1, s32[16]{0:T(128)S(1)} %copy-done.3, f32[16]{0:T(128)S(1)} %copy-done.2, f32[16]{0:T(128)S(1)} %collective-permute-done.1.refs_3_, bf16[1024,1280]{1,0:T(8,128)(2,1)} %refs_4_.5, ...), custom_call_target="tpu_custom_call" | custom-call | tf_op jit(solution)/shard_map/group_grads/pallas_call | solution.py:502
  18.9 2.9 %collective-permute-start.3 = (bf16[2,128,256]{2,1,0:T(8,128)(2,1)S(1)}, bf16[2,128,256]{2,1,0:T(8,128)(2,1)S(1)}, u32[]{:S(2)}, u32[]{:S(2)}) collective-permute-start(bf16[2,128,256]{2,1,0:T(8,128)(2,1)S(1)} %get-tuple-element.24), channel_id=1, source_target_pairs={{0,8},{4,12},{8,0},{12,4},{1,9},{5,13},{9,1},{13,5},{2,10},{6,14},... | collective-permute-start | bytes 393224 | tf_op jit(solution)/shard_map/ppermute | solution.py:464
  21.8 0.0 collective-permute-done.4.refs_10_
  21.8 6.3 %group_grads.3 = (bf16[1024,1280]{1,0:T(8,128)(2,1)}, bf16[2,1024,256]{2,1,0:T(8,128)(2,1)}, bf16[2,128,256]{2,1,0:T(8,128)(2,1)S(1)}, bf16[2,128,256]{2,1,0:T(8,128)(2,1)S(1)}) custom-call(s32[64]{0:T(128)S(1)} %copy-done.1, s32[16]{0:T(128)S(1)} %copy-done.3, f32[16]{0:T(128)S(1)} %copy-done.2, ...), custom_call_target="tpu_custom_call", output_to_operand_aliasing={{0}: (14, {}), {1}: (15, {})} | custom-call | tf_op jit(solution)/shard_map/group_grads/pallas_call | solution.py:502
  28.1 0.8 %collective-permute-start.5 = (bf16[2,128,256]{2,1,0:T(8,128)(2,1)S(1)}, bf16[2,128,256]{2,1,0:T(8,128)(2,1)S(1)}, u32[]{:S(2)}, u32[]{:S(2)}) collective-permute-start(bf16[2,128,256]{2,1,0:T(8,128)(2,1)S(1)} %get-tuple-element.33), channel_id=1, source_target_pairs={{0,12},{4,8},{8,4},{12,0},{1,13},{5,9},{9,5},{13,1},{2,14},{6,10},... | collective-permute-start | bytes 393224 | tf_op jit(solution)/shard_map/ppermute | solution.py:464
  28.9 0.6 %collective-permute-start.6 = (bf16[2,128,256]{2,1,0:T(8,128)(2,1)S(1)}, bf16[2,128,256]{2,1,0:T(8,128)(2,1)S(1)}, u32[]{:S(2)}, u32[]{:S(2)}) collective-permute-start(bf16[2,128,256]{2,1,0:T(8,128)(2,1)S(1)} %get-tuple-element.34), channel_id=1, source_target_pairs={{0,4},{4,0},{8,12},{12,8},{1,5},{5,1},{9,13},{13,9},{2,6},{6,2},{1... | collective-permute-start | bytes 393224 | tf_op jit(solution)/shard_map/ppermute | solution.py:464
  29.5 0.0 collective-permute-done.3.refs_11_
  29.5 4.9 %own_grads.1 = (bf16[1024,1280]{1,0:T(8,128)(2,1)}, bf16[2,1024,256]{2,1,0:T(8,128)(2,1)}, f32[2,128,256]{2,1,0:T(8,128)S(1)}) custom-call(s32[64]{0:T(128)S(1)} %copy-done.1, s32[16]{0:T(128)S(1)} %copy-done.3, f32[16]{0:T(128)S(1)} %copy-done.2, f32[16]{0:T(128)S(1)} %collective-permute-done.1.refs_3_, ...), custom_call_target="tpu_custom_call", output_to_operand_aliasing={{0}: (12, {}), {1}: (13, {})} | custom-call | tf_op jit(solution)/shard_map/own_grads/pallas_call | solution.py:502
  34.5 1.7 %collective-permute-done.5 = bf16[2,128,256]{2,1,0:T(8,128)(2,1)S(1)} collective-permute-done((bf16[2,128,256]{2,1,0:T(8,128)(2,1)S(1)}, bf16[2,128,256]{2,1,0:T(8,128)(2,1)S(1)}, u32[]{:S(2)}, u32[]{:S(2)}) %collective-permute-start.5) | collective-permute-done | bytes 131104 | tf_op jit(solution)/shard_map/ppermute | solution.py:464
  36.2 0.0 collective-permute-done.6
  36.2 0.7 %add_convert_fusion = bf16[2,128,256]{2,1,0:T(8,128)(2,1)} fusion(f32[2,128,256]{2,1,0:T(8,128)S(1)} %get-tuple-element.32, bf16[2,128,256]{2,1,0:T(8,128)(2,1)S(1)} %collective-permute-done.6, bf16[2,128,256]{2,1,0:T(8,128)(2,1)S(1)} %collective-permute-done.5), kind=kLoop, calls=%fused_computation | loop fusion | flops 327680 | bytes 655360 | tf_op jit(solution)/shard_map/convert_element_type | solution.py:541
Async XLA Ops:
  2.2 12.4 %copy-start = (bf16[272,256]{1,0:T(8,128)(2,1)S(1)}, bf16[272,256]{1,0:T(8,128)(2,1)}, u32[]{:S(2)}) copy-start(bf16[272,256]{1,0:T(8,128)(2,1)} %pack.1.refs_7_.refs_10_) | copy-start | bytes 417796
  2.2 12.4 %copy-start.1 = (s32[64]{0:T(128)S(1)}, s32[64]{0:T(128)}, u32[]{:S(2)}) copy-start(s32[64]{0:T(128)} %refs_0_.5) | copy-start | bytes 772
  2.2 12.4 %copy-start.2 = (f32[16]{0:T(128)S(1)}, f32[16]{0:T(128)}, u32[]{:S(2)}) copy-start(f32[16]{0:T(128)} %refs_2_.5) | copy-start | bytes 196
  2.2 12.4 %copy-start.3 = (s32[16]{0:T(128)S(1)}, s32[16]{0:T(128)}, u32[]{:S(2)}) copy-start(s32[16]{0:T(128)} %refs_1_.5) | copy-start | bytes 196
  2.3 11.1 %collective-permute-start = (bf16[272,256]{1,0:T(8,128)(2,1)}, bf16[272,256]{1,0:T(8,128)(2,1)S(1)}, u32[]{:S(2)}, u32[]{:S(2)}) collective-permute-start(bf16[272,256]{1,0:T(8,128)(2,1)} %pack.1.refs_7_.refs_10_), channel_id=1, source_target_pairs={{0,8},{4,12},{8,0},{12,4},{1,9},{5,13},{9,1},{13,5},{2,10},{6,14},... | collective-permute-start | bytes 417800 | tf_op jit(solution)/shard_map/ppermute | solution.py:464
  6.4 5.6 %collective-permute-start.1 = (f32[16]{0:T(128)}, f32[16]{0:T(128)S(1)}, u32[]{:S(2)}, u32[]{:S(2)}) collective-permute-start(f32[16]{0:T(128)} %refs_2_.5), channel_id=1, source_target_pairs={{0,12},{4,8},{8,4},{12,0},{1,13},{5,9},{9,5},{13,1},{2,14},{6,10},... | collective-permute-start | bytes 200 | tf_op jit(solution)/shard_map/ppermute | solution.py:464
  7.7 6.9 %collective-permute-start.2 = (bf16[272,256]{1,0:T(8,128)(2,1)}, bf16[272,256]{1,0:T(8,128)(2,1)S(1)}, u32[]{:S(2)}, u32[]{:S(2)}) collective-permute-start(bf16[272,256]{1,0:T(8,128)(2,1)} %pack.1.refs_7_.refs_10_), channel_id=1, source_target_pairs={{0,4},{4,0},{8,12},{12,8},{1,5},{5,1},{9,13},{13,9},{2,6},{6,2},{1... | collective-permute-start | bytes 417800 | tf_op jit(solution)/shard_map/ppermute | solution.py:464
  13.3 8.5 %collective-permute-start.4 = (bf16[272,256]{1,0:T(8,128)(2,1)S(1)}, bf16[272,256]{1,0:T(8,128)(2,1)S(1)}, u32[]{:S(2)}, u32[]{:S(2)}) collective-permute-start(bf16[272,256]{1,0:T(8,128)(2,1)S(1)} %collective-permute-done.refs_9_.refs_10_), channel_id=1, source_target_pairs={{0,4},{4,0},{8,12},{12,8},{1,5},{5,1},{9,13},{13,9},{2,6},{6,2},{1... | collective-permute-start | bytes 417800 | tf_op jit(solution)/shard_map/ppermute | solution.py:464
  18.9 10.6 %collective-permute-start.3 = (bf16[2,128,256]{2,1,0:T(8,128)(2,1)S(1)}, bf16[2,128,256]{2,1,0:T(8,128)(2,1)S(1)}, u32[]{:S(2)}, u32[]{:S(2)}) collective-permute-start(bf16[2,128,256]{2,1,0:T(8,128)(2,1)S(1)} %get-tuple-element.24), channel_id=1, source_target_pairs={{0,8},{4,12},{8,0},{12,4},{1,9},{5,13},{9,1},{13,5},{2,10},{6,14},... | collective-permute-start | bytes 393224 | tf_op jit(solution)/shard_map/ppermute | solution.py:464
  28.1 8.1 %collective-permute-start.5 = (bf16[2,128,256]{2,1,0:T(8,128)(2,1)S(1)}, bf16[2,128,256]{2,1,0:T(8,128)(2,1)S(1)}, u32[]{:S(2)}, u32[]{:S(2)}) collective-permute-start(bf16[2,128,256]{2,1,0:T(8,128)(2,1)S(1)} %get-tuple-element.33), channel_id=1, source_target_pairs={{0,12},{4,8},{8,4},{12,0},{1,13},{5,9},{9,5},{13,1},{2,14},{6,10},... | collective-permute-start | bytes 393224 | tf_op jit(solution)/shard_map/ppermute | solution.py:464
  28.9 7.3 %collective-permute-start.6 = (bf16[2,128,256]{2,1,0:T(8,128)(2,1)S(1)}, bf16[2,128,256]{2,1,0:T(8,128)(2,1)S(1)}, u32[]{:S(2)}, u32[]{:S(2)}) collective-permute-start(bf16[2,128,256]{2,1,0:T(8,128)(2,1)S(1)} %get-tuple-element.34), channel_id=1, source_target_pairs={{0,4},{4,0},{8,12},{12,8},{1,5},{5,1},{9,13},{13,9},{2,6},{6,2},{1... | collective-permute-start | bytes 393224 | tf_op jit(solution)/shard_map/ppermute | solution.py:464

commit v13 on v12

--- a/solution.py
+++ b/solution.py
@@ -15,9 +15,9 @@
 F32 = jnp.float32
 BF16 = jnp.bfloat16
 PAIR = 2
-FAR = 3
 VMEM_BYTES = 63 * 1024 * 1024
-GROUP_BYTES = 53 * 1024 * 1024
+GROUP_BYTES = 55 * 1024 * 1024
+OWN_BYTES = 53 * 1024 * 1024
 ANYWHERE = pl.BlockSpec(memory_space=pl.ANY)
 
 
@@ -216,16 +216,13 @@
             found = found + (resp_prompt[me * z.count + i] == prompt).astype(jnp.int32)
 
 
-def prompt_total(z, me, prompt, resp_prompt, tails, far_rewards):
+def prompt_total(z, prompt, tails):
     sums = jnp.zeros((1, z.width), F32)
-    for s in range(tails.shape[0]):
+    for s in range(z.n_dp):
         tail = tails[s].astype(F32)
         sums += tail[0:1] + tail[1:2] + tail[2:3]
     lane = lax.broadcasted_iota(jnp.int32, sums.shape, 1)
-    total = jnp.sum(jnp.where(lane == prompt, sums, 0.0))
-    for i in range(z.count):
-        total += jnp.where(resp_prompt[(me ^ FAR) * z.count + i] == prompt, far_rewards[i], 0.0)
-    return total
+    return jnp.sum(jnp.where(lane == prompt, sums, 0.0))
 
 
 def reward_factor(z, reward, total, length):
@@ -265,13 +262,6 @@
     last.wait()
 
 
-def tail_copies(z, payloads, tails, sems):
-    return [
-        pltpu.make_async_copy(payload.at[pl.ds(2 * z.prefix_len, TAIL)], tails.at[n], sems.at[n])
-        for n, payload in enumerate(payloads)
-    ]
-
-
 def row_copies(here, there, at_here, at_there, sems):
     (q0, og0, kv0), (q1, og1, kv1) = here, there
     return (
@@ -292,15 +282,14 @@
     ]
 
 
-def sort_kernel(z, ahead, resp_prompt_hbm, q_hbm, og_hbm, kv_hbm, both_out, kv_out, *scratch):
+def sort_kernel(z, resp_prompt_hbm, q_hbm, og_hbm, kv_hbm, both_out, kv_out, *scratch):
     resp_prompt, order, q, og, kv, sem_small, sem_in, sem_out = scratch
     me = lax.axis_index("dp")
     small = pltpu.make_async_copy(resp_prompt_hbm, resp_prompt, sem_small)
     small.start()
     small.wait()
-    find_responses(z, me, ahead, resp_prompt, order)
+    find_responses(z, me, range(z.n_dp), resp_prompt, order)
     held, in_order = (q, og, kv), (both_out.at[0], both_out.at[1], kv_out)
-    slots = range(len(ahead) * z.slots)
 
     def copies_in(slot):
         return row_copies(
@@ -311,72 +300,60 @@
         rows = token_rows(z, slot)
         return row_copies(held, in_order, rows, rows, sem_out.at[slot])
 
-    for slot in slots:
+    for slot in range(z.count):
         for copy in copies_in(slot):
             copy.start()
-    for slot in slots:
+    for slot in range(z.count):
         for copy in copies_in(slot):
             copy.wait()
         for copy in copies_out(slot):
             copy.start()
-    for slot in slots:
+    for slot in range(z.count):
         for copy in copies_out(slot):
             copy.wait()
 
 
-def group_kernel(z, turns, ahead, n_come, aliased, *refs):
-    small_hbm, given, tail_hbm = refs[:4], refs[4:7], refs[7 : 7 + FAR]
-    refs = refs[7 + FAR :]
-    prompts, refs = refs[: len(turns)], refs[len(turns) :]
-    come_hbm, refs = refs[:n_come], refs[n_come:]
-    if ahead is not None:
-        (both, kv_ordered), refs = refs[:2], refs[2:]
-    (q_out, self_out), refs = refs[aliased : aliased + 2], refs[aliased + 2 :]
-    grads_out, refs = refs[: len(turns)], refs[len(turns) :]
-    (resp_prompt, resp_len, rewards, far_rewards, order, lens, factors, q, og, kv, prefix, tails, come, acc, out, own,
-     grads, sem_small, sem_tails, sem_prefix, sem_in, sem_out, sem_grads, sem_first) = refs
+def group_kernel(z, turns, n_come, aliased, *refs):
+    small_hbm, (both, kv_hbm, everyone), refs = refs[:3], refs[3:6], refs[6:]
+    come_hbm, refs = refs[:n_come], refs[n_come + aliased :]
+    (q_out, self_out), grads_out, refs = refs[:2], refs[2 : 2 + len(turns)], refs[2 + len(turns) :]
+    (resp_prompt, resp_len, rewards, order, lens, factors, q, og, kv, prefix, tails, come, acc, out, own,
+     grads, sem_small, sem_late, sem_prefix, sem_in, sem_out, sem_grads) = refs
     me = lax.axis_index("dp")
     n_slots = len(turns) * z.slots
     span = z.slots * z.tokens
 
     small = [
         pltpu.make_async_copy(src, dst, sem_small.at[n])
-        for n, (src, dst) in enumerate(zip(small_hbm, (resp_prompt, resp_len, rewards, far_rewards)))
+        for n, (src, dst) in enumerate(zip(small_hbm, (resp_prompt, resp_len, rewards)))
     ]
-    first_rows = ()
-    if ahead is not None:
-        first_rows = row_copies(
-            (both.at[0], both.at[1], kv_ordered), (q, og, kv), pl.ds(ahead * span, span), pl.ds(0, span), sem_first
+    late = [pltpu.make_async_copy(everyone.at[:, pl.ds(2 * z.prefix_len, TAIL)], tails, sem_late.at[0])]
+    late += [pltpu.make_async_copy(src, come, sem_late.at[1]) for src in come_hbm]
+    groups_in = []
+    for t, turn in enumerate(turns):
+        copies = list(
+            row_copies(
+                (both.at[0], both.at[1], kv_hbm),
+                (q, og, kv),
+                pl.ds(turn * span, span),
+                pl.ds(t * span, span),
+                sem_in.at[t],
+            )
         )
-    prefix_copies = [
-        pltpu.make_async_copy(
-            prompts[t].at[pl.ds(n * z.prefix_len, z.prefix_len)], prefix.at[t, n], sem_prefix.at[t, n]
-        )
-        for t in range(len(turns))
-        for n in range(2)
-    ]
-    late = tail_copies(z, tail_hbm, tails, sem_tails)
-    late += [pltpu.make_async_copy(src, come, sem_grads.at[0]) for src in come_hbm]
-    for copy in [*small, *first_rows, *prefix_copies, *late]:
+        copies += [
+            pltpu.make_async_copy(
+                everyone.at[me ^ turn, pl.ds(n * z.prefix_len, z.prefix_len)], prefix.at[t, n], sem_prefix.at[t, n]
+            )
+            for n in range(2)
+        ]
+        groups_in.append(copies)
+    for copy in [*small, *late, *sum(groups_in, [])]:
         copy.start()
-    small[0].wait()
+    for copy in small + late:
+        copy.wait()
     find_responses(z, me, turns, resp_prompt, order)
-
-    def copies_in(slot):
-        return row_copies(
-            given, (q, og, kv), token_rows(z, order[slot]), token_rows(z, slot), sem_in.at[slot]
-        )
-
-    def copies_out(slot):
-        return result_copies(out, own, q_out, self_out, slot, token_rows(z, order[slot]), sem_out)
-
-    for slot in range(0 if ahead is None else z.slots, n_slots):
-        for copy in copies_in(slot):
-            copy.start()
-    for copy in small[1:] + late:
-        copy.wait()
     for t, turn in enumerate(turns):
-        total = prompt_total(z, me, me ^ turn, resp_prompt, tails, far_rewards)
+        total = prompt_total(z, me ^ turn, tails)
         for slot in range(t * z.slots, (t + 1) * z.slots):
             i = order[slot]
             lens[slot] = resp_len[i]
@@ -385,28 +362,18 @@
         acc[0] = come[...].astype(F32)
     else:
         acc[...] = jnp.zeros(acc.shape, F32)
-    for copy in prefix_copies:
-        copy.wait()
+
+    def copies_out(slot):
+        return result_copies(out, own, q_out, self_out, slot, token_rows(z, order[slot]), sem_out)
 
     def step(t, _):
         slots = [t * z.slots + n for n in range(z.slots)]
-
-        def wait_for_slots():
-            for slot in slots:
-                for copy in copies_in(slot):
+        for n, copies in enumerate(groups_in):
+
+            @pl.when(t == n)
+            def _():
+                for copy in copies:
                     copy.wait()
-
-        if ahead is None:
-            wait_for_slots()
-        else:
-
-            @pl.when(t == 0)
-            def _():
-                for copy in first_rows:
-                    copy.wait()
-
-            if len(turns) > 1:
-                pl.when(t > 0)(wait_for_slots)
 
         def sink(_, cols, key_grad, value_grad):
             acc[t, 0, :, cols] += key_grad
@@ -458,49 +425,40 @@
         name="pack",
     )(prompt_kv, rewards, resp_prompt)
 
-    assert n_dp == FAR + 1
+    assert n_dp & (n_dp - 1) == 0
 
     def swap(x, s):
         return lax.ppermute(x, "dp", [(i, i ^ s) for i in range(n_dp)])
 
-    payloads = {0: payload, 2: swap(payload, 2), 1: swap(payload, 1)}
-    tails = [payloads[s] for s in range(FAR)]
     small = (resp_prompt, resp_len, rewards)
-    far_rewards = swap(rewards, FAR)
-    smem = [pltpu.SMEM(x.shape, x.dtype) for x in (*small, rewards)]
+    smem = [pltpu.SMEM(x.shape, x.dtype) for x in small]
     slots = z.slots
-
-    given = (resp_q, out_grad, resp_kv)
-    n_ahead = 2 * slots * z.tokens
+    everyone = lax.all_gather(payload, "dp")
     in_order = pl.pallas_call(
-        functools.partial(sort_kernel, z, (2, FAR)),
-        out_shape=[shape((2, n_ahead, z.lanes), BF16), shape((2, n_ahead, z.width), BF16)],
+        functools.partial(sort_kernel, z),
+        out_shape=[shape((2,) + resp_q.shape, BF16), shape(resp_kv.shape, BF16)],
         in_specs=[ANYWHERE] * 4,
         out_specs=[ANYWHERE] * 2,
         scratch_shapes=[
             smem[0],
-            pltpu.SMEM((2 * slots + 1,), jnp.int32),
-            pltpu.VMEM((n_ahead, z.lanes), BF16),
-            pltpu.VMEM((n_ahead, z.lanes), BF16),
-            pltpu.VMEM((2, n_ahead, z.width), BF16),
+            pltpu.SMEM((z.count + 1,), jnp.int32),
+            pltpu.VMEM(resp_q.shape, BF16),
+            pltpu.VMEM(resp_q.shape, BF16),
+            pltpu.VMEM(resp_kv.shape, BF16),
             pltpu.SemaphoreType.DMA,
-            pltpu.SemaphoreType.DMA((2 * slots, 3)),
-            pltpu.SemaphoreType.DMA((2 * slots, 3)),
+            pltpu.SemaphoreType.DMA((z.count, 3)),
+            pltpu.SemaphoreType.DMA((z.count, 3)),
         ],
         compiler_params=params,
         cost_estimate=cost,
         name="sort_rows",
-    )(resp_prompt, *given)
-    onward, far_rewards, *in_order = lax.optimization_barrier((payloads[2], far_rewards, *in_order))
-    payloads[FAR] = swap(onward, 1)
-
-    def grads_of(turns, ahead, written, come=(), kind=BF16):
+    )(resp_prompt, resp_q, out_grad, resp_kv)
+
+    def grads_of(turns, written, come=(), kind=BF16):
         n_slots, n_turns = len(turns) * slots, len(turns)
-        rows = () if ahead is None else in_order
-        prompts = [payloads[turn] for turn in turns]
-        operands = [*small, far_rewards, *given, *tails, *prompts, *come, *rows, *written]
+        operands = [*small, *in_order, everyone, *come, *written]
         return pl.pallas_call(
-            functools.partial(group_kernel, z, turns, ahead, len(come), len(written)),
+            functools.partial(group_kernel, z, turns, len(come), len(written)),
             out_shape=[shape(resp_q.shape, BF16), shape(resp_kv.shape, BF16)] + [shape(one, kind)] * n_turns,
             in_specs=[ANYWHERE] * len(operands),
             out_specs=[ANYWHERE] * (2 + n_turns),
@@ -514,30 +472,29 @@
                 pltpu.VMEM((n_slots * z.tokens, z.lanes), BF16),
                 pltpu.VMEM((2, n_slots * z.tokens, z.width), BF16),
                 pltpu.VMEM((n_turns,) + one, BF16),
-                pltpu.VMEM((FAR, TAIL, z.width), BF16),
+                pltpu.VMEM((n_dp, TAIL, z.width), BF16),
                 pltpu.VMEM(one, BF16),
                 pltpu.VMEM((n_turns,) + one, F32),
                 pltpu.VMEM((n_slots, z.tokens, z.lanes), BF16),
                 pltpu.VMEM((n_slots, 2, z.tokens, z.width), BF16),
                 pltpu.VMEM((n_turns,) + one, kind),
                 pltpu.SemaphoreType.DMA((len(smem),)),
-                pltpu.SemaphoreType.DMA((FAR,)),
+                pltpu.SemaphoreType.DMA((2,)),
                 pltpu.SemaphoreType.DMA((n_turns, 2)),
-                pltpu.SemaphoreType.DMA((n_slots, 3)),
+                pltpu.SemaphoreType.DMA((n_turns, 3)),
                 pltpu.SemaphoreType.DMA((n_slots, 2)),
                 pltpu.SemaphoreType.DMA((n_turns,)),
-                pltpu.SemaphoreType.DMA((3,)),
             ],
-            compiler_params=pltpu.CompilerParams(vmem_limit_bytes=GROUP_BYTES),
+            compiler_params=pltpu.CompilerParams(vmem_limit_bytes=GROUP_BYTES if turns[0] else OWN_BYTES),
             cost_estimate=cost,
             name="group_grads" if turns[0] else "own_grads",
         )(*operands)
 
-    *written, for_2 = grads_of((2,), 0, ())
+    *written, for_2 = grads_of((2,), ())
     come = [swap(for_2, 2)]
-    *written, for_far, for_1 = grads_of((FAR, 1), 1, written)
-    last = [swap(for_far, FAR), swap(for_1, 1)]
-    q_out, self_out, summed = grads_of((0,), None, written, come, F32)
+    *written, for_far, for_1 = grads_of((3, 1), written)
+    last = [swap(for_far, 3), swap(for_1, 1)]
+    q_out, self_out, summed = grads_of((0,), written, come, F32)
     prefix_out = (summed + sum(part.astype(F32) for part in last)).astype(BF16)
     return (q_out, self_out, prefix_out)
 

time: 37.1 us -> 49.9 us (1.35)
  blocking collectives: 0 us -> 19.6 us
  starting transfers between devices: 10.8 us -> 3.61 us
  Pallas kernels: 21 us -> 23.6 us
  waiting for transfers between devices: 3.72 us -> 1.36 us
    all_gather x0 -> x1, blocking collectives: none -> 19.6 us  [near_shards(): everyone = lax.all_gather(payload, 'dp')]
    ppermute x7 -> x3, starting transfers between devices: 10.8 us -> 3.61 us  [swap(): return lax.ppermute(x, 'dp', [(i, i ^ s) for i in range(n_dp)])]
    pallas_call x4, Pallas kernels: 19.4 us -> 22 us  [the longest x3 15.2 us: grads_of(): pl.pallas_call(functools.partial(group_kernel, z, turns, len(come), len(w...]
    ppermute x7 -> x3, waiting for transfers between devices: 3.72 us -> 1.36 us  [swap(): return lax.ppermute(x, 'dp', [(i, i ^ s) for i in range(n_dp)])]
  transfers between devices with their start and end apart: 7 -> 3, of which waited for: 4 -> 2; matrix products, arithmetic and copies ran while one was open for 0% -> 0% of each run, Pallas kernels for 53% -> 22%
where the time goes in v13:
time: 49.9 us; the launch traced here: 49.6 us
  Pallas kernels  23.6 us (47%)
  blocking collectives  19.6 us (39%)
  starting transfers between devices  3.61 us (7%)
  waiting for transfers between devices  1.36 us (3%)
  other arithmetic  0.7 us (1%)
  between operations  0.7 us (1%)
    all_gather x1, blocking collectives, near_shards(): everyone = lax.all_gather(payload, 'dp')  19.6 us
    pallas_call x3, Pallas kernels, grads_of(): pl.pallas_call(functools.partial(group_kernel, z, turns, len(come), len(w...  15.2 us
    pallas_call x1, Pallas kernels, near_shards(): pl.pallas_call(functools.partial(sort_kernel, z), out_shape=[shape((2,) +...  6.84 us
    ppermute x3, starting transfers between devices, swap(): return lax.ppermute(x, 'dp', [(i, i ^ s) for i in range(n_dp)])  3.61 us
    pallas_call x1, Pallas kernels, near_shards(): pl.pallas_call(functools.partial(pack_kernel, z), out_shape=jax.ShapeDtyp...  1.57 us
    ppermute x3, waiting for transfers between devices, swap(): return lax.ppermute(x, 'dp', [(i, i ^ s) for i in range(n_dp)])  1.36 us
  transfers between devices with their start and end apart: 3, of which 2 were waited for; matrix products, arithmetic and copies ran while one was open for 0% of the time, Pallas kernels for 22%

profile of v13, /device:TPU:0, one launch (start us, length us, event | category | flops | bytes accessed | tf_op | source)
XLA Modules:
  0.0 49.6 jit_solution(10865490087960107485)
XLA Ops:
  0.6 1.6 %pack.1 = bf16[272,256]{1,0:T(8,128)(2,1)} custom-call(bf16[2,128,256]{2,1,0:T(8,128)(2,1)} %prompt_hbm.1, f32[16]{0:T(128)} %refs_2_.5, s32[64]{0:T(128)} %refs_0_.5), custom_call_target="tpu_custom_call" | custom-call | tf_op jit(solution)/shard_map/pack/pallas_call | solution.py:413
  2.2 19.6 %all-gather = bf16[1088,256]{1,0:T(8,128)(2,1)} all-gather(bf16[272,256]{1,0:T(8,128)(2,1)} %pack.1), channel_id=2, replica_groups=mesh['groups'=2,'dp'=4,'tensor'=4] {'dp'}, dimensions={0}, use_global_device_ids=true | all-gather | bytes 696320 | tf_op jit(solution)/shard_map/all_gather | solution.py:436
  21.8 6.8 %sort_rows.1 = (bf16[2,1024,1280]{2,1,0:T(8,128)(2,1)}, bf16[2,1024,256]{2,1,0:T(8,128)(2,1)}) custom-call(s32[64]{0:T(128)} %refs_0_.5, bf16[1024,1280]{1,0:T(8,128)(2,1)} %q_hbm.1, bf16[1024,1280]{1,0:T(8,128)(2,1)} %og_hbm.1, bf16[2,1024,256]{2,1,0:T(8,128)(2,1)} %kv_hbm.1), custom_call_target="tpu_custom_call" | custom-call | tf_op jit(solution)/shard_map/sort_rows/pallas_call | solution.py:437
  28.7 4.2 %group_grads.2 = (bf16[1024,1280]{1,0:T(8,128)(2,1)}, bf16[2,1024,256]{2,1,0:T(8,128)(2,1)}, bf16[2,128,256]{2,1,0:T(8,128)(2,1)}) custom-call(s32[64]{0:T(128)} %refs_0_.5, s32[16]{0:T(128)} %refs_1_.5, f32[16]{0:T(128)} %refs_2_.5, bf16[2,1024,1280]{2,1,0:T(8,128)(2,1)} %get-tuple-element.15.refs_3_, bf16[2,1024,256]{2,1,0:T(8,128)(2,1)} %get-tuple-element.16.refs_4_, ...), custom_call_target="tpu_custom_call" | custom-call | tf_op jit(solution)/shard_map/group_grads/pallas_call | solution.py:460
  32.9 0.8 %collective-permute-start = (bf16[2,128,256]{2,1,0:T(8,128)(2,1)}, bf16[2,128,256]{2,1,0:T(8,128)(2,1)S(1)}, u32[]{:S(2)}, u32[]{:S(2)}) collective-permute-start(bf16[2,128,256]{2,1,0:T(8,128)(2,1)} %get-tuple-element.17), channel_id=1, source_target_pairs={{0,8},{4,12},{8,0},{12,4},{1,9},{5,13},{9,1},{13,5},{2,10},{6,14},... | collective-permute-start | bytes 393224 | tf_op jit(solution)/shard_map/ppermute | solution.py:431
  33.7 0.0 copy-start
  33.7 0.0 copy-start.1
  33.7 0.0 copy-start.2
  33.7 0.0 copy-start.3
  33.7 6.7 %group_grads.3 = (bf16[1024,1280]{1,0:T(8,128)(2,1)}, bf16[2,1024,256]{2,1,0:T(8,128)(2,1)}, bf16[2,128,256]{2,1,0:T(8,128)(2,1)}, bf16[2,128,256]{2,1,0:T(8,128)(2,1)}) custom-call(s32[64]{0:T(128)} %refs_0_.5, s32[16]{0:T(128)} %refs_1_.5, f32[16]{0:T(128)} %refs_2_.5, ...), custom_call_target="tpu_custom_call", output_to_operand_aliasing={{0}: (6, {}), {1}: (7, {})} | custom-call | tf_op jit(solution)/shard_map/group_grads/pallas_call | solution.py:460
  40.4 2.0 %collective-permute-start.1 = (bf16[2,128,256]{2,1,0:T(8,128)(2,1)}, bf16[2,128,256]{2,1,0:T(8,128)(2,1)S(1)}, u32[]{:S(2)}, u32[]{:S(2)}) collective-permute-start(bf16[2,128,256]{2,1,0:T(8,128)(2,1)} %get-tuple-element.25), channel_id=1, source_target_pairs={{0,12},{4,8},{8,4},{12,0},{1,13},{5,9},{9,5},{13,1},{2,14},{6,10},... | collective-permute-start | bytes 393224 | tf_op jit(solution)/shard_map/ppermute | solution.py:431
  42.3 0.8 %collective-permute-start.2 = (bf16[2,128,256]{2,1,0:T(8,128)(2,1)}, bf16[2,128,256]{2,1,0:T(8,128)(2,1)S(1)}, u32[]{:S(2)}, u32[]{:S(2)}) collective-permute-start(bf16[2,128,256]{2,1,0:T(8,128)(2,1)} %get-tuple-element.26), channel_id=1, source_target_pairs={{0,4},{4,0},{8,12},{12,8},{1,5},{5,1},{9,13},{13,9},{2,6},{6,2},{1... | collective-permute-start | bytes 393224 | tf_op jit(solution)/shard_map/ppermute | solution.py:431
  43.2 0.0 collective-permute-done.refs_6_
  43.2 0.0 copy-done
  43.2 0.0 copy-done.1
  43.2 0.0 copy-done.2
  43.2 0.0 copy-done.3
  43.2 4.3 %own_grads.1 = (bf16[1024,1280]{1,0:T(8,128)(2,1)}, bf16[2,1024,256]{2,1,0:T(8,128)(2,1)}, f32[2,128,256]{2,1,0:T(8,128)S(1)}) custom-call(s32[64]{0:T(128)S(1)} %copy-done.1, s32[16]{0:T(128)S(1)} %copy-done.3, f32[16]{0:T(128)S(1)} %copy-done.2, bf16[2,1024,1280]{2,1,0:T(8,128)(2,1)} %get-tuple-element.15.refs_3_, ...), custom_call_target="tpu_custom_call", output_to_operand_aliasing={{0}: (7, {}), {1}: (8, {})} | custom-call | tf_op jit(solution)/shard_map/own_grads/pallas_call | solution.py:460
  47.5 0.1 collective-permute-done.1
  47.6 1.3 %collective-permute-done.2 = bf16[2,128,256]{2,1,0:T(8,128)(2,1)S(1)} collective-permute-done((bf16[2,128,256]{2,1,0:T(8,128)(2,1)}, bf16[2,128,256]{2,1,0:T(8,128)(2,1)S(1)}, u32[]{:S(2)}, u32[]{:S(2)}) %collective-permute-start.2) | collective-permute-done | bytes 131104 | tf_op jit(solution)/shard_map/ppermute | solution.py:431
  48.9 0.7 %add_convert_fusion = bf16[2,128,256]{2,1,0:T(8,128)(2,1)} fusion(f32[2,128,256]{2,1,0:T(8,128)S(1)} %get-tuple-element.24, bf16[2,128,256]{2,1,0:T(8,128)(2,1)S(1)} %collective-permute-done.2, bf16[2,128,256]{2,1,0:T(8,128)(2,1)S(1)} %collective-permute-done.1), kind=kLoop, calls=%fused_computation | loop fusion | flops 327680 | bytes 655360 | tf_op jit(solution)/shard_map/convert_element_type | solution.py:498
Async XLA Ops:
  32.9 10.3 %collective-permute-start = (bf16[2,128,256]{2,1,0:T(8,128)(2,1)}, bf16[2,128,256]{2,1,0:T(8,128)(2,1)S(1)}, u32[]{:S(2)}, u32[]{:S(2)}) collective-permute-start(bf16[2,128,256]{2,1,0:T(8,128)(2,1)} %get-tuple-element.17), channel_id=1, source_target_pairs={{0,8},{4,12},{8,0},{12,4},{1,9},{5,13},{9,1},{13,5},{2,10},{6,14},... | collective-permute-start | bytes 393224 | tf_op jit(solution)/shard_map/ppermute | solution.py:431
  33.7 9.5 %copy-start = (bf16[1088,256]{1,0:T(8,128)(2,1)S(1)}, bf16[1088,256]{1,0:T(8,128)(2,1)}, u32[]{:S(2)}) copy-start(bf16[1088,256]{1,0:T(8,128)(2,1)} %all-gather) | copy-start | bytes 1671172
  33.7 9.5 %copy-start.1 = (s32[64]{0:T(128)S(1)}, s32[64]{0:T(128)}, u32[]{:S(2)}) copy-start(s32[64]{0:T(128)} %refs_0_.5) | copy-start | bytes 772
  33.7 9.5 %copy-start.2 = (f32[16]{0:T(128)S(1)}, f32[16]{0:T(128)}, u32[]{:S(2)}) copy-start(f32[16]{0:T(128)} %refs_2_.5) | copy-start | bytes 196
  33.7 9.5 %copy-start.3 = (s32[16]{0:T(128)S(1)}, s32[16]{0:T(128)}, u32[]{:S(2)}) copy-start(s32[16]{0:T(128)} %refs_1_.5) | copy-start | bytes 196
  40.4 7.2 %collective-permute-start.1 = (bf16[2,128,256]{2,1,0:T(8,128)(2,1)}, bf16[2,128,256]{2,1,0:T(8,128)(2,1)S(1)}, u32[]{:S(2)}, u32[]{:S(2)}) collective-permute-start(bf16[2,128,256]{2,1,0:T(8,128)(2,1)} %get-tuple-element.25), channel_id=1, source_target_pairs={{0,12},{4,8},{8,4},{12,0},{1,13},{5,9},{9,5},{13,1},{2,14},{6,10},... | collective-permute-start | bytes 393224 | tf_op jit(solution)/shard_map/ppermute | solution.py:431
  42.3 6.6 %collective-permute-start.2 = (bf16[2,128,256]{2,1,0:T(8,128)(2,1)}, bf16[2,128,256]{2,1,0:T(8,128)(2,1)S(1)}, u32[]{:S(2)}, u32[]{:S(2)}) collective-permute-start(bf16[2,128,256]{2,1,0:T(8,128)(2,1)} %get-tuple-element.26), channel_id=1, source_target_pairs={{0,4},{4,0},{8,12},{12,8},{1,5},{5,1},{9,13},{13,9},{2,6},{6,2},{1... | collective-permute-start | bytes 393224 | tf_op jit(solution)/shard_map/ppermute | solution.py:431

commit v14 on v10

--- a/solution.py
+++ b/solution.py
@@ -571,10 +571,9 @@
     onward, per_resp, far_rewards = lax.optimization_barrier((payloads[2], per_resp, far_rewards))
     payloads[FAR] = swap(onward, 1)
     *written, for_2, for_1 = grads_of((2, 1), False, slots // PAIR, 0, in_order, written)
-    come = [swap(for_2, 2)]
+    come = [swap(for_2, 2), swap(for_1, 1)]
     *written, for_far = grads_of((FAR,), False, slots // PAIR, 1, in_order, written)
-    for_far, for_1 = lax.optimization_barrier((for_far, for_1))
-    last = [swap(for_far, FAR), swap(for_1, 1)]
+    last = swap(for_far, FAR)
     operands = [*small, far_rewards, *tails, per_resp, *come, *written]
     q_out, self_out, own_grads = pl.pallas_call(
         functools.partial(finish_kernel, z, len(tails), len(come)),
@@ -601,7 +600,7 @@
         cost_estimate=cost,
         name="finish_own",
     )(*operands)
-    prefix_out = (own_grads + sum(part.astype(F32) for part in last)).astype(BF16)
+    prefix_out = (own_grads + last.astype(F32)).astype(BF16)
     return (q_out, self_out, prefix_out)
 
 

time: 37.2 us -> 37.3 us (level)
  starting transfers between devices: 11.2 us -> 12.1 us
  waiting for transfers between devices: 3.48 us -> 2.68 us
    ppermute x7, starting transfers between devices: 11.2 us -> 12.1 us  [swap(): return lax.ppermute(x, 'dp', [(i, i ^ s) for i in range(n_dp)])]
    ppermute x7, waiting for transfers between devices: 3.48 us -> 2.68 us  [swap(): return lax.ppermute(x, 'dp', [(i, i ^ s) for i in range(n_dp)])]
  transfers between devices with their start and end apart: 7 -> 7, of which waited for: 1 -> 2; matrix products, arithmetic and copies ran while one was open for 0% -> 0% of each run, Pallas kernels for 52% -> 52%
where the time goes in v14:
time: 37.3 us; the launch traced here: 37 us
  Pallas kernels  20.9 us (56%)
  starting transfers between devices  12.1 us (32%)
  waiting for transfers between devices  2.68 us (7%)
  between operations  0.74 us (2%)
  other arithmetic  0.68 us (2%)
    pallas_call x3, Pallas kernels, grads_of(): pl.pallas_call(functools.partial(group_kernel, z, turns, raw, body, ahead...  16.5 us
    ppermute x7, starting transfers between devices, swap(): return lax.ppermute(x, 'dp', [(i, i ^ s) for i in range(n_dp)])  12.1 us
    pallas_call x1, Pallas kernels, near_shards(): pl.pallas_call(functools.partial(finish_kernel, z, len(tails), len(come))...  2.84 us
    ppermute x7, waiting for transfers between devices, swap(): return lax.ppermute(x, 'dp', [(i, i ^ s) for i in range(n_dp)])  2.68 us
    pallas_call x1, Pallas kernels, near_shards(): pl.pallas_call(functools.partial(pack_kernel, z), out_shape=jax.ShapeDtyp...  1.56 us
  transfers between devices with their start and end apart: 7, of which 2 were waited for; matrix products, arithmetic and copies ran while one was open for 0% of the time, Pallas kernels for 52%

profile of v14, /device:TPU:0, one launch (start us, length us, event | category | flops | bytes accessed | tf_op | source)
XLA Modules:
  0.0 37.0 jit_solution(1453773345076361857)
XLA Ops:
  0.6 1.6 %pack.1.refs_7_.refs_4_ = bf16[272,256]{1,0:T(8,128)(2,1)} custom-call(bf16[2,128,256]{2,1,0:T(8,128)(2,1)} %prompt_hbm.1, f32[16]{0:T(128)} %refs_2_.7, s32[64]{0:T(128)} %refs_0_.7), custom_call_target="tpu_custom_call" | custom-call | tf_op jit(solution)/shard_map/pack/pallas_call | solution.py:498
  2.2 0.0 copy-start
  2.2 0.0 copy-start.2
  2.2 0.0 copy-start.3
  2.2 0.0 copy-start.4
  2.2 4.1 %collective-permute-start = (bf16[272,256]{1,0:T(8,128)(2,1)}, bf16[272,256]{1,0:T(8,128)(2,1)S(1)}, u32[]{:S(2)}, u32[]{:S(2)}) collective-permute-start(bf16[272,256]{1,0:T(8,128)(2,1)} %pack.1.refs_7_.refs_4_), channel_id=1, source_target_pairs={{0,8},{4,12},{8,0},{12,4},{1,9},{5,13},{9,1},{13,5},{2,10},{6,14},... | collective-permute-start | bytes 417800 | tf_op jit(solution)/shard_map/ppermute | solution.py:516
  6.3 1.3 %collective-permute-start.1 = (f32[16]{0:T(128)}, f32[16]{0:T(128)S(1)}, u32[]{:S(2)}, u32[]{:S(2)}) collective-permute-start(f32[16]{0:T(128)} %refs_2_.7), channel_id=1, source_target_pairs={{0,12},{4,8},{8,4},{12,0},{1,13},{5,9},{9,5},{13,1},{2,14},{6,10},... | collective-permute-start | bytes 200 | tf_op jit(solution)/shard_map/ppermute | solution.py:516
  7.7 0.2 collective-permute-start.2
  7.9 5.8 %raw_grads.1 = (bf16[1024,1280]{1,0:T(8,128)(2,1)}, bf16[2,1024,256]{2,1,0:T(8,128)(2,1)}, bf16[4,2,128,256]{3,2,1,0:T(8,128)(2,1)}, bf16[2,512,1280]{2,1,0:T(8,128)(2,1)}, bf16[2,512,256]{2,1,0:T(8,128)(2,1)}) custom-call(s32[64]{0:T(128)} %refs_0_.7, s32[16]{0:T(128)} %refs_1_.7, f32[16]{0:T(128)} %refs_2_.7, f32[16]{0:T(128)} %refs_2_.7, ...), custom_call_target="tpu_custom_call" | custom-call | tf_op jit(solution)/shard_map/raw_grads/pallas_call | solution.py:535
  13.8 0.0 collective-permute-done.1.refs_3_
  13.8 0.0 collective-permute-done.refs_9_.refs_10_.refs_6_
  13.8 1.9 %collective-permute-start.5 = (bf16[272,256]{1,0:T(8,128)(2,1)S(1)}, bf16[272,256]{1,0:T(8,128)(2,1)S(1)}, u32[]{:S(2)}, u32[]{:S(2)}) collective-permute-start(bf16[272,256]{1,0:T(8,128)(2,1)S(1)} %collective-permute-done.refs_9_.refs_10_.refs_6_), channel_id=1, source_target_pairs={{0,4},{4,0},{8,12},{12,8},{1,5},{5,1},{9,13},{13,9},{2,6},{6,2},{1... | collective-permute-start | bytes 417800 | tf_op jit(solution)/shard_map/ppermute | solution.py:516
  15.6 0.0 collective-permute-done.2.refs_8_.refs_11_.refs_5_
  15.7 0.0 copy-done
  15.7 0.0 copy-done.2
  15.7 0.0 copy-done.3
  15.7 0.0 copy-done.4
  15.7 6.3 %group_grads.2 = (bf16[1024,1280]{1,0:T(8,128)(2,1)}, bf16[2,1024,256]{2,1,0:T(8,128)(2,1)}, bf16[2,128,256]{2,1,0:T(8,128)(2,1)S(1)}, bf16[2,128,256]{2,1,0:T(8,128)(2,1)S(1)}) custom-call(s32[64]{0:T(128)S(1)} %copy-done.3, s32[16]{0:T(128)S(1)} %copy-done.4, f32[16]{0:T(128)S(1)} %copy-done.2, ...), custom_call_target="tpu_custom_call", output_to_operand_aliasing={{0}: (14, {}), {1}: (15, {})} | custom-call | tf_op jit(solution)/shard_map/group_grads/pallas_call | solution.py:535
  22.0 1.9 %collective-permute-start.3 = (bf16[2,128,256]{2,1,0:T(8,128)(2,1)S(1)}, bf16[2,128,256]{2,1,0:T(8,128)(2,1)S(1)}, u32[]{:S(2)}, u32[]{:S(2)}) collective-permute-start(bf16[2,128,256]{2,1,0:T(8,128)(2,1)S(1)} %get-tuple-element.28), channel_id=1, source_target_pairs={{0,8},{4,12},{8,0},{12,4},{1,9},{5,13},{9,1},{13,5},{2,10},{6,14},... | collective-permute-start | bytes 393224 | tf_op jit(solution)/shard_map/ppermute | solution.py:516
  23.8 1.2 %collective-permute-start.4 = (bf16[2,128,256]{2,1,0:T(8,128)(2,1)S(1)}, bf16[2,128,256]{2,1,0:T(8,128)(2,1)S(1)}, u32[]{:S(2)}, u32[]{:S(2)}) collective-permute-start(bf16[2,128,256]{2,1,0:T(8,128)(2,1)S(1)} %get-tuple-element.29), channel_id=1, source_target_pairs={{0,4},{4,0},{8,12},{12,8},{1,5},{5,1},{9,13},{13,9},{2,6},{6,2},{1... | collective-permute-start | bytes 393224 | tf_op jit(solution)/shard_map/ppermute | solution.py:516
  25.1 0.0 collective-permute-done.5.refs_10_
  25.1 0.0 copy-start.1
  25.1 4.3 %group_grads.3 = (bf16[1024,1280]{1,0:T(8,128)(2,1)}, bf16[2,1024,256]{2,1,0:T(8,128)(2,1)}, bf16[2,128,256]{2,1,0:T(8,128)(2,1)S(1)}) custom-call(s32[64]{0:T(128)S(1)} %copy-done.3, s32[16]{0:T(128)S(1)} %copy-done.4, f32[16]{0:T(128)S(1)} %copy-done.2, f32[16]{0:T(128)S(1)} %collective-permute-done.1.refs_3_, ...), custom_call_target="tpu_custom_call", output_to_operand_aliasing={{0}: (13, {}), {1}: (14, {})} | custom-call | tf_op jit(solution)/shard_map/group_grads/pallas_call | solution.py:535
  29.4 1.4 %collective-permute-start.6 = (bf16[2,128,256]{2,1,0:T(8,128)(2,1)S(1)}, bf16[2,128,256]{2,1,0:T(8,128)(2,1)S(1)}, u32[]{:S(2)}, u32[]{:S(2)}) collective-permute-start(bf16[2,128,256]{2,1,0:T(8,128)(2,1)S(1)} %get-tuple-element.38), channel_id=1, source_target_pairs={{0,12},{4,8},{8,4},{12,0},{1,13},{5,9},{9,5},{13,1},{2,14},{6,10},... | collective-permute-start | bytes 393224 | tf_op jit(solution)/shard_map/ppermute | solution.py:516
  30.8 0.0 collective-permute-done.3.refs_8_
  30.8 0.5 %collective-permute-done.4.refs_9_ = bf16[2,128,256]{2,1,0:T(8,128)(2,1)S(1)} collective-permute-done((bf16[2,128,256]{2,1,0:T(8,128)(2,1)S(1)}, bf16[2,128,256]{2,1,0:T(8,128)(2,1)S(1)}, u32[]{:S(2)}, u32[]{:S(2)}) %collective-permute-start.4) | collective-permute-done | bytes 131104 | tf_op jit(solution)/shard_map/ppermute | solution.py:516
  31.3 0.0 copy-done.1
  31.3 2.8 %finish_own.1 = (bf16[1024,1280]{1,0:T(8,128)(2,1)}, bf16[2,1024,256]{2,1,0:T(8,128)(2,1)}, f32[2,128,256]{2,1,0:T(8,128)S(1)}) custom-call(s32[64]{0:T(128)S(1)} %copy-done.3, s32[16]{0:T(128)S(1)} %copy-done.4, f32[16]{0:T(128)S(1)} %copy-done.2, f32[16]{0:T(128)S(1)} %collective-permute-done.1.refs_3_, ...), custom_call_target="tpu_custom_call", output_to_operand_aliasing={{0}: (10, {}), {1}: (11, {})} | custom-call | tf_op jit(solution)/shard_map/finish_own/pallas_call | solution.py:578
  34.2 2.2 %collective-permute-done.6 = bf16[2,128,256]{2,1,0:T(8,128)(2,1)S(1)} collective-permute-done((bf16[2,128,256]{2,1,0:T(8,128)(2,1)S(1)}, bf16[2,128,256]{2,1,0:T(8,128)(2,1)S(1)}, u32[]{:S(2)}, u32[]{:S(2)}) %collective-permute-start.6) | collective-permute-done | bytes 131104 | tf_op jit(solution)/shard_map/ppermute | solution.py:516
  36.4 0.7 %add_convert_fusion = bf16[2,128,256]{2,1,0:T(8,128)(2,1)} fusion(f32[2,128,256]{2,1,0:T(8,128)S(1)} %get-tuple-element.37, bf16[2,128,256]{2,1,0:T(8,128)(2,1)S(1)} %collective-permute-done.6), kind=kLoop, calls=%fused_computation | loop fusion | flops 196608 | bytes 524288 | tf_op jit(solution)/shard_map/convert_element_type | solution.py:603
Async XLA Ops:
  2.2 13.5 %copy-start = (bf16[272,256]{1,0:T(8,128)(2,1)S(1)}, bf16[272,256]{1,0:T(8,128)(2,1)}, u32[]{:S(2)}) copy-start(bf16[272,256]{1,0:T(8,128)(2,1)} %pack.1.refs_7_.refs_4_) | copy-start | bytes 417796
  2.2 13.4 %copy-start.2 = (f32[16]{0:T(128)S(1)}, f32[16]{0:T(128)}, u32[]{:S(2)}) copy-start(f32[16]{0:T(128)} %refs_2_.7) | copy-start | bytes 196
  2.2 13.4 %copy-start.3 = (s32[64]{0:T(128)S(1)}, s32[64]{0:T(128)}, u32[]{:S(2)}) copy-start(s32[64]{0:T(128)} %refs_0_.7) | copy-start | bytes 772
  2.2 13.4 %copy-start.4 = (s32[16]{0:T(128)S(1)}, s32[16]{0:T(128)}, u32[]{:S(2)}) copy-start(s32[16]{0:T(128)} %refs_1_.7) | copy-start | bytes 196
  2.2 11.5 %collective-permute-start = (bf16[272,256]{1,0:T(8,128)(2,1)}, bf16[272,256]{1,0:T(8,128)(2,1)S(1)}, u32[]{:S(2)}, u32[]{:S(2)}) collective-permute-start(bf16[272,256]{1,0:T(8,128)(2,1)} %pack.1.refs_7_.refs_4_), channel_id=1, source_target_pairs={{0,8},{4,12},{8,0},{12,4},{1,9},{5,13},{9,1},{13,5},{2,10},{6,14},... | collective-permute-start | bytes 417800 | tf_op jit(solution)/shard_map/ppermute | solution.py:516
  6.3 7.4 %collective-permute-start.1 = (f32[16]{0:T(128)}, f32[16]{0:T(128)S(1)}, u32[]{:S(2)}, u32[]{:S(2)}) collective-permute-start(f32[16]{0:T(128)} %refs_2_.7), channel_id=1, source_target_pairs={{0,12},{4,8},{8,4},{12,0},{1,13},{5,9},{9,5},{13,1},{2,14},{6,10},... | collective-permute-start | bytes 200 | tf_op jit(solution)/shard_map/ppermute | solution.py:516
  7.7 8.0 %collective-permute-start.2 = (bf16[272,256]{1,0:T(8,128)(2,1)}, bf16[272,256]{1,0:T(8,128)(2,1)S(1)}, u32[]{:S(2)}, u32[]{:S(2)}) collective-permute-start(bf16[272,256]{1,0:T(8,128)(2,1)} %pack.1.refs_7_.refs_4_), channel_id=1, source_target_pairs={{0,4},{4,0},{8,12},{12,8},{1,5},{5,1},{9,13},{13,9},{2,6},{6,2},{1... | collective-permute-start | bytes 417800 | tf_op jit(solution)/shard_map/ppermute | solution.py:516
  13.8 11.3 %collective-permute-start.5 = (bf16[272,256]{1,0:T(8,128)(2,1)S(1)}, bf16[272,256]{1,0:T(8,128)(2,1)S(1)}, u32[]{:S(2)}, u32[]{:S(2)}) collective-permute-start(bf16[272,256]{1,0:T(8,128)(2,1)S(1)} %collective-permute-done.refs_9_.refs_10_.refs_6_), channel_id=1, source_target_pairs={{0,4},{4,0},{8,12},{12,8},{1,5},{5,1},{9,13},{13,9},{2,6},{6,2},{1... | collective-permute-start | bytes 417800 | tf_op jit(solution)/shard_map/ppermute | solution.py:516
  22.0 8.9 %collective-permute-start.3 = (bf16[2,128,256]{2,1,0:T(8,128)(2,1)S(1)}, bf16[2,128,256]{2,1,0:T(8,128)(2,1)S(1)}, u32[]{:S(2)}, u32[]{:S(2)}) collective-permute-start(bf16[2,128,256]{2,1,0:T(8,128)(2,1)S(1)} %get-tuple-element.28), channel_id=1, source_target_pairs={{0,8},{4,12},{8,0},{12,4},{1,9},{5,13},{9,1},{13,5},{2,10},{6,14},... | collective-permute-start | bytes 393224 | tf_op jit(solution)/shard_map/ppermute | solution.py:516
  23.8 7.5 %collective-permute-start.4 = (bf16[2,128,256]{2,1,0:T(8,128)(2,1)S(1)}, bf16[2,128,256]{2,1,0:T(8,128)(2,1)S(1)}, u32[]{:S(2)}, u32[]{:S(2)}) collective-permute-start(bf16[2,128,256]{2,1,0:T(8,128)(2,1)S(1)} %get-tuple-element.29), channel_id=1, source_target_pairs={{0,4},{4,0},{8,12},{12,8},{1,5},{5,1},{9,13},{13,9},{2,6},{6,2},{1... | collective-permute-start | bytes 393224 | tf_op jit(solution)/shard_map/ppermute | solution.py:516
  25.1 6.2 %copy-start.1 = (bf16[4,2,128,256]{3,2,1,0:T(8,128)(2,1)S(1)}, bf16[4,2,128,256]{3,2,1,0:T(8,128)(2,1)}, u32[]{:S(2)}) copy-start(bf16[4,2,128,256]{3,2,1,0:T(8,128)(2,1)} %get-tuple-element.23.refs_7_) | copy-start | bytes 1572868
  29.4 6.9 %collective-permute-start.6 = (bf16[2,128,256]{2,1,0:T(8,128)(2,1)S(1)}, bf16[2,128,256]{2,1,0:T(8,128)(2,1)S(1)}, u32[]{:S(2)}, u32[]{:S(2)}) collective-permute-start(bf16[2,128,256]{2,1,0:T(8,128)(2,1)S(1)} %get-tuple-element.38), channel_id=1, source_target_pairs={{0,12},{4,8},{8,4},{12,0},{1,13},{5,9},{9,5},{13,1},{2,14},{6,10},... | collective-permute-start | bytes 393224 | tf_op jit(solution)/shard_map/ppermute | solution.py:516

commit v15 on v11

--- a/solution.py
+++ b/solution.py
@@ -65,12 +65,12 @@
     scale = 1.0 / math.sqrt(HD)
     log_scale = scale * math.log2(math.e)
     whole = group_size - group_size % 2
-    most = max(whole, 2) * tokens
+    most = max([whole, 2, *(len(unit.at) for unit in units)]) * tokens
     assert tokens & (tokens - 1) == 0
-    token = lax.broadcasted_iota(jnp.int32, (1, most), 1) & (tokens - 1)
+    lane = lax.broadcasted_iota(jnp.int32, (1, most), 1)
+    token = lane & (tokens - 1)
     key = lax.broadcasted_iota(jnp.int32, (tokens, most), 0)
     causal = key <= (lax.broadcasted_iota(jnp.int32, (tokens, most), 1) & (tokens - 1))
-    left = lax.broadcasted_iota(jnp.int32, (1, 2 * tokens), 1) < tokens
 
     def columns(index):
         if isinstance(index, int):
@@ -83,17 +83,28 @@
     def rows(ref, c):
         return jnp.concatenate([ref[c.t.at[n], head(c.t.k, h)] for n, h in c.blocks], axis=0)
 
-    def halves(part):
+    def side_lanes(n, lanes):
+        return (lane[:, :lanes] >= n * tokens) & (lane[:, :lanes] < (n + 1) * tokens)
+
+    def by_side(parts):
+        lanes = len(parts) * tokens
+        chosen = parts[0]
+        for n, part in enumerate(parts[1:], 1):
+            chosen = jnp.where(lane[:, :lanes] >= n * tokens, part, chosen)
+        return chosen
+
+    def apart_by_side(part):
         none = jnp.zeros_like(part)
-        return [jnp.where(left, part, none), jnp.where(left, none, part)]
+        lanes = part.shape[1]
+        return [jnp.where(side_lanes(n, lanes), part, none) for n in range(lanes // tokens)]
 
     def over_keys(combine, *parts):
         reduce = jnp.max if combine is jnp.maximum else jnp.sum
         eights = [reduce(part.reshape(-1, 8, part.shape[1]), axis=0) for part in parts]
         return reduce(functools.reduce(combine, eights), axis=0, keepdims=True)
 
-    def own_half(both):
-        return jnp.where(left, both[:tokens], both[tokens:])
+    def own_rows(every):
+        return by_side([every[n * tokens : (n + 1) * tokens] for n in range(every.shape[0] // tokens)])
 
     def rounded(*parts):
         return jnp.concatenate([part.astype(BF16) for part in parts], axis=0)
@@ -102,16 +113,14 @@
     for unit in units:
         t = Bag()
         t.at, t.places, t.k, t.lens, t.factors = unit
-        t.single = len(t.at) == 1
         t.members = range(len(t.at))
-        sides = (0, 0) if t.single else (0, 1)
+        sides = (0, 0) if len(t.at) == 1 else t.members
         t.cols = columns(t.k)
         t.key_p, t.value_p = prefix[0, :, t.cols], prefix[1, :, t.cols]
         t.keys = [kv[0, t.at[n], t.cols] for n in sides]
         t.values = [kv[1, t.at[n], t.cols] for n in sides]
-        t.key_pair = jnp.concatenate(t.keys, axis=0)
-        t.value_pair = jnp.concatenate(t.values, axis=0)
-        t.key_t = jnp.concatenate([t.key_p.T, t.key_pair.T], axis=1)
+        t.key_pt = t.key_p.T
+        t.key_st = [jnp.concatenate(t.keys[n : n + 2], axis=0).T for n in range(0, len(sides), 2)]
         t.prefix_sums = {n: [] for n in t.members}
         t.self_sums = {n: [] for n in t.members}
         mine = []
@@ -130,17 +139,17 @@
         t = c.t
         c.q_rows, c.g_rows = rows(q, c), rows(og, c)
         if c.side is None:
-            key_s, value_s = t.key_pair, t.value_pair
+            keys, values = t.keys, t.values
         else:
-            key_s, value_s = t.keys[c.side], t.values[c.side]
-        c.scores = dot(jnp.concatenate([t.key_p, key_s], axis=0), c.q_rows, NT)
-        c.gw = dot(jnp.concatenate([t.value_p, value_s], axis=0), c.g_rows, NT)
+            keys, values = t.keys[c.side : c.side + 1], t.values[c.side : c.side + 1]
+        c.scores = dot(jnp.concatenate([t.key_p, *keys], axis=0), c.q_rows, NT)
+        c.gw = dot(jnp.concatenate([t.value_p, *values], axis=0), c.g_rows, NT)
 
     def weigh(c):
         scores_p, scores_s = c.scores[:prefix_len], c.scores[prefix_len:]
         c.gw_p, c.gw_s = c.gw[:prefix_len], c.gw[prefix_len:]
         if c.side is None:
-            scores_s, c.gw_s = own_half(scores_s), own_half(c.gw_s)
+            scores_s, c.gw_s = own_rows(scores_s), own_rows(c.gw_s)
         scores_s = jnp.where(causal[:, : scores_s.shape[1]], scores_s, NEG)
         top = over_keys(jnp.maximum, scores_p, scores_s)
         c.e_p = jnp.exp2((scores_p - top) * log_scale)
@@ -148,8 +157,9 @@
         total = over_keys(jnp.add, c.e_p, c.e_s)
         weighted = over_keys(jnp.add, c.e_p * c.gw_p, c.e_s * c.gw_s)
         if c.side is None:
-            length = jnp.where(left, c.t.lens[0], 0 if c.t.single else c.t.lens[1])
-            gain = jnp.where(left, c.t.factors[0], c.t.factors[-1])
+            single = len(c.t.at) == 1
+            length = by_side([c.t.lens[0], 0] if single else c.t.lens)
+            gain = by_side([c.t.factors[0]] * 2 if single else c.t.factors)
         else:
             length, gain = c.t.lens[c.side], c.t.factors[c.side]
         inverse = 1.0 / total
@@ -160,26 +170,28 @@
         w_p, w_s = c.e_p * c.gain, c.e_s * c.gain
         d_p, d_s = w_p * (c.gw_p - c.delta), w_s * (c.gw_s - c.delta)
         if c.side is None:
-            d_s, w_s = halves(d_s), halves(w_s)
+            d_s, w_s = apart_by_side(d_s), apart_by_side(w_s)
             c.d_wide = rounded(d_p, *d_s)
-            c.d_all = rounded(*halves(d_p), *d_s) if apart else c.d_wide
-            c.w_all = rounded(*(halves(w_p) if apart else [w_p]), *w_s)
+            c.d_all = rounded(*apart_by_side(d_p), *d_s) if apart else c.d_wide
+            c.w_all = rounded(*(apart_by_side(w_p) if apart else [w_p]), *w_s)
         else:
             empty = jnp.zeros_like(d_s)
-            c.d_wide = rounded(*([d_p, empty, d_s] if c.side else [d_p, d_s, empty]))
+            c.d_wide = rounded(*([d_p, empty, d_s] if c.side % 2 else [d_p, d_s, empty]))
             c.d_all = rounded(d_p, d_s)
             c.w_all = rounded(w_p, w_s)
 
     def outgoing(c):
         t = c.t
-        q_grad = (dot(t.key_t, c.d_wide, NN) * scale).astype(BF16).T
+        key_st = t.key_st if c.side is None else [t.key_st[c.side // 2]]
+        key_t = jnp.concatenate([t.key_pt, *key_st], axis=1)
+        q_grad = (dot(key_t, c.d_wide, NN) * scale).astype(BF16).T
         kg = dot(c.d_all, c.q_rows, NN)
         vg = dot(c.w_all, c.g_rows, NN)
         targets = t.members if c.side is None else [c.side]
         for place, (n, h) in enumerate(c.blocks):
             if c.side is not None or place < len(targets):
                 out[t.places[n], :, head(t.k, h)] = q_grad[place * tokens : (place + 1) * tokens]
-        many = 2 if c.side is None and apart else 1
+        many = len(c.blocks) if c.side is None and apart else 1
         for place, n in enumerate(targets):
             if place < many:
                 rows_p = slice(place * prefix_len, (place + 1) * prefix_len)
@@ -391,12 +403,11 @@
                 acc[t, 0, :, cols] += key_grad
                 acc[t, 1, :, cols] += value_grad
 
-        units = []
-        for pair in range(pairs_in_body):
-            places = [first + pair * PAIR + n for n in range(PAIR)]
-            at = [token_rows(z, n) for n in places]
-            for k in range(z.kv_heads):
-                units.append(Unit(at, places, k, [lens[n] for n in places], [factors[n] for n in places]))
+        places = [first + n for n in mine]
+        at = [token_rows(z, n) for n in places]
+        units = [
+            Unit(at, places, k, [lens[n] for n in places], [factors[n] for n in places]) for k in range(z.kv_heads)
+        ]
         attend(z, units, q, og, kv, prefix.at[t], out, own, sink, raw)
         for n in mine:
             for copy in copies_out(first + n):
@@ -573,7 +584,8 @@
     *written, for_2 = grads_of((2,), False, slots // PAIR, 0, in_order, written)
     come = [swap(for_2, 2)]
     *written, for_far, for_1 = grads_of((FAR, 1), False, slots // PAIR, 1, in_order, written)
-    last = [swap(for_far, FAR), swap(for_1, 1)]
+    come.append(swap(for_1, 1))
+    last = swap(for_far, FAR)
     operands = [*small, far_rewards, *tails, per_resp, *come, *written]
     q_out, self_out, own_grads = pl.pallas_call(
         functools.partial(finish_kernel, z, len(tails), len(come)),
@@ -600,7 +612,7 @@
         cost_estimate=cost,
         name="finish_own",
     )(*operands)
-    prefix_out = (own_grads + sum(part.astype(F32) for part in last)).astype(BF16)
+    prefix_out = (own_grads + last.astype(F32)).astype(BF16)
     return (q_out, self_out, prefix_out)
 
 

time: 37.2 us -> 38.4 us (1.032)
  starting transfers between devices: 11.2 us -> 12.1 us
  Pallas kernels: 20.8 us -> 21.2 us
    ppermute x7, starting transfers between devices: 11.2 us -> 12.1 us  [swap(): return lax.ppermute(x, 'dp', [(i, i ^ s) for i in range(n_dp)])]
  transfers between devices with their start and end apart: 7 -> 7, of which waited for: 1 -> 1; matrix products, arithmetic and copies ran while one was open for 0% -> 0% of each run, Pallas kernels for 52% -> 51%
where the time goes in v15:
time: 38.4 us; the launch traced here: 38.1 us
  Pallas kernels  21.2 us (55%)
  starting transfers between devices  12.1 us (32%)
  waiting for transfers between devices  3.45 us (9%)
  between operations  0.75 us (2%)
  other arithmetic  0.68 us (2%)
    pallas_call x3, Pallas kernels, grads_of(): pl.pallas_call(functools.partial(group_kernel, z, turns, raw, body, ahead...  16.7 us
    ppermute x7, starting transfers between devices, swap(): return lax.ppermute(x, 'dp', [(i, i ^ s) for i in range(n_dp)])  12.1 us
    ppermute x7, waiting for transfers between devices, swap(): return lax.ppermute(x, 'dp', [(i, i ^ s) for i in range(n_dp)])  3.45 us
    pallas_call x1, Pallas kernels, near_shards(): pl.pallas_call(functools.partial(finish_kernel, z, len(tails), len(come))...  2.84 us
    pallas_call x1, Pallas kernels, near_shards(): pl.pallas_call(functools.partial(pack_kernel, z), out_shape=jax.ShapeDtyp...  1.56 us
  transfers between devices with their start and end apart: 7, of which 1 were waited for; matrix products, arithmetic and copies ran while one was open for 0% of the time, Pallas kernels for 51%

profile of v15, /device:TPU:0, one launch (start us, length us, event | category | flops | bytes accessed | tf_op | source)
XLA Modules:
  0.0 38.1 jit_solution(7716243660683102085)
XLA Ops:
  0.6 1.6 %pack.1.refs_7_.refs_4_ = bf16[272,256]{1,0:T(8,128)(2,1)} custom-call(bf16[2,128,256]{2,1,0:T(8,128)(2,1)} %prompt_hbm.1, f32[16]{0:T(128)} %refs_2_.7, s32[64]{0:T(128)} %refs_0_.7), custom_call_target="tpu_custom_call" | custom-call | tf_op jit(solution)/shard_map/pack/pallas_call | solution.py:509
  2.2 0.0 copy-start
  2.2 0.0 copy-start.2
  2.2 0.0 copy-start.3
  2.2 0.0 copy-start.4
  2.2 4.1 %collective-permute-start = (bf16[272,256]{1,0:T(8,128)(2,1)}, bf16[272,256]{1,0:T(8,128)(2,1)S(1)}, u32[]{:S(2)}, u32[]{:S(2)}) collective-permute-start(bf16[272,256]{1,0:T(8,128)(2,1)} %pack.1.refs_7_.refs_4_), channel_id=1, source_target_pairs={{0,8},{4,12},{8,0},{12,4},{1,9},{5,13},{9,1},{13,5},{2,10},{6,14},... | collective-permute-start | bytes 417800 | tf_op jit(solution)/shard_map/ppermute | solution.py:527
  6.3 1.3 %collective-permute-start.1 = (f32[16]{0:T(128)}, f32[16]{0:T(128)S(1)}, u32[]{:S(2)}, u32[]{:S(2)}) collective-permute-start(f32[16]{0:T(128)} %refs_2_.7), channel_id=1, source_target_pairs={{0,12},{4,8},{8,4},{12,0},{1,13},{5,9},{9,5},{13,1},{2,14},{6,10},... | collective-permute-start | bytes 200 | tf_op jit(solution)/shard_map/ppermute | solution.py:527
  7.7 0.2 collective-permute-start.2
  7.9 5.8 %raw_grads.1 = (bf16[1024,1280]{1,0:T(8,128)(2,1)}, bf16[2,1024,256]{2,1,0:T(8,128)(2,1)}, bf16[4,2,128,256]{3,2,1,0:T(8,128)(2,1)}, bf16[2,512,1280]{2,1,0:T(8,128)(2,1)}, bf16[2,512,256]{2,1,0:T(8,128)(2,1)}) custom-call(s32[64]{0:T(128)} %refs_0_.7, s32[16]{0:T(128)} %refs_1_.7, f32[16]{0:T(128)} %refs_2_.7, f32[16]{0:T(128)} %refs_2_.7, ...), custom_call_target="tpu_custom_call" | custom-call | tf_op jit(solution)/shard_map/raw_grads/pallas_call | solution.py:546
  13.8 0.0 collective-permute-done.1.refs_3_
  13.8 0.0 collective-permute-done.refs_9_.refs_10_.refs_6_
  13.8 1.9 %collective-permute-start.4 = (bf16[272,256]{1,0:T(8,128)(2,1)S(1)}, bf16[272,256]{1,0:T(8,128)(2,1)S(1)}, u32[]{:S(2)}, u32[]{:S(2)}) collective-permute-start(bf16[272,256]{1,0:T(8,128)(2,1)S(1)} %collective-permute-done.refs_9_.refs_10_.refs_6_), channel_id=1, source_target_pairs={{0,4},{4,0},{8,12},{12,8},{1,5},{5,1},{9,13},{13,9},{2,6},{6,2},{1... | collective-permute-start | bytes 417800 | tf_op jit(solution)/shard_map/ppermute | solution.py:527
  15.6 0.0 collective-permute-done.2.refs_8_.refs_11_.refs_5_
  15.7 0.0 copy-done
  15.7 0.0 copy-done.2
  15.7 0.0 copy-done.3
  15.7 0.0 copy-done.4
  15.7 4.4 %group_grads.2 = (bf16[1024,1280]{1,0:T(8,128)(2,1)}, bf16[2,1024,256]{2,1,0:T(8,128)(2,1)}, bf16[2,128,256]{2,1,0:T(8,128)(2,1)S(1)}) custom-call(s32[64]{0:T(128)S(1)} %copy-done.3, s32[16]{0:T(128)S(1)} %copy-done.4, f32[16]{0:T(128)S(1)} %copy-done.2, f32[16]{0:T(128)S(1)} %collective-permute-done.1.refs_3_, ...), custom_call_target="tpu_custom_call", output_to_operand_aliasing={{0}: (13, {}), {1}: (14, {})} | custom-call | tf_op jit(solution)/shard_map/group_grads/pallas_call | solution.py:546
  20.1 1.9 %collective-permute-start.3 = (bf16[2,128,256]{2,1,0:T(8,128)(2,1)S(1)}, bf16[2,128,256]{2,1,0:T(8,128)(2,1)S(1)}, u32[]{:S(2)}, u32[]{:S(2)}) collective-permute-start(bf16[2,128,256]{2,1,0:T(8,128)(2,1)S(1)} %get-tuple-element.28), channel_id=1, source_target_pairs={{0,8},{4,12},{8,0},{12,4},{1,9},{5,13},{9,1},{13,5},{2,10},{6,14},... | collective-permute-start | bytes 393224 | tf_op jit(solution)/shard_map/ppermute | solution.py:527
  21.9 0.0 collective-permute-done.4.refs_10_
  21.9 0.0 copy-start.1
  21.9 6.5 %group_grads.3 = (bf16[1024,1280]{1,0:T(8,128)(2,1)}, bf16[2,1024,256]{2,1,0:T(8,128)(2,1)}, bf16[2,128,256]{2,1,0:T(8,128)(2,1)S(1)}, bf16[2,128,256]{2,1,0:T(8,128)(2,1)S(1)}) custom-call(s32[64]{0:T(128)S(1)} %copy-done.3, s32[16]{0:T(128)S(1)} %copy-done.4, f32[16]{0:T(128)S(1)} %copy-done.2, ...), custom_call_target="tpu_custom_call", output_to_operand_aliasing={{0}: (14, {}), {1}: (15, {})} | custom-call | tf_op jit(solution)/shard_map/group_grads/pallas_call | solution.py:546
  28.5 1.3 %collective-permute-start.5 = (bf16[2,128,256]{2,1,0:T(8,128)(2,1)S(1)}, bf16[2,128,256]{2,1,0:T(8,128)(2,1)S(1)}, u32[]{:S(2)}, u32[]{:S(2)}) collective-permute-start(bf16[2,128,256]{2,1,0:T(8,128)(2,1)S(1)} %get-tuple-element.32), channel_id=1, source_target_pairs={{0,4},{4,0},{8,12},{12,8},{1,5},{5,1},{9,13},{13,9},{2,6},{6,2},{1... | collective-permute-start | bytes 393224 | tf_op jit(solution)/shard_map/ppermute | solution.py:527
  29.8 1.3 %collective-permute-start.6 = (bf16[2,128,256]{2,1,0:T(8,128)(2,1)S(1)}, bf16[2,128,256]{2,1,0:T(8,128)(2,1)S(1)}, u32[]{:S(2)}, u32[]{:S(2)}) collective-permute-start(bf16[2,128,256]{2,1,0:T(8,128)(2,1)S(1)} %get-tuple-element.38), channel_id=1, source_target_pairs={{0,12},{4,8},{8,4},{12,0},{1,13},{5,9},{9,5},{13,1},{2,14},{6,10},... | collective-permute-start | bytes 393224 | tf_op jit(solution)/shard_map/ppermute | solution.py:527
  31.1 0.0 collective-permute-done.3.refs_8_
  31.1 3.4 %collective-permute-done.5.refs_9_ = bf16[2,128,256]{2,1,0:T(8,128)(2,1)S(1)} collective-permute-done((bf16[2,128,256]{2,1,0:T(8,128)(2,1)S(1)}, bf16[2,128,256]{2,1,0:T(8,128)(2,1)S(1)}, u32[]{:S(2)}, u32[]{:S(2)}) %collective-permute-start.5) | collective-permute-done | bytes 131104 | tf_op jit(solution)/shard_map/ppermute | solution.py:527
  34.6 0.0 copy-done.1
  34.6 2.8 %finish_own.1 = (bf16[1024,1280]{1,0:T(8,128)(2,1)}, bf16[2,1024,256]{2,1,0:T(8,128)(2,1)}, f32[2,128,256]{2,1,0:T(8,128)S(1)}) custom-call(s32[64]{0:T(128)S(1)} %copy-done.3, s32[16]{0:T(128)S(1)} %copy-done.4, f32[16]{0:T(128)S(1)} %copy-done.2, f32[16]{0:T(128)S(1)} %collective-permute-done.1.refs_3_, ...), custom_call_target="tpu_custom_call", output_to_operand_aliasing={{0}: (10, {}), {1}: (11, {})} | custom-call | tf_op jit(solution)/shard_map/finish_own/pallas_call | solution.py:590
  37.4 0.0 collective-permute-done.6
  37.4 0.7 %add_convert_fusion = bf16[2,128,256]{2,1,0:T(8,128)(2,1)} fusion(f32[2,128,256]{2,1,0:T(8,128)S(1)} %get-tuple-element.37, bf16[2,128,256]{2,1,0:T(8,128)(2,1)S(1)} %collective-permute-done.6), kind=kLoop, calls=%fused_computation | loop fusion | flops 196608 | bytes 524288 | tf_op jit(solution)/shard_map/convert_element_type | solution.py:615
Async XLA Ops:
  2.2 13.5 %copy-start = (bf16[272,256]{1,0:T(8,128)(2,1)S(1)}, bf16[272,256]{1,0:T(8,128)(2,1)}, u32[]{:S(2)}) copy-start(bf16[272,256]{1,0:T(8,128)(2,1)} %pack.1.refs_7_.refs_4_) | copy-start | bytes 417796
  2.2 13.4 %copy-start.2 = (f32[16]{0:T(128)S(1)}, f32[16]{0:T(128)}, u32[]{:S(2)}) copy-start(f32[16]{0:T(128)} %refs_2_.7) | copy-start | bytes 196
  2.2 13.4 %copy-start.3 = (s32[64]{0:T(128)S(1)}, s32[64]{0:T(128)}, u32[]{:S(2)}) copy-start(s32[64]{0:T(128)} %refs_0_.7) | copy-start | bytes 772
  2.2 13.4 %copy-start.4 = (s32[16]{0:T(128)S(1)}, s32[16]{0:T(128)}, u32[]{:S(2)}) copy-start(s32[16]{0:T(128)} %refs_1_.7) | copy-start | bytes 196
  2.2 11.5 %collective-permute-start = (bf16[272,256]{1,0:T(8,128)(2,1)}, bf16[272,256]{1,0:T(8,128)(2,1)S(1)}, u32[]{:S(2)}, u32[]{:S(2)}) collective-permute-start(bf16[272,256]{1,0:T(8,128)(2,1)} %pack.1.refs_7_.refs_4_), channel_id=1, source_target_pairs={{0,8},{4,12},{8,0},{12,4},{1,9},{5,13},{9,1},{13,5},{2,10},{6,14},... | collective-permute-start | bytes 417800 | tf_op jit(solution)/shard_map/ppermute | solution.py:527
  6.3 7.4 %collective-permute-start.1 = (f32[16]{0:T(128)}, f32[16]{0:T(128)S(1)}, u32[]{:S(2)}, u32[]{:S(2)}) collective-permute-start(f32[16]{0:T(128)} %refs_2_.7), channel_id=1, source_target_pairs={{0,12},{4,8},{8,4},{12,0},{1,13},{5,9},{9,5},{13,1},{2,14},{6,10},... | collective-permute-start | bytes 200 | tf_op jit(solution)/shard_map/ppermute | solution.py:527
  7.7 8.0 %collective-permute-start.2 = (bf16[272,256]{1,0:T(8,128)(2,1)}, bf16[272,256]{1,0:T(8,128)(2,1)S(1)}, u32[]{:S(2)}, u32[]{:S(2)}) collective-permute-start(bf16[272,256]{1,0:T(8,128)(2,1)} %pack.1.refs_7_.refs_4_), channel_id=1, source_target_pairs={{0,4},{4,0},{8,12},{12,8},{1,5},{5,1},{9,13},{13,9},{2,6},{6,2},{1... | collective-permute-start | bytes 417800 | tf_op jit(solution)/shard_map/ppermute | solution.py:527
  13.8 8.1 %collective-permute-start.4 = (bf16[272,256]{1,0:T(8,128)(2,1)S(1)}, bf16[272,256]{1,0:T(8,128)(2,1)S(1)}, u32[]{:S(2)}, u32[]{:S(2)}) collective-permute-start(bf16[272,256]{1,0:T(8,128)(2,1)S(1)} %collective-permute-done.refs_9_.refs_10_.refs_6_), channel_id=1, source_target_pairs={{0,4},{4,0},{8,12},{12,8},{1,5},{5,1},{9,13},{13,9},{2,6},{6,2},{1... | collective-permute-start | bytes 417800 | tf_op jit(solution)/shard_map/ppermute | solution.py:527
  20.1 11.1 %collective-permute-start.3 = (bf16[2,128,256]{2,1,0:T(8,128)(2,1)S(1)}, bf16[2,128,256]{2,1,0:T(8,128)(2,1)S(1)}, u32[]{:S(2)}, u32[]{:S(2)}) collective-permute-start(bf16[2,128,256]{2,1,0:T(8,128)(2,1)S(1)} %get-tuple-element.28), channel_id=1, source_target_pairs={{0,8},{4,12},{8,0},{12,4},{1,9},{5,13},{9,1},{13,5},{2,10},{6,14},... | collective-permute-start | bytes 393224 | tf_op jit(solution)/shard_map/ppermute | solution.py:527
  21.9 12.6 %copy-start.1 = (bf16[4,2,128,256]{3,2,1,0:T(8,128)(2,1)S(1)}, bf16[4,2,128,256]{3,2,1,0:T(8,128)(2,1)}, u32[]{:S(2)}) copy-start(bf16[4,2,128,256]{3,2,1,0:T(8,128)(2,1)} %get-tuple-element.23.refs_7_) | copy-start | bytes 1572868
  28.5 6.1 %collective-permute-start.5 = (bf16[2,128,256]{2,1,0:T(8,128)(2,1)S(1)}, bf16[2,128,256]{2,1,0:T(8,128)(2,1)S(1)}, u32[]{:S(2)}, u32[]{:S(2)}) collective-permute-start(bf16[2,128,256]{2,1,0:T(8,128)(2,1)S(1)} %get-tuple-element.32), channel_id=1, source_target_pairs={{0,4},{4,0},{8,12},{12,8},{1,5},{5,1},{9,13},{13,9},{2,6},{6,2},{1... | collective-permute-start | bytes 393224 | tf_op jit(solution)/shard_map/ppermute | solution.py:527
  29.8 7.6 %collective-permute-start.6 = (bf16[2,128,256]{2,1,0:T(8,128)(2,1)S(1)}, bf16[2,128,256]{2,1,0:T(8,128)(2,1)S(1)}, u32[]{:S(2)}, u32[]{:S(2)}) collective-permute-start(bf16[2,128,256]{2,1,0:T(8,128)(2,1)S(1)} %get-tuple-element.38), channel_id=1, source_target_pairs={{0,12},{4,8},{8,4},{12,0},{1,13},{5,9},{9,5},{13,1},{2,14},{6,10},... | collective-permute-start | bytes 393224 | tf_op jit(solution)/shard_map/ppermute | solution.py:527

commit v16 on v11

--- a/solution.py
+++ b/solution.py
@@ -303,7 +303,7 @@
         in_order, refs = refs[:2], refs[2 + aliased :]
         (q_out, self_out), grads_out, refs = refs[:2], refs[2 : 2 + len(turns)], refs[2 + len(turns) :]
     in_order = (in_order[0].at[0], in_order[0].at[1], in_order[1])
-    (resp_prompt, resp_len, rewards, far_rewards, order, lens, factors, q, og, kv, prefix, tails, acc, out, own, grads,
+    (resp_prompt, resp_len, rewards, far_rewards, order, q, og, kv, prefix, tails, acc, out, own, grads,
      sem_small, sem_tails, sem_prefix, sem_in, sem_out, sem_grads, sem_order) = refs
     me = lax.axis_index("dp")
     n_slots = len(turns) * z.slots
@@ -347,12 +347,6 @@
             copy.start()
     for copy in small[1:] + late:
         copy.wait()
-    for t, turn in enumerate(turns):
-        total = None if raw else prompt_total(z, me, me ^ turn, resp_prompt, tails, far_rewards)
-        for slot in range(t * z.slots, (t + 1) * z.slots):
-            i = order[slot]
-            lens[slot] = resp_len[i]
-            factors[slot] = 1.0 if raw else reward_factor(z, rewards[i], total, resp_len[i])
     if not raw:
         acc[...] = jnp.zeros(acc.shape, F32)
     for copy in prefix_copies:
@@ -391,12 +385,22 @@
                 acc[t, 0, :, cols] += key_grad
                 acc[t, 1, :, cols] += value_grad
 
+        turn = turns[0]
+        for n, other in enumerate(turns[1:], 1):
+            turn = jnp.where(t == n, other, turn)
+        total = None if raw else prompt_total(z, me, me ^ turn, resp_prompt, tails, far_rewards)
+        lens, factors = {}, {}
+        for n in mine:
+            i = order[first + n]
+            lens[n] = resp_len[i]
+            factors[n] = 1.0 if raw else reward_factor(z, rewards[i], total, resp_len[i])
         units = []
         for pair in range(pairs_in_body):
             places = [first + pair * PAIR + n for n in range(PAIR)]
+            own_places = range(pair * PAIR, (pair + 1) * PAIR)
             at = [token_rows(z, n) for n in places]
             for k in range(z.kv_heads):
-                units.append(Unit(at, places, k, [lens[n] for n in places], [factors[n] for n in places]))
+                units.append(Unit(at, places, k, [lens[n] for n in own_places], [factors[n] for n in own_places]))
         attend(z, units, q, og, kv, prefix.at[t], out, own, sink, raw)
         for n in mine:
             for copy in copies_out(first + n):
@@ -542,8 +546,6 @@
             scratch_shapes=[
                 *smem,
                 pltpu.SMEM((n_held + 1,), jnp.int32),
-                pltpu.SMEM((n_slots,), jnp.int32),
-                pltpu.SMEM((n_slots,), F32),
                 pltpu.VMEM((n_held * z.tokens, z.lanes), BF16),
                 pltpu.VMEM((n_held * z.tokens, z.lanes), BF16),
                 pltpu.VMEM((2, n_held * z.tokens, z.width), BF16),

time: 37.2 us -> 37.2 us (level)
  no operation moved by 1% of the time
where the time goes in v16:
time: 37.2 us; the launch traced here: 37 us
  Pallas kernels  20.9 us (56%)
  starting transfers between devices  11.2 us (30%)
  waiting for transfers between devices  3.46 us (9%)
  between operations  0.74 us (2%)
  other arithmetic  0.7 us (2%)
    pallas_call x3, Pallas kernels, grads_of(): pl.pallas_call(functools.partial(group_kernel, z, turns, raw, body, ahead...  16.5 us
    ppermute x7, starting transfers between devices, swap(): return lax.ppermute(x, 'dp', [(i, i ^ s) for i in range(n_dp)])  11.2 us
    ppermute x7, waiting for transfers between devices, swap(): return lax.ppermute(x, 'dp', [(i, i ^ s) for i in range(n_dp)])  3.46 us
    pallas_call x1, Pallas kernels, near_shards(): pl.pallas_call(functools.partial(finish_kernel, z, len(tails), len(come))...  2.83 us
    pallas_call x1, Pallas kernels, near_shards(): pl.pallas_call(functools.partial(pack_kernel, z), out_shape=jax.ShapeDtyp...  1.56 us
  transfers between devices with their start and end apart: 7, of which 1 were waited for; matrix products, arithmetic and copies ran while one was open for 0% of the time, Pallas kernels for 52%

profile of v16, /device:TPU:0, one launch (start us, length us, event | category | flops | bytes accessed | tf_op | source)
XLA Modules:
  0.0 37.0 jit_solution(13185870240490335073)
XLA Ops:
  0.6 1.6 %pack.1.refs_7_.refs_4_ = bf16[272,256]{1,0:T(8,128)(2,1)} custom-call(bf16[2,128,256]{2,1,0:T(8,128)(2,1)} %prompt_hbm.1, f32[16]{0:T(128)} %refs_2_.7, s32[64]{0:T(128)} %refs_0_.7), custom_call_target="tpu_custom_call" | custom-call | tf_op jit(solution)/shard_map/pack/pallas_call | solution.py:502
  2.2 0.0 copy-start
  2.2 0.0 copy-start.2
  2.2 0.0 copy-start.3
  2.2 0.0 copy-start.4
  2.2 4.1 %collective-permute-start = (bf16[272,256]{1,0:T(8,128)(2,1)}, bf16[272,256]{1,0:T(8,128)(2,1)S(1)}, u32[]{:S(2)}, u32[]{:S(2)}) collective-permute-start(bf16[272,256]{1,0:T(8,128)(2,1)} %pack.1.refs_7_.refs_4_), channel_id=1, source_target_pairs={{0,8},{4,12},{8,0},{12,4},{1,9},{5,13},{9,1},{13,5},{2,10},{6,14},... | collective-permute-start | bytes 417800 | tf_op jit(solution)/shard_map/ppermute | solution.py:520
  6.3 1.3 %collective-permute-start.1 = (f32[16]{0:T(128)}, f32[16]{0:T(128)S(1)}, u32[]{:S(2)}, u32[]{:S(2)}) collective-permute-start(f32[16]{0:T(128)} %refs_2_.7), channel_id=1, source_target_pairs={{0,12},{4,8},{8,4},{12,0},{1,13},{5,9},{9,5},{13,1},{2,14},{6,10},... | collective-permute-start | bytes 200 | tf_op jit(solution)/shard_map/ppermute | solution.py:520
  7.7 0.2 collective-permute-start.2
  7.9 5.8 %raw_grads.1 = (bf16[1024,1280]{1,0:T(8,128)(2,1)}, bf16[2,1024,256]{2,1,0:T(8,128)(2,1)}, bf16[4,2,128,256]{3,2,1,0:T(8,128)(2,1)}, bf16[2,512,1280]{2,1,0:T(8,128)(2,1)}, bf16[2,512,256]{2,1,0:T(8,128)(2,1)}) custom-call(s32[64]{0:T(128)} %refs_0_.7, s32[16]{0:T(128)} %refs_1_.7, f32[16]{0:T(128)} %refs_2_.7, f32[16]{0:T(128)} %refs_2_.7, ...), custom_call_target="tpu_custom_call" | custom-call | tf_op jit(solution)/shard_map/raw_grads/pallas_call | solution.py:539
  13.8 0.0 collective-permute-done.1.refs_3_
  13.8 0.0 collective-permute-done.refs_9_.refs_10_.refs_6_
  13.8 1.9 %collective-permute-start.4 = (bf16[272,256]{1,0:T(8,128)(2,1)S(1)}, bf16[272,256]{1,0:T(8,128)(2,1)S(1)}, u32[]{:S(2)}, u32[]{:S(2)}) collective-permute-start(bf16[272,256]{1,0:T(8,128)(2,1)S(1)} %collective-permute-done.refs_9_.refs_10_.refs_6_), channel_id=1, source_target_pairs={{0,4},{4,0},{8,12},{12,8},{1,5},{5,1},{9,13},{13,9},{2,6},{6,2},{1... | collective-permute-start | bytes 417800 | tf_op jit(solution)/shard_map/ppermute | solution.py:520
  15.7 0.0 collective-permute-done.2.refs_8_.refs_11_.refs_5_
  15.7 0.0 copy-done
  15.7 0.0 copy-done.2
  15.7 0.0 copy-done.3
  15.7 0.0 copy-done.4
  15.7 4.3 %group_grads.2 = (bf16[1024,1280]{1,0:T(8,128)(2,1)}, bf16[2,1024,256]{2,1,0:T(8,128)(2,1)}, bf16[2,128,256]{2,1,0:T(8,128)(2,1)S(1)}) custom-call(s32[64]{0:T(128)S(1)} %copy-done.3, s32[16]{0:T(128)S(1)} %copy-done.4, f32[16]{0:T(128)S(1)} %copy-done.2, f32[16]{0:T(128)S(1)} %collective-permute-done.1.refs_3_, ...), custom_call_target="tpu_custom_call", output_to_operand_aliasing={{0}: (13, {}), {1}: (14, {})} | custom-call | tf_op jit(solution)/shard_map/group_grads/pallas_call | solution.py:539
  20.0 1.8 %collective-permute-start.3 = (bf16[2,128,256]{2,1,0:T(8,128)(2,1)S(1)}, bf16[2,128,256]{2,1,0:T(8,128)(2,1)S(1)}, u32[]{:S(2)}, u32[]{:S(2)}) collective-permute-start(bf16[2,128,256]{2,1,0:T(8,128)(2,1)S(1)} %get-tuple-element.28), channel_id=1, source_target_pairs={{0,8},{4,12},{8,0},{12,4},{1,9},{5,13},{9,1},{13,5},{2,10},{6,14},... | collective-permute-start | bytes 393224 | tf_op jit(solution)/shard_map/ppermute | solution.py:520
  21.8 0.0 collective-permute-done.4.refs_10_
  21.8 0.0 copy-start.1
  21.8 6.3 %group_grads.3 = (bf16[1024,1280]{1,0:T(8,128)(2,1)}, bf16[2,1024,256]{2,1,0:T(8,128)(2,1)}, bf16[2,128,256]{2,1,0:T(8,128)(2,1)S(1)}, bf16[2,128,256]{2,1,0:T(8,128)(2,1)S(1)}) custom-call(s32[64]{0:T(128)S(1)} %copy-done.3, s32[16]{0:T(128)S(1)} %copy-done.4, f32[16]{0:T(128)S(1)} %copy-done.2, ...), custom_call_target="tpu_custom_call", output_to_operand_aliasing={{0}: (14, {}), {1}: (15, {})} | custom-call | tf_op jit(solution)/shard_map/group_grads/pallas_call | solution.py:539
  28.2 0.9 %collective-permute-start.5 = (bf16[2,128,256]{2,1,0:T(8,128)(2,1)S(1)}, bf16[2,128,256]{2,1,0:T(8,128)(2,1)S(1)}, u32[]{:S(2)}, u32[]{:S(2)}) collective-permute-start(bf16[2,128,256]{2,1,0:T(8,128)(2,1)S(1)} %get-tuple-element.37), channel_id=1, source_target_pairs={{0,12},{4,8},{8,4},{12,0},{1,13},{5,9},{9,5},{13,1},{2,14},{6,10},... | collective-permute-start | bytes 393224 | tf_op jit(solution)/shard_map/ppermute | solution.py:520
  29.1 0.9 %collective-permute-start.6 = (bf16[2,128,256]{2,1,0:T(8,128)(2,1)S(1)}, bf16[2,128,256]{2,1,0:T(8,128)(2,1)S(1)}, u32[]{:S(2)}, u32[]{:S(2)}) collective-permute-start(bf16[2,128,256]{2,1,0:T(8,128)(2,1)S(1)} %get-tuple-element.38), channel_id=1, source_target_pairs={{0,4},{4,0},{8,12},{12,8},{1,5},{5,1},{9,13},{13,9},{2,6},{6,2},{1... | collective-permute-start | bytes 393224 | tf_op jit(solution)/shard_map/ppermute | solution.py:520
  30.0 0.0 collective-permute-done.3.refs_8_
  30.0 0.0 copy-done.1
  30.0 2.8 %finish_own.1 = (bf16[1024,1280]{1,0:T(8,128)(2,1)}, bf16[2,1024,256]{2,1,0:T(8,128)(2,1)}, f32[2,128,256]{2,1,0:T(8,128)S(1)}) custom-call(s32[64]{0:T(128)S(1)} %copy-done.3, s32[16]{0:T(128)S(1)} %copy-done.4, f32[16]{0:T(128)S(1)} %copy-done.2, f32[16]{0:T(128)S(1)} %collective-permute-done.1.refs_3_, ...), custom_call_target="tpu_custom_call", output_to_operand_aliasing={{0}: (9, {}), {1}: (10, {})} | custom-call | tf_op jit(solution)/shard_map/finish_own/pallas_call | solution.py:580
  32.8 3.4 %collective-permute-done.5 = bf16[2,128,256]{2,1,0:T(8,128)(2,1)S(1)} collective-permute-done((bf16[2,128,256]{2,1,0:T(8,128)(2,1)S(1)}, bf16[2,128,256]{2,1,0:T(8,128)(2,1)S(1)}, u32[]{:S(2)}, u32[]{:S(2)}) %collective-permute-start.5) | collective-permute-done | bytes 131104 | tf_op jit(solution)/shard_map/ppermute | solution.py:520
  36.2 0.0 collective-permute-done.6
  36.2 0.7 %add_convert_fusion = bf16[2,128,256]{2,1,0:T(8,128)(2,1)} fusion(f32[2,128,256]{2,1,0:T(8,128)S(1)} %get-tuple-element.36, bf16[2,128,256]{2,1,0:T(8,128)(2,1)S(1)} %collective-permute-done.6, bf16[2,128,256]{2,1,0:T(8,128)(2,1)S(1)} %collective-permute-done.5), kind=kLoop, calls=%fused_computation | loop fusion | flops 327680 | bytes 655360 | tf_op jit(solution)/shard_map/convert_element_type | solution.py:605
Async XLA Ops:
  2.2 13.5 %copy-start = (bf16[272,256]{1,0:T(8,128)(2,1)S(1)}, bf16[272,256]{1,0:T(8,128)(2,1)}, u32[]{:S(2)}) copy-start(bf16[272,256]{1,0:T(8,128)(2,1)} %pack.1.refs_7_.refs_4_) | copy-start | bytes 417796
  2.2 13.5 %copy-start.2 = (f32[16]{0:T(128)S(1)}, f32[16]{0:T(128)}, u32[]{:S(2)}) copy-start(f32[16]{0:T(128)} %refs_2_.7) | copy-start | bytes 196
  2.2 13.4 %copy-start.3 = (s32[64]{0:T(128)S(1)}, s32[64]{0:T(128)}, u32[]{:S(2)}) copy-start(s32[64]{0:T(128)} %refs_0_.7) | copy-start | bytes 772
  2.2 13.4 %copy-start.4 = (s32[16]{0:T(128)S(1)}, s32[16]{0:T(128)}, u32[]{:S(2)}) copy-start(s32[16]{0:T(128)} %refs_1_.7) | copy-start | bytes 196
  2.2 11.5 %collective-permute-start = (bf16[272,256]{1,0:T(8,128)(2,1)}, bf16[272,256]{1,0:T(8,128)(2,1)S(1)}, u32[]{:S(2)}, u32[]{:S(2)}) collective-permute-start(bf16[272,256]{1,0:T(8,128)(2,1)} %pack.1.refs_7_.refs_4_), channel_id=1, source_target_pairs={{0,8},{4,12},{8,0},{12,4},{1,9},{5,13},{9,1},{13,5},{2,10},{6,14},... | collective-permute-start | bytes 417800 | tf_op jit(solution)/shard_map/ppermute | solution.py:520
  6.3 7.4 %collective-permute-start.1 = (f32[16]{0:T(128)}, f32[16]{0:T(128)S(1)}, u32[]{:S(2)}, u32[]{:S(2)}) collective-permute-start(f32[16]{0:T(128)} %refs_2_.7), channel_id=1, source_target_pairs={{0,12},{4,8},{8,4},{12,0},{1,13},{5,9},{9,5},{13,1},{2,14},{6,10},... | collective-permute-start | bytes 200 | tf_op jit(solution)/shard_map/ppermute | solution.py:520
  7.7 8.0 %collective-permute-start.2 = (bf16[272,256]{1,0:T(8,128)(2,1)}, bf16[272,256]{1,0:T(8,128)(2,1)S(1)}, u32[]{:S(2)}, u32[]{:S(2)}) collective-permute-start(bf16[272,256]{1,0:T(8,128)(2,1)} %pack.1.refs_7_.refs_4_), channel_id=1, source_target_pairs={{0,4},{4,0},{8,12},{12,8},{1,5},{5,1},{9,13},{13,9},{2,6},{6,2},{1... | collective-permute-start | bytes 417800 | tf_op jit(solution)/shard_map/ppermute | solution.py:520
  13.8 8.0 %collective-permute-start.4 = (bf16[272,256]{1,0:T(8,128)(2,1)S(1)}, bf16[272,256]{1,0:T(8,128)(2,1)S(1)}, u32[]{:S(2)}, u32[]{:S(2)}) collective-permute-start(bf16[272,256]{1,0:T(8,128)(2,1)S(1)} %collective-permute-done.refs_9_.refs_10_.refs_6_), channel_id=1, source_target_pairs={{0,4},{4,0},{8,12},{12,8},{1,5},{5,1},{9,13},{13,9},{2,6},{6,2},{1... | collective-permute-start | bytes 417800 | tf_op jit(solution)/shard_map/ppermute | solution.py:520
  20.0 10.0 %collective-permute-start.3 = (bf16[2,128,256]{2,1,0:T(8,128)(2,1)S(1)}, bf16[2,128,256]{2,1,0:T(8,128)(2,1)S(1)}, u32[]{:S(2)}, u32[]{:S(2)}) collective-permute-start(bf16[2,128,256]{2,1,0:T(8,128)(2,1)S(1)} %get-tuple-element.28), channel_id=1, source_target_pairs={{0,8},{4,12},{8,0},{12,4},{1,9},{5,13},{9,1},{13,5},{2,10},{6,14},... | collective-permute-start | bytes 393224 | tf_op jit(solution)/shard_map/ppermute | solution.py:520
  21.8 8.1 %copy-start.1 = (bf16[4,2,128,256]{3,2,1,0:T(8,128)(2,1)S(1)}, bf16[4,2,128,256]{3,2,1,0:T(8,128)(2,1)}, u32[]{:S(2)}) copy-start(bf16[4,2,128,256]{3,2,1,0:T(8,128)(2,1)} %get-tuple-element.23.refs_7_) | copy-start | bytes 1572868
  28.2 8.1 %collective-permute-start.5 = (bf16[2,128,256]{2,1,0:T(8,128)(2,1)S(1)}, bf16[2,128,256]{2,1,0:T(8,128)(2,1)S(1)}, u32[]{:S(2)}, u32[]{:S(2)}) collective-permute-start(bf16[2,128,256]{2,1,0:T(8,128)(2,1)S(1)} %get-tuple-element.37), channel_id=1, source_target_pairs={{0,12},{4,8},{8,4},{12,0},{1,13},{5,9},{9,5},{13,1},{2,14},{6,10},... | collective-permute-start | bytes 393224 | tf_op jit(solution)/shard_map/ppermute | solution.py:520
  29.1 7.2 %collective-permute-start.6 = (bf16[2,128,256]{2,1,0:T(8,128)(2,1)S(1)}, bf16[2,128,256]{2,1,0:T(8,128)(2,1)S(1)}, u32[]{:S(2)}, u32[]{:S(2)}) collective-permute-start(bf16[2,128,256]{2,1,0:T(8,128)(2,1)S(1)} %get-tuple-element.38), channel_id=1, source_target_pairs={{0,4},{4,0},{8,12},{12,8},{1,5},{5,1},{9,13},{13,9},{2,6},{6,2},{1... | collective-permute-start | bytes 393224 | tf_op jit(solution)/shard_map/ppermute | solution.py:520

commit v17 on v16

--- a/solution.py
+++ b/solution.py
@@ -58,6 +58,8 @@
     k: object
     lens: list
     factors: list
+    ready: object = None
+    done: object = None
 
 
 def attend(z, units, q, og, kv, prefix, out, own_out, sink, apart):
@@ -101,17 +103,13 @@
     chunks = []
     for unit in units:
         t = Bag()
-        t.at, t.places, t.k, t.lens, t.factors = unit
+        t.unit = unit
+        t.at, t.places, t.k, t.lens, t.factors = unit[:5]
         t.single = len(t.at) == 1
         t.members = range(len(t.at))
         sides = (0, 0) if t.single else (0, 1)
         t.cols = columns(t.k)
-        t.key_p, t.value_p = prefix[0, :, t.cols], prefix[1, :, t.cols]
-        t.keys = [kv[0, t.at[n], t.cols] for n in sides]
-        t.values = [kv[1, t.at[n], t.cols] for n in sides]
-        t.key_pair = jnp.concatenate(t.keys, axis=0)
-        t.value_pair = jnp.concatenate(t.values, axis=0)
-        t.key_t = jnp.concatenate([t.key_p.T, t.key_pair.T], axis=1)
+        t.keys = None
         t.prefix_sums = {n: [] for n in t.members}
         t.self_sums = {n: [] for n in t.members}
         mine = []
@@ -126,8 +124,21 @@
         t.left_over = len(mine)
         chunks += mine
 
+    def prepare(t):
+        if t.unit.ready is not None:
+            t.unit.ready()
+        sides = (0, 0) if t.single else (0, 1)
+        t.key_p, t.value_p = prefix[0, :, t.cols], prefix[1, :, t.cols]
+        t.keys = [kv[0, t.at[n], t.cols] for n in sides]
+        t.values = [kv[1, t.at[n], t.cols] for n in sides]
+        t.key_pair = jnp.concatenate(t.keys, axis=0)
+        t.value_pair = jnp.concatenate(t.values, axis=0)
+        t.key_t = jnp.concatenate([t.key_p.T, t.key_pair.T], axis=1)
+
     def products(c):
         t = c.t
+        if t.keys is None:
+            prepare(t)
         c.q_rows, c.g_rows = rows(q, c), rows(og, c)
         if c.side is None:
             key_s, value_s = t.key_pair, t.value_pair
@@ -196,6 +207,8 @@
                 if apart or n == 0:
                     keys, values = zip(*t.prefix_sums[n])
                     sink(t.places[n], t.cols, sum(keys) * scale, sum(values))
+            if t.unit.done is not None:
+                t.unit.done()
 
     stages = (products, weigh, gradients, outgoing)
     for step in range(len(chunks) + len(stages) - 1):
@@ -323,7 +336,14 @@
     late = tail_copies(z, tail_hbm, tails, sem_tails)
     first_rows = []
     if not raw:
-        first_rows = row_copies(in_order, (q, og, kv), pl.ds(ahead * span, span), pl.ds(0, span), sem_order.at[0])
+        for slot in range(z.slots):
+            first_rows += row_copies(
+                in_order,
+                (q, og, kv),
+                pl.ds((ahead * z.slots + slot) * z.tokens, z.tokens),
+                token_rows(z, slot),
+                sem_in.at[slot],
+            )
     for copy in [*small, *first_rows, *prefix_copies, *late]:
         copy.start()
     small[0].wait()
@@ -360,22 +380,15 @@
         first = u * pairs_in_body * PAIR
         mine = range(pairs_in_body * PAIR)
 
-        def wait_for_slots():
-            for n in mine:
+        def ready(pair):
+            for n in range(pair * PAIR, (pair + 1) * PAIR):
                 for copy in copies_in(first + n):
                     copy.wait()
 
-        if raw:
-            wait_for_slots()
-        else:
-
-            @pl.when(u == 0)
-            def _():
-                for copy in first_rows:
-                    copy.wait()
-
-            if len(turns) > 1:
-                pl.when(u >= steps_per_turn)(wait_for_slots)
+        def done(pair):
+            for n in range(pair * PAIR, (pair + 1) * PAIR):
+                for copy in copies_out(first + n):
+                    copy.start()
 
         def sink(place, cols, key_grad, value_grad):
             if raw:
@@ -400,11 +413,18 @@
             own_places = range(pair * PAIR, (pair + 1) * PAIR)
             at = [token_rows(z, n) for n in places]
             for k in range(z.kv_heads):
-                units.append(Unit(at, places, k, [lens[n] for n in own_places], [factors[n] for n in own_places]))
+                units.append(
+                    Unit(
+                        at,
+                        places,
+                        k,
+                        [lens[n] for n in own_places],
+                        [factors[n] for n in own_places],
+                        functools.partial(ready, pair) if k == 0 else None,
+                        functools.partial(done, pair) if k == z.kv_heads - 1 else None,
+                    )
+                )
         attend(z, units, q, og, kv, prefix.at[t], out, own, sink, raw)
-        for n in mine:
-            for copy in copies_out(first + n):
-                copy.start()
         if raw:
 
             @pl.when(u == 0)
@@ -575,7 +595,7 @@
     *written, for_2 = grads_of((2,), False, slots // PAIR, 0, in_order, written)
     come = [swap(for_2, 2)]
     *written, for_far, for_1 = grads_of((FAR, 1), False, slots // PAIR, 1, in_order, written)
-    last = [swap(for_far, FAR), swap(for_1, 1)]
+    last = [swap(for_1, 1), swap(for_far, FAR)]
     operands = [*small, far_rewards, *tails, per_resp, *come, *written]
     q_out, self_out, own_grads = pl.pallas_call(
         functools.partial(finish_kernel, z, len(tails), len(come)),

time: 37.2 us -> 38 us (1.022)
  starting transfers between devices: 11.2 us -> 12.1 us
  waiting for transfers between devices: 3.46 us -> 2.83 us
  Pallas kernels: 20.9 us -> 21.3 us
    ppermute x7, starting transfers between devices: 11.2 us -> 12.1 us  [swap(): return lax.ppermute(x, 'dp', [(i, i ^ s) for i in range(n_dp)])]
    ppermute x7, waiting for transfers between devices: 3.46 us -> 2.83 us  [swap(): return lax.ppermute(x, 'dp', [(i, i ^ s) for i in range(n_dp)])]
    pallas_call x3, Pallas kernels: 16.5 us -> 16.9 us  [grads_of(): pl.pallas_call(functools.partial(group_kernel, z, turns, raw, body, ahead...]
  transfers between devices with their start and end apart: 7 -> 7, of which waited for: 1 -> 2; matrix products, arithmetic and copies ran while one was open for 0% -> 0% of each run, Pallas kernels for 52% -> 52%
where the time goes in v17:
time: 38 us; the launch traced here: 37.7 us
  Pallas kernels  21.3 us (56%)
  starting transfers between devices  12.1 us (32%)
  waiting for transfers between devices  2.83 us (7%)
  between operations  0.74 us (2%)
  other arithmetic  0.7 us (2%)
    pallas_call x3, Pallas kernels, grads_of(): pl.pallas_call(functools.partial(group_kernel, z, turns, raw, body, ahead...  16.9 us
    ppermute x7, starting transfers between devices, swap(): return lax.ppermute(x, 'dp', [(i, i ^ s) for i in range(n_dp)])  12.1 us
    pallas_call x1, Pallas kernels, near_shards(): pl.pallas_call(functools.partial(finish_kernel, z, len(tails), len(come))...  2.83 us
    ppermute x7, waiting for transfers between devices, swap(): return lax.ppermute(x, 'dp', [(i, i ^ s) for i in range(n_dp)])  2.83 us
    pallas_call x1, Pallas kernels, near_shards(): pl.pallas_call(functools.partial(pack_kernel, z), out_shape=jax.ShapeDtyp...  1.56 us
  transfers between devices with their start and end apart: 7, of which 2 were waited for; matrix products, arithmetic and copies ran while one was open for 0% of the time, Pallas kernels for 52%

profile of v17, /device:TPU:0, one launch (start us, length us, event | category | flops | bytes accessed | tf_op | source)
XLA Modules:
  0.0 37.7 jit_solution(13765376917245781088)
XLA Ops:
  0.6 1.6 %pack.1.refs_7_.refs_4_ = bf16[272,256]{1,0:T(8,128)(2,1)} custom-call(bf16[2,128,256]{2,1,0:T(8,128)(2,1)} %prompt_hbm.1, f32[16]{0:T(128)} %refs_2_.7, s32[64]{0:T(128)} %refs_0_.7), custom_call_target="tpu_custom_call" | custom-call | tf_op jit(solution)/shard_map/pack/pallas_call | solution.py:522
  2.2 0.0 copy-start
  2.2 0.0 copy-start.2
  2.2 0.0 copy-start.3
  2.2 0.0 copy-start.4
  2.2 4.1 %collective-permute-start = (bf16[272,256]{1,0:T(8,128)(2,1)}, bf16[272,256]{1,0:T(8,128)(2,1)S(1)}, u32[]{:S(2)}, u32[]{:S(2)}) collective-permute-start(bf16[272,256]{1,0:T(8,128)(2,1)} %pack.1.refs_7_.refs_4_), channel_id=1, source_target_pairs={{0,8},{4,12},{8,0},{12,4},{1,9},{5,13},{9,1},{13,5},{2,10},{6,14},... | collective-permute-start | bytes 417800 | tf_op jit(solution)/shard_map/ppermute | solution.py:540
  6.3 1.3 %collective-permute-start.1 = (f32[16]{0:T(128)}, f32[16]{0:T(128)S(1)}, u32[]{:S(2)}, u32[]{:S(2)}) collective-permute-start(f32[16]{0:T(128)} %refs_2_.7), channel_id=1, source_target_pairs={{0,12},{4,8},{8,4},{12,0},{1,13},{5,9},{9,5},{13,1},{2,14},{6,10},... | collective-permute-start | bytes 200 | tf_op jit(solution)/shard_map/ppermute | solution.py:540
  7.7 0.2 collective-permute-start.2
  7.9 5.8 %raw_grads.1 = (bf16[1024,1280]{1,0:T(8,128)(2,1)}, bf16[2,1024,256]{2,1,0:T(8,128)(2,1)}, bf16[4,2,128,256]{3,2,1,0:T(8,128)(2,1)}, bf16[2,512,1280]{2,1,0:T(8,128)(2,1)}, bf16[2,512,256]{2,1,0:T(8,128)(2,1)}) custom-call(s32[64]{0:T(128)} %refs_0_.7, s32[16]{0:T(128)} %refs_1_.7, f32[16]{0:T(128)} %refs_2_.7, f32[16]{0:T(128)} %refs_2_.7, ...), custom_call_target="tpu_custom_call" | custom-call | tf_op jit(solution)/shard_map/raw_grads/pallas_call | solution.py:559
  13.8 0.0 collective-permute-done.1.refs_3_
  13.8 0.0 collective-permute-done.refs_9_.refs_10_.refs_6_
  13.8 1.9 %collective-permute-start.4 = (bf16[272,256]{1,0:T(8,128)(2,1)S(1)}, bf16[272,256]{1,0:T(8,128)(2,1)S(1)}, u32[]{:S(2)}, u32[]{:S(2)}) collective-permute-start(bf16[272,256]{1,0:T(8,128)(2,1)S(1)} %collective-permute-done.refs_9_.refs_10_.refs_6_), channel_id=1, source_target_pairs={{0,4},{4,0},{8,12},{12,8},{1,5},{5,1},{9,13},{13,9},{2,6},{6,2},{1... | collective-permute-start | bytes 417800 | tf_op jit(solution)/shard_map/ppermute | solution.py:540
  15.7 0.0 collective-permute-done.2.refs_8_.refs_11_.refs_5_
  15.7 0.0 copy-done
  15.7 0.0 copy-done.2
  15.7 0.0 copy-done.3
  15.7 0.0 copy-done.4
  15.7 4.3 %group_grads.2 = (bf16[1024,1280]{1,0:T(8,128)(2,1)}, bf16[2,1024,256]{2,1,0:T(8,128)(2,1)}, bf16[2,128,256]{2,1,0:T(8,128)(2,1)S(1)}) custom-call(s32[64]{0:T(128)S(1)} %copy-done.3, s32[16]{0:T(128)S(1)} %copy-done.4, f32[16]{0:T(128)S(1)} %copy-done.2, f32[16]{0:T(128)S(1)} %collective-permute-done.1.refs_3_, ...), custom_call_target="tpu_custom_call", output_to_operand_aliasing={{0}: (13, {}), {1}: (14, {})} | custom-call | tf_op jit(solution)/shard_map/group_grads/pallas_call | solution.py:559
  20.0 1.8 %collective-permute-start.3 = (bf16[2,128,256]{2,1,0:T(8,128)(2,1)S(1)}, bf16[2,128,256]{2,1,0:T(8,128)(2,1)S(1)}, u32[]{:S(2)}, u32[]{:S(2)}) collective-permute-start(bf16[2,128,256]{2,1,0:T(8,128)(2,1)S(1)} %get-tuple-element.28), channel_id=1, source_target_pairs={{0,8},{4,12},{8,0},{12,4},{1,9},{5,13},{9,1},{13,5},{2,10},{6,14},... | collective-permute-start | bytes 393224 | tf_op jit(solution)/shard_map/ppermute | solution.py:540
  21.8 0.0 collective-permute-done.4.refs_10_
  21.8 0.0 copy-start.1
  21.8 6.8 %group_grads.3 = (bf16[1024,1280]{1,0:T(8,128)(2,1)}, bf16[2,1024,256]{2,1,0:T(8,128)(2,1)}, bf16[2,128,256]{2,1,0:T(8,128)(2,1)S(1)}, bf16[2,128,256]{2,1,0:T(8,128)(2,1)S(1)}) custom-call(s32[64]{0:T(128)S(1)} %copy-done.3, s32[16]{0:T(128)S(1)} %copy-done.4, f32[16]{0:T(128)S(1)} %copy-done.2, ...), custom_call_target="tpu_custom_call", output_to_operand_aliasing={{0}: (14, {}), {1}: (15, {})} | custom-call | tf_op jit(solution)/shard_map/group_grads/pallas_call | solution.py:559
  28.6 1.3 %collective-permute-start.5 = (bf16[2,128,256]{2,1,0:T(8,128)(2,1)S(1)}, bf16[2,128,256]{2,1,0:T(8,128)(2,1)S(1)}, u32[]{:S(2)}, u32[]{:S(2)}) collective-permute-start(bf16[2,128,256]{2,1,0:T(8,128)(2,1)S(1)} %get-tuple-element.37), channel_id=1, source_target_pairs={{0,4},{4,0},{8,12},{12,8},{1,5},{5,1},{9,13},{13,9},{2,6},{6,2},{1... | collective-permute-start | bytes 393224 | tf_op jit(solution)/shard_map/ppermute | solution.py:540
  30.0 1.4 %collective-permute-start.6 = (bf16[2,128,256]{2,1,0:T(8,128)(2,1)S(1)}, bf16[2,128,256]{2,1,0:T(8,128)(2,1)S(1)}, u32[]{:S(2)}, u32[]{:S(2)}) collective-permute-start(bf16[2,128,256]{2,1,0:T(8,128)(2,1)S(1)} %get-tuple-element.38), channel_id=1, source_target_pairs={{0,12},{4,8},{8,4},{12,0},{1,13},{5,9},{9,5},{13,1},{2,14},{6,10},... | collective-permute-start | bytes 393224 | tf_op jit(solution)/shard_map/ppermute | solution.py:540
  31.3 0.0 collective-permute-done.3.refs_8_
  31.3 0.0 copy-done.1
  31.3 2.8 %finish_own.1 = (bf16[1024,1280]{1,0:T(8,128)(2,1)}, bf16[2,1024,256]{2,1,0:T(8,128)(2,1)}, f32[2,128,256]{2,1,0:T(8,128)S(1)}) custom-call(s32[64]{0:T(128)S(1)} %copy-done.3, s32[16]{0:T(128)S(1)} %copy-done.4, f32[16]{0:T(128)S(1)} %copy-done.2, f32[16]{0:T(128)S(1)} %collective-permute-done.1.refs_3_, ...), custom_call_target="tpu_custom_call", output_to_operand_aliasing={{0}: (9, {}), {1}: (10, {})} | custom-call | tf_op jit(solution)/shard_map/finish_own/pallas_call | solution.py:600
  34.2 0.6 %collective-permute-done.5 = bf16[2,128,256]{2,1,0:T(8,128)(2,1)S(1)} collective-permute-done((bf16[2,128,256]{2,1,0:T(8,128)(2,1)S(1)}, bf16[2,128,256]{2,1,0:T(8,128)(2,1)S(1)}, u32[]{:S(2)}, u32[]{:S(2)}) %collective-permute-start.5) | collective-permute-done | bytes 131104 | tf_op jit(solution)/shard_map/ppermute | solution.py:540
  34.8 2.2 %collective-permute-done.6 = bf16[2,128,256]{2,1,0:T(8,128)(2,1)S(1)} collective-permute-done((bf16[2,128,256]{2,1,0:T(8,128)(2,1)S(1)}, bf16[2,128,256]{2,1,0:T(8,128)(2,1)S(1)}, u32[]{:S(2)}, u32[]{:S(2)}) %collective-permute-start.6) | collective-permute-done | bytes 131104 | tf_op jit(solution)/shard_map/ppermute | solution.py:540
  37.0 0.7 %add_convert_fusion = bf16[2,128,256]{2,1,0:T(8,128)(2,1)} fusion(f32[2,128,256]{2,1,0:T(8,128)S(1)} %get-tuple-element.36, bf16[2,128,256]{2,1,0:T(8,128)(2,1)S(1)} %collective-permute-done.6, bf16[2,128,256]{2,1,0:T(8,128)(2,1)S(1)} %collective-permute-done.5), kind=kLoop, calls=%fused_computation | loop fusion | flops 327680 | bytes 655360 | tf_op jit(solution)/shard_map/convert_element_type | solution.py:625
Async XLA Ops:
  2.2 13.5 %copy-start = (bf16[272,256]{1,0:T(8,128)(2,1)S(1)}, bf16[272,256]{1,0:T(8,128)(2,1)}, u32[]{:S(2)}) copy-start(bf16[272,256]{1,0:T(8,128)(2,1)} %pack.1.refs_7_.refs_4_) | copy-start | bytes 417796
  2.2 13.5 %copy-start.2 = (f32[16]{0:T(128)S(1)}, f32[16]{0:T(128)}, u32[]{:S(2)}) copy-start(f32[16]{0:T(128)} %refs_2_.7) | copy-start | bytes 196
  2.2 13.5 %copy-start.3 = (s32[64]{0:T(128)S(1)}, s32[64]{0:T(128)}, u32[]{:S(2)}) copy-start(s32[64]{0:T(128)} %refs_0_.7) | copy-start | bytes 772
  2.2 13.5 %copy-start.4 = (s32[16]{0:T(128)S(1)}, s32[16]{0:T(128)}, u32[]{:S(2)}) copy-start(s32[16]{0:T(128)} %refs_1_.7) | copy-start | bytes 196
  2.2 11.5 %collective-permute-start = (bf16[272,256]{1,0:T(8,128)(2,1)}, bf16[272,256]{1,0:T(8,128)(2,1)S(1)}, u32[]{:S(2)}, u32[]{:S(2)}) collective-permute-start(bf16[272,256]{1,0:T(8,128)(2,1)} %pack.1.refs_7_.refs_4_), channel_id=1, source_target_pairs={{0,8},{4,12},{8,0},{12,4},{1,9},{5,13},{9,1},{13,5},{2,10},{6,14},... | collective-permute-start | bytes 417800 | tf_op jit(solution)/shard_map/ppermute | solution.py:540
  6.3 7.4 %collective-permute-start.1 = (f32[16]{0:T(128)}, f32[16]{0:T(128)S(1)}, u32[]{:S(2)}, u32[]{:S(2)}) collective-permute-start(f32[16]{0:T(128)} %refs_2_.7), channel_id=1, source_target_pairs={{0,12},{4,8},{8,4},{12,0},{1,13},{5,9},{9,5},{13,1},{2,14},{6,10},... | collective-permute-start | bytes 200 | tf_op jit(solution)/shard_map/ppermute | solution.py:540
  7.7 8.0 %collective-permute-start.2 = (bf16[272,256]{1,0:T(8,128)(2,1)}, bf16[272,256]{1,0:T(8,128)(2,1)S(1)}, u32[]{:S(2)}, u32[]{:S(2)}) collective-permute-start(bf16[272,256]{1,0:T(8,128)(2,1)} %pack.1.refs_7_.refs_4_), channel_id=1, source_target_pairs={{0,4},{4,0},{8,12},{12,8},{1,5},{5,1},{9,13},{13,9},{2,6},{6,2},{1... | collective-permute-start | bytes 417800 | tf_op jit(solution)/shard_map/ppermute | solution.py:540
  13.8 8.0 %collective-permute-start.4 = (bf16[272,256]{1,0:T(8,128)(2,1)S(1)}, bf16[272,256]{1,0:T(8,128)(2,1)S(1)}, u32[]{:S(2)}, u32[]{:S(2)}) collective-permute-start(bf16[272,256]{1,0:T(8,128)(2,1)S(1)} %collective-permute-done.refs_9_.refs_10_.refs_6_), channel_id=1, source_target_pairs={{0,4},{4,0},{8,12},{12,8},{1,5},{5,1},{9,13},{13,9},{2,6},{6,2},{1... | collective-permute-start | bytes 417800 | tf_op jit(solution)/shard_map/ppermute | solution.py:540
  20.0 11.3 %collective-permute-start.3 = (bf16[2,128,256]{2,1,0:T(8,128)(2,1)S(1)}, bf16[2,128,256]{2,1,0:T(8,128)(2,1)S(1)}, u32[]{:S(2)}, u32[]{:S(2)}) collective-permute-start(bf16[2,128,256]{2,1,0:T(8,128)(2,1)S(1)} %get-tuple-element.28), channel_id=1, source_target_pairs={{0,8},{4,12},{8,0},{12,4},{1,9},{5,13},{9,1},{13,5},{2,10},{6,14},... | collective-permute-start | bytes 393224 | tf_op jit(solution)/shard_map/ppermute | solution.py:540
  21.8 9.5 %copy-start.1 = (bf16[4,2,128,256]{3,2,1,0:T(8,128)(2,1)S(1)}, bf16[4,2,128,256]{3,2,1,0:T(8,128)(2,1)}, u32[]{:S(2)}) copy-start(bf16[4,2,128,256]{3,2,1,0:T(8,128)(2,1)} %get-tuple-element.23.refs_7_) | copy-start | bytes 1572868
  28.6 6.1 %collective-permute-start.5 = (bf16[2,128,256]{2,1,0:T(8,128)(2,1)S(1)}, bf16[2,128,256]{2,1,0:T(8,128)(2,1)S(1)}, u32[]{:S(2)}, u32[]{:S(2)}) collective-permute-start(bf16[2,128,256]{2,1,0:T(8,128)(2,1)S(1)} %get-tuple-element.37), channel_id=1, source_target_pairs={{0,4},{4,0},{8,12},{12,8},{1,5},{5,1},{9,13},{13,9},{2,6},{6,2},{1... | collective-permute-start | bytes 393224 | tf_op jit(solution)/shard_map/ppermute | solution.py:540
  30.0 7.0 %collective-permute-start.6 = (bf16[2,128,256]{2,1,0:T(8,128)(2,1)S(1)}, bf16[2,128,256]{2,1,0:T(8,128)(2,1)S(1)}, u32[]{:S(2)}, u32[]{:S(2)}) collective-permute-start(bf16[2,128,256]{2,1,0:T(8,128)(2,1)S(1)} %get-tuple-element.38), channel_id=1, source_target_pairs={{0,12},{4,8},{8,4},{12,0},{1,13},{5,9},{9,5},{13,1},{2,14},{6,10},... | collective-permute-start | bytes 393224 | tf_op jit(solution)/shard_map/ppermute | solution.py:540

commit v18 on v16

--- a/solution.py
+++ b/solution.py
@@ -11,13 +11,12 @@
 
 HD = 128
 NEG = -1e30
-TAIL = 16
 F32 = jnp.float32
 BF16 = jnp.bfloat16
 PAIR = 2
 FAR = 3
 VMEM_BYTES = 63 * 1024 * 1024
-GROUP_BYTES = 53 * 1024 * 1024
+GROUP_BYTES = 54528 * 1024
 FINISH_BYTES = 24 * 1024 * 1024
 ANYWHERE = pl.BlockSpec(memory_space=pl.ANY)
 
@@ -217,60 +216,16 @@
             found = found + (resp_prompt[me * z.count + i] == prompt).astype(jnp.int32)
 
 
-def prompt_total(z, me, prompt, resp_prompt, tails, far_rewards):
-    sums = jnp.zeros((1, z.width), F32)
-    for s in range(tails.shape[0]):
-        tail = tails[s].astype(F32)
-        sums += tail[0:1] + tail[1:2] + tail[2:3]
-    lane = lax.broadcasted_iota(jnp.int32, sums.shape, 1)
-    total = jnp.sum(jnp.where(lane == prompt, sums, 0.0))
-    for i in range(z.count):
-        total += jnp.where(resp_prompt[(me ^ FAR) * z.count + i] == prompt, far_rewards[i], 0.0)
+def prompt_total(z, me, prompt, resp_prompt, rewards):
+    total = jnp.float32(0.0)
+    for s in range(z.n_dp):
+        for i in range(z.count):
+            total += jnp.where(resp_prompt[(me ^ s) * z.count + i] == prompt, rewards[s][i], 0.0)
     return total
 
 
 def reward_factor(z, reward, total, length):
     return (reward - total / z.count) * (z.tokens / length.astype(F32))
-
-
-def pack_kernel(z, prompt_hbm, rewards_hbm, resp_prompt_hbm, payload, rewards, resp_prompt, staged, sems):
-    me = lax.axis_index("dp")
-    small = [
-        pltpu.make_async_copy(rewards_hbm, rewards, sems.at[0]),
-        pltpu.make_async_copy(resp_prompt_hbm, resp_prompt, sems.at[1]),
-    ]
-    large = [
-        pltpu.make_async_copy(
-            prompt_hbm.at[n], staged.at[pl.ds(n * z.prefix_len, z.prefix_len)], sems.at[2 + n]
-        )
-        for n in range(2)
-    ]
-    for copy in small + large:
-        copy.start()
-    for copy in small:
-        copy.wait()
-    lane = lax.broadcasted_iota(jnp.int32, (1, z.width), 1)
-    sums = jnp.zeros((1, z.width), F32)
-    for i in range(z.count):
-        sums += jnp.where(lane == resp_prompt[me * z.count + i], rewards[i], 0.0)
-    high = sums.astype(BF16).astype(F32)
-    middle = (sums - high).astype(BF16).astype(F32)
-    low = sums - high - middle
-    row = lax.broadcasted_iota(jnp.int32, (TAIL, z.width), 0)
-    pieces = jnp.where(row == 0, high, jnp.where(row == 1, middle, jnp.where(row == 2, low, 0.0)))
-    staged[2 * z.prefix_len :, :] = pieces.astype(BF16)
-    for copy in large:
-        copy.wait()
-    last = pltpu.make_async_copy(staged, payload, sems.at[0])
-    last.start()
-    last.wait()
-
-
-def tail_copies(z, payloads, tails, sems):
-    return [
-        pltpu.make_async_copy(payload.at[pl.ds(2 * z.prefix_len, TAIL)], tails.at[n], sems.at[n])
-        for n, payload in enumerate(payloads)
-    ]
 
 
 def row_copies(here, there, at_here, at_there, sems):
@@ -293,38 +248,34 @@
     ]
 
 
-def group_kernel(z, turns, raw, body, ahead, n_tails, aliased, *refs):
-    small_hbm, given = refs[:4], refs[4:7]
-    tail_hbm, prompts = refs[7 : 7 + n_tails], refs[7 + n_tails : 7 + n_tails + len(turns)]
-    refs = refs[7 + n_tails + len(turns) :]
+def group_kernel(z, turns, raw, body, ahead, n_rewards, aliased, *refs):
+    n_small = 2 + n_rewards
+    small_hbm, given, refs = refs[:n_small], refs[n_small : n_small + 3], refs[n_small + 3 :]
+    prompts, refs = refs[: len(turns)], refs[len(turns) :]
     if raw:
         (q_out, self_out), grads_out, in_order, refs = refs[:2], refs[2:3], refs[3:5], refs[5:]
     else:
         in_order, refs = refs[:2], refs[2 + aliased :]
         (q_out, self_out), grads_out, refs = refs[:2], refs[2 : 2 + len(turns)], refs[2 + len(turns) :]
     in_order = (in_order[0].at[0], in_order[0].at[1], in_order[1])
-    (resp_prompt, resp_len, rewards, far_rewards, order, q, og, kv, prefix, tails, acc, out, own, grads,
-     sem_small, sem_tails, sem_prefix, sem_in, sem_out, sem_grads, sem_order) = refs
+    resp_prompt, resp_len, *rewards = refs[:n_small]
+    (order, q, og, kv, prefix, acc, out, own, grads,
+     sem_small, sem_prefix, sem_in, sem_out, sem_grads, sem_order) = refs[n_small:]
     me = lax.axis_index("dp")
     n_slots = len(turns) * z.slots
     span = z.slots * z.tokens
 
     small = [
         pltpu.make_async_copy(src, dst, sem_small.at[n])
-        for n, (src, dst) in enumerate(zip(small_hbm, (resp_prompt, resp_len, rewards, far_rewards)))
+        for n, (src, dst) in enumerate(zip(small_hbm, (resp_prompt, resp_len, *rewards)))
     ]
     prefix_copies = [
-        pltpu.make_async_copy(
-            prompts[t].at[pl.ds(n * z.prefix_len, z.prefix_len)], prefix.at[t, n], sem_prefix.at[t, n]
-        )
-        for t in range(len(turns))
-        for n in range(2)
+        pltpu.make_async_copy(prompts[t], prefix.at[t], sem_prefix.at[t]) for t in range(len(turns))
     ]
-    late = tail_copies(z, tail_hbm, tails, sem_tails)
     first_rows = []
     if not raw:
         first_rows = row_copies(in_order, (q, og, kv), pl.ds(ahead * span, span), pl.ds(0, span), sem_order.at[0])
-    for copy in [*small, *first_rows, *prefix_copies, *late]:
+    for copy in [*small, *first_rows, *prefix_copies]:
         copy.start()
     small[0].wait()
     ordered = [*turns, *ahead] if raw else turns
@@ -345,7 +296,7 @@
     for slot in range(0 if raw else z.slots, len(ordered) * z.slots):
         for copy in copies_in(slot):
             copy.start()
-    for copy in small[1:] + late:
+    for copy in small[1:]:
         copy.wait()
     if not raw:
         acc[...] = jnp.zeros(acc.shape, F32)
@@ -388,12 +339,12 @@
         turn = turns[0]
         for n, other in enumerate(turns[1:], 1):
             turn = jnp.where(t == n, other, turn)
-        total = None if raw else prompt_total(z, me, me ^ turn, resp_prompt, tails, far_rewards)
+        total = None if raw else prompt_total(z, me, me ^ turn, resp_prompt, rewards)
         lens, factors = {}, {}
         for n in mine:
             i = order[first + n]
             lens[n] = resp_len[i]
-            factors[n] = 1.0 if raw else reward_factor(z, rewards[i], total, resp_len[i])
+            factors[n] = 1.0 if raw else reward_factor(z, rewards[0][i], total, resp_len[i])
         units = []
         for pair in range(pairs_in_body):
             places = [first + pair * PAIR + n for n in range(PAIR)]
@@ -441,19 +392,18 @@
         copy.wait()
 
 
-def finish_kernel(z, n_tails, n_come, *refs):
-    small_hbm, tail_hbm = refs[:4], refs[4 : 4 + n_tails]
-    per_resp_hbm, come_hbm = refs[4 + n_tails], refs[5 + n_tails : 5 + n_tails + n_come]
-    q_out, self_out, grads_out = refs[7 + n_tails + n_come : 10 + n_tails + n_come]
-    (resp_prompt, resp_len, rewards, far_rewards, order, tails, out, own, per_resp, come, grads,
-     sem_small, sem_tails, sem_come, sem_in, sem_out) = refs[10 + n_tails + n_come :]
+def finish_kernel(z, n_come, *refs):
+    n_small = 2 + z.n_dp
+    small_hbm, per_resp_hbm, refs = refs[:n_small], refs[n_small], refs[n_small + 1 :]
+    come_hbm, (q_out, self_out, grads_out), refs = refs[:n_come], refs[n_come + 2 : n_come + 5], refs[n_come + 5 :]
+    resp_prompt, resp_len, *rewards = refs[:n_small]
+    order, out, own, per_resp, come, grads, sem_small, sem_come, sem_in, sem_out = refs[n_small:]
     me = lax.axis_index("dp")
     small = [
         pltpu.make_async_copy(src, dst, sem_small.at[n])
-        for n, (src, dst) in enumerate(zip(small_hbm, (resp_prompt, resp_len, rewards, far_rewards)))
+        for n, (src, dst) in enumerate(zip(small_hbm, (resp_prompt, resp_len, *rewards)))
     ]
-    late = tail_copies(z, tail_hbm, tails, sem_tails)
-    late += [pltpu.make_async_copy(src, come.at[n], sem_come.at[n]) for n, src in enumerate(come_hbm)]
+    late = [pltpu.make_async_copy(src, come.at[n], sem_come.at[n]) for n, src in enumerate(come_hbm)]
     late += [pltpu.make_async_copy(per_resp_hbm, per_resp, sem_come.at[n_come])]
     for copy in small + late:
         copy.start()
@@ -469,11 +419,11 @@
             copy.start()
     for copy in small[1:] + late:
         copy.wait()
-    total = prompt_total(z, me, me, resp_prompt, tails, far_rewards)
+    total = prompt_total(z, me, me, resp_prompt, rewards)
     summed = come[0].astype(F32)
     for n in range(1, n_come):
         summed += come[n].astype(F32)
-    factors = [reward_factor(z, rewards[order[n]], total, resp_len[order[n]]) for n in range(z.slots)]
+    factors = [reward_factor(z, rewards[0][order[n]], total, resp_len[order[n]]) for n in range(z.slots)]
     for slot in range(z.slots):
         summed += per_resp[slot].astype(F32) * factors[slot]
     grads[...] = summed
@@ -499,65 +449,49 @@
     one = (2, z.prefix_len, z.width)
     params = pltpu.CompilerParams(vmem_limit_bytes=VMEM_BYTES)
     cost = pl.CostEstimate(flops=0, bytes_accessed=0, transcendentals=0)
-    payload = pl.pallas_call(
-        functools.partial(pack_kernel, z),
-        out_shape=jax.ShapeDtypeStruct((2 * z.prefix_len + TAIL, z.width), BF16),
-        in_specs=[ANYWHERE] * 3,
-        out_specs=ANYWHERE,
-        scratch_shapes=[
-            pltpu.SMEM(rewards.shape, F32),
-            pltpu.SMEM(resp_prompt.shape, jnp.int32),
-            pltpu.VMEM((2 * z.prefix_len + TAIL, z.width), BF16),
-            pltpu.SemaphoreType.DMA((4,)),
-        ],
-        compiler_params=pltpu.CompilerParams(vmem_limit_bytes=VMEM_BYTES),
-        name="pack",
-    )(prompt_kv, rewards, resp_prompt)
-
     assert n_dp == FAR + 1
 
     def swap(x, s):
         return lax.ppermute(x, "dp", [(i, i ^ s) for i in range(n_dp)])
 
-    payloads = {0: payload, 2: swap(payload, 2), 1: swap(payload, 1)}
-    tails = [payloads[s] for s in range(FAR)]
-    small = (resp_prompt, resp_len, rewards)
-    far_rewards = swap(rewards, FAR)
-    smem = [pltpu.SMEM(x.shape, x.dtype) for x in (*small, rewards)]
+    prompts = {0: prompt_kv, 2: swap(prompt_kv, 2), 1: swap(prompt_kv, 1)}
+    others = [swap(rewards, s) for s in range(1, n_dp)]
+    small = (resp_prompt, resp_len)
     slots = z.slots
+
+    def smem_like(arrays):
+        return [pltpu.SMEM(x.shape, x.dtype) for x in arrays]
 
     def grads_of(turns, raw, body, ahead, in_order=(), written=()):
         n_slots, n_turns = len(turns) * slots, len(turns)
         n_ahead = len(ahead) * slots if raw else 0
         n_held = n_slots + n_ahead
-        used_tails = [] if raw else tails
-        used_small = (*small, rewards if raw else far_rewards)
-        prompts = [payloads[turn] for turn in turns]
-        operands = [*used_small, resp_q, out_grad, resp_kv, *used_tails, *prompts, *in_order, *written]
+        used_rewards = [] if raw else [rewards, *others]
+        used_small = [*small, *used_rewards]
+        used_prompts = [prompts[turn] for turn in turns]
+        operands = [*used_small, resp_q, out_grad, resp_kv, *used_prompts, *in_order, *written]
         grads_shapes = [(slots,) + one] if raw else [one] * n_turns
         ordered_shapes = [(2, n_ahead * z.tokens, z.lanes), (2, n_ahead * z.tokens, z.width)] if raw else []
         return pl.pallas_call(
-            functools.partial(group_kernel, z, turns, raw, body, ahead, len(used_tails), len(written)),
+            functools.partial(group_kernel, z, turns, raw, body, ahead, len(used_rewards), len(written)),
             out_shape=[shape(resp_q.shape, BF16), shape(resp_kv.shape, BF16)]
             + [shape(x, BF16) for x in grads_shapes + ordered_shapes],
             in_specs=[ANYWHERE] * len(operands),
             out_specs=[ANYWHERE] * (2 + len(grads_shapes) + len(ordered_shapes)),
             input_output_aliases={len(operands) - 2: 0, len(operands) - 1: 1} if written else {},
             scratch_shapes=[
-                *smem,
+                *smem_like(used_small),
                 pltpu.SMEM((n_held + 1,), jnp.int32),
                 pltpu.VMEM((n_held * z.tokens, z.lanes), BF16),
                 pltpu.VMEM((n_held * z.tokens, z.lanes), BF16),
                 pltpu.VMEM((2, n_held * z.tokens, z.width), BF16),
                 pltpu.VMEM((n_turns,) + one, BF16),
-                pltpu.VMEM((FAR, TAIL, z.width), BF16),
                 pltpu.VMEM((n_turns,) + one, F32),
                 pltpu.VMEM((n_slots, z.tokens, z.lanes), BF16),
                 pltpu.VMEM((n_slots, 2, z.tokens, z.width), BF16),
                 pltpu.VMEM(grads_shapes[0] if raw else (n_turns,) + one, BF16),
-                pltpu.SemaphoreType.DMA((len(smem),)),
-                pltpu.SemaphoreType.DMA((FAR,)),
-                pltpu.SemaphoreType.DMA((n_turns, 2)),
+                pltpu.SemaphoreType.DMA((len(used_small),)),
+                pltpu.SemaphoreType.DMA((n_turns,)),
                 pltpu.SemaphoreType.DMA((n_held, 3)),
                 pltpu.SemaphoreType.DMA((n_slots, 2)),
                 pltpu.SemaphoreType.DMA((n_turns,)),
@@ -570,30 +504,29 @@
 
     *written, per_resp, rows_ahead, kv_ahead = grads_of((0,), True, 1, (2, FAR))
     in_order = (rows_ahead, kv_ahead)
-    onward, per_resp, far_rewards = lax.optimization_barrier((payloads[2], per_resp, far_rewards))
-    payloads[FAR] = swap(onward, 1)
+    onward, per_resp, *others = lax.optimization_barrier((prompts[2], per_resp, *others))
+    prompts[FAR] = swap(onward, 1)
     *written, for_2 = grads_of((2,), False, slots // PAIR, 0, in_order, written)
     come = [swap(for_2, 2)]
     *written, for_far, for_1 = grads_of((FAR, 1), False, slots // PAIR, 1, in_order, written)
     last = [swap(for_far, FAR), swap(for_1, 1)]
-    operands = [*small, far_rewards, *tails, per_resp, *come, *written]
+    all_small = [*small, rewards, *others]
+    operands = [*all_small, per_resp, *come, *written]
     q_out, self_out, own_grads = pl.pallas_call(
-        functools.partial(finish_kernel, z, len(tails), len(come)),
+        functools.partial(finish_kernel, z, len(come)),
         out_shape=[shape(resp_q.shape, BF16), shape(resp_kv.shape, BF16), shape(one, F32)],
         in_specs=[ANYWHERE] * len(operands),
         out_specs=[ANYWHERE] * 3,
         input_output_aliases={len(operands) - 2: 0, len(operands) - 1: 1},
         scratch_shapes=[
-            *smem,
+            *smem_like(all_small),
             pltpu.SMEM((slots + 1,), jnp.int32),
-            pltpu.VMEM((FAR, TAIL, z.width), BF16),
             pltpu.VMEM((slots, z.tokens, z.lanes), BF16),
             pltpu.VMEM((slots, 2, z.tokens, z.width), BF16),
             pltpu.VMEM((slots,) + one, BF16),
             pltpu.VMEM((len(come),) + one, BF16),
             pltpu.VMEM(one, F32),
-            pltpu.SemaphoreType.DMA((len(smem),)),
-            pltpu.SemaphoreType.DMA((FAR,)),
+            pltpu.SemaphoreType.DMA((len(all_small),)),
             pltpu.SemaphoreType.DMA((len(come) + 1,)),
             pltpu.SemaphoreType.DMA((slots, 3)),
             pltpu.SemaphoreType.DMA((slots, 3)),

time: 37.2 us -> 37.2 us (level)
  starting transfers between devices: 11.2 us -> 14.2 us
  Pallas kernels: 20.9 us -> 19.2 us
  waiting for transfers between devices: 3.46 us -> 2.12 us
    ppermute x7 -> x9, starting transfers between devices: 11.2 us -> 14.2 us  [swap(): return lax.ppermute(x, 'dp', [(i, i ^ s) for i in range(n_dp)])]
    pallas_call x2 -> x1, Pallas kernels: 4.39 us -> 2.82 us  [near_shards(): pl.pallas_call(functools.partial(finish_kernel, z, len(come)), out_shape=...]
    ppermute x7 -> x9, waiting for transfers between devices: 3.46 us -> 2.12 us  [swap(): return lax.ppermute(x, 'dp', [(i, i ^ s) for i in range(n_dp)])]
  transfers between devices with their start and end apart: 7 -> 9, of which waited for: 1 -> 2; matrix products, arithmetic and copies ran while one was open for 0% -> 0% of each run, Pallas kernels for 52% -> 52%
where the time goes in v18:
time: 37.2 us; the launch traced here: 37 us
  Pallas kernels  19.2 us (52%)
  starting transfers between devices  14.2 us (38%)
  waiting for transfers between devices  2.12 us (6%)
  between operations  0.73 us (2%)
  other arithmetic  0.7 us (2%)
    pallas_call x3, Pallas kernels, grads_of(): pl.pallas_call(functools.partial(group_kernel, z, turns, raw, body, ahead...  16.4 us
    ppermute x9, starting transfers between devices, swap(): return lax.ppermute(x, 'dp', [(i, i ^ s) for i in range(n_dp)])  14.2 us
    pallas_call x1, Pallas kernels, near_shards(): pl.pallas_call(functools.partial(finish_kernel, z, len(come)), out_shape=...  2.82 us
    ppermute x9, waiting for transfers between devices, swap(): return lax.ppermute(x, 'dp', [(i, i ^ s) for i in range(n_dp)])  2.12 us
  transfers between devices with their start and end apart: 9, of which 2 were waited for; matrix products, arithmetic and copies ran while one was open for 0% of the time, Pallas kernels for 52%

profile of v18, /device:TPU:0, one launch (start us, length us, event | category | flops | bytes accessed | tf_op | source)
XLA Modules:
  0.0 37.0 jit_solution(9784779812818317893)
XLA Ops:
  0.6 0.0 copy-start.3
  0.6 0.0 copy-start.2
  0.7 0.0 copy-start.1
  0.7 4.1 %collective-permute-start = (bf16[2,128,256]{2,1,0:T(8,128)(2,1)}, bf16[2,128,256]{2,1,0:T(8,128)(2,1)S(1)}, u32[]{:S(2)}, u32[]{:S(2)}) collective-permute-start(bf16[2,128,256]{2,1,0:T(8,128)(2,1)} %refs_5_.1), channel_id=1, source_target_pairs={{0,8},{4,12},{8,0},{12,4},{1,9},{5,13},{9,1},{13,5},{2,10},{6,14},... | collective-permute-start | bytes 393224 | tf_op jit(solution)/shard_map/ppermute | solution.py:455
  4.8 1.3 %collective-permute-start.3 = (f32[16]{0:T(128)}, f32[16]{0:T(128)S(1)}, u32[]{:S(2)}, u32[]{:S(2)}) collective-permute-start(f32[16]{0:T(128)} %refs_2_.7), channel_id=1, source_target_pairs={{0,12},{4,8},{8,4},{12,0},{1,13},{5,9},{9,5},{13,1},{2,14},{6,10},... | collective-permute-start | bytes 200 | tf_op jit(solution)/shard_map/ppermute | solution.py:455
  6.1 1.7 %collective-permute-start.2 = (f32[16]{0:T(128)}, f32[16]{0:T(128)S(1)}, u32[]{:S(2)}, u32[]{:S(2)}) collective-permute-start(f32[16]{0:T(128)} %refs_2_.7), channel_id=1, source_target_pairs={{0,8},{4,12},{8,0},{12,4},{1,9},{5,13},{9,1},{13,5},{2,10},{6,14},... | collective-permute-start | bytes 200 | tf_op jit(solution)/shard_map/ppermute | solution.py:455
  7.8 1.3 %collective-permute-start.1 = (f32[16]{0:T(128)}, f32[16]{0:T(128)S(1)}, u32[]{:S(2)}, u32[]{:S(2)}) collective-permute-start(f32[16]{0:T(128)} %refs_2_.7), channel_id=1, source_target_pairs={{0,4},{4,0},{8,12},{12,8},{1,5},{5,1},{9,13},{13,9},{2,6},{6,2},{1... | collective-permute-start | bytes 200 | tf_op jit(solution)/shard_map/ppermute | solution.py:455
  9.2 0.7 %collective-permute-start.6 = (bf16[2,128,256]{2,1,0:T(8,128)(2,1)}, bf16[2,128,256]{2,1,0:T(8,128)(2,1)S(1)}, u32[]{:S(2)}, u32[]{:S(2)}) collective-permute-start(bf16[2,128,256]{2,1,0:T(8,128)(2,1)} %refs_5_.1), channel_id=1, source_target_pairs={{0,4},{4,0},{8,12},{12,8},{1,5},{5,1},{9,13},{13,9},{2,6},{6,2},{1... | collective-permute-start | bytes 393224 | tf_op jit(solution)/shard_map/ppermute | solution.py:455
  9.8 5.8 %raw_grads.1 = (bf16[1024,1280]{1,0:T(8,128)(2,1)}, bf16[2,1024,256]{2,1,0:T(8,128)(2,1)}, bf16[4,2,128,256]{3,2,1,0:T(8,128)(2,1)}, bf16[2,512,1280]{2,1,0:T(8,128)(2,1)}, bf16[2,512,256]{2,1,0:T(8,128)(2,1)}) custom-call(s32[64]{0:T(128)} %refs_0_.7, s32[16]{0:T(128)} %refs_1_.7, bf16[1024,1280]{1,0:T(8,128)(2,1)} %refs_6_.3, bf16[1024,1280]{1,0:T(8,128)(2,1)} %refs_7_.3, ...), custom_call_target="tpu_custom_call" | custom-call | tf_op jit(solution)/shard_map/raw_grads/pallas_call | solution.py:475
  15.6 0.0 collective-permute-done.3.refs_5_
  15.6 0.0 collective-permute-done.2.refs_4_
  15.6 0.0 collective-permute-done.1.refs_3_
  15.7 0.0 collective-permute-done.refs_9_
  15.7 1.4 %collective-permute-start.5 = (bf16[2,128,256]{2,1,0:T(8,128)(2,1)S(1)}, bf16[2,128,256]{2,1,0:T(8,128)(2,1)S(1)}, u32[]{:S(2)}, u32[]{:S(2)}) collective-permute-start(bf16[2,128,256]{2,1,0:T(8,128)(2,1)S(1)} %collective-permute-done.refs_9_), channel_id=1, source_target_pairs={{0,4},{4,0},{8,12},{12,8},{1,5},{5,1},{9,13},{13,9},{2,6},{6,2},{1... | collective-permute-start | bytes 393224 | tf_op jit(solution)/shard_map/ppermute | solution.py:455
  17.1 0.0 copy-done.3
  17.1 0.0 copy-done.2
  17.1 0.0 copy-done.1
  17.1 4.3 %group_grads.2 = (bf16[1024,1280]{1,0:T(8,128)(2,1)}, bf16[2,1024,256]{2,1,0:T(8,128)(2,1)}, bf16[2,128,256]{2,1,0:T(8,128)(2,1)S(1)}) custom-call(s32[64]{0:T(128)S(1)} %copy-done.1, s32[16]{0:T(128)S(1)} %copy-done.2, f32[16]{0:T(128)S(1)} %copy-done.3, f32[16]{0:T(128)S(1)} %collective-permute-done.1.refs_3_, ...), custom_call_target="tpu_custom_call", output_to_operand_aliasing={{0}: (12, {}), {1}: (13, {})} | custom-call | tf_op jit(solution)/shard_map/group_grads/pallas_call | solution.py:475
  21.4 0.2 collective-permute-start.4
  21.6 0.0 collective-permute-done.6.refs_10_
  21.6 0.0 collective-permute-done.5.refs_9_
  21.6 0.0 copy-start
  21.6 6.3 %group_grads.3 = (bf16[1024,1280]{1,0:T(8,128)(2,1)}, bf16[2,1024,256]{2,1,0:T(8,128)(2,1)}, bf16[2,128,256]{2,1,0:T(8,128)(2,1)S(1)}, bf16[2,128,256]{2,1,0:T(8,128)(2,1)S(1)}) custom-call(s32[64]{0:T(128)S(1)} %copy-done.1, s32[16]{0:T(128)S(1)} %copy-done.2, f32[16]{0:T(128)S(1)} %copy-done.3, ...), custom_call_target="tpu_custom_call", output_to_operand_aliasing={{0}: (13, {}), {1}: (14, {})} | custom-call | tf_op jit(solution)/shard_map/group_grads/pallas_call | solution.py:475
  27.9 3.0 %collective-permute-start.7 = (bf16[2,128,256]{2,1,0:T(8,128)(2,1)S(1)}, bf16[2,128,256]{2,1,0:T(8,128)(2,1)S(1)}, u32[]{:S(2)}, u32[]{:S(2)}) collective-permute-start(bf16[2,128,256]{2,1,0:T(8,128)(2,1)S(1)} %get-tuple-element.41), channel_id=1, source_target_pairs={{0,12},{4,8},{8,4},{12,0},{1,13},{5,9},{9,5},{13,1},{2,14},{6,10},... | collective-permute-start | bytes 393224 | tf_op jit(solution)/shard_map/ppermute | solution.py:455
  30.9 0.5 %collective-permute-start.8 = (bf16[2,128,256]{2,1,0:T(8,128)(2,1)S(1)}, bf16[2,128,256]{2,1,0:T(8,128)(2,1)S(1)}, u32[]{:S(2)}, u32[]{:S(2)}) collective-permute-start(bf16[2,128,256]{2,1,0:T(8,128)(2,1)S(1)} %get-tuple-element.42), channel_id=1, source_target_pairs={{0,4},{4,0},{8,12},{12,8},{1,5},{5,1},{9,13},{13,9},{2,6},{6,2},{1... | collective-permute-start | bytes 393224 | tf_op jit(solution)/shard_map/ppermute | solution.py:455
  31.3 0.0 collective-permute-done.4.refs_7_
  31.3 0.0 copy-done
  31.3 2.8 %finish_own.1 = (bf16[1024,1280]{1,0:T(8,128)(2,1)}, bf16[2,1024,256]{2,1,0:T(8,128)(2,1)}, f32[2,128,256]{2,1,0:T(8,128)S(1)}) custom-call(s32[64]{0:T(128)S(1)} %copy-done.1, s32[16]{0:T(128)S(1)} %copy-done.2, f32[16]{0:T(128)S(1)} %copy-done.3, f32[16]{0:T(128)S(1)} %collective-permute-done.1.refs_3_, ...), custom_call_target="tpu_custom_call", output_to_operand_aliasing={{0}: (8, {}), {1}: (9, {})} | custom-call | tf_op jit(solution)/shard_map/finish_own/pallas_call | solution.py:515
  34.2 0.7 %collective-permute-done.7 = bf16[2,128,256]{2,1,0:T(8,128)(2,1)S(1)} collective-permute-done((bf16[2,128,256]{2,1,0:T(8,128)(2,1)S(1)}, bf16[2,128,256]{2,1,0:T(8,128)(2,1)S(1)}, u32[]{:S(2)}, u32[]{:S(2)}) %collective-permute-start.7) | collective-permute-done | bytes 131104 | tf_op jit(solution)/shard_map/ppermute | solution.py:455
  34.9 1.4 %collective-permute-done.8 = bf16[2,128,256]{2,1,0:T(8,128)(2,1)S(1)} collective-permute-done((bf16[2,128,256]{2,1,0:T(8,128)(2,1)S(1)}, bf16[2,128,256]{2,1,0:T(8,128)(2,1)S(1)}, u32[]{:S(2)}, u32[]{:S(2)}) %collective-permute-start.8) | collective-permute-done | bytes 131104 | tf_op jit(solution)/shard_map/ppermute | solution.py:455
  36.3 0.7 %add_convert_fusion = bf16[2,128,256]{2,1,0:T(8,128)(2,1)} fusion(f32[2,128,256]{2,1,0:T(8,128)S(1)} %get-tuple-element.40, bf16[2,128,256]{2,1,0:T(8,128)(2,1)S(1)} %collective-permute-done.8, bf16[2,128,256]{2,1,0:T(8,128)(2,1)S(1)} %collective-permute-done.7), kind=kLoop, calls=%fused_computation | loop fusion | flops 327680 | bytes 655360 | tf_op jit(solution)/shard_map/convert_element_type | solution.py:538
Async XLA Ops:
  0.6 16.4 %copy-start.3 = (f32[16]{0:T(128)S(1)}, f32[16]{0:T(128)}, u32[]{:S(2)}) copy-start(f32[16]{0:T(128)} %refs_2_.7) | copy-start | bytes 196
  0.6 16.4 %copy-start.2 = (s32[16]{0:T(128)S(1)}, s32[16]{0:T(128)}, u32[]{:S(2)}) copy-start(s32[16]{0:T(128)} %refs_1_.7) | copy-start | bytes 196
  0.7 16.4 %copy-start.1 = (s32[64]{0:T(128)S(1)}, s32[64]{0:T(128)}, u32[]{:S(2)}) copy-start(s32[64]{0:T(128)} %refs_0_.7) | copy-start | bytes 772
  0.7 15.0 %collective-permute-start = (bf16[2,128,256]{2,1,0:T(8,128)(2,1)}, bf16[2,128,256]{2,1,0:T(8,128)(2,1)S(1)}, u32[]{:S(2)}, u32[]{:S(2)}) collective-permute-start(bf16[2,128,256]{2,1,0:T(8,128)(2,1)} %refs_5_.1), channel_id=1, source_target_pairs={{0,8},{4,12},{8,0},{12,4},{1,9},{5,13},{9,1},{13,5},{2,10},{6,14},... | collective-permute-start | bytes 393224 | tf_op jit(solution)/shard_map/ppermute | solution.py:455
  4.8 10.9 %collective-permute-start.3 = (f32[16]{0:T(128)}, f32[16]{0:T(128)S(1)}, u32[]{:S(2)}, u32[]{:S(2)}) collective-permute-start(f32[16]{0:T(128)} %refs_2_.7), channel_id=1, source_target_pairs={{0,12},{4,8},{8,4},{12,0},{1,13},{5,9},{9,5},{13,1},{2,14},{6,10},... | collective-permute-start | bytes 200 | tf_op jit(solution)/shard_map/ppermute | solution.py:455
  6.1 9.5 %collective-permute-start.2 = (f32[16]{0:T(128)}, f32[16]{0:T(128)S(1)}, u32[]{:S(2)}, u32[]{:S(2)}) collective-permute-start(f32[16]{0:T(128)} %refs_2_.7), channel_id=1, source_target_pairs={{0,8},{4,12},{8,0},{12,4},{1,9},{5,13},{9,1},{13,5},{2,10},{6,14},... | collective-permute-start | bytes 200 | tf_op jit(solution)/shard_map/ppermute | solution.py:455
  7.8 7.8 %collective-permute-start.1 = (f32[16]{0:T(128)}, f32[16]{0:T(128)S(1)}, u32[]{:S(2)}, u32[]{:S(2)}) collective-permute-start(f32[16]{0:T(128)} %refs_2_.7), channel_id=1, source_target_pairs={{0,4},{4,0},{8,12},{12,8},{1,5},{5,1},{9,13},{13,9},{2,6},{6,2},{1... | collective-permute-start | bytes 200 | tf_op jit(solution)/shard_map/ppermute | solution.py:455
  9.2 12.4 %collective-permute-start.6 = (bf16[2,128,256]{2,1,0:T(8,128)(2,1)}, bf16[2,128,256]{2,1,0:T(8,128)(2,1)S(1)}, u32[]{:S(2)}, u32[]{:S(2)}) collective-permute-start(bf16[2,128,256]{2,1,0:T(8,128)(2,1)} %refs_5_.1), channel_id=1, source_target_pairs={{0,4},{4,0},{8,12},{12,8},{1,5},{5,1},{9,13},{13,9},{2,6},{6,2},{1... | collective-permute-start | bytes 393224 | tf_op jit(solution)/shard_map/ppermute | solution.py:455
  15.7 5.9 %collective-permute-start.5 = (bf16[2,128,256]{2,1,0:T(8,128)(2,1)S(1)}, bf16[2,128,256]{2,1,0:T(8,128)(2,1)S(1)}, u32[]{:S(2)}, u32[]{:S(2)}) collective-permute-start(bf16[2,128,256]{2,1,0:T(8,128)(2,1)S(1)} %collective-permute-done.refs_9_), channel_id=1, source_target_pairs={{0,4},{4,0},{8,12},{12,8},{1,5},{5,1},{9,13},{13,9},{2,6},{6,2},{1... | collective-permute-start | bytes 393224 | tf_op jit(solution)/shard_map/ppermute | solution.py:455
  21.4 10.0 %collective-permute-start.4 = (bf16[2,128,256]{2,1,0:T(8,128)(2,1)S(1)}, bf16[2,128,256]{2,1,0:T(8,128)(2,1)S(1)}, u32[]{:S(2)}, u32[]{:S(2)}) collective-permute-start(bf16[2,128,256]{2,1,0:T(8,128)(2,1)S(1)} %get-tuple-element.32), channel_id=1, source_target_pairs={{0,8},{4,12},{8,0},{12,4},{1,9},{5,13},{9,1},{13,5},{2,10},{6,14},... | collective-permute-start | bytes 393224 | tf_op jit(solution)/shard_map/ppermute | solution.py:455
  21.6 9.8 %copy-start = (bf16[4,2,128,256]{3,2,1,0:T(8,128)(2,1)S(1)}, bf16[4,2,128,256]{3,2,1,0:T(8,128)(2,1)}, u32[]{:S(2)}) copy-start(bf16[4,2,128,256]{3,2,1,0:T(8,128)(2,1)} %get-tuple-element.27.refs_6_) | copy-start | bytes 1572868
  27.9 7.0 %collective-permute-start.7 = (bf16[2,128,256]{2,1,0:T(8,128)(2,1)S(1)}, bf16[2,128,256]{2,1,0:T(8,128)(2,1)S(1)}, u32[]{:S(2)}, u32[]{:S(2)}) collective-permute-start(bf16[2,128,256]{2,1,0:T(8,128)(2,1)S(1)} %get-tuple-element.41), channel_id=1, source_target_pairs={{0,12},{4,8},{8,4},{12,0},{1,13},{5,9},{9,5},{13,1},{2,14},{6,10},... | collective-permute-start | bytes 393224 | tf_op jit(solution)/shard_map/ppermute | solution.py:455
  30.9 5.4 %collective-permute-start.8 = (bf16[2,128,256]{2,1,0:T(8,128)(2,1)S(1)}, bf16[2,128,256]{2,1,0:T(8,128)(2,1)S(1)}, u32[]{:S(2)}, u32[]{:S(2)}) collective-permute-start(bf16[2,128,256]{2,1,0:T(8,128)(2,1)S(1)} %get-tuple-element.42), channel_id=1, source_target_pairs={{0,4},{4,0},{8,12},{12,8},{1,5},{5,1},{9,13},{13,9},{2,6},{6,2},{1... | collective-permute-start | bytes 393224 | tf_op jit(solution)/shard_map/ppermute | solution.py:455

commit v19 on v16

--- a/solution.py
+++ b/solution.py
@@ -60,7 +60,7 @@
     factors: list
 
 
-def attend(z, units, q, og, kv, prefix, out, own_out, sink, apart):
+def attend(z, units, q, og, kv, prefix, out, own_out, sink, apart, fine=False):
     tokens, prefix_len, group_size = z.tokens, z.prefix_len, z.group_size
     scale = 1.0 / math.sqrt(HD)
     log_scale = scale * math.log2(math.e)
@@ -128,13 +128,12 @@
 
     def products(c):
         t = c.t
-        c.q_rows, c.g_rows = rows(q, c), rows(og, c)
         if c.side is None:
             key_s, value_s = t.key_pair, t.value_pair
         else:
             key_s, value_s = t.keys[c.side], t.values[c.side]
-        c.scores = dot(jnp.concatenate([t.key_p, key_s], axis=0), c.q_rows, NT)
-        c.gw = dot(jnp.concatenate([t.value_p, value_s], axis=0), c.g_rows, NT)
+        c.scores = dot(jnp.concatenate([t.key_p, key_s], axis=0), rows(q, c), NT)
+        c.gw = dot(jnp.concatenate([t.value_p, value_s], axis=0), rows(og, c), NT)
 
     def weigh(c):
         scores_p, scores_s = c.scores[:prefix_len], c.scores[prefix_len:]
@@ -145,6 +144,8 @@
         top = over_keys(jnp.maximum, scores_p, scores_s)
         c.e_p = jnp.exp2((scores_p - top) * log_scale)
         c.e_s = jnp.exp2((scores_s - top) * log_scale)
+
+    def totals(c):
         total = over_keys(jnp.add, c.e_p, c.e_s)
         weighted = over_keys(jnp.add, c.e_p * c.gw_p, c.e_s * c.gw_s)
         if c.side is None:
@@ -173,8 +174,8 @@
     def outgoing(c):
         t = c.t
         q_grad = (dot(t.key_t, c.d_wide, NN) * scale).astype(BF16).T
-        kg = dot(c.d_all, c.q_rows, NN)
-        vg = dot(c.w_all, c.g_rows, NN)
+        kg = dot(c.d_all, rows(q, c), NN)
+        vg = dot(c.w_all, rows(og, c), NN)
         targets = t.members if c.side is None else [c.side]
         for place, (n, h) in enumerate(c.blocks):
             if c.side is not None or place < len(targets):
@@ -197,7 +198,14 @@
                     keys, values = zip(*t.prefix_sums[n])
                     sink(t.places[n], t.cols, sum(keys) * scale, sum(values))
 
-    stages = (products, weigh, gradients, outgoing)
+    def weigh_and_totals(c):
+        weigh(c)
+        totals(c)
+
+    if fine:
+        stages = (products, weigh, totals, gradients, outgoing)
+    else:
+        stages = (products, weigh_and_totals, gradients, outgoing)
     for step in range(len(chunks) + len(stages) - 1):
         for late, stage in enumerate(stages):
             if 0 <= step - late < len(chunks):
@@ -401,7 +409,7 @@
             at = [token_rows(z, n) for n in places]
             for k in range(z.kv_heads):
                 units.append(Unit(at, places, k, [lens[n] for n in own_places], [factors[n] for n in own_places]))
-        attend(z, units, q, og, kv, prefix.at[t], out, own, sink, raw)
+        attend(z, units, q, og, kv, prefix.at[t], out, own, sink, raw, len(turns) > 1)
         for n in mine:
             for copy in copies_out(first + n):
                 copy.start()

time: 37.2 us -> 37.3 us (level)
  no operation moved by 1% of the time
where the time goes in v19:
time: 37.3 us; the launch traced here: 37 us
  Pallas kernels  20.9 us (56%)
  starting transfers between devices  11.2 us (30%)
  waiting for transfers between devices  3.47 us (9%)
  between operations  0.74 us (2%)
  other arithmetic  0.7 us (2%)
    pallas_call x3, Pallas kernels, grads_of(): pl.pallas_call(functools.partial(group_kernel, z, turns, raw, body, ahead...  16.5 us
    ppermute x7, starting transfers between devices, swap(): return lax.ppermute(x, 'dp', [(i, i ^ s) for i in range(n_dp)])  11.2 us
    ppermute x7, waiting for transfers between devices, swap(): return lax.ppermute(x, 'dp', [(i, i ^ s) for i in range(n_dp)])  3.47 us
    pallas_call x1, Pallas kernels, near_shards(): pl.pallas_call(functools.partial(finish_kernel, z, len(tails), len(come))...  2.83 us
    pallas_call x1, Pallas kernels, near_shards(): pl.pallas_call(functools.partial(pack_kernel, z), out_shape=jax.ShapeDtyp...  1.56 us
  transfers between devices with their start and end apart: 7, of which 1 were waited for; matrix products, arithmetic and copies ran while one was open for 0% of the time, Pallas kernels for 52%

profile of v19, /device:TPU:0, one launch (start us, length us, event | category | flops | bytes accessed | tf_op | source)
XLA Modules:
  0.0 37.0 jit_solution(17896891707605593554)
XLA Ops:
  0.6 1.6 %pack.1.refs_7_.refs_4_ = bf16[272,256]{1,0:T(8,128)(2,1)} custom-call(bf16[2,128,256]{2,1,0:T(8,128)(2,1)} %prompt_hbm.1, f32[16]{0:T(128)} %refs_2_.7, s32[64]{0:T(128)} %refs_0_.7), custom_call_target="tpu_custom_call" | custom-call | tf_op jit(solution)/shard_map/pack/pallas_call | solution.py:510
  2.2 0.0 copy-start
  2.2 0.0 copy-start.2
  2.2 0.0 copy-start.3
  2.2 0.0 copy-start.4
  2.2 4.1 %collective-permute-start = (bf16[272,256]{1,0:T(8,128)(2,1)}, bf16[272,256]{1,0:T(8,128)(2,1)S(1)}, u32[]{:S(2)}, u32[]{:S(2)}) collective-permute-start(bf16[272,256]{1,0:T(8,128)(2,1)} %pack.1.refs_7_.refs_4_), channel_id=1, source_target_pairs={{0,8},{4,12},{8,0},{12,4},{1,9},{5,13},{9,1},{13,5},{2,10},{6,14},... | collective-permute-start | bytes 417800 | tf_op jit(solution)/shard_map/ppermute | solution.py:528
  6.3 1.3 %collective-permute-start.1 = (f32[16]{0:T(128)}, f32[16]{0:T(128)S(1)}, u32[]{:S(2)}, u32[]{:S(2)}) collective-permute-start(f32[16]{0:T(128)} %refs_2_.7), channel_id=1, source_target_pairs={{0,12},{4,8},{8,4},{12,0},{1,13},{5,9},{9,5},{13,1},{2,14},{6,10},... | collective-permute-start | bytes 200 | tf_op jit(solution)/shard_map/ppermute | solution.py:528
  7.7 0.2 collective-permute-start.2
  7.9 5.8 %raw_grads.1 = (bf16[1024,1280]{1,0:T(8,128)(2,1)}, bf16[2,1024,256]{2,1,0:T(8,128)(2,1)}, bf16[4,2,128,256]{3,2,1,0:T(8,128)(2,1)}, bf16[2,512,1280]{2,1,0:T(8,128)(2,1)}, bf16[2,512,256]{2,1,0:T(8,128)(2,1)}) custom-call(s32[64]{0:T(128)} %refs_0_.7, s32[16]{0:T(128)} %refs_1_.7, f32[16]{0:T(128)} %refs_2_.7, f32[16]{0:T(128)} %refs_2_.7, ...), custom_call_target="tpu_custom_call" | custom-call | tf_op jit(solution)/shard_map/raw_grads/pallas_call | solution.py:547
  13.8 0.0 collective-permute-done.1.refs_3_
  13.8 0.0 collective-permute-done.refs_9_.refs_10_.refs_6_
  13.8 1.9 %collective-permute-start.4 = (bf16[272,256]{1,0:T(8,128)(2,1)S(1)}, bf16[272,256]{1,0:T(8,128)(2,1)S(1)}, u32[]{:S(2)}, u32[]{:S(2)}) collective-permute-start(bf16[272,256]{1,0:T(8,128)(2,1)S(1)} %collective-permute-done.refs_9_.refs_10_.refs_6_), channel_id=1, source_target_pairs={{0,4},{4,0},{8,12},{12,8},{1,5},{5,1},{9,13},{13,9},{2,6},{6,2},{1... | collective-permute-start | bytes 417800 | tf_op jit(solution)/shard_map/ppermute | solution.py:528
  15.7 0.0 collective-permute-done.2.refs_8_.refs_11_.refs_5_
  15.7 0.0 copy-done
  15.7 0.0 copy-done.2
  15.7 0.0 copy-done.3
  15.7 0.0 copy-done.4
  15.7 4.3 %group_grads.2 = (bf16[1024,1280]{1,0:T(8,128)(2,1)}, bf16[2,1024,256]{2,1,0:T(8,128)(2,1)}, bf16[2,128,256]{2,1,0:T(8,128)(2,1)S(1)}) custom-call(s32[64]{0:T(128)S(1)} %copy-done.3, s32[16]{0:T(128)S(1)} %copy-done.4, f32[16]{0:T(128)S(1)} %copy-done.2, f32[16]{0:T(128)S(1)} %collective-permute-done.1.refs_3_, ...), custom_call_target="tpu_custom_call", output_to_operand_aliasing={{0}: (13, {}), {1}: (14, {})} | custom-call | tf_op jit(solution)/shard_map/group_grads/pallas_call | solution.py:547
  20.0 1.8 %collective-permute-start.3 = (bf16[2,128,256]{2,1,0:T(8,128)(2,1)S(1)}, bf16[2,128,256]{2,1,0:T(8,128)(2,1)S(1)}, u32[]{:S(2)}, u32[]{:S(2)}) collective-permute-start(bf16[2,128,256]{2,1,0:T(8,128)(2,1)S(1)} %get-tuple-element.28), channel_id=1, source_target_pairs={{0,8},{4,12},{8,0},{12,4},{1,9},{5,13},{9,1},{13,5},{2,10},{6,14},... | collective-permute-start | bytes 393224 | tf_op jit(solution)/shard_map/ppermute | solution.py:528
  21.8 0.0 collective-permute-done.4.refs_10_
  21.8 0.0 copy-start.1
  21.8 6.4 %group_grads.3 = (bf16[1024,1280]{1,0:T(8,128)(2,1)}, bf16[2,1024,256]{2,1,0:T(8,128)(2,1)}, bf16[2,128,256]{2,1,0:T(8,128)(2,1)S(1)}, bf16[2,128,256]{2,1,0:T(8,128)(2,1)S(1)}) custom-call(s32[64]{0:T(128)S(1)} %copy-done.3, s32[16]{0:T(128)S(1)} %copy-done.4, f32[16]{0:T(128)S(1)} %copy-done.2, ...), custom_call_target="tpu_custom_call", output_to_operand_aliasing={{0}: (14, {}), {1}: (15, {})} | custom-call | tf_op jit(solution)/shard_map/group_grads/pallas_call | solution.py:547
  28.2 0.9 %collective-permute-start.5 = (bf16[2,128,256]{2,1,0:T(8,128)(2,1)S(1)}, bf16[2,128,256]{2,1,0:T(8,128)(2,1)S(1)}, u32[]{:S(2)}, u32[]{:S(2)}) collective-permute-start(bf16[2,128,256]{2,1,0:T(8,128)(2,1)S(1)} %get-tuple-element.37), channel_id=1, source_target_pairs={{0,12},{4,8},{8,4},{12,0},{1,13},{5,9},{9,5},{13,1},{2,14},{6,10},... | collective-permute-start | bytes 393224 | tf_op jit(solution)/shard_map/ppermute | solution.py:528
  29.1 0.9 %collective-permute-start.6 = (bf16[2,128,256]{2,1,0:T(8,128)(2,1)S(1)}, bf16[2,128,256]{2,1,0:T(8,128)(2,1)S(1)}, u32[]{:S(2)}, u32[]{:S(2)}) collective-permute-start(bf16[2,128,256]{2,1,0:T(8,128)(2,1)S(1)} %get-tuple-element.38), channel_id=1, source_target_pairs={{0,4},{4,0},{8,12},{12,8},{1,5},{5,1},{9,13},{13,9},{2,6},{6,2},{1... | collective-permute-start | bytes 393224 | tf_op jit(solution)/shard_map/ppermute | solution.py:528
  30.0 0.0 collective-permute-done.3.refs_8_
  30.0 0.0 copy-done.1
  30.0 2.8 %finish_own.1 = (bf16[1024,1280]{1,0:T(8,128)(2,1)}, bf16[2,1024,256]{2,1,0:T(8,128)(2,1)}, f32[2,128,256]{2,1,0:T(8,128)S(1)}) custom-call(s32[64]{0:T(128)S(1)} %copy-done.3, s32[16]{0:T(128)S(1)} %copy-done.4, f32[16]{0:T(128)S(1)} %copy-done.2, f32[16]{0:T(128)S(1)} %collective-permute-done.1.refs_3_, ...), custom_call_target="tpu_custom_call", output_to_operand_aliasing={{0}: (9, {}), {1}: (10, {})} | custom-call | tf_op jit(solution)/shard_map/finish_own/pallas_call | solution.py:588
  32.8 3.5 %collective-permute-done.5 = bf16[2,128,256]{2,1,0:T(8,128)(2,1)S(1)} collective-permute-done((bf16[2,128,256]{2,1,0:T(8,128)(2,1)S(1)}, bf16[2,128,256]{2,1,0:T(8,128)(2,1)S(1)}, u32[]{:S(2)}, u32[]{:S(2)}) %collective-permute-start.5) | collective-permute-done | bytes 131104 | tf_op jit(solution)/shard_map/ppermute | solution.py:528
  36.3 0.0 collective-permute-done.6
  36.3 0.7 %add_convert_fusion = bf16[2,128,256]{2,1,0:T(8,128)(2,1)} fusion(f32[2,128,256]{2,1,0:T(8,128)S(1)} %get-tuple-element.36, bf16[2,128,256]{2,1,0:T(8,128)(2,1)S(1)} %collective-permute-done.6, bf16[2,128,256]{2,1,0:T(8,128)(2,1)S(1)} %collective-permute-done.5), kind=kLoop, calls=%fused_computation | loop fusion | flops 327680 | bytes 655360 | tf_op jit(solution)/shard_map/convert_element_type | solution.py:613
Async XLA Ops:
  2.2 13.5 %copy-start = (bf16[272,256]{1,0:T(8,128)(2,1)S(1)}, bf16[272,256]{1,0:T(8,128)(2,1)}, u32[]{:S(2)}) copy-start(bf16[272,256]{1,0:T(8,128)(2,1)} %pack.1.refs_7_.refs_4_) | copy-start | bytes 417796
  2.2 13.4 %copy-start.2 = (f32[16]{0:T(128)S(1)}, f32[16]{0:T(128)}, u32[]{:S(2)}) copy-start(f32[16]{0:T(128)} %refs_2_.7) | copy-start | bytes 196
  2.2 13.4 %copy-start.3 = (s32[64]{0:T(128)S(1)}, s32[64]{0:T(128)}, u32[]{:S(2)}) copy-start(s32[64]{0:T(128)} %refs_0_.7) | copy-start | bytes 772
  2.2 13.4 %copy-start.4 = (s32[16]{0:T(128)S(1)}, s32[16]{0:T(128)}, u32[]{:S(2)}) copy-start(s32[16]{0:T(128)} %refs_1_.7) | copy-start | bytes 196
  2.2 11.5 %collective-permute-start = (bf16[272,256]{1,0:T(8,128)(2,1)}, bf16[272,256]{1,0:T(8,128)(2,1)S(1)}, u32[]{:S(2)}, u32[]{:S(2)}) collective-permute-start(bf16[272,256]{1,0:T(8,128)(2,1)} %pack.1.refs_7_.refs_4_), channel_id=1, source_target_pairs={{0,8},{4,12},{8,0},{12,4},{1,9},{5,13},{9,1},{13,5},{2,10},{6,14},... | collective-permute-start | bytes 417800 | tf_op jit(solution)/shard_map/ppermute | solution.py:528
  6.3 7.4 %collective-permute-start.1 = (f32[16]{0:T(128)}, f32[16]{0:T(128)S(1)}, u32[]{:S(2)}, u32[]{:S(2)}) collective-permute-start(f32[16]{0:T(128)} %refs_2_.7), channel_id=1, source_target_pairs={{0,12},{4,8},{8,4},{12,0},{1,13},{5,9},{9,5},{13,1},{2,14},{6,10},... | collective-permute-start | bytes 200 | tf_op jit(solution)/shard_map/ppermute | solution.py:528
  7.7 8.0 %collective-permute-start.2 = (bf16[272,256]{1,0:T(8,128)(2,1)}, bf16[272,256]{1,0:T(8,128)(2,1)S(1)}, u32[]{:S(2)}, u32[]{:S(2)}) collective-permute-start(bf16[272,256]{1,0:T(8,128)(2,1)} %pack.1.refs_7_.refs_4_), channel_id=1, source_target_pairs={{0,4},{4,0},{8,12},{12,8},{1,5},{5,1},{9,13},{13,9},{2,6},{6,2},{1... | collective-permute-start | bytes 417800 | tf_op jit(solution)/shard_map/ppermute | solution.py:528
  13.8 8.0 %collective-permute-start.4 = (bf16[272,256]{1,0:T(8,128)(2,1)S(1)}, bf16[272,256]{1,0:T(8,128)(2,1)S(1)}, u32[]{:S(2)}, u32[]{:S(2)}) collective-permute-start(bf16[272,256]{1,0:T(8,128)(2,1)S(1)} %collective-permute-done.refs_9_.refs_10_.refs_6_), channel_id=1, source_target_pairs={{0,4},{4,0},{8,12},{12,8},{1,5},{5,1},{9,13},{13,9},{2,6},{6,2},{1... | collective-permute-start | bytes 417800 | tf_op jit(solution)/shard_map/ppermute | solution.py:528
  20.0 10.0 %collective-permute-start.3 = (bf16[2,128,256]{2,1,0:T(8,128)(2,1)S(1)}, bf16[2,128,256]{2,1,0:T(8,128)(2,1)S(1)}, u32[]{:S(2)}, u32[]{:S(2)}) collective-permute-start(bf16[2,128,256]{2,1,0:T(8,128)(2,1)S(1)} %get-tuple-element.28), channel_id=1, source_target_pairs={{0,8},{4,12},{8,0},{12,4},{1,9},{5,13},{9,1},{13,5},{2,10},{6,14},... | collective-permute-start | bytes 393224 | tf_op jit(solution)/shard_map/ppermute | solution.py:528
  21.8 8.2 %copy-start.1 = (bf16[4,2,128,256]{3,2,1,0:T(8,128)(2,1)S(1)}, bf16[4,2,128,256]{3,2,1,0:T(8,128)(2,1)}, u32[]{:S(2)}) copy-start(bf16[4,2,128,256]{3,2,1,0:T(8,128)(2,1)} %get-tuple-element.23.refs_7_) | copy-start | bytes 1572868
  28.2 8.1 %collective-permute-start.5 = (bf16[2,128,256]{2,1,0:T(8,128)(2,1)S(1)}, bf16[2,128,256]{2,1,0:T(8,128)(2,1)S(1)}, u32[]{:S(2)}, u32[]{:S(2)}) collective-permute-start(bf16[2,128,256]{2,1,0:T(8,128)(2,1)S(1)} %get-tuple-element.37), channel_id=1, source_target_pairs={{0,12},{4,8},{8,4},{12,0},{1,13},{5,9},{9,5},{13,1},{2,14},{6,10},... | collective-permute-start | bytes 393224 | tf_op jit(solution)/shard_map/ppermute | solution.py:528
  29.1 7.2 %collective-permute-start.6 = (bf16[2,128,256]{2,1,0:T(8,128)(2,1)S(1)}, bf16[2,128,256]{2,1,0:T(8,128)(2,1)S(1)}, u32[]{:S(2)}, u32[]{:S(2)}) collective-permute-start(bf16[2,128,256]{2,1,0:T(8,128)(2,1)S(1)} %get-tuple-element.38), channel_id=1, source_target_pairs={{0,4},{4,0},{8,12},{12,8},{1,5},{5,1},{9,13},{13,9},{2,6},{6,2},{1... | collective-permute-start | bytes 393224 | tf_op jit(solution)/shard_map/ppermute | solution.py:528

commit v20 on v16

--- a/solution.py
+++ b/solution.py
@@ -16,6 +16,7 @@
 BF16 = jnp.bfloat16
 PAIR = 2
 FAR = 3
+STRAIGHT = (2,)
 VMEM_BYTES = 63 * 1024 * 1024
 GROUP_BYTES = 53 * 1024 * 1024
 FINISH_BYTES = 24 * 1024 * 1024
@@ -46,6 +47,7 @@
 
 NN = ((1,), (0,))
 NT = ((1,), (1,))
+TN = ((0,), (0,))
 
 
 class Bag:
@@ -60,7 +62,7 @@
     factors: list
 
 
-def attend(z, units, q, og, kv, prefix, out, own_out, sink, apart):
+def attend(z, units, q, og, kv, prefix, out, own_out, sink, apart, straight=False):
     tokens, prefix_len, group_size = z.tokens, z.prefix_len, z.group_size
     scale = 1.0 / math.sqrt(HD)
     log_scale = scale * math.log2(math.e)
@@ -111,7 +113,10 @@
         t.values = [kv[1, t.at[n], t.cols] for n in sides]
         t.key_pair = jnp.concatenate(t.keys, axis=0)
         t.value_pair = jnp.concatenate(t.values, axis=0)
-        t.key_t = jnp.concatenate([t.key_p.T, t.key_pair.T], axis=1)
+        if straight:
+            t.key_all = jnp.concatenate([t.key_p, t.key_pair], axis=0)
+        else:
+            t.key_t = jnp.concatenate([t.key_p.T, t.key_pair.T], axis=1)
         t.prefix_sums = {n: [] for n in t.members}
         t.self_sums = {n: [] for n in t.members}
         mine = []
@@ -172,7 +177,10 @@
 
     def outgoing(c):
         t = c.t
-        q_grad = (dot(t.key_t, c.d_wide, NN) * scale).astype(BF16).T
+        if straight:
+            q_grad = (dot(c.d_wide, t.key_all, TN) * scale).astype(BF16)
+        else:
+            q_grad = (dot(t.key_t, c.d_wide, NN) * scale).astype(BF16).T
         kg = dot(c.d_all, c.q_rows, NN)
         vg = dot(c.w_all, c.g_rows, NN)
         targets = t.members if c.side is None else [c.side]
@@ -401,7 +409,7 @@
             at = [token_rows(z, n) for n in places]
             for k in range(z.kv_heads):
                 units.append(Unit(at, places, k, [lens[n] for n in own_places], [factors[n] for n in own_places]))
-        attend(z, units, q, og, kv, prefix.at[t], out, own, sink, raw)
+        attend(z, units, q, og, kv, prefix.at[t], out, own, sink, raw, turns == STRAIGHT)
         for n in mine:
             for copy in copies_out(first + n):
                 copy.start()
@@ -563,7 +571,9 @@
                 pltpu.SemaphoreType.DMA((n_turns,)),
                 pltpu.SemaphoreType.DMA((max(n_ahead, 1), 3)),
             ],
-            compiler_params=params if raw else pltpu.CompilerParams(vmem_limit_bytes=GROUP_BYTES),
+            compiler_params=params if raw else pltpu.CompilerParams(
+                vmem_limit_bytes=GROUP_BYTES, fuse_transposed_lhs_in_matmul=turns == STRAIGHT
+            ),
             cost_estimate=cost,
             name="raw_grads" if raw else "group_grads",
         )(*operands)

time: 37.2 us -> 37.6 us (1.011)
  transfers between devices with their start and end apart: 7 -> 7, of which waited for: 1 -> 1; matrix products, arithmetic and copies ran while one was open for 0% -> 0% of each run, Pallas kernels for 52% -> 53%
where the time goes in v20:
time: 37.6 us; the launch traced here: 37.3 us
  Pallas kernels  21.2 us (56%)
  starting transfers between devices  11.2 us (30%)
  waiting for transfers between devices  3.47 us (9%)
  between operations  0.74 us (2%)
  other arithmetic  0.7 us (2%)
    pallas_call x3, Pallas kernels, grads_of(): pl.pallas_call(functools.partial(group_kernel, z, turns, raw, body, ahead...  16.8 us
    ppermute x7, starting transfers between devices, swap(): return lax.ppermute(x, 'dp', [(i, i ^ s) for i in range(n_dp)])  11.2 us
    ppermute x7, waiting for transfers between devices, swap(): return lax.ppermute(x, 'dp', [(i, i ^ s) for i in range(n_dp)])  3.47 us
    pallas_call x1, Pallas kernels, near_shards(): pl.pallas_call(functools.partial(finish_kernel, z, len(tails), len(come))...  2.83 us
    pallas_call x1, Pallas kernels, near_shards(): pl.pallas_call(functools.partial(pack_kernel, z), out_shape=jax.ShapeDtyp...  1.56 us
  transfers between devices with their start and end apart: 7, of which 1 were waited for; matrix products, arithmetic and copies ran while one was open for 0% of the time, Pallas kernels for 53%

profile of v20, /device:TPU:0, one launch (start us, length us, event | category | flops | bytes accessed | tf_op | source)
XLA Modules:
  0.0 37.3 jit_solution(11328278486962208205)
XLA Ops:
  0.6 1.6 %pack.1.refs_7_.refs_4_ = bf16[272,256]{1,0:T(8,128)(2,1)} custom-call(bf16[2,128,256]{2,1,0:T(8,128)(2,1)} %prompt_hbm.1, f32[16]{0:T(128)} %refs_2_.7, s32[64]{0:T(128)} %refs_0_.7), custom_call_target="tpu_custom_call" | custom-call | tf_op jit(solution)/shard_map/pack/pallas_call | solution.py:510
  2.2 0.0 copy-start
  2.2 0.0 copy-start.2
  2.2 0.0 copy-start.3
  2.2 0.0 copy-start.4
  2.2 4.1 %collective-permute-start = (bf16[272,256]{1,0:T(8,128)(2,1)}, bf16[272,256]{1,0:T(8,128)(2,1)S(1)}, u32[]{:S(2)}, u32[]{:S(2)}) collective-permute-start(bf16[272,256]{1,0:T(8,128)(2,1)} %pack.1.refs_7_.refs_4_), channel_id=1, source_target_pairs={{0,8},{4,12},{8,0},{12,4},{1,9},{5,13},{9,1},{13,5},{2,10},{6,14},... | collective-permute-start | bytes 417800 | tf_op jit(solution)/shard_map/ppermute | solution.py:528
  6.3 1.3 %collective-permute-start.1 = (f32[16]{0:T(128)}, f32[16]{0:T(128)S(1)}, u32[]{:S(2)}, u32[]{:S(2)}) collective-permute-start(f32[16]{0:T(128)} %refs_2_.7), channel_id=1, source_target_pairs={{0,12},{4,8},{8,4},{12,0},{1,13},{5,9},{9,5},{13,1},{2,14},{6,10},... | collective-permute-start | bytes 200 | tf_op jit(solution)/shard_map/ppermute | solution.py:528
  7.7 0.2 collective-permute-start.2
  7.9 5.8 %raw_grads.1 = (bf16[1024,1280]{1,0:T(8,128)(2,1)}, bf16[2,1024,256]{2,1,0:T(8,128)(2,1)}, bf16[4,2,128,256]{3,2,1,0:T(8,128)(2,1)}, bf16[2,512,1280]{2,1,0:T(8,128)(2,1)}, bf16[2,512,256]{2,1,0:T(8,128)(2,1)}) custom-call(s32[64]{0:T(128)} %refs_0_.7, s32[16]{0:T(128)} %refs_1_.7, f32[16]{0:T(128)} %refs_2_.7, f32[16]{0:T(128)} %refs_2_.7, ...), custom_call_target="tpu_custom_call" | custom-call | tf_op jit(solution)/shard_map/raw_grads/pallas_call | solution.py:547
  13.8 0.0 collective-permute-done.1.refs_3_
  13.8 0.0 collective-permute-done.refs_9_.refs_10_.refs_6_
  13.8 1.9 %collective-permute-start.4 = (bf16[272,256]{1,0:T(8,128)(2,1)S(1)}, bf16[272,256]{1,0:T(8,128)(2,1)S(1)}, u32[]{:S(2)}, u32[]{:S(2)}) collective-permute-start(bf16[272,256]{1,0:T(8,128)(2,1)S(1)} %collective-permute-done.refs_9_.refs_10_.refs_6_), channel_id=1, source_target_pairs={{0,4},{4,0},{8,12},{12,8},{1,5},{5,1},{9,13},{13,9},{2,6},{6,2},{1... | collective-permute-start | bytes 417800 | tf_op jit(solution)/shard_map/ppermute | solution.py:528
  15.7 0.0 collective-permute-done.2.refs_8_.refs_11_.refs_5_
  15.7 0.0 copy-done
  15.7 0.0 copy-done.2
  15.7 0.0 copy-done.3
  15.7 0.0 copy-done.4
  15.7 4.7 %group_grads.2 = (bf16[1024,1280]{1,0:T(8,128)(2,1)}, bf16[2,1024,256]{2,1,0:T(8,128)(2,1)}, bf16[2,128,256]{2,1,0:T(8,128)(2,1)S(1)}) custom-call(s32[64]{0:T(128)S(1)} %copy-done.3, s32[16]{0:T(128)S(1)} %copy-done.4, f32[16]{0:T(128)S(1)} %copy-done.2, f32[16]{0:T(128)S(1)} %collective-permute-done.1.refs_3_, ...), custom_call_target="tpu_custom_call", output_to_operand_aliasing={{0}: (13, {}), {1}: (14, {})} | custom-call | tf_op jit(solution)/shard_map/group_grads/pallas_call | solution.py:547
  20.4 1.8 %collective-permute-start.3 = (bf16[2,128,256]{2,1,0:T(8,128)(2,1)S(1)}, bf16[2,128,256]{2,1,0:T(8,128)(2,1)S(1)}, u32[]{:S(2)}, u32[]{:S(2)}) collective-permute-start(bf16[2,128,256]{2,1,0:T(8,128)(2,1)S(1)} %get-tuple-element.28), channel_id=1, source_target_pairs={{0,8},{4,12},{8,0},{12,4},{1,9},{5,13},{9,1},{13,5},{2,10},{6,14},... | collective-permute-start | bytes 393224 | tf_op jit(solution)/shard_map/ppermute | solution.py:528
  22.2 0.0 collective-permute-done.4.refs_10_
  22.2 0.0 copy-start.1
  22.2 6.3 %group_grads.3 = (bf16[1024,1280]{1,0:T(8,128)(2,1)}, bf16[2,1024,256]{2,1,0:T(8,128)(2,1)}, bf16[2,128,256]{2,1,0:T(8,128)(2,1)S(1)}, bf16[2,128,256]{2,1,0:T(8,128)(2,1)S(1)}) custom-call(s32[64]{0:T(128)S(1)} %copy-done.3, s32[16]{0:T(128)S(1)} %copy-done.4, f32[16]{0:T(128)S(1)} %copy-done.2, ...), custom_call_target="tpu_custom_call", output_to_operand_aliasing={{0}: (14, {}), {1}: (15, {})} | custom-call | tf_op jit(solution)/shard_map/group_grads/pallas_call | solution.py:547
  28.6 0.9 %collective-permute-start.5 = (bf16[2,128,256]{2,1,0:T(8,128)(2,1)S(1)}, bf16[2,128,256]{2,1,0:T(8,128)(2,1)S(1)}, u32[]{:S(2)}, u32[]{:S(2)}) collective-permute-start(bf16[2,128,256]{2,1,0:T(8,128)(2,1)S(1)} %get-tuple-element.37), channel_id=1, source_target_pairs={{0,12},{4,8},{8,4},{12,0},{1,13},{5,9},{9,5},{13,1},{2,14},{6,10},... | collective-permute-start | bytes 393224 | tf_op jit(solution)/shard_map/ppermute | solution.py:528
  29.4 0.9 %collective-permute-start.6 = (bf16[2,128,256]{2,1,0:T(8,128)(2,1)S(1)}, bf16[2,128,256]{2,1,0:T(8,128)(2,1)S(1)}, u32[]{:S(2)}, u32[]{:S(2)}) collective-permute-start(bf16[2,128,256]{2,1,0:T(8,128)(2,1)S(1)} %get-tuple-element.38), channel_id=1, source_target_pairs={{0,4},{4,0},{8,12},{12,8},{1,5},{5,1},{9,13},{13,9},{2,6},{6,2},{1... | collective-permute-start | bytes 393224 | tf_op jit(solution)/shard_map/ppermute | solution.py:528
  30.3 0.0 collective-permute-done.3.refs_8_
  30.3 0.0 copy-done.1
  30.3 2.8 %finish_own.1 = (bf16[1024,1280]{1,0:T(8,128)(2,1)}, bf16[2,1024,256]{2,1,0:T(8,128)(2,1)}, f32[2,128,256]{2,1,0:T(8,128)S(1)}) custom-call(s32[64]{0:T(128)S(1)} %copy-done.3, s32[16]{0:T(128)S(1)} %copy-done.4, f32[16]{0:T(128)S(1)} %copy-done.2, f32[16]{0:T(128)S(1)} %collective-permute-done.1.refs_3_, ...), custom_call_target="tpu_custom_call", output_to_operand_aliasing={{0}: (9, {}), {1}: (10, {})} | custom-call | tf_op jit(solution)/shard_map/finish_own/pallas_call | solution.py:590
  33.2 3.5 %collective-permute-done.5 = bf16[2,128,256]{2,1,0:T(8,128)(2,1)S(1)} collective-permute-done((bf16[2,128,256]{2,1,0:T(8,128)(2,1)S(1)}, bf16[2,128,256]{2,1,0:T(8,128)(2,1)S(1)}, u32[]{:S(2)}, u32[]{:S(2)}) %collective-permute-start.5) | collective-permute-done | bytes 131104 | tf_op jit(solution)/shard_map/ppermute | solution.py:528
  36.6 0.0 collective-permute-done.6
  36.6 0.7 %add_convert_fusion = bf16[2,128,256]{2,1,0:T(8,128)(2,1)} fusion(f32[2,128,256]{2,1,0:T(8,128)S(1)} %get-tuple-element.36, bf16[2,128,256]{2,1,0:T(8,128)(2,1)S(1)} %collective-permute-done.6, bf16[2,128,256]{2,1,0:T(8,128)(2,1)S(1)} %collective-permute-done.5), kind=kLoop, calls=%fused_computation | loop fusion | flops 327680 | bytes 655360 | tf_op jit(solution)/shard_map/convert_element_type | solution.py:615
Async XLA Ops:
  2.2 13.5 %copy-start = (bf16[272,256]{1,0:T(8,128)(2,1)S(1)}, bf16[272,256]{1,0:T(8,128)(2,1)}, u32[]{:S(2)}) copy-start(bf16[272,256]{1,0:T(8,128)(2,1)} %pack.1.refs_7_.refs_4_) | copy-start | bytes 417796
  2.2 13.5 %copy-start.2 = (f32[16]{0:T(128)S(1)}, f32[16]{0:T(128)}, u32[]{:S(2)}) copy-start(f32[16]{0:T(128)} %refs_2_.7) | copy-start | bytes 196
  2.2 13.4 %copy-start.3 = (s32[64]{0:T(128)S(1)}, s32[64]{0:T(128)}, u32[]{:S(2)}) copy-start(s32[64]{0:T(128)} %refs_0_.7) | copy-start | bytes 772
  2.2 13.4 %copy-start.4 = (s32[16]{0:T(128)S(1)}, s32[16]{0:T(128)}, u32[]{:S(2)}) copy-start(s32[16]{0:T(128)} %refs_1_.7) | copy-start | bytes 196
  2.2 11.5 %collective-permute-start = (bf16[272,256]{1,0:T(8,128)(2,1)}, bf16[272,256]{1,0:T(8,128)(2,1)S(1)}, u32[]{:S(2)}, u32[]{:S(2)}) collective-permute-start(bf16[272,256]{1,0:T(8,128)(2,1)} %pack.1.refs_7_.refs_4_), channel_id=1, source_target_pairs={{0,8},{4,12},{8,0},{12,4},{1,9},{5,13},{9,1},{13,5},{2,10},{6,14},... | collective-permute-start | bytes 417800 | tf_op jit(solution)/shard_map/ppermute | solution.py:528
  6.3 7.4 %collective-permute-start.1 = (f32[16]{0:T(128)}, f32[16]{0:T(128)S(1)}, u32[]{:S(2)}, u32[]{:S(2)}) collective-permute-start(f32[16]{0:T(128)} %refs_2_.7), channel_id=1, source_target_pairs={{0,12},{4,8},{8,4},{12,0},{1,13},{5,9},{9,5},{13,1},{2,14},{6,10},... | collective-permute-start | bytes 200 | tf_op jit(solution)/shard_map/ppermute | solution.py:528
  7.7 8.0 %collective-permute-start.2 = (bf16[272,256]{1,0:T(8,128)(2,1)}, bf16[272,256]{1,0:T(8,128)(2,1)S(1)}, u32[]{:S(2)}, u32[]{:S(2)}) collective-permute-start(bf16[272,256]{1,0:T(8,128)(2,1)} %pack.1.refs_7_.refs_4_), channel_id=1, source_target_pairs={{0,4},{4,0},{8,12},{12,8},{1,5},{5,1},{9,13},{13,9},{2,6},{6,2},{1... | collective-permute-start | bytes 417800 | tf_op jit(solution)/shard_map/ppermute | solution.py:528
  13.8 8.4 %collective-permute-start.4 = (bf16[272,256]{1,0:T(8,128)(2,1)S(1)}, bf16[272,256]{1,0:T(8,128)(2,1)S(1)}, u32[]{:S(2)}, u32[]{:S(2)}) collective-permute-start(bf16[272,256]{1,0:T(8,128)(2,1)S(1)} %collective-permute-done.refs_9_.refs_10_.refs_6_), channel_id=1, source_target_pairs={{0,4},{4,0},{8,12},{12,8},{1,5},{5,1},{9,13},{13,9},{2,6},{6,2},{1... | collective-permute-start | bytes 417800 | tf_op jit(solution)/shard_map/ppermute | solution.py:528
  20.4 10.0 %collective-permute-start.3 = (bf16[2,128,256]{2,1,0:T(8,128)(2,1)S(1)}, bf16[2,128,256]{2,1,0:T(8,128)(2,1)S(1)}, u32[]{:S(2)}, u32[]{:S(2)}) collective-permute-start(bf16[2,128,256]{2,1,0:T(8,128)(2,1)S(1)} %get-tuple-element.28), channel_id=1, source_target_pairs={{0,8},{4,12},{8,0},{12,4},{1,9},{5,13},{9,1},{13,5},{2,10},{6,14},... | collective-permute-start | bytes 393224 | tf_op jit(solution)/shard_map/ppermute | solution.py:528
  22.2 8.1 %copy-start.1 = (bf16[4,2,128,256]{3,2,1,0:T(8,128)(2,1)S(1)}, bf16[4,2,128,256]{3,2,1,0:T(8,128)(2,1)}, u32[]{:S(2)}) copy-start(bf16[4,2,128,256]{3,2,1,0:T(8,128)(2,1)} %get-tuple-element.23.refs_7_) | copy-start | bytes 1572868
  28.6 8.1 %collective-permute-start.5 = (bf16[2,128,256]{2,1,0:T(8,128)(2,1)S(1)}, bf16[2,128,256]{2,1,0:T(8,128)(2,1)S(1)}, u32[]{:S(2)}, u32[]{:S(2)}) collective-permute-start(bf16[2,128,256]{2,1,0:T(8,128)(2,1)S(1)} %get-tuple-element.37), channel_id=1, source_target_pairs={{0,12},{4,8},{8,4},{12,0},{1,13},{5,9},{9,5},{13,1},{2,14},{6,10},... | collective-permute-start | bytes 393224 | tf_op jit(solution)/shard_map/ppermute | solution.py:528
  29.4 7.2 %collective-permute-start.6 = (bf16[2,128,256]{2,1,0:T(8,128)(2,1)S(1)}, bf16[2,128,256]{2,1,0:T(8,128)(2,1)S(1)}, u32[]{:S(2)}, u32[]{:S(2)}) collective-permute-start(bf16[2,128,256]{2,1,0:T(8,128)(2,1)S(1)} %get-tuple-element.38), channel_id=1, source_target_pairs={{0,4},{4,0},{8,12},{12,8},{1,5},{5,1},{9,13},{13,9},{2,6},{6,2},{1... | collective-permute-start | bytes 393224 | tf_op jit(solution)/shard_map/ppermute | solution.py:528

commit v21 on v16

--- a/solution.py
+++ b/solution.py
@@ -60,7 +60,7 @@
     factors: list
 
 
-def attend(z, units, q, og, kv, prefix, out, own_out, sink, apart):
+def attend(z, units, q, og, kv, prefix, out, own_out, sink, apart, by_product=False):
     tokens, prefix_len, group_size = z.tokens, z.prefix_len, z.group_size
     scale = 1.0 / math.sqrt(HD)
     log_scale = scale * math.log2(math.e)
@@ -71,6 +71,10 @@
     key = lax.broadcasted_iota(jnp.int32, (tokens, most), 0)
     causal = key <= (lax.broadcasted_iota(jnp.int32, (tokens, most), 1) & (tokens - 1))
     left = lax.broadcasted_iota(jnp.int32, (1, 2 * tokens), 1) < tokens
+
+    identity = (
+        lax.broadcasted_iota(jnp.int32, (most, most), 0) == lax.broadcasted_iota(jnp.int32, (most, most), 1)
+    ).astype(F32).astype(BF16)
 
     def columns(index):
         if isinstance(index, int):
@@ -172,7 +176,12 @@
 
     def outgoing(c):
         t = c.t
-        q_grad = (dot(t.key_t, c.d_wide, NN) * scale).astype(BF16).T
+        q_grad = (dot(t.key_t, c.d_wide, NN) * scale).astype(BF16)
+        if by_product:
+            lanes = q_grad.shape[1]
+            q_grad = dot(identity[:lanes, :lanes], q_grad, NT).astype(BF16)
+        else:
+            q_grad = q_grad.T
         kg = dot(c.d_all, c.q_rows, NN)
         vg = dot(c.w_all, c.g_rows, NN)
         targets = t.members if c.side is None else [c.side]
@@ -401,7 +410,7 @@
             at = [token_rows(z, n) for n in places]
             for k in range(z.kv_heads):
                 units.append(Unit(at, places, k, [lens[n] for n in own_places], [factors[n] for n in own_places]))
-        attend(z, units, q, og, kv, prefix.at[t], out, own, sink, raw)
+        attend(z, units, q, og, kv, prefix.at[t], out, own, sink, raw, turns == (2,))
         for n in mine:
             for copy in copies_out(first + n):
                 copy.start()

time: 37.2 us -> 38.1 us (1.024)
  Pallas kernels: 20.9 us -> 21.7 us
    pallas_call x3, Pallas kernels: 16.5 us -> 17.3 us  [grads_of(): pl.pallas_call(functools.partial(group_kernel, z, turns, raw, body, ahead...]
  transfers between devices with their start and end apart: 7 -> 7, of which waited for: 1 -> 1; matrix products, arithmetic and copies ran while one was open for 0% -> 0% of each run, Pallas kernels for 52% -> 53%
where the time goes in v21:
time: 38.1 us; the launch traced here: 37.8 us
  Pallas kernels  21.7 us (57%)
  starting transfers between devices  11.2 us (29%)
  waiting for transfers between devices  3.48 us (9%)
  between operations  0.74 us (2%)
  other arithmetic  0.7 us (2%)
    pallas_call x3, Pallas kernels, grads_of(): pl.pallas_call(functools.partial(group_kernel, z, turns, raw, body, ahead...  17.3 us
    ppermute x7, starting transfers between devices, swap(): return lax.ppermute(x, 'dp', [(i, i ^ s) for i in range(n_dp)])  11.2 us
    ppermute x7, waiting for transfers between devices, swap(): return lax.ppermute(x, 'dp', [(i, i ^ s) for i in range(n_dp)])  3.48 us
    pallas_call x1, Pallas kernels, near_shards(): pl.pallas_call(functools.partial(finish_kernel, z, len(tails), len(come))...  2.83 us
    pallas_call x1, Pallas kernels, near_shards(): pl.pallas_call(functools.partial(pack_kernel, z), out_shape=jax.ShapeDtyp...  1.56 us
  transfers between devices with their start and end apart: 7, of which 1 were waited for; matrix products, arithmetic and copies ran while one was open for 0% of the time, Pallas kernels for 53%

profile of v21, /device:TPU:0, one launch (start us, length us, event | category | flops | bytes accessed | tf_op | source)
XLA Modules:
  0.0 37.8 jit_solution(11818497840684681937)
XLA Ops:
  0.6 1.6 %pack.1.refs_7_.refs_4_ = bf16[272,256]{1,0:T(8,128)(2,1)} custom-call(bf16[2,128,256]{2,1,0:T(8,128)(2,1)} %prompt_hbm.1, f32[16]{0:T(128)} %refs_2_.7, s32[64]{0:T(128)} %refs_0_.7), custom_call_target="tpu_custom_call" | custom-call | tf_op jit(solution)/shard_map/pack/pallas_call | solution.py:511
  2.2 0.0 copy-start
  2.2 0.0 copy-start.2
  2.2 0.0 copy-start.3
  2.2 0.0 copy-start.4
  2.2 4.1 %collective-permute-start = (bf16[272,256]{1,0:T(8,128)(2,1)}, bf16[272,256]{1,0:T(8,128)(2,1)S(1)}, u32[]{:S(2)}, u32[]{:S(2)}) collective-permute-start(bf16[272,256]{1,0:T(8,128)(2,1)} %pack.1.refs_7_.refs_4_), channel_id=1, source_target_pairs={{0,8},{4,12},{8,0},{12,4},{1,9},{5,13},{9,1},{13,5},{2,10},{6,14},... | collective-permute-start | bytes 417800 | tf_op jit(solution)/shard_map/ppermute | solution.py:529
  6.3 1.3 %collective-permute-start.1 = (f32[16]{0:T(128)}, f32[16]{0:T(128)S(1)}, u32[]{:S(2)}, u32[]{:S(2)}) collective-permute-start(f32[16]{0:T(128)} %refs_2_.7), channel_id=1, source_target_pairs={{0,12},{4,8},{8,4},{12,0},{1,13},{5,9},{9,5},{13,1},{2,14},{6,10},... | collective-permute-start | bytes 200 | tf_op jit(solution)/shard_map/ppermute | solution.py:529
  7.7 0.2 collective-permute-start.2
  7.9 5.8 %raw_grads.1 = (bf16[1024,1280]{1,0:T(8,128)(2,1)}, bf16[2,1024,256]{2,1,0:T(8,128)(2,1)}, bf16[4,2,128,256]{3,2,1,0:T(8,128)(2,1)}, bf16[2,512,1280]{2,1,0:T(8,128)(2,1)}, bf16[2,512,256]{2,1,0:T(8,128)(2,1)}) custom-call(s32[64]{0:T(128)} %refs_0_.7, s32[16]{0:T(128)} %refs_1_.7, f32[16]{0:T(128)} %refs_2_.7, f32[16]{0:T(128)} %refs_2_.7, ...), custom_call_target="tpu_custom_call" | custom-call | tf_op jit(solution)/shard_map/raw_grads/pallas_call | solution.py:548
  13.8 0.0 collective-permute-done.1.refs_3_
  13.8 0.0 collective-permute-done.refs_9_.refs_10_.refs_6_
  13.8 1.9 %collective-permute-start.4 = (bf16[272,256]{1,0:T(8,128)(2,1)S(1)}, bf16[272,256]{1,0:T(8,128)(2,1)S(1)}, u32[]{:S(2)}, u32[]{:S(2)}) collective-permute-start(bf16[272,256]{1,0:T(8,128)(2,1)S(1)} %collective-permute-done.refs_9_.refs_10_.refs_6_), channel_id=1, source_target_pairs={{0,4},{4,0},{8,12},{12,8},{1,5},{5,1},{9,13},{13,9},{2,6},{6,2},{1... | collective-permute-start | bytes 417800 | tf_op jit(solution)/shard_map/ppermute | solution.py:529
  15.7 0.0 collective-permute-done.2.refs_8_.refs_11_.refs_5_
  15.7 0.0 copy-done
  15.7 0.0 copy-done.2
  15.7 0.0 copy-done.3
  15.7 0.0 copy-done.4
  15.7 5.2 %group_grads.2 = (bf16[1024,1280]{1,0:T(8,128)(2,1)}, bf16[2,1024,256]{2,1,0:T(8,128)(2,1)}, bf16[2,128,256]{2,1,0:T(8,128)(2,1)S(1)}) custom-call(s32[64]{0:T(128)S(1)} %copy-done.3, s32[16]{0:T(128)S(1)} %copy-done.4, f32[16]{0:T(128)S(1)} %copy-done.2, f32[16]{0:T(128)S(1)} %collective-permute-done.1.refs_3_, ...), custom_call_target="tpu_custom_call", output_to_operand_aliasing={{0}: (13, {}), {1}: (14, {})} | custom-call | tf_op jit(solution)/shard_map/group_grads/pallas_call | solution.py:548
  20.9 1.8 %collective-permute-start.3 = (bf16[2,128,256]{2,1,0:T(8,128)(2,1)S(1)}, bf16[2,128,256]{2,1,0:T(8,128)(2,1)S(1)}, u32[]{:S(2)}, u32[]{:S(2)}) collective-permute-start(bf16[2,128,256]{2,1,0:T(8,128)(2,1)S(1)} %get-tuple-element.28), channel_id=1, source_target_pairs={{0,8},{4,12},{8,0},{12,4},{1,9},{5,13},{9,1},{13,5},{2,10},{6,14},... | collective-permute-start | bytes 393224 | tf_op jit(solution)/shard_map/ppermute | solution.py:529
  22.7 0.0 collective-permute-done.4.refs_10_
  22.7 0.0 copy-start.1
  22.7 6.3 %group_grads.3 = (bf16[1024,1280]{1,0:T(8,128)(2,1)}, bf16[2,1024,256]{2,1,0:T(8,128)(2,1)}, bf16[2,128,256]{2,1,0:T(8,128)(2,1)S(1)}, bf16[2,128,256]{2,1,0:T(8,128)(2,1)S(1)}) custom-call(s32[64]{0:T(128)S(1)} %copy-done.3, s32[16]{0:T(128)S(1)} %copy-done.4, f32[16]{0:T(128)S(1)} %copy-done.2, ...), custom_call_target="tpu_custom_call", output_to_operand_aliasing={{0}: (14, {}), {1}: (15, {})} | custom-call | tf_op jit(solution)/shard_map/group_grads/pallas_call | solution.py:548
  29.0 0.9 %collective-permute-start.5 = (bf16[2,128,256]{2,1,0:T(8,128)(2,1)S(1)}, bf16[2,128,256]{2,1,0:T(8,128)(2,1)S(1)}, u32[]{:S(2)}, u32[]{:S(2)}) collective-permute-start(bf16[2,128,256]{2,1,0:T(8,128)(2,1)S(1)} %get-tuple-element.37), channel_id=1, source_target_pairs={{0,12},{4,8},{8,4},{12,0},{1,13},{5,9},{9,5},{13,1},{2,14},{6,10},... | collective-permute-start | bytes 393224 | tf_op jit(solution)/shard_map/ppermute | solution.py:529
  29.9 0.9 %collective-permute-start.6 = (bf16[2,128,256]{2,1,0:T(8,128)(2,1)S(1)}, bf16[2,128,256]{2,1,0:T(8,128)(2,1)S(1)}, u32[]{:S(2)}, u32[]{:S(2)}) collective-permute-start(bf16[2,128,256]{2,1,0:T(8,128)(2,1)S(1)} %get-tuple-element.38), channel_id=1, source_target_pairs={{0,4},{4,0},{8,12},{12,8},{1,5},{5,1},{9,13},{13,9},{2,6},{6,2},{1... | collective-permute-start | bytes 393224 | tf_op jit(solution)/shard_map/ppermute | solution.py:529
  30.8 0.0 collective-permute-done.3.refs_8_
  30.8 0.0 copy-done.1
  30.8 2.8 %finish_own.1 = (bf16[1024,1280]{1,0:T(8,128)(2,1)}, bf16[2,1024,256]{2,1,0:T(8,128)(2,1)}, f32[2,128,256]{2,1,0:T(8,128)S(1)}) custom-call(s32[64]{0:T(128)S(1)} %copy-done.3, s32[16]{0:T(128)S(1)} %copy-done.4, f32[16]{0:T(128)S(1)} %copy-done.2, f32[16]{0:T(128)S(1)} %collective-permute-done.1.refs_3_, ...), custom_call_target="tpu_custom_call", output_to_operand_aliasing={{0}: (9, {}), {1}: (10, {})} | custom-call | tf_op jit(solution)/shard_map/finish_own/pallas_call | solution.py:589
  33.7 3.5 %collective-permute-done.5 = bf16[2,128,256]{2,1,0:T(8,128)(2,1)S(1)} collective-permute-done((bf16[2,128,256]{2,1,0:T(8,128)(2,1)S(1)}, bf16[2,128,256]{2,1,0:T(8,128)(2,1)S(1)}, u32[]{:S(2)}, u32[]{:S(2)}) %collective-permute-start.5) | collective-permute-done | bytes 131104 | tf_op jit(solution)/shard_map/ppermute | solution.py:529
  37.1 0.0 collective-permute-done.6
  37.1 0.7 %add_convert_fusion = bf16[2,128,256]{2,1,0:T(8,128)(2,1)} fusion(f32[2,128,256]{2,1,0:T(8,128)S(1)} %get-tuple-element.36, bf16[2,128,256]{2,1,0:T(8,128)(2,1)S(1)} %collective-permute-done.6, bf16[2,128,256]{2,1,0:T(8,128)(2,1)S(1)} %collective-permute-done.5), kind=kLoop, calls=%fused_computation | loop fusion | flops 327680 | bytes 655360 | tf_op jit(solution)/shard_map/convert_element_type | solution.py:614
Async XLA Ops:
  2.2 13.5 %copy-start = (bf16[272,256]{1,0:T(8,128)(2,1)S(1)}, bf16[272,256]{1,0:T(8,128)(2,1)}, u32[]{:S(2)}) copy-start(bf16[272,256]{1,0:T(8,128)(2,1)} %pack.1.refs_7_.refs_4_) | copy-start | bytes 417796
  2.2 13.5 %copy-start.2 = (f32[16]{0:T(128)S(1)}, f32[16]{0:T(128)}, u32[]{:S(2)}) copy-start(f32[16]{0:T(128)} %refs_2_.7) | copy-start | bytes 196
  2.2 13.4 %copy-start.3 = (s32[64]{0:T(128)S(1)}, s32[64]{0:T(128)}, u32[]{:S(2)}) copy-start(s32[64]{0:T(128)} %refs_0_.7) | copy-start | bytes 772
  2.2 13.4 %copy-start.4 = (s32[16]{0:T(128)S(1)}, s32[16]{0:T(128)}, u32[]{:S(2)}) copy-start(s32[16]{0:T(128)} %refs_1_.7) | copy-start | bytes 196
  2.2 11.5 %collective-permute-start = (bf16[272,256]{1,0:T(8,128)(2,1)}, bf16[272,256]{1,0:T(8,128)(2,1)S(1)}, u32[]{:S(2)}, u32[]{:S(2)}) collective-permute-start(bf16[272,256]{1,0:T(8,128)(2,1)} %pack.1.refs_7_.refs_4_), channel_id=1, source_target_pairs={{0,8},{4,12},{8,0},{12,4},{1,9},{5,13},{9,1},{13,5},{2,10},{6,14},... | collective-permute-start | bytes 417800 | tf_op jit(solution)/shard_map/ppermute | solution.py:529
  6.3 7.4 %collective-permute-start.1 = (f32[16]{0:T(128)}, f32[16]{0:T(128)S(1)}, u32[]{:S(2)}, u32[]{:S(2)}) collective-permute-start(f32[16]{0:T(128)} %refs_2_.7), channel_id=1, source_target_pairs={{0,12},{4,8},{8,4},{12,0},{1,13},{5,9},{9,5},{13,1},{2,14},{6,10},... | collective-permute-start | bytes 200 | tf_op jit(solution)/shard_map/ppermute | solution.py:529
  7.7 8.0 %collective-permute-start.2 = (bf16[272,256]{1,0:T(8,128)(2,1)}, bf16[272,256]{1,0:T(8,128)(2,1)S(1)}, u32[]{:S(2)}, u32[]{:S(2)}) collective-permute-start(bf16[272,256]{1,0:T(8,128)(2,1)} %pack.1.refs_7_.refs_4_), channel_id=1, source_target_pairs={{0,4},{4,0},{8,12},{12,8},{1,5},{5,1},{9,13},{13,9},{2,6},{6,2},{1... | collective-permute-start | bytes 417800 | tf_op jit(solution)/shard_map/ppermute | solution.py:529
  13.8 8.9 %collective-permute-start.4 = (bf16[272,256]{1,0:T(8,128)(2,1)S(1)}, bf16[272,256]{1,0:T(8,128)(2,1)S(1)}, u32[]{:S(2)}, u32[]{:S(2)}) collective-permute-start(bf16[272,256]{1,0:T(8,128)(2,1)S(1)} %collective-permute-done.refs_9_.refs_10_.refs_6_), channel_id=1, source_target_pairs={{0,4},{4,0},{8,12},{12,8},{1,5},{5,1},{9,13},{13,9},{2,6},{6,2},{1... | collective-permute-start | bytes 417800 | tf_op jit(solution)/shard_map/ppermute | solution.py:529
  20.9 10.0 %collective-permute-start.3 = (bf16[2,128,256]{2,1,0:T(8,128)(2,1)S(1)}, bf16[2,128,256]{2,1,0:T(8,128)(2,1)S(1)}, u32[]{:S(2)}, u32[]{:S(2)}) collective-permute-start(bf16[2,128,256]{2,1,0:T(8,128)(2,1)S(1)} %get-tuple-element.28), channel_id=1, source_target_pairs={{0,8},{4,12},{8,0},{12,4},{1,9},{5,13},{9,1},{13,5},{2,10},{6,14},... | collective-permute-start | bytes 393224 | tf_op jit(solution)/shard_map/ppermute | solution.py:529
  22.7 8.1 %copy-start.1 = (bf16[4,2,128,256]{3,2,1,0:T(8,128)(2,1)S(1)}, bf16[4,2,128,256]{3,2,1,0:T(8,128)(2,1)}, u32[]{:S(2)}) copy-start(bf16[4,2,128,256]{3,2,1,0:T(8,128)(2,1)} %get-tuple-element.23.refs_7_) | copy-start | bytes 1572868
  29.0 8.1 %collective-permute-start.5 = (bf16[2,128,256]{2,1,0:T(8,128)(2,1)S(1)}, bf16[2,128,256]{2,1,0:T(8,128)(2,1)S(1)}, u32[]{:S(2)}, u32[]{:S(2)}) collective-permute-start(bf16[2,128,256]{2,1,0:T(8,128)(2,1)S(1)} %get-tuple-element.37), channel_id=1, source_target_pairs={{0,12},{4,8},{8,4},{12,0},{1,13},{5,9},{9,5},{13,1},{2,14},{6,10},... | collective-permute-start | bytes 393224 | tf_op jit(solution)/shard_map/ppermute | solution.py:529
  29.9 7.2 %collective-permute-start.6 = (bf16[2,128,256]{2,1,0:T(8,128)(2,1)S(1)}, bf16[2,128,256]{2,1,0:T(8,128)(2,1)S(1)}, u32[]{:S(2)}, u32[]{:S(2)}) collective-permute-start(bf16[2,128,256]{2,1,0:T(8,128)(2,1)S(1)} %get-tuple-element.38), channel_id=1, source_target_pairs={{0,4},{4,0},{8,12},{12,8},{1,5},{5,1},{9,13},{13,9},{2,6},{6,2},{1... | collective-permute-start | bytes 393224 | tf_op jit(solution)/shard_map/ppermute | solution.py:529

commit v22 on v12

--- a/solution.py
+++ b/solution.py
@@ -11,13 +11,12 @@
 
 HD = 128
 NEG = -1e30
-TAIL = 16
 F32 = jnp.float32
 BF16 = jnp.bfloat16
 PAIR = 2
 FAR = 3
 VMEM_BYTES = 63 * 1024 * 1024
-GROUP_BYTES = 53 * 1024 * 1024
+GROUP_BYTES = 54528 * 1024
 ANYWHERE = pl.BlockSpec(memory_space=pl.ANY)
 
 
@@ -216,60 +215,16 @@
             found = found + (resp_prompt[me * z.count + i] == prompt).astype(jnp.int32)
 
 
-def prompt_total(z, me, prompt, resp_prompt, tails, far_rewards):
-    sums = jnp.zeros((1, z.width), F32)
-    for s in range(tails.shape[0]):
-        tail = tails[s].astype(F32)
-        sums += tail[0:1] + tail[1:2] + tail[2:3]
-    lane = lax.broadcasted_iota(jnp.int32, sums.shape, 1)
-    total = jnp.sum(jnp.where(lane == prompt, sums, 0.0))
-    for i in range(z.count):
-        total += jnp.where(resp_prompt[(me ^ FAR) * z.count + i] == prompt, far_rewards[i], 0.0)
+def prompt_total(z, me, prompt, resp_prompt, rewards):
+    total = jnp.float32(0.0)
+    for s in range(z.n_dp):
+        for i in range(z.count):
+            total += jnp.where(resp_prompt[(me ^ s) * z.count + i] == prompt, rewards[s][i], 0.0)
     return total
 
 
 def reward_factor(z, reward, total, length):
     return (reward - total / z.count) * (z.tokens / length.astype(F32))
-
-
-def pack_kernel(z, prompt_hbm, rewards_hbm, resp_prompt_hbm, payload, rewards, resp_prompt, staged, sems):
-    me = lax.axis_index("dp")
-    small = [
-        pltpu.make_async_copy(rewards_hbm, rewards, sems.at[0]),
-        pltpu.make_async_copy(resp_prompt_hbm, resp_prompt, sems.at[1]),
-    ]
-    large = [
-        pltpu.make_async_copy(
-            prompt_hbm.at[n], staged.at[pl.ds(n * z.prefix_len, z.prefix_len)], sems.at[2 + n]
-        )
-        for n in range(2)
-    ]
-    for copy in small + large:
-        copy.start()
-    for copy in small:
-        copy.wait()
-    lane = lax.broadcasted_iota(jnp.int32, (1, z.width), 1)
-    sums = jnp.zeros((1, z.width), F32)
-    for i in range(z.count):
-        sums += jnp.where(lane == resp_prompt[me * z.count + i], rewards[i], 0.0)
-    high = sums.astype(BF16).astype(F32)
-    middle = (sums - high).astype(BF16).astype(F32)
-    low = sums - high - middle
-    row = lax.broadcasted_iota(jnp.int32, (TAIL, z.width), 0)
-    pieces = jnp.where(row == 0, high, jnp.where(row == 1, middle, jnp.where(row == 2, low, 0.0)))
-    staged[2 * z.prefix_len :, :] = pieces.astype(BF16)
-    for copy in large:
-        copy.wait()
-    last = pltpu.make_async_copy(staged, payload, sems.at[0])
-    last.start()
-    last.wait()
-
-
-def tail_copies(z, payloads, tails, sems):
-    return [
-        pltpu.make_async_copy(payload.at[pl.ds(2 * z.prefix_len, TAIL)], tails.at[n], sems.at[n])
-        for n, payload in enumerate(payloads)
-    ]
 
 
 def row_copies(here, there, at_here, at_there, sems):
@@ -325,23 +280,24 @@
 
 
 def group_kernel(z, turns, ahead, n_come, aliased, *refs):
-    small_hbm, given, tail_hbm = refs[:4], refs[4:7], refs[7 : 7 + FAR]
-    refs = refs[7 + FAR :]
+    n_small = 2 + z.n_dp
+    small_hbm, given, refs = refs[:n_small], refs[n_small : n_small + 3], refs[n_small + 3 :]
     prompts, refs = refs[: len(turns)], refs[len(turns) :]
     come_hbm, refs = refs[:n_come], refs[n_come:]
     if ahead is not None:
         (both, kv_ordered), refs = refs[:2], refs[2:]
     (q_out, self_out), refs = refs[aliased : aliased + 2], refs[aliased + 2 :]
     grads_out, refs = refs[: len(turns)], refs[len(turns) :]
-    (resp_prompt, resp_len, rewards, far_rewards, order, lens, factors, q, og, kv, prefix, tails, come, acc, out, own,
-     grads, sem_small, sem_tails, sem_prefix, sem_in, sem_out, sem_grads, sem_first) = refs
+    resp_prompt, resp_len, *rewards = refs[:n_small]
+    (order, lens, factors, q, og, kv, prefix, come, acc, out, own, grads,
+     sem_small, sem_prefix, sem_come, sem_in, sem_out, sem_grads, sem_first) = refs[n_small:]
     me = lax.axis_index("dp")
     n_slots = len(turns) * z.slots
     span = z.slots * z.tokens
 
     small = [
         pltpu.make_async_copy(src, dst, sem_small.at[n])
-        for n, (src, dst) in enumerate(zip(small_hbm, (resp_prompt, resp_len, rewards, far_rewards)))
+        for n, (src, dst) in enumerate(zip(small_hbm, (resp_prompt, resp_len, *rewards)))
     ]
     first_rows = ()
     if ahead is not None:
@@ -349,14 +305,9 @@
             (both.at[0], both.at[1], kv_ordered), (q, og, kv), pl.ds(ahead * span, span), pl.ds(0, span), sem_first
         )
     prefix_copies = [
-        pltpu.make_async_copy(
-            prompts[t].at[pl.ds(n * z.prefix_len, z.prefix_len)], prefix.at[t, n], sem_prefix.at[t, n]
-        )
-        for t in range(len(turns))
-        for n in range(2)
+        pltpu.make_async_copy(prompts[t], prefix.at[t], sem_prefix.at[t]) for t in range(len(turns))
     ]
-    late = tail_copies(z, tail_hbm, tails, sem_tails)
-    late += [pltpu.make_async_copy(src, come, sem_grads.at[0]) for src in come_hbm]
+    late = [pltpu.make_async_copy(src, come, sem_come) for src in come_hbm]
     for copy in [*small, *first_rows, *prefix_copies, *late]:
         copy.start()
     small[0].wait()
@@ -376,11 +327,11 @@
     for copy in small[1:] + late:
         copy.wait()
     for t, turn in enumerate(turns):
-        total = prompt_total(z, me, me ^ turn, resp_prompt, tails, far_rewards)
+        total = prompt_total(z, me, me ^ turn, resp_prompt, rewards)
         for slot in range(t * z.slots, (t + 1) * z.slots):
             i = order[slot]
             lens[slot] = resp_len[i]
-            factors[slot] = reward_factor(z, rewards[i], total, resp_len[i])
+            factors[slot] = reward_factor(z, rewards[0][i], total, resp_len[i])
     if n_come:
         acc[0] = come[...].astype(F32)
     else:
@@ -443,33 +394,16 @@
     one = (2, z.prefix_len, z.width)
     params = pltpu.CompilerParams(vmem_limit_bytes=VMEM_BYTES)
     cost = pl.CostEstimate(flops=0, bytes_accessed=0, transcendentals=0)
-    payload = pl.pallas_call(
-        functools.partial(pack_kernel, z),
-        out_shape=jax.ShapeDtypeStruct((2 * z.prefix_len + TAIL, z.width), BF16),
-        in_specs=[ANYWHERE] * 3,
-        out_specs=ANYWHERE,
-        scratch_shapes=[
-            pltpu.SMEM(rewards.shape, F32),
-            pltpu.SMEM(resp_prompt.shape, jnp.int32),
-            pltpu.VMEM((2 * z.prefix_len + TAIL, z.width), BF16),
-            pltpu.SemaphoreType.DMA((4,)),
-        ],
-        compiler_params=pltpu.CompilerParams(vmem_limit_bytes=VMEM_BYTES),
-        name="pack",
-    )(prompt_kv, rewards, resp_prompt)
-
     assert n_dp == FAR + 1
 
     def swap(x, s):
         return lax.ppermute(x, "dp", [(i, i ^ s) for i in range(n_dp)])
 
-    payloads = {0: payload, 2: swap(payload, 2), 1: swap(payload, 1)}
-    tails = [payloads[s] for s in range(FAR)]
-    small = (resp_prompt, resp_len, rewards)
-    far_rewards = swap(rewards, FAR)
-    smem = [pltpu.SMEM(x.shape, x.dtype) for x in (*small, rewards)]
+    prompts = {0: prompt_kv, 2: swap(prompt_kv, 2), 1: swap(prompt_kv, 1)}
+    others = [swap(rewards, s) for s in range(1, n_dp)]
+    small = (resp_prompt, resp_len)
+    smem = [pltpu.SMEM(x.shape, x.dtype) for x in (*small, rewards, *others)]
     slots = z.slots
-
     given = (resp_q, out_grad, resp_kv)
     n_ahead = 2 * slots * z.tokens
     in_order = pl.pallas_call(
@@ -491,14 +425,15 @@
         cost_estimate=cost,
         name="sort_rows",
     )(resp_prompt, *given)
-    onward, far_rewards, *in_order = lax.optimization_barrier((payloads[2], far_rewards, *in_order))
-    payloads[FAR] = swap(onward, 1)
+    onward, *barred = lax.optimization_barrier((prompts[2], *others, *in_order))
+    others, in_order = barred[: n_dp - 1], barred[n_dp - 1 :]
+    prompts[FAR] = swap(onward, 1)
 
     def grads_of(turns, ahead, written, come=(), kind=BF16):
         n_slots, n_turns = len(turns) * slots, len(turns)
         rows = () if ahead is None else in_order
-        prompts = [payloads[turn] for turn in turns]
-        operands = [*small, far_rewards, *given, *tails, *prompts, *come, *rows, *written]
+        used_prompts = [prompts[turn] for turn in turns]
+        operands = [*small, rewards, *others, *given, *used_prompts, *come, *rows, *written]
         return pl.pallas_call(
             functools.partial(group_kernel, z, turns, ahead, len(come), len(written)),
             out_shape=[shape(resp_q.shape, BF16), shape(resp_kv.shape, BF16)] + [shape(one, kind)] * n_turns,
@@ -514,15 +449,14 @@
                 pltpu.VMEM((n_slots * z.tokens, z.lanes), BF16),
                 pltpu.VMEM((2, n_slots * z.tokens, z.width), BF16),
                 pltpu.VMEM((n_turns,) + one, BF16),
-                pltpu.VMEM((FAR, TAIL, z.width), BF16),
                 pltpu.VMEM(one, BF16),
                 pltpu.VMEM((n_turns,) + one, F32),
                 pltpu.VMEM((n_slots, z.tokens, z.lanes), BF16),
                 pltpu.VMEM((n_slots, 2, z.tokens, z.width), BF16),
                 pltpu.VMEM((n_turns,) + one, kind),
                 pltpu.SemaphoreType.DMA((len(smem),)),
-                pltpu.SemaphoreType.DMA((FAR,)),
-                pltpu.SemaphoreType.DMA((n_turns, 2)),
+                pltpu.SemaphoreType.DMA((n_turns,)),
+                pltpu.SemaphoreType.DMA,
                 pltpu.SemaphoreType.DMA((n_slots, 3)),
                 pltpu.SemaphoreType.DMA((n_slots, 2)),
                 pltpu.SemaphoreType.DMA((n_turns,)),

time: 37.1 us -> 35.8 us (0.965)
  starting transfers between devices: 10.8 us -> 14.2 us
  waiting for transfers between devices: 3.72 us -> 0.59 us
  Pallas kernels: 21 us -> 19.4 us
    ppermute x7 -> x9, starting transfers between devices: 10.8 us -> 14.2 us  [swap(): return lax.ppermute(x, 'dp', [(i, i ^ s) for i in range(n_dp)])]
    ppermute x7 -> x9, waiting for transfers between devices: 3.72 us -> 0.59 us  [swap(): return lax.ppermute(x, 'dp', [(i, i ^ s) for i in range(n_dp)])]
    pallas_call x1 -> x0, Pallas kernels: 1.57 us -> none  [near_shards(): pl.pallas_call(functools.partial(pack_kernel, z), out_shape=jax.ShapeDtyp...]
  transfers between devices with their start and end apart: 7 -> 9, of which waited for: 4 -> 1; matrix products, arithmetic and copies ran while one was open for 0% -> 0% of each run, Pallas kernels for 53% -> 54%
where the time goes in v22:
time: 35.8 us; the launch traced here: 35.6 us
  Pallas kernels  19.4 us (54%)
  starting transfers between devices  14.2 us (40%)
  between operations  0.74 us (2%)
  other arithmetic  0.7 us (2%)
  waiting for transfers between devices  0.59 us (2%)
    pallas_call x3, Pallas kernels, grads_of(): pl.pallas_call(functools.partial(group_kernel, z, turns, ahead, len(come)...  15.5 us
    ppermute x9, starting transfers between devices, swap(): return lax.ppermute(x, 'dp', [(i, i ^ s) for i in range(n_dp)])  14.2 us
    pallas_call x1, Pallas kernels, near_shards(): pl.pallas_call(functools.partial(sort_kernel, z, (2, FAR)), out_shape=[sh...  3.92 us
  transfers between devices with their start and end apart: 9, of which 1 were waited for; matrix products, arithmetic and copies ran while one was open for 0% of the time, Pallas kernels for 54%

profile of v22, /device:TPU:0, one launch (start us, length us, event | category | flops | bytes accessed | tf_op | source)
XLA Modules:
  0.0 35.6 jit_solution(10427922760443909428)
XLA Ops:
  0.6 0.0 copy-start.3
  0.6 0.0 copy-start.1
  0.7 0.0 copy-start.2
  0.7 4.1 %collective-permute-start = (bf16[2,128,256]{2,1,0:T(8,128)(2,1)}, bf16[2,128,256]{2,1,0:T(8,128)(2,1)S(1)}, u32[]{:S(2)}, u32[]{:S(2)}) collective-permute-start(bf16[2,128,256]{2,1,0:T(8,128)(2,1)} %refs_9_.1), channel_id=1, source_target_pairs={{0,8},{4,12},{8,0},{12,4},{1,9},{5,13},{9,1},{13,5},{2,10},{6,14},... | collective-permute-start | bytes 393224 | tf_op jit(solution)/shard_map/ppermute | solution.py:400
  4.8 1.3 %collective-permute-start.3 = (f32[16]{0:T(128)}, f32[16]{0:T(128)S(1)}, u32[]{:S(2)}, u32[]{:S(2)}) collective-permute-start(f32[16]{0:T(128)} %refs_2_.5), channel_id=1, source_target_pairs={{0,12},{4,8},{8,4},{12,0},{1,13},{5,9},{9,5},{13,1},{2,14},{6,10},... | collective-permute-start | bytes 200 | tf_op jit(solution)/shard_map/ppermute | solution.py:400
  6.1 1.7 %collective-permute-start.2 = (f32[16]{0:T(128)}, f32[16]{0:T(128)S(1)}, u32[]{:S(2)}, u32[]{:S(2)}) collective-permute-start(f32[16]{0:T(128)} %refs_2_.5), channel_id=1, source_target_pairs={{0,8},{4,12},{8,0},{12,4},{1,9},{5,13},{9,1},{13,5},{2,10},{6,14},... | collective-permute-start | bytes 200 | tf_op jit(solution)/shard_map/ppermute | solution.py:400
  7.8 1.3 %collective-permute-start.1 = (f32[16]{0:T(128)}, f32[16]{0:T(128)S(1)}, u32[]{:S(2)}, u32[]{:S(2)}) collective-permute-start(f32[16]{0:T(128)} %refs_2_.5), channel_id=1, source_target_pairs={{0,4},{4,0},{8,12},{12,8},{1,5},{5,1},{9,13},{13,9},{2,6},{6,2},{1... | collective-permute-start | bytes 200 | tf_op jit(solution)/shard_map/ppermute | solution.py:400
  9.2 0.7 %collective-permute-start.6 = (bf16[2,128,256]{2,1,0:T(8,128)(2,1)}, bf16[2,128,256]{2,1,0:T(8,128)(2,1)S(1)}, u32[]{:S(2)}, u32[]{:S(2)}) collective-permute-start(bf16[2,128,256]{2,1,0:T(8,128)(2,1)} %refs_9_.1), channel_id=1, source_target_pairs={{0,4},{4,0},{8,12},{12,8},{1,5},{5,1},{9,13},{13,9},{2,6},{6,2},{1... | collective-permute-start | bytes 393224 | tf_op jit(solution)/shard_map/ppermute | solution.py:400
  9.8 3.9 %sort_rows.1 = (bf16[2,512,1280]{2,1,0:T(8,128)(2,1)}, bf16[2,512,256]{2,1,0:T(8,128)(2,1)}) custom-call(s32[64]{0:T(128)} %refs_0_.5, bf16[1024,1280]{1,0:T(8,128)(2,1)} %refs_6_.5, bf16[1024,1280]{1,0:T(8,128)(2,1)} %refs_7_.5, bf16[2,1024,256]{2,1,0:T(8,128)(2,1)} %refs_8_.5), custom_call_target="tpu_custom_call" | custom-call | tf_op jit(solution)/shard_map/sort_rows/pallas_call | solution.py:409
  13.8 0.0 collective-permute-done.3.refs_5_
  13.8 0.0 collective-permute-done.2.refs_4_
  13.8 0.0 collective-permute-done.1.refs_3_
  13.8 0.0 collective-permute-done.refs_9_
  13.8 1.4 %collective-permute-start.5 = (bf16[2,128,256]{2,1,0:T(8,128)(2,1)S(1)}, bf16[2,128,256]{2,1,0:T(8,128)(2,1)S(1)}, u32[]{:S(2)}, u32[]{:S(2)}) collective-permute-start(bf16[2,128,256]{2,1,0:T(8,128)(2,1)S(1)} %collective-permute-done.refs_9_), channel_id=1, source_target_pairs={{0,4},{4,0},{8,12},{12,8},{1,5},{5,1},{9,13},{13,9},{2,6},{6,2},{1... | collective-permute-start | bytes 393224 | tf_op jit(solution)/shard_map/ppermute | solution.py:400
  15.2 0.0 copy-done.3
  15.2 0.0 copy-done.1
  15.2 0.0 copy-done.2
  15.2 4.3 %group_grads.2 = (bf16[1024,1280]{1,0:T(8,128)(2,1)}, bf16[2,1024,256]{2,1,0:T(8,128)(2,1)}, bf16[2,128,256]{2,1,0:T(8,128)(2,1)S(1)}) custom-call(s32[64]{0:T(128)S(1)} %copy-done.1, s32[16]{0:T(128)S(1)} %copy-done.2, f32[16]{0:T(128)S(1)} %copy-done.3, f32[16]{0:T(128)S(1)} %collective-permute-done.1.refs_3_, f32[16]{0:T(128)S(1)} %collective-permute-done.2.refs_4_, ...), custom_call_target="tpu_custom_call" | custom-call | tf_op jit(solution)/shard_map/group_grads/pallas_call | solution.py:437
  19.5 0.4 %collective-permute-start.4 = (bf16[2,128,256]{2,1,0:T(8,128)(2,1)S(1)}, bf16[2,128,256]{2,1,0:T(8,128)(2,1)S(1)}, u32[]{:S(2)}, u32[]{:S(2)}) collective-permute-start(bf16[2,128,256]{2,1,0:T(8,128)(2,1)S(1)} %get-tuple-element.28), channel_id=1, source_target_pairs={{0,8},{4,12},{8,0},{12,4},{1,9},{5,13},{9,1},{13,5},{2,10},{6,14},... | collective-permute-start | bytes 393224 | tf_op jit(solution)/shard_map/ppermute | solution.py:400
  19.9 0.0 collective-permute-done.6.refs_10_
  19.9 0.0 collective-permute-done.5.refs_9_
  19.9 0.0 copy-start
  20.0 6.3 %group_grads.3 = (bf16[1024,1280]{1,0:T(8,128)(2,1)}, bf16[2,1024,256]{2,1,0:T(8,128)(2,1)}, bf16[2,128,256]{2,1,0:T(8,128)(2,1)S(1)}, bf16[2,128,256]{2,1,0:T(8,128)(2,1)S(1)}) custom-call(s32[64]{0:T(128)S(1)} %copy-done.1, s32[16]{0:T(128)S(1)} %copy-done.2, f32[16]{0:T(128)S(1)} %copy-done.3, ...), custom_call_target="tpu_custom_call", output_to_operand_aliasing={{0}: (13, {}), {1}: (14, {})} | custom-call | tf_op jit(solution)/shard_map/group_grads/pallas_call | solution.py:437
  26.2 2.7 %collective-permute-start.7 = (bf16[2,128,256]{2,1,0:T(8,128)(2,1)S(1)}, bf16[2,128,256]{2,1,0:T(8,128)(2,1)S(1)}, u32[]{:S(2)}, u32[]{:S(2)}) collective-permute-start(bf16[2,128,256]{2,1,0:T(8,128)(2,1)S(1)} %get-tuple-element.37), channel_id=1, source_target_pairs={{0,12},{4,8},{8,4},{12,0},{1,13},{5,9},{9,5},{13,1},{2,14},{6,10},... | collective-permute-start | bytes 393224 | tf_op jit(solution)/shard_map/ppermute | solution.py:400
  29.0 0.4 %collective-permute-start.8 = (bf16[2,128,256]{2,1,0:T(8,128)(2,1)S(1)}, bf16[2,128,256]{2,1,0:T(8,128)(2,1)S(1)}, u32[]{:S(2)}, u32[]{:S(2)}) collective-permute-start(bf16[2,128,256]{2,1,0:T(8,128)(2,1)S(1)} %get-tuple-element.38), channel_id=1, source_target_pairs={{0,4},{4,0},{8,12},{12,8},{1,5},{5,1},{9,13},{13,9},{2,6},{6,2},{1... | collective-permute-start | bytes 393224 | tf_op jit(solution)/shard_map/ppermute | solution.py:400
  29.4 0.0 collective-permute-done.4.refs_10_
  29.4 0.0 copy-done
  29.4 4.9 %own_grads.1 = (bf16[1024,1280]{1,0:T(8,128)(2,1)}, bf16[2,1024,256]{2,1,0:T(8,128)(2,1)}, f32[2,128,256]{2,1,0:T(8,128)S(1)}) custom-call(s32[64]{0:T(128)S(1)} %copy-done.1, s32[16]{0:T(128)S(1)} %copy-done.2, f32[16]{0:T(128)S(1)} %copy-done.3, f32[16]{0:T(128)S(1)} %collective-permute-done.1.refs_3_, ...), custom_call_target="tpu_custom_call", output_to_operand_aliasing={{0}: (11, {}), {1}: (12, {})} | custom-call | tf_op jit(solution)/shard_map/own_grads/pallas_call | solution.py:437
  34.3 0.0 collective-permute-done.7
  34.4 0.6 %collective-permute-done.8 = bf16[2,128,256]{2,1,0:T(8,128)(2,1)S(1)} collective-permute-done((bf16[2,128,256]{2,1,0:T(8,128)(2,1)S(1)}, bf16[2,128,256]{2,1,0:T(8,128)(2,1)S(1)}, u32[]{:S(2)}, u32[]{:S(2)}) %collective-permute-start.8) | collective-permute-done | bytes 131104 | tf_op jit(solution)/shard_map/ppermute | solution.py:400
  34.9 0.7 %add_convert_fusion = bf16[2,128,256]{2,1,0:T(8,128)(2,1)} fusion(f32[2,128,256]{2,1,0:T(8,128)S(1)} %get-tuple-element.36, bf16[2,128,256]{2,1,0:T(8,128)(2,1)S(1)} %collective-permute-done.8, bf16[2,128,256]{2,1,0:T(8,128)(2,1)S(1)} %collective-permute-done.7), kind=kLoop, calls=%fused_computation | loop fusion | flops 327680 | bytes 655360 | tf_op jit(solution)/shard_map/convert_element_type | solution.py:475
Async XLA Ops:
  0.6 14.6 %copy-start.3 = (f32[16]{0:T(128)S(1)}, f32[16]{0:T(128)}, u32[]{:S(2)}) copy-start(f32[16]{0:T(128)} %refs_2_.5) | copy-start | bytes 196
  0.6 14.6 %copy-start.1 = (s32[64]{0:T(128)S(1)}, s32[64]{0:T(128)}, u32[]{:S(2)}) copy-start(s32[64]{0:T(128)} %refs_0_.5) | copy-start | bytes 772
  0.7 14.6 %copy-start.2 = (s32[16]{0:T(128)S(1)}, s32[16]{0:T(128)}, u32[]{:S(2)}) copy-start(s32[16]{0:T(128)} %refs_1_.5) | copy-start | bytes 196
  0.7 13.1 %collective-permute-start = (bf16[2,128,256]{2,1,0:T(8,128)(2,1)}, bf16[2,128,256]{2,1,0:T(8,128)(2,1)S(1)}, u32[]{:S(2)}, u32[]{:S(2)}) collective-permute-start(bf16[2,128,256]{2,1,0:T(8,128)(2,1)} %refs_9_.1), channel_id=1, source_target_pairs={{0,8},{4,12},{8,0},{12,4},{1,9},{5,13},{9,1},{13,5},{2,10},{6,14},... | collective-permute-start | bytes 393224 | tf_op jit(solution)/shard_map/ppermute | solution.py:400
  4.8 9.0 %collective-permute-start.3 = (f32[16]{0:T(128)}, f32[16]{0:T(128)S(1)}, u32[]{:S(2)}, u32[]{:S(2)}) collective-permute-start(f32[16]{0:T(128)} %refs_2_.5), channel_id=1, source_target_pairs={{0,12},{4,8},{8,4},{12,0},{1,13},{5,9},{9,5},{13,1},{2,14},{6,10},... | collective-permute-start | bytes 200 | tf_op jit(solution)/shard_map/ppermute | solution.py:400
  6.1 7.7 %collective-permute-start.2 = (f32[16]{0:T(128)}, f32[16]{0:T(128)S(1)}, u32[]{:S(2)}, u32[]{:S(2)}) collective-permute-start(f32[16]{0:T(128)} %refs_2_.5), channel_id=1, source_target_pairs={{0,8},{4,12},{8,0},{12,4},{1,9},{5,13},{9,1},{13,5},{2,10},{6,14},... | collective-permute-start | bytes 200 | tf_op jit(solution)/shard_map/ppermute | solution.py:400
  7.8 6.0 %collective-permute-start.1 = (f32[16]{0:T(128)}, f32[16]{0:T(128)S(1)}, u32[]{:S(2)}, u32[]{:S(2)}) collective-permute-start(f32[16]{0:T(128)} %refs_2_.5), channel_id=1, source_target_pairs={{0,4},{4,0},{8,12},{12,8},{1,5},{5,1},{9,13},{13,9},{2,6},{6,2},{1... | collective-permute-start | bytes 200 | tf_op jit(solution)/shard_map/ppermute | solution.py:400
  9.2 10.8 %collective-permute-start.6 = (bf16[2,128,256]{2,1,0:T(8,128)(2,1)}, bf16[2,128,256]{2,1,0:T(8,128)(2,1)S(1)}, u32[]{:S(2)}, u32[]{:S(2)}) collective-permute-start(bf16[2,128,256]{2,1,0:T(8,128)(2,1)} %refs_9_.1), channel_id=1, source_target_pairs={{0,4},{4,0},{8,12},{12,8},{1,5},{5,1},{9,13},{13,9},{2,6},{6,2},{1... | collective-permute-start | bytes 393224 | tf_op jit(solution)/shard_map/ppermute | solution.py:400
  13.8 6.1 %collective-permute-start.5 = (bf16[2,128,256]{2,1,0:T(8,128)(2,1)S(1)}, bf16[2,128,256]{2,1,0:T(8,128)(2,1)S(1)}, u32[]{:S(2)}, u32[]{:S(2)}) collective-permute-start(bf16[2,128,256]{2,1,0:T(8,128)(2,1)S(1)} %collective-permute-done.refs_9_), channel_id=1, source_target_pairs={{0,4},{4,0},{8,12},{12,8},{1,5},{5,1},{9,13},{13,9},{2,6},{6,2},{1... | collective-permute-start | bytes 393224 | tf_op jit(solution)/shard_map/ppermute | solution.py:400
  19.5 9.9 %collective-permute-start.4 = (bf16[2,128,256]{2,1,0:T(8,128)(2,1)S(1)}, bf16[2,128,256]{2,1,0:T(8,128)(2,1)S(1)}, u32[]{:S(2)}, u32[]{:S(2)}) collective-permute-start(bf16[2,128,256]{2,1,0:T(8,128)(2,1)S(1)} %get-tuple-element.28), channel_id=1, source_target_pairs={{0,8},{4,12},{8,0},{12,4},{1,9},{5,13},{9,1},{13,5},{2,10},{6,14},... | collective-permute-start | bytes 393224 | tf_op jit(solution)/shard_map/ppermute | solution.py:400
  19.9 9.5 %copy-start = (bf16[2,128,256]{2,1,0:T(8,128)(2,1)S(1)}, bf16[2,128,256]{2,1,0:T(8,128)(2,1)}, u32[]{:S(2)}) copy-start(bf16[2,128,256]{2,1,0:T(8,128)(2,1)} %refs_9_.1) | copy-start | bytes 393220
  26.2 8.1 %collective-permute-start.7 = (bf16[2,128,256]{2,1,0:T(8,128)(2,1)S(1)}, bf16[2,128,256]{2,1,0:T(8,128)(2,1)S(1)}, u32[]{:S(2)}, u32[]{:S(2)}) collective-permute-start(bf16[2,128,256]{2,1,0:T(8,128)(2,1)S(1)} %get-tuple-element.37), channel_id=1, source_target_pairs={{0,12},{4,8},{8,4},{12,0},{1,13},{5,9},{9,5},{13,1},{2,14},{6,10},... | collective-permute-start | bytes 393224 | tf_op jit(solution)/shard_map/ppermute | solution.py:400
  29.0 6.0 %collective-permute-start.8 = (bf16[2,128,256]{2,1,0:T(8,128)(2,1)S(1)}, bf16[2,128,256]{2,1,0:T(8,128)(2,1)S(1)}, u32[]{:S(2)}, u32[]{:S(2)}) collective-permute-start(bf16[2,128,256]{2,1,0:T(8,128)(2,1)S(1)} %get-tuple-element.38), channel_id=1, source_target_pairs={{0,4},{4,0},{8,12},{12,8},{1,5},{5,1},{9,13},{13,9},{2,6},{6,2},{1... | collective-permute-start | bytes 393224 | tf_op jit(solution)/shard_map/ppermute | solution.py:400

commit v23 on v22

--- a/solution.py
+++ b/solution.py
@@ -216,10 +216,11 @@
 
 
 def prompt_total(z, me, prompt, resp_prompt, rewards):
+    own, near, two = rewards
     total = jnp.float32(0.0)
-    for s in range(z.n_dp):
+    for s, (held, start) in enumerate([(own, 0), (near, 0), (two, 0), (two, z.count)]):
         for i in range(z.count):
-            total += jnp.where(resp_prompt[(me ^ s) * z.count + i] == prompt, rewards[s][i], 0.0)
+            total += jnp.where(resp_prompt[(me ^ s) * z.count + i] == prompt, held[start + i], 0.0)
     return total
 
 
@@ -280,7 +281,7 @@
 
 
 def group_kernel(z, turns, ahead, n_come, aliased, *refs):
-    n_small = 2 + z.n_dp
+    n_small = 5
     small_hbm, given, refs = refs[:n_small], refs[n_small : n_small + 3], refs[n_small + 3 :]
     prompts, refs = refs[: len(turns)], refs[len(turns) :]
     come_hbm, refs = refs[:n_come], refs[n_come:]
@@ -400,7 +401,8 @@
         return lax.ppermute(x, "dp", [(i, i ^ s) for i in range(n_dp)])
 
     prompts = {0: prompt_kv, 2: swap(prompt_kv, 2), 1: swap(prompt_kv, 1)}
-    others = [swap(rewards, s) for s in range(1, n_dp)]
+    near_rewards = swap(rewards, 1)
+    others = [near_rewards, swap(jnp.concatenate([rewards, near_rewards]), 2)]
     small = (resp_prompt, resp_len)
     smem = [pltpu.SMEM(x.shape, x.dtype) for x in (*small, rewards, *others)]
     slots = z.slots
@@ -426,7 +428,7 @@
         name="sort_rows",
     )(resp_prompt, *given)
     onward, *barred = lax.optimization_barrier((prompts[2], *others, *in_order))
-    others, in_order = barred[: n_dp - 1], barred[n_dp - 1 :]
+    others, in_order = barred[: len(others)], barred[len(others) :]
     prompts[FAR] = swap(onward, 1)
 
     def grads_of(turns, ahead, written, come=(), kind=BF16):

time: 35.8 us -> 38.3 us (1.070)
  waiting for transfers between devices: 0.59 us -> 3.64 us
  starting transfers between devices: 14.2 us -> 13 us
  other arithmetic: 0.7 us -> 1.44 us
    ppermute x9 -> x8, waiting for transfers between devices: 0.59 us -> 3.64 us  [swap(): return lax.ppermute(x, 'dp', [(i, i ^ s) for i in range(n_dp)])]
    ppermute x9 -> x8, starting transfers between devices: 14.2 us -> 13 us  [swap(): return lax.ppermute(x, 'dp', [(i, i ^ s) for i in range(n_dp)])]
    concatenate x0 -> x1, other arithmetic: none -> 0.73 us  [near_shards(): others = [near_rewards, swap(jnp.concatenate([rewards, near_rewards]), 2)]]
  transfers between devices with their start and end apart: 9 -> 8, of which waited for: 1 -> 3; matrix products, arithmetic and copies ran while one was open for 0% -> 2% of each run, Pallas kernels for 54% -> 51%
where the time goes in v23:
time: 38.3 us; the launch traced here: 38.1 us
  Pallas kernels  19.3 us (50%)
  starting transfers between devices  13 us (34%)
  waiting for transfers between devices  3.64 us (10%)
  other arithmetic  1.44 us (4%)
  between operations  0.69 us (2%)
    pallas_call x3, Pallas kernels, grads_of(): pl.pallas_call(functools.partial(group_kernel, z, turns, ahead, len(come)...  15.4 us
    ppermute x8, starting transfers between devices, swap(): return lax.ppermute(x, 'dp', [(i, i ^ s) for i in range(n_dp)])  13 us
    pallas_call x1, Pallas kernels, near_shards(): pl.pallas_call(functools.partial(sort_kernel, z, (2, FAR)), out_shape=[sh...  3.9 us
    ppermute x8, waiting for transfers between devices, swap(): return lax.ppermute(x, 'dp', [(i, i ^ s) for i in range(n_dp)])  3.64 us
  transfers between devices with their start and end apart: 8, of which 3 were waited for; matrix products, arithmetic and copies ran while one was open for 2% of the time, Pallas kernels for 51%

profile of v23, /device:TPU:0, one launch (start us, length us, event | category | flops | bytes accessed | tf_op | source)
XLA Modules:
  0.0 38.1 jit_solution(214062776040166761)
XLA Ops:
  0.6 4.1 %collective-permute-start = (bf16[2,128,256]{2,1,0:T(8,128)(2,1)}, bf16[2,128,256]{2,1,0:T(8,128)(2,1)S(1)}, u32[]{:S(2)}, u32[]{:S(2)}) collective-permute-start(bf16[2,128,256]{2,1,0:T(8,128)(2,1)} %refs_8_.1), channel_id=1, source_target_pairs={{0,8},{4,12},{8,0},{12,4},{1,9},{5,13},{9,1},{13,5},{2,10},{6,14},... | collective-permute-start | bytes 393224 | tf_op jit(solution)/shard_map/ppermute | solution.py:401
  4.7 1.6 %collective-permute-start.1 = (f32[16]{0:T(128)}, f32[16]{0:T(128)S(1)}, u32[]{:S(2)}, u32[]{:S(2)}) collective-permute-start(f32[16]{0:T(128)} %refs_2_.5), channel_id=1, source_target_pairs={{0,4},{4,0},{8,12},{12,8},{1,5},{5,1},{9,13},{13,9},{2,6},{6,2},{1... | collective-permute-start | bytes 200 | tf_op jit(solution)/shard_map/ppermute | solution.py:401
  6.3 0.4 %collective-permute-start.5 = (bf16[2,128,256]{2,1,0:T(8,128)(2,1)}, bf16[2,128,256]{2,1,0:T(8,128)(2,1)S(1)}, u32[]{:S(2)}, u32[]{:S(2)}) collective-permute-start(bf16[2,128,256]{2,1,0:T(8,128)(2,1)} %refs_8_.1), channel_id=1, source_target_pairs={{0,4},{4,0},{8,12},{12,8},{1,5},{5,1},{9,13},{13,9},{2,6},{6,2},{1... | collective-permute-start | bytes 393224 | tf_op jit(solution)/shard_map/ppermute | solution.py:401
  6.8 2.2 %collective-permute-done.1.refs_3_ = f32[16]{0:T(128)S(1)} collective-permute-done((f32[16]{0:T(128)}, f32[16]{0:T(128)S(1)}, u32[]{:S(2)}, u32[]{:S(2)}) %collective-permute-start.1) | collective-permute-done | bytes 96 | tf_op jit(solution)/shard_map/ppermute | solution.py:401
  9.0 0.7 %pad_maximum_fusion = f32[32]{0:T(128)S(1)} fusion(f32[16]{0:T(128)S(1)} %collective-permute-done.1.refs_3_, f32[16]{0:T(128)} %refs_2_.5), kind=kLoop, calls=%fused_computation.1 | loop fusion | flops 32 | bytes 256 | tf_op jit(solution)/shard_map/concatenate | solution.py:405
  9.7 0.0 copy-start.1
  9.7 0.0 copy-start.2
  9.7 0.0 copy-start.3
  9.7 2.3 %collective-permute-start.2 = (f32[32]{0:T(128)S(1)}, f32[32]{0:T(128)S(1)}, u32[]{:S(2)}, u32[]{:S(2)}) collective-permute-start(f32[32]{0:T(128)S(1)} %pad_maximum_fusion), channel_id=1, source_target_pairs={{0,8},{4,12},{8,0},{12,4},{1,9},{5,13},{9,1},{13,5},{2,10},{6,14},... | collective-permute-start | bytes 392 | tf_op jit(solution)/shard_map/ppermute | solution.py:401
  12.0 3.9 %sort_rows.1 = (bf16[2,512,1280]{2,1,0:T(8,128)(2,1)}, bf16[2,512,256]{2,1,0:T(8,128)(2,1)}) custom-call(s32[64]{0:T(128)} %refs_0_.5, bf16[1024,1280]{1,0:T(8,128)(2,1)} %refs_5_.5, bf16[1024,1280]{1,0:T(8,128)(2,1)} %refs_6_.5, bf16[2,1024,256]{2,1,0:T(8,128)(2,1)} %refs_7_.5), custom_call_target="tpu_custom_call" | custom-call | tf_op jit(solution)/shard_map/sort_rows/pallas_call | solution.py:411
  15.9 0.0 collective-permute-done.2.refs_4_
  15.9 0.0 collective-permute-done.refs_8_
  15.9 0.6 %collective-permute-start.4 = (bf16[2,128,256]{2,1,0:T(8,128)(2,1)S(1)}, bf16[2,128,256]{2,1,0:T(8,128)(2,1)S(1)}, u32[]{:S(2)}, u32[]{:S(2)}) collective-permute-start(bf16[2,128,256]{2,1,0:T(8,128)(2,1)S(1)} %collective-permute-done.refs_8_), channel_id=1, source_target_pairs={{0,4},{4,0},{8,12},{12,8},{1,5},{5,1},{9,13},{13,9},{2,6},{6,2},{1... | collective-permute-start | bytes 393224 | tf_op jit(solution)/shard_map/ppermute | solution.py:401
  16.5 0.0 copy-done.1
  16.5 0.0 copy-done.2
  16.5 0.0 copy-done.3
  16.5 4.3 %group_grads.2 = (bf16[1024,1280]{1,0:T(8,128)(2,1)}, bf16[2,1024,256]{2,1,0:T(8,128)(2,1)}, bf16[2,128,256]{2,1,0:T(8,128)(2,1)S(1)}) custom-call(s32[64]{0:T(128)S(1)} %copy-done.1, s32[16]{0:T(128)S(1)} %copy-done.2, f32[16]{0:T(128)S(1)} %copy-done.3, f32[16]{0:T(128)S(1)} %collective-permute-done.1.refs_3_, f32[32]{0:T(128)S(1)} %collective-permute-done.2.refs_4_, ...), custom_call_target="tpu_custom_call" | custom-call | tf_op jit(solution)/shard_map/group_grads/pallas_call | solution.py:439
  20.8 2.5 %collective-permute-start.3 = (bf16[2,128,256]{2,1,0:T(8,128)(2,1)S(1)}, bf16[2,128,256]{2,1,0:T(8,128)(2,1)S(1)}, u32[]{:S(2)}, u32[]{:S(2)}) collective-permute-start(bf16[2,128,256]{2,1,0:T(8,128)(2,1)S(1)} %get-tuple-element.26), channel_id=1, source_target_pairs={{0,8},{4,12},{8,0},{12,4},{1,9},{5,13},{9,1},{13,5},{2,10},{6,14},... | collective-permute-start | bytes 393224 | tf_op jit(solution)/shard_map/ppermute | solution.py:401
  23.3 0.0 collective-permute-done.5.refs_9_
  23.4 0.0 collective-permute-done.4.refs_8_
  23.4 0.0 copy-start
  23.4 6.3 %group_grads.3 = (bf16[1024,1280]{1,0:T(8,128)(2,1)}, bf16[2,1024,256]{2,1,0:T(8,128)(2,1)}, bf16[2,128,256]{2,1,0:T(8,128)(2,1)S(1)}, bf16[2,128,256]{2,1,0:T(8,128)(2,1)S(1)}) custom-call(s32[64]{0:T(128)S(1)} %copy-done.1, s32[16]{0:T(128)S(1)} %copy-done.2, f32[16]{0:T(128)S(1)} %copy-done.3, ...), custom_call_target="tpu_custom_call", output_to_operand_aliasing={{0}: (12, {}), {1}: (13, {})} | custom-call | tf_op jit(solution)/shard_map/group_grads/pallas_call | solution.py:439
  29.6 1.4 %collective-permute-start.6 = (bf16[2,128,256]{2,1,0:T(8,128)(2,1)S(1)}, bf16[2,128,256]{2,1,0:T(8,128)(2,1)S(1)}, u32[]{:S(2)}, u32[]{:S(2)}) collective-permute-start(bf16[2,128,256]{2,1,0:T(8,128)(2,1)S(1)} %get-tuple-element.35), channel_id=1, source_target_pairs={{0,12},{4,8},{8,4},{12,0},{1,13},{5,9},{9,5},{13,1},{2,14},{6,10},... | collective-permute-start | bytes 393224 | tf_op jit(solution)/shard_map/ppermute | solution.py:401
  31.0 0.0 collective-permute-start.7
  31.0 0.0 collective-permute-done.3.refs_9_
  31.0 0.0 copy-done
  31.0 4.9 %own_grads.1 = (bf16[1024,1280]{1,0:T(8,128)(2,1)}, bf16[2,1024,256]{2,1,0:T(8,128)(2,1)}, f32[2,128,256]{2,1,0:T(8,128)S(1)}) custom-call(s32[64]{0:T(128)S(1)} %copy-done.1, s32[16]{0:T(128)S(1)} %copy-done.2, f32[16]{0:T(128)S(1)} %copy-done.3, f32[16]{0:T(128)S(1)} %collective-permute-done.1.refs_3_, ...), custom_call_target="tpu_custom_call", output_to_operand_aliasing={{0}: (10, {}), {1}: (11, {})} | custom-call | tf_op jit(solution)/shard_map/own_grads/pallas_call | solution.py:439
  36.0 0.6 %collective-permute-done.6 = bf16[2,128,256]{2,1,0:T(8,128)(2,1)S(1)} collective-permute-done((bf16[2,128,256]{2,1,0:T(8,128)(2,1)S(1)}, bf16[2,128,256]{2,1,0:T(8,128)(2,1)S(1)}, u32[]{:S(2)}, u32[]{:S(2)}) %collective-permute-start.6) | collective-permute-done | bytes 131104 | tf_op jit(solution)/shard_map/ppermute | solution.py:401
  36.6 0.8 %collective-permute-done.7 = bf16[2,128,256]{2,1,0:T(8,128)(2,1)S(1)} collective-permute-done((bf16[2,128,256]{2,1,0:T(8,128)(2,1)S(1)}, bf16[2,128,256]{2,1,0:T(8,128)(2,1)S(1)}, u32[]{:S(2)}, u32[]{:S(2)}) %collective-permute-start.7) | collective-permute-done | bytes 131104 | tf_op jit(solution)/shard_map/ppermute | solution.py:401
  37.4 0.7 %add_convert_fusion = bf16[2,128,256]{2,1,0:T(8,128)(2,1)} fusion(f32[2,128,256]{2,1,0:T(8,128)S(1)} %get-tuple-element.34, bf16[2,128,256]{2,1,0:T(8,128)(2,1)S(1)} %collective-permute-done.7, bf16[2,128,256]{2,1,0:T(8,128)(2,1)S(1)} %collective-permute-done.6), kind=kLoop, calls=%fused_computation | loop fusion | flops 327680 | bytes 655360 | tf_op jit(solution)/shard_map/convert_element_type | solution.py:477
Async XLA Ops:
  0.6 15.3 %collective-permute-start = (bf16[2,128,256]{2,1,0:T(8,128)(2,1)}, bf16[2,128,256]{2,1,0:T(8,128)(2,1)S(1)}, u32[]{:S(2)}, u32[]{:S(2)}) collective-permute-start(bf16[2,128,256]{2,1,0:T(8,128)(2,1)} %refs_8_.1), channel_id=1, source_target_pairs={{0,8},{4,12},{8,0},{12,4},{1,9},{5,13},{9,1},{13,5},{2,10},{6,14},... | collective-permute-start | bytes 393224 | tf_op jit(solution)/shard_map/ppermute | solution.py:401
  4.7 4.2 %collective-permute-start.1 = (f32[16]{0:T(128)}, f32[16]{0:T(128)S(1)}, u32[]{:S(2)}, u32[]{:S(2)}) collective-permute-start(f32[16]{0:T(128)} %refs_2_.5), channel_id=1, source_target_pairs={{0,4},{4,0},{8,12},{12,8},{1,5},{5,1},{9,13},{13,9},{2,6},{6,2},{1... | collective-permute-start | bytes 200 | tf_op jit(solution)/shard_map/ppermute | solution.py:401
  6.3 17.0 %collective-permute-start.5 = (bf16[2,128,256]{2,1,0:T(8,128)(2,1)}, bf16[2,128,256]{2,1,0:T(8,128)(2,1)S(1)}, u32[]{:S(2)}, u32[]{:S(2)}) collective-permute-start(bf16[2,128,256]{2,1,0:T(8,128)(2,1)} %refs_8_.1), channel_id=1, source_target_pairs={{0,4},{4,0},{8,12},{12,8},{1,5},{5,1},{9,13},{13,9},{2,6},{6,2},{1... | collective-permute-start | bytes 393224 | tf_op jit(solution)/shard_map/ppermute | solution.py:401
  9.7 6.9 %copy-start.1 = (s32[64]{0:T(128)S(1)}, s32[64]{0:T(128)}, u32[]{:S(2)}) copy-start(s32[64]{0:T(128)} %refs_0_.5) | copy-start | bytes 772
  9.7 6.9 %copy-start.2 = (s32[16]{0:T(128)S(1)}, s32[16]{0:T(128)}, u32[]{:S(2)}) copy-start(s32[16]{0:T(128)} %refs_1_.5) | copy-start | bytes 196
  9.7 6.9 %copy-start.3 = (f32[16]{0:T(128)S(1)}, f32[16]{0:T(128)}, u32[]{:S(2)}) copy-start(f32[16]{0:T(128)} %refs_2_.5) | copy-start | bytes 196
  9.7 6.2 %collective-permute-start.2 = (f32[32]{0:T(128)S(1)}, f32[32]{0:T(128)S(1)}, u32[]{:S(2)}, u32[]{:S(2)}) collective-permute-start(f32[32]{0:T(128)S(1)} %pad_maximum_fusion), channel_id=1, source_target_pairs={{0,8},{4,12},{8,0},{12,4},{1,9},{5,13},{9,1},{13,5},{2,10},{6,14},... | collective-permute-start | bytes 392 | tf_op jit(solution)/shard_map/ppermute | solution.py:401
  15.9 7.5 %collective-permute-start.4 = (bf16[2,128,256]{2,1,0:T(8,128)(2,1)S(1)}, bf16[2,128,256]{2,1,0:T(8,128)(2,1)S(1)}, u32[]{:S(2)}, u32[]{:S(2)}) collective-permute-start(bf16[2,128,256]{2,1,0:T(8,128)(2,1)S(1)} %collective-permute-done.refs_8_), channel_id=1, source_target_pairs={{0,4},{4,0},{8,12},{12,8},{1,5},{5,1},{9,13},{13,9},{2,6},{6,2},{1... | collective-permute-start | bytes 393224 | tf_op jit(solution)/shard_map/ppermute | solution.py:401
  20.8 10.2 %collective-permute-start.3 = (bf16[2,128,256]{2,1,0:T(8,128)(2,1)S(1)}, bf16[2,128,256]{2,1,0:T(8,128)(2,1)S(1)}, u32[]{:S(2)}, u32[]{:S(2)}) collective-permute-start(bf16[2,128,256]{2,1,0:T(8,128)(2,1)S(1)} %get-tuple-element.26), channel_id=1, source_target_pairs={{0,8},{4,12},{8,0},{12,4},{1,9},{5,13},{9,1},{13,5},{2,10},{6,14},... | collective-permute-start | bytes 393224 | tf_op jit(solution)/shard_map/ppermute | solution.py:401
  23.4 7.7 %copy-start = (bf16[2,128,256]{2,1,0:T(8,128)(2,1)S(1)}, bf16[2,128,256]{2,1,0:T(8,128)(2,1)}, u32[]{:S(2)}) copy-start(bf16[2,128,256]{2,1,0:T(8,128)(2,1)} %refs_8_.1) | copy-start | bytes 393220
  29.6 6.9 %collective-permute-start.6 = (bf16[2,128,256]{2,1,0:T(8,128)(2,1)S(1)}, bf16[2,128,256]{2,1,0:T(8,128)(2,1)S(1)}, u32[]{:S(2)}, u32[]{:S(2)}) collective-permute-start(bf16[2,128,256]{2,1,0:T(8,128)(2,1)S(1)} %get-tuple-element.35), channel_id=1, source_target_pairs={{0,12},{4,8},{8,4},{12,0},{1,13},{5,9},{9,5},{13,1},{2,14},{6,10},... | collective-permute-start | bytes 393224 | tf_op jit(solution)/shard_map/ppermute | solution.py:401
  31.0 6.4 %collective-permute-start.7 = (bf16[2,128,256]{2,1,0:T(8,128)(2,1)S(1)}, bf16[2,128,256]{2,1,0:T(8,128)(2,1)S(1)}, u32[]{:S(2)}, u32[]{:S(2)}) collective-permute-start(bf16[2,128,256]{2,1,0:T(8,128)(2,1)S(1)} %get-tuple-element.36), channel_id=1, source_target_pairs={{0,4},{4,0},{8,12},{12,8},{1,5},{5,1},{9,13},{13,9},{2,6},{6,2},{1... | collective-permute-start | bytes 393224 | tf_op jit(solution)/shard_map/ppermute | solution.py:401

commit v24 on v22

--- a/solution.py
+++ b/solution.py
@@ -17,6 +17,7 @@
 FAR = 3
 VMEM_BYTES = 63 * 1024 * 1024
 GROUP_BYTES = 54528 * 1024
+FIRST_BYTES = 54784 * 1024
 ANYWHERE = pl.BlockSpec(memory_space=pl.ANY)
 
 
@@ -279,18 +280,20 @@
             copy.wait()
 
 
-def group_kernel(z, turns, ahead, n_come, aliased, *refs):
+def group_kernel(z, turns, ahead, stage, n_come, aliased, *refs):
     n_small = 2 + z.n_dp
     small_hbm, given, refs = refs[:n_small], refs[n_small : n_small + 3], refs[n_small + 3 :]
     prompts, refs = refs[: len(turns)], refs[len(turns) :]
     come_hbm, refs = refs[:n_come], refs[n_come:]
-    if ahead is not None:
+    if ahead:
         (both, kv_ordered), refs = refs[:2], refs[2:]
     (q_out, self_out), refs = refs[aliased : aliased + 2], refs[aliased + 2 :]
     grads_out, refs = refs[: len(turns)], refs[len(turns) :]
+    if stage is not None:
+        (next_both, next_kv), refs = refs[:2], refs[2:]
     resp_prompt, resp_len, *rewards = refs[:n_small]
     (order, lens, factors, q, og, kv, prefix, come, acc, out, own, grads,
-     sem_small, sem_prefix, sem_come, sem_in, sem_out, sem_grads, sem_first) = refs[n_small:]
+     sem_small, sem_prefix, sem_come, sem_in, sem_out, sem_grads, sem_first, sem_stage) = refs[n_small:]
     me = lax.axis_index("dp")
     n_slots = len(turns) * z.slots
     span = z.slots * z.tokens
@@ -300,9 +303,9 @@
         for n, (src, dst) in enumerate(zip(small_hbm, (resp_prompt, resp_len, *rewards)))
     ]
     first_rows = ()
-    if ahead is not None:
+    if ahead:
         first_rows = row_copies(
-            (both.at[0], both.at[1], kv_ordered), (q, og, kv), pl.ds(ahead * span, span), pl.ds(0, span), sem_first
+            (both.at[0], both.at[1], kv_ordered), (q, og, kv), pl.ds(0, span), pl.ds(0, span), sem_first
         )
     prefix_copies = [
         pltpu.make_async_copy(prompts[t], prefix.at[t], sem_prefix.at[t]) for t in range(len(turns))
@@ -311,7 +314,8 @@
     for copy in [*small, *first_rows, *prefix_copies, *late]:
         copy.start()
     small[0].wait()
-    find_responses(z, me, turns, resp_prompt, order)
+    staged = range(n_slots, n_slots + (0 if stage is None else z.slots))
+    find_responses(z, me, [*turns, *([] if stage is None else [stage])], resp_prompt, order)
 
     def copies_in(slot):
         return row_copies(
@@ -321,7 +325,16 @@
     def copies_out(slot):
         return result_copies(out, own, q_out, self_out, slot, token_rows(z, order[slot]), sem_out)
 
-    for slot in range(0 if ahead is None else z.slots, n_slots):
+    def copies_staged(slot):
+        return row_copies(
+            (q, og, kv),
+            (next_both.at[0], next_both.at[1], next_kv),
+            token_rows(z, slot),
+            token_rows(z, slot - n_slots),
+            sem_stage.at[slot - n_slots],
+        )
+
+    for slot in [*range(z.slots if ahead else 0, n_slots), *staged]:
         for copy in copies_in(slot):
             copy.start()
     for copy in small[1:] + late:
@@ -347,7 +360,7 @@
                 for copy in copies_in(slot):
                     copy.wait()
 
-        if ahead is None:
+        if not ahead:
             wait_for_slots()
         else:
 
@@ -380,8 +393,16 @@
     last = [pltpu.make_async_copy(grads.at[t], grads_out[t], sem_grads.at[t]) for t in range(len(turns))]
     for copy in last:
         copy.start()
+    for slot in staged:
+        for copy in copies_in(slot):
+            copy.wait()
+        for copy in copies_staged(slot):
+            copy.start()
     for slot in range(n_slots):
         for copy in copies_out(slot):
+            copy.wait()
+    for slot in staged:
+        for copy in copies_staged(slot):
             copy.wait()
     for copy in last:
         copy.wait()
@@ -405,21 +426,21 @@
     smem = [pltpu.SMEM(x.shape, x.dtype) for x in (*small, rewards, *others)]
     slots = z.slots
     given = (resp_q, out_grad, resp_kv)
-    n_ahead = 2 * slots * z.tokens
+    n_ahead = slots * z.tokens
     in_order = pl.pallas_call(
-        functools.partial(sort_kernel, z, (2, FAR)),
+        functools.partial(sort_kernel, z, (2,)),
         out_shape=[shape((2, n_ahead, z.lanes), BF16), shape((2, n_ahead, z.width), BF16)],
         in_specs=[ANYWHERE] * 4,
         out_specs=[ANYWHERE] * 2,
         scratch_shapes=[
             smem[0],
-            pltpu.SMEM((2 * slots + 1,), jnp.int32),
+            pltpu.SMEM((slots + 1,), jnp.int32),
             pltpu.VMEM((n_ahead, z.lanes), BF16),
             pltpu.VMEM((n_ahead, z.lanes), BF16),
             pltpu.VMEM((2, n_ahead, z.width), BF16),
             pltpu.SemaphoreType.DMA,
-            pltpu.SemaphoreType.DMA((2 * slots, 3)),
-            pltpu.SemaphoreType.DMA((2 * slots, 3)),
+            pltpu.SemaphoreType.DMA((slots, 3)),
+            pltpu.SemaphoreType.DMA((slots, 3)),
         ],
         compiler_params=params,
         cost_estimate=cost,
@@ -429,25 +450,28 @@
     others, in_order = barred[: n_dp - 1], barred[n_dp - 1 :]
     prompts[FAR] = swap(onward, 1)
 
-    def grads_of(turns, ahead, written, come=(), kind=BF16):
+    def grads_of(turns, rows, stage, written, come=(), kind=BF16):
         n_slots, n_turns = len(turns) * slots, len(turns)
-        rows = () if ahead is None else in_order
+        n_held = n_slots + (0 if stage is None else slots)
+        next_shapes = [] if stage is None else [(2, n_ahead, z.lanes), (2, n_ahead, z.width)]
         used_prompts = [prompts[turn] for turn in turns]
         operands = [*small, rewards, *others, *given, *used_prompts, *come, *rows, *written]
         return pl.pallas_call(
-            functools.partial(group_kernel, z, turns, ahead, len(come), len(written)),
-            out_shape=[shape(resp_q.shape, BF16), shape(resp_kv.shape, BF16)] + [shape(one, kind)] * n_turns,
+            functools.partial(group_kernel, z, turns, bool(rows), stage, len(come), len(written)),
+            out_shape=[shape(resp_q.shape, BF16), shape(resp_kv.shape, BF16)]
+            + [shape(one, kind)] * n_turns
+            + [shape(x, BF16) for x in next_shapes],
             in_specs=[ANYWHERE] * len(operands),
-            out_specs=[ANYWHERE] * (2 + n_turns),
+            out_specs=[ANYWHERE] * (2 + n_turns + len(next_shapes)),
             input_output_aliases={len(operands) - 2: 0, len(operands) - 1: 1} if written else {},
             scratch_shapes=[
                 *smem,
-                pltpu.SMEM((n_slots + 1,), jnp.int32),
+                pltpu.SMEM((n_held + 1,), jnp.int32),
                 pltpu.SMEM((n_slots,), jnp.int32),
                 pltpu.SMEM((n_slots,), F32),
-                pltpu.VMEM((n_slots * z.tokens, z.lanes), BF16),
-                pltpu.VMEM((n_slots * z.tokens, z.lanes), BF16),
-                pltpu.VMEM((2, n_slots * z.tokens, z.width), BF16),
+                pltpu.VMEM((n_held * z.tokens, z.lanes), BF16),
+                pltpu.VMEM((n_held * z.tokens, z.lanes), BF16),
+                pltpu.VMEM((2, n_held * z.tokens, z.width), BF16),
                 pltpu.VMEM((n_turns,) + one, BF16),
                 pltpu.VMEM(one, BF16),
                 pltpu.VMEM((n_turns,) + one, F32),
@@ -457,21 +481,22 @@
                 pltpu.SemaphoreType.DMA((len(smem),)),
                 pltpu.SemaphoreType.DMA((n_turns,)),
                 pltpu.SemaphoreType.DMA,
-                pltpu.SemaphoreType.DMA((n_slots, 3)),
+                pltpu.SemaphoreType.DMA((n_held, 3)),
                 pltpu.SemaphoreType.DMA((n_slots, 2)),
                 pltpu.SemaphoreType.DMA((n_turns,)),
                 pltpu.SemaphoreType.DMA((3,)),
+                pltpu.SemaphoreType.DMA((slots, 3)),
             ],
-            compiler_params=pltpu.CompilerParams(vmem_limit_bytes=GROUP_BYTES),
+            compiler_params=pltpu.CompilerParams(vmem_limit_bytes=GROUP_BYTES if stage is None else FIRST_BYTES),
             cost_estimate=cost,
             name="group_grads" if turns[0] else "own_grads",
         )(*operands)
 
-    *written, for_2 = grads_of((2,), 0, ())
+    *written, for_2, next_both, next_kv = grads_of((2,), in_order, FAR, ())
     come = [swap(for_2, 2)]
-    *written, for_far, for_1 = grads_of((FAR, 1), 1, written)
+    *written, for_far, for_1 = grads_of((FAR, 1), (next_both, next_kv), None, written)
     last = [swap(for_far, FAR), swap(for_1, 1)]
-    q_out, self_out, summed = grads_of((0,), None, written, come, F32)
+    q_out, self_out, summed = grads_of((0,), (), None, written, come, F32)
     prefix_out = (summed + sum(part.astype(F32) for part in last)).astype(BF16)
     return (q_out, self_out, prefix_out)
 

time: 35.8 us -> 36.3 us (1.014)
  transfers between devices with their start and end apart: 9 -> 9, of which waited for: 1 -> 2; matrix products, arithmetic and copies ran while one was open for 0% -> 0% of each run, Pallas kernels for 54% -> 54%
where the time goes in v24:
time: 36.3 us; the launch traced here: 36.1 us
  Pallas kernels  19.6 us (54%)
  starting transfers between devices  14.2 us (39%)
  waiting for transfers between devices  0.86 us (2%)
  between operations  0.73 us (2%)
  other arithmetic  0.7 us (2%)
    pallas_call x3, Pallas kernels, grads_of(): pl.pallas_call(functools.partial(group_kernel, z, turns, bool(rows), stag...  16.4 us
    ppermute x9, starting transfers between devices, swap(): return lax.ppermute(x, 'dp', [(i, i ^ s) for i in range(n_dp)])  14.2 us
    pallas_call x1, Pallas kernels, near_shards(): pl.pallas_call(functools.partial(sort_kernel, z, (2,)), out_shape=[shape(...  3.18 us
    ppermute x9, waiting for transfers between devices, swap(): return lax.ppermute(x, 'dp', [(i, i ^ s) for i in range(n_dp)])  0.86 us
  transfers between devices with their start and end apart: 9, of which 2 were waited for; matrix products, arithmetic and copies ran while one was open for 0% of the time, Pallas kernels for 54%

profile of v24, /device:TPU:0, one launch (start us, length us, event | category | flops | bytes accessed | tf_op | source)
XLA Modules:
  0.0 36.1 jit_solution(13524441978563224518)
XLA Ops:
  0.6 0.0 copy-start.3
  0.6 0.0 copy-start.1
  0.7 0.0 copy-start.2
  0.7 4.1 %collective-permute-start = (bf16[2,128,256]{2,1,0:T(8,128)(2,1)}, bf16[2,128,256]{2,1,0:T(8,128)(2,1)S(1)}, u32[]{:S(2)}, u32[]{:S(2)}) collective-permute-start(bf16[2,128,256]{2,1,0:T(8,128)(2,1)} %refs_9_.1), channel_id=1, source_target_pairs={{0,8},{4,12},{8,0},{12,4},{1,9},{5,13},{9,1},{13,5},{2,10},{6,14},... | collective-permute-start | bytes 393224 | tf_op jit(solution)/shard_map/ppermute | solution.py:421
  4.8 1.3 %collective-permute-start.3 = (f32[16]{0:T(128)}, f32[16]{0:T(128)S(1)}, u32[]{:S(2)}, u32[]{:S(2)}) collective-permute-start(f32[16]{0:T(128)} %refs_2_.5), channel_id=1, source_target_pairs={{0,12},{4,8},{8,4},{12,0},{1,13},{5,9},{9,5},{13,1},{2,14},{6,10},... | collective-permute-start | bytes 200 | tf_op jit(solution)/shard_map/ppermute | solution.py:421
  6.1 1.7 %collective-permute-start.2 = (f32[16]{0:T(128)}, f32[16]{0:T(128)S(1)}, u32[]{:S(2)}, u32[]{:S(2)}) collective-permute-start(f32[16]{0:T(128)} %refs_2_.5), channel_id=1, source_target_pairs={{0,8},{4,12},{8,0},{12,4},{1,9},{5,13},{9,1},{13,5},{2,10},{6,14},... | collective-permute-start | bytes 200 | tf_op jit(solution)/shard_map/ppermute | solution.py:421
  7.8 1.3 %collective-permute-start.1 = (f32[16]{0:T(128)}, f32[16]{0:T(128)S(1)}, u32[]{:S(2)}, u32[]{:S(2)}) collective-permute-start(f32[16]{0:T(128)} %refs_2_.5), channel_id=1, source_target_pairs={{0,4},{4,0},{8,12},{12,8},{1,5},{5,1},{9,13},{13,9},{2,6},{6,2},{1... | collective-permute-start | bytes 200 | tf_op jit(solution)/shard_map/ppermute | solution.py:421
  9.2 0.7 %collective-permute-start.6 = (bf16[2,128,256]{2,1,0:T(8,128)(2,1)}, bf16[2,128,256]{2,1,0:T(8,128)(2,1)S(1)}, u32[]{:S(2)}, u32[]{:S(2)}) collective-permute-start(bf16[2,128,256]{2,1,0:T(8,128)(2,1)} %refs_9_.1), channel_id=1, source_target_pairs={{0,4},{4,0},{8,12},{12,8},{1,5},{5,1},{9,13},{13,9},{2,6},{6,2},{1... | collective-permute-start | bytes 393224 | tf_op jit(solution)/shard_map/ppermute | solution.py:421
  9.8 3.2 %sort_rows.1 = (bf16[2,256,1280]{2,1,0:T(8,128)(2,1)}, bf16[2,256,256]{2,1,0:T(8,128)(2,1)}) custom-call(s32[64]{0:T(128)} %refs_0_.5, bf16[1024,1280]{1,0:T(8,128)(2,1)} %refs_6_.5, bf16[1024,1280]{1,0:T(8,128)(2,1)} %refs_7_.5, bf16[2,1024,256]{2,1,0:T(8,128)(2,1)} %refs_8_.5), custom_call_target="tpu_custom_call" | custom-call | tf_op jit(solution)/shard_map/sort_rows/pallas_call | solution.py:430
  13.0 0.0 collective-permute-done.3.refs_5_
  13.0 0.0 collective-permute-done.2.refs_4_
  13.0 0.0 collective-permute-done.1.refs_3_
  13.0 0.0 collective-permute-done.refs_9_
  13.1 1.4 %collective-permute-start.5 = (bf16[2,128,256]{2,1,0:T(8,128)(2,1)S(1)}, bf16[2,128,256]{2,1,0:T(8,128)(2,1)S(1)}, u32[]{:S(2)}, u32[]{:S(2)}) collective-permute-start(bf16[2,128,256]{2,1,0:T(8,128)(2,1)S(1)} %collective-permute-done.refs_9_), channel_id=1, source_target_pairs={{0,4},{4,0},{8,12},{12,8},{1,5},{5,1},{9,13},{13,9},{2,6},{6,2},{1... | collective-permute-start | bytes 393224 | tf_op jit(solution)/shard_map/ppermute | solution.py:421
  14.5 0.0 copy-done.3
  14.5 0.0 copy-done.1
  14.5 0.0 copy-done.2
  14.5 5.0 %group_grads.2 = (bf16[1024,1280]{1,0:T(8,128)(2,1)}, bf16[2,1024,256]{2,1,0:T(8,128)(2,1)}, bf16[2,128,256]{2,1,0:T(8,128)(2,1)S(1)}, bf16[2,256,1280]{2,1,0:T(8,128)(2,1)}, bf16[2,256,256]{2,1,0:T(8,128)(2,1)}) custom-call(s32[64]{0:T(128)S(1)} %copy-done.1, s32[16]{0:T(128)S(1)} %copy-done.2, f32[16]{0:T(128)S(1)} %copy-done.3, ...), custom_call_target="tpu_custom_call" | custom-call | tf_op jit(solution)/shard_map/group_grads/pallas_call | solution.py:459
  19.5 1.2 %collective-permute-start.4 = (bf16[2,128,256]{2,1,0:T(8,128)(2,1)S(1)}, bf16[2,128,256]{2,1,0:T(8,128)(2,1)S(1)}, u32[]{:S(2)}, u32[]{:S(2)}) collective-permute-start(bf16[2,128,256]{2,1,0:T(8,128)(2,1)S(1)} %get-tuple-element.30), channel_id=1, source_target_pairs={{0,8},{4,12},{8,0},{12,4},{1,9},{5,13},{9,1},{13,5},{2,10},{6,14},... | collective-permute-start | bytes 393224 | tf_op jit(solution)/shard_map/ppermute | solution.py:421
  20.7 0.0 collective-permute-done.6.refs_10_
  20.7 0.0 collective-permute-done.5.refs_9_
  20.7 0.0 copy-start
  20.7 6.4 %group_grads.3 = (bf16[1024,1280]{1,0:T(8,128)(2,1)}, bf16[2,1024,256]{2,1,0:T(8,128)(2,1)}, bf16[2,128,256]{2,1,0:T(8,128)(2,1)S(1)}, bf16[2,128,256]{2,1,0:T(8,128)(2,1)S(1)}) custom-call(s32[64]{0:T(128)S(1)} %copy-done.1, s32[16]{0:T(128)S(1)} %copy-done.2, f32[16]{0:T(128)S(1)} %copy-done.3, ...), custom_call_target="tpu_custom_call", output_to_operand_aliasing={{0}: (13, {}), {1}: (14, {})} | custom-call | tf_op jit(solution)/shard_map/group_grads/pallas_call | solution.py:459
  27.0 2.0 %collective-permute-start.7 = (bf16[2,128,256]{2,1,0:T(8,128)(2,1)S(1)}, bf16[2,128,256]{2,1,0:T(8,128)(2,1)S(1)}, u32[]{:S(2)}, u32[]{:S(2)}) collective-permute-start(bf16[2,128,256]{2,1,0:T(8,128)(2,1)S(1)} %get-tuple-element.41), channel_id=1, source_target_pairs={{0,12},{4,8},{8,4},{12,0},{1,13},{5,9},{9,5},{13,1},{2,14},{6,10},... | collective-permute-start | bytes 393224 | tf_op jit(solution)/shard_map/ppermute | solution.py:421
  29.0 0.5 %collective-permute-start.8 = (bf16[2,128,256]{2,1,0:T(8,128)(2,1)S(1)}, bf16[2,128,256]{2,1,0:T(8,128)(2,1)S(1)}, u32[]{:S(2)}, u32[]{:S(2)}) collective-permute-start(bf16[2,128,256]{2,1,0:T(8,128)(2,1)S(1)} %get-tuple-element.42), channel_id=1, source_target_pairs={{0,4},{4,0},{8,12},{12,8},{1,5},{5,1},{9,13},{13,9},{2,6},{6,2},{1... | collective-permute-start | bytes 393224 | tf_op jit(solution)/shard_map/ppermute | solution.py:421
  29.5 0.0 collective-permute-done.4.refs_10_
  29.5 0.0 copy-done
  29.5 5.0 %own_grads.1 = (bf16[1024,1280]{1,0:T(8,128)(2,1)}, bf16[2,1024,256]{2,1,0:T(8,128)(2,1)}, f32[2,128,256]{2,1,0:T(8,128)S(1)}) custom-call(s32[64]{0:T(128)S(1)} %copy-done.1, s32[16]{0:T(128)S(1)} %copy-done.2, f32[16]{0:T(128)S(1)} %copy-done.3, f32[16]{0:T(128)S(1)} %collective-permute-done.1.refs_3_, ...), custom_call_target="tpu_custom_call", output_to_operand_aliasing={{0}: (11, {}), {1}: (12, {})} | custom-call | tf_op jit(solution)/shard_map/own_grads/pallas_call | solution.py:459
  34.5 0.6 %collective-permute-done.7 = bf16[2,128,256]{2,1,0:T(8,128)(2,1)S(1)} collective-permute-done((bf16[2,128,256]{2,1,0:T(8,128)(2,1)S(1)}, bf16[2,128,256]{2,1,0:T(8,128)(2,1)S(1)}, u32[]{:S(2)}, u32[]{:S(2)}) %collective-permute-start.7) | collective-permute-done | bytes 131104 | tf_op jit(solution)/shard_map/ppermute | solution.py:421
  35.2 0.2 collective-permute-done.8
  35.4 0.7 %add_convert_fusion = bf16[2,128,256]{2,1,0:T(8,128)(2,1)} fusion(f32[2,128,256]{2,1,0:T(8,128)S(1)} %get-tuple-element.40, bf16[2,128,256]{2,1,0:T(8,128)(2,1)S(1)} %collective-permute-done.8, bf16[2,128,256]{2,1,0:T(8,128)(2,1)S(1)} %collective-permute-done.7), kind=kLoop, calls=%fused_computation | loop fusion | flops 327680 | bytes 655360 | tf_op jit(solution)/shard_map/convert_element_type | solution.py:500
Async XLA Ops:
  0.6 13.8 %copy-start.3 = (f32[16]{0:T(128)S(1)}, f32[16]{0:T(128)}, u32[]{:S(2)}) copy-start(f32[16]{0:T(128)} %refs_2_.5) | copy-start | bytes 196
  0.6 13.8 %copy-start.1 = (s32[64]{0:T(128)S(1)}, s32[64]{0:T(128)}, u32[]{:S(2)}) copy-start(s32[64]{0:T(128)} %refs_0_.5) | copy-start | bytes 772
  0.7 13.8 %copy-start.2 = (s32[16]{0:T(128)S(1)}, s32[16]{0:T(128)}, u32[]{:S(2)}) copy-start(s32[16]{0:T(128)} %refs_1_.5) | copy-start | bytes 196
  0.7 12.4 %collective-permute-start = (bf16[2,128,256]{2,1,0:T(8,128)(2,1)}, bf16[2,128,256]{2,1,0:T(8,128)(2,1)S(1)}, u32[]{:S(2)}, u32[]{:S(2)}) collective-permute-start(bf16[2,128,256]{2,1,0:T(8,128)(2,1)} %refs_9_.1), channel_id=1, source_target_pairs={{0,8},{4,12},{8,0},{12,4},{1,9},{5,13},{9,1},{13,5},{2,10},{6,14},... | collective-permute-start | bytes 393224 | tf_op jit(solution)/shard_map/ppermute | solution.py:421
  4.8 8.3 %collective-permute-start.3 = (f32[16]{0:T(128)}, f32[16]{0:T(128)S(1)}, u32[]{:S(2)}, u32[]{:S(2)}) collective-permute-start(f32[16]{0:T(128)} %refs_2_.5), channel_id=1, source_target_pairs={{0,12},{4,8},{8,4},{12,0},{1,13},{5,9},{9,5},{13,1},{2,14},{6,10},... | collective-permute-start | bytes 200 | tf_op jit(solution)/shard_map/ppermute | solution.py:421
  6.1 6.9 %collective-permute-start.2 = (f32[16]{0:T(128)}, f32[16]{0:T(128)S(1)}, u32[]{:S(2)}, u32[]{:S(2)}) collective-permute-start(f32[16]{0:T(128)} %refs_2_.5), channel_id=1, source_target_pairs={{0,8},{4,12},{8,0},{12,4},{1,9},{5,13},{9,1},{13,5},{2,10},{6,14},... | collective-permute-start | bytes 200 | tf_op jit(solution)/shard_map/ppermute | solution.py:421
  7.8 5.2 %collective-permute-start.1 = (f32[16]{0:T(128)}, f32[16]{0:T(128)S(1)}, u32[]{:S(2)}, u32[]{:S(2)}) collective-permute-start(f32[16]{0:T(128)} %refs_2_.5), channel_id=1, source_target_pairs={{0,4},{4,0},{8,12},{12,8},{1,5},{5,1},{9,13},{13,9},{2,6},{6,2},{1... | collective-permute-start | bytes 200 | tf_op jit(solution)/shard_map/ppermute | solution.py:421
  9.2 11.5 %collective-permute-start.6 = (bf16[2,128,256]{2,1,0:T(8,128)(2,1)}, bf16[2,128,256]{2,1,0:T(8,128)(2,1)S(1)}, u32[]{:S(2)}, u32[]{:S(2)}) collective-permute-start(bf16[2,128,256]{2,1,0:T(8,128)(2,1)} %refs_9_.1), channel_id=1, source_target_pairs={{0,4},{4,0},{8,12},{12,8},{1,5},{5,1},{9,13},{13,9},{2,6},{6,2},{1... | collective-permute-start | bytes 393224 | tf_op jit(solution)/shard_map/ppermute | solution.py:421
  13.1 7.6 %collective-permute-start.5 = (bf16[2,128,256]{2,1,0:T(8,128)(2,1)S(1)}, bf16[2,128,256]{2,1,0:T(8,128)(2,1)S(1)}, u32[]{:S(2)}, u32[]{:S(2)}) collective-permute-start(bf16[2,128,256]{2,1,0:T(8,128)(2,1)S(1)} %collective-permute-done.refs_9_), channel_id=1, source_target_pairs={{0,4},{4,0},{8,12},{12,8},{1,5},{5,1},{9,13},{13,9},{2,6},{6,2},{1... | collective-permute-start | bytes 393224 | tf_op jit(solution)/shard_map/ppermute | solution.py:421
  19.5 10.0 %collective-permute-start.4 = (bf16[2,128,256]{2,1,0:T(8,128)(2,1)S(1)}, bf16[2,128,256]{2,1,0:T(8,128)(2,1)S(1)}, u32[]{:S(2)}, u32[]{:S(2)}) collective-permute-start(bf16[2,128,256]{2,1,0:T(8,128)(2,1)S(1)} %get-tuple-element.30), channel_id=1, source_target_pairs={{0,8},{4,12},{8,0},{12,4},{1,9},{5,13},{9,1},{13,5},{2,10},{6,14},... | collective-permute-start | bytes 393224 | tf_op jit(solution)/shard_map/ppermute | solution.py:421
  20.7 8.8 %copy-start = (bf16[2,128,256]{2,1,0:T(8,128)(2,1)S(1)}, bf16[2,128,256]{2,1,0:T(8,128)(2,1)}, u32[]{:S(2)}) copy-start(bf16[2,128,256]{2,1,0:T(8,128)(2,1)} %refs_9_.1) | copy-start | bytes 393220
  27.0 8.1 %collective-permute-start.7 = (bf16[2,128,256]{2,1,0:T(8,128)(2,1)S(1)}, bf16[2,128,256]{2,1,0:T(8,128)(2,1)S(1)}, u32[]{:S(2)}, u32[]{:S(2)}) collective-permute-start(bf16[2,128,256]{2,1,0:T(8,128)(2,1)S(1)} %get-tuple-element.41), channel_id=1, source_target_pairs={{0,12},{4,8},{8,4},{12,0},{1,13},{5,9},{9,5},{13,1},{2,14},{6,10},... | collective-permute-start | bytes 393224 | tf_op jit(solution)/shard_map/ppermute | solution.py:421
  29.0 6.3 %collective-permute-start.8 = (bf16[2,128,256]{2,1,0:T(8,128)(2,1)S(1)}, bf16[2,128,256]{2,1,0:T(8,128)(2,1)S(1)}, u32[]{:S(2)}, u32[]{:S(2)}) collective-permute-start(bf16[2,128,256]{2,1,0:T(8,128)(2,1)S(1)} %get-tuple-element.42), channel_id=1, source_target_pairs={{0,4},{4,0},{8,12},{12,8},{1,5},{5,1},{9,13},{13,9},{2,6},{6,2},{1... | collective-permute-start | bytes 393224 | tf_op jit(solution)/shard_map/ppermute | solution.py:421

commit v25 on v22

--- a/solution.py
+++ b/solution.py
@@ -470,7 +470,7 @@
     *written, for_2 = grads_of((2,), 0, ())
     come = [swap(for_2, 2)]
     *written, for_far, for_1 = grads_of((FAR, 1), 1, written)
-    last = [swap(for_far, FAR), swap(for_1, 1)]
+    last = [swap(for_1, 1), swap(for_far, FAR)]
     q_out, self_out, summed = grads_of((0,), None, written, come, F32)
     prefix_out = (summed + sum(part.astype(F32) for part in last)).astype(BF16)
     return (q_out, self_out, prefix_out)

time: 35.8 us -> 36.2 us (1.011)
  starting transfers between devices: 14.2 us -> 15.1 us
  waiting for transfers between devices: 0.59 us -> 0.02 us
    ppermute x9, starting transfers between devices: 14.2 us -> 15.1 us  [swap(): return lax.ppermute(x, 'dp', [(i, i ^ s) for i in range(n_dp)])]
    ppermute x9, waiting for transfers between devices: 0.59 us -> 0.02 us  [swap(): return lax.ppermute(x, 'dp', [(i, i ^ s) for i in range(n_dp)])]
  transfers between devices with their start and end apart: 9 -> 9, of which waited for: 1 -> 0; matrix products, arithmetic and copies ran while one was open for 0% -> 0% of each run, Pallas kernels for 54% -> 54%
where the time goes in v25:
time: 36.2 us; the launch traced here: 36 us
  Pallas kernels  19.4 us (54%)
  starting transfers between devices  15.1 us (42%)
  between operations  0.75 us (2%)
  other arithmetic  0.7 us (2%)
    pallas_call x3, Pallas kernels, grads_of(): pl.pallas_call(functools.partial(group_kernel, z, turns, ahead, len(come)...  15.5 us
    ppermute x9, starting transfers between devices, swap(): return lax.ppermute(x, 'dp', [(i, i ^ s) for i in range(n_dp)])  15.1 us
    pallas_call x1, Pallas kernels, near_shards(): pl.pallas_call(functools.partial(sort_kernel, z, (2, FAR)), out_shape=[sh...  3.92 us
  transfers between devices with their start and end apart: 9, of which 0 were waited for; matrix products, arithmetic and copies ran while one was open for 0% of the time, Pallas kernels for 54%

profile of v25, /device:TPU:0, one launch (start us, length us, event | category | flops | bytes accessed | tf_op | source)
XLA Modules:
  0.0 36.0 jit_solution(11502147642579269692)
XLA Ops:
  0.6 0.0 copy-start.3
  0.6 0.0 copy-start.1
  0.7 0.0 copy-start.2
  0.7 4.1 %collective-permute-start = (bf16[2,128,256]{2,1,0:T(8,128)(2,1)}, bf16[2,128,256]{2,1,0:T(8,128)(2,1)S(1)}, u32[]{:S(2)}, u32[]{:S(2)}) collective-permute-start(bf16[2,128,256]{2,1,0:T(8,128)(2,1)} %refs_9_.1), channel_id=1, source_target_pairs={{0,8},{4,12},{8,0},{12,4},{1,9},{5,13},{9,1},{13,5},{2,10},{6,14},... | collective-permute-start | bytes 393224 | tf_op jit(solution)/shard_map/ppermute | solution.py:400
  4.8 1.3 %collective-permute-start.3 = (f32[16]{0:T(128)}, f32[16]{0:T(128)S(1)}, u32[]{:S(2)}, u32[]{:S(2)}) collective-permute-start(f32[16]{0:T(128)} %refs_2_.5), channel_id=1, source_target_pairs={{0,12},{4,8},{8,4},{12,0},{1,13},{5,9},{9,5},{13,1},{2,14},{6,10},... | collective-permute-start | bytes 200 | tf_op jit(solution)/shard_map/ppermute | solution.py:400
  6.1 1.7 %collective-permute-start.2 = (f32[16]{0:T(128)}, f32[16]{0:T(128)S(1)}, u32[]{:S(2)}, u32[]{:S(2)}) collective-permute-start(f32[16]{0:T(128)} %refs_2_.5), channel_id=1, source_target_pairs={{0,8},{4,12},{8,0},{12,4},{1,9},{5,13},{9,1},{13,5},{2,10},{6,14},... | collective-permute-start | bytes 200 | tf_op jit(solution)/shard_map/ppermute | solution.py:400
  7.8 1.3 %collective-permute-start.1 = (f32[16]{0:T(128)}, f32[16]{0:T(128)S(1)}, u32[]{:S(2)}, u32[]{:S(2)}) collective-permute-start(f32[16]{0:T(128)} %refs_2_.5), channel_id=1, source_target_pairs={{0,4},{4,0},{8,12},{12,8},{1,5},{5,1},{9,13},{13,9},{2,6},{6,2},{1... | collective-permute-start | bytes 200 | tf_op jit(solution)/shard_map/ppermute | solution.py:400
  9.2 0.7 %collective-permute-start.6 = (bf16[2,128,256]{2,1,0:T(8,128)(2,1)}, bf16[2,128,256]{2,1,0:T(8,128)(2,1)S(1)}, u32[]{:S(2)}, u32[]{:S(2)}) collective-permute-start(bf16[2,128,256]{2,1,0:T(8,128)(2,1)} %refs_9_.1), channel_id=1, source_target_pairs={{0,4},{4,0},{8,12},{12,8},{1,5},{5,1},{9,13},{13,9},{2,6},{6,2},{1... | collective-permute-start | bytes 393224 | tf_op jit(solution)/shard_map/ppermute | solution.py:400
  9.8 3.9 %sort_rows.1 = (bf16[2,512,1280]{2,1,0:T(8,128)(2,1)}, bf16[2,512,256]{2,1,0:T(8,128)(2,1)}) custom-call(s32[64]{0:T(128)} %refs_0_.5, bf16[1024,1280]{1,0:T(8,128)(2,1)} %refs_6_.5, bf16[1024,1280]{1,0:T(8,128)(2,1)} %refs_7_.5, bf16[2,1024,256]{2,1,0:T(8,128)(2,1)} %refs_8_.5), custom_call_target="tpu_custom_call" | custom-call | tf_op jit(solution)/shard_map/sort_rows/pallas_call | solution.py:409
  13.8 0.0 collective-permute-done.3.refs_5_
  13.8 0.0 collective-permute-done.2.refs_4_
  13.8 0.0 collective-permute-done.1.refs_3_
  13.8 0.0 collective-permute-done.refs_9_
  13.8 1.4 %collective-permute-start.5 = (bf16[2,128,256]{2,1,0:T(8,128)(2,1)S(1)}, bf16[2,128,256]{2,1,0:T(8,128)(2,1)S(1)}, u32[]{:S(2)}, u32[]{:S(2)}) collective-permute-start(bf16[2,128,256]{2,1,0:T(8,128)(2,1)S(1)} %collective-permute-done.refs_9_), channel_id=1, source_target_pairs={{0,4},{4,0},{8,12},{12,8},{1,5},{5,1},{9,13},{13,9},{2,6},{6,2},{1... | collective-permute-start | bytes 393224 | tf_op jit(solution)/shard_map/ppermute | solution.py:400
  15.2 0.0 copy-done.3
  15.2 0.0 copy-done.1
  15.2 0.0 copy-done.2
  15.2 4.3 %group_grads.2 = (bf16[1024,1280]{1,0:T(8,128)(2,1)}, bf16[2,1024,256]{2,1,0:T(8,128)(2,1)}, bf16[2,128,256]{2,1,0:T(8,128)(2,1)S(1)}) custom-call(s32[64]{0:T(128)S(1)} %copy-done.1, s32[16]{0:T(128)S(1)} %copy-done.2, f32[16]{0:T(128)S(1)} %copy-done.3, f32[16]{0:T(128)S(1)} %collective-permute-done.1.refs_3_, f32[16]{0:T(128)S(1)} %collective-permute-done.2.refs_4_, ...), custom_call_target="tpu_custom_call" | custom-call | tf_op jit(solution)/shard_map/group_grads/pallas_call | solution.py:437
  19.5 0.4 %collective-permute-start.4 = (bf16[2,128,256]{2,1,0:T(8,128)(2,1)S(1)}, bf16[2,128,256]{2,1,0:T(8,128)(2,1)S(1)}, u32[]{:S(2)}, u32[]{:S(2)}) collective-permute-start(bf16[2,128,256]{2,1,0:T(8,128)(2,1)S(1)} %get-tuple-element.28), channel_id=1, source_target_pairs={{0,8},{4,12},{8,0},{12,4},{1,9},{5,13},{9,1},{13,5},{2,10},{6,14},... | collective-permute-start | bytes 393224 | tf_op jit(solution)/shard_map/ppermute | solution.py:400
  19.9 0.0 collective-permute-done.6.refs_10_
  19.9 0.0 collective-permute-done.5.refs_9_
  19.9 0.0 copy-start
  20.0 6.3 %group_grads.3 = (bf16[1024,1280]{1,0:T(8,128)(2,1)}, bf16[2,1024,256]{2,1,0:T(8,128)(2,1)}, bf16[2,128,256]{2,1,0:T(8,128)(2,1)S(1)}, bf16[2,128,256]{2,1,0:T(8,128)(2,1)S(1)}) custom-call(s32[64]{0:T(128)S(1)} %copy-done.1, s32[16]{0:T(128)S(1)} %copy-done.2, f32[16]{0:T(128)S(1)} %copy-done.3, ...), custom_call_target="tpu_custom_call", output_to_operand_aliasing={{0}: (13, {}), {1}: (14, {})} | custom-call | tf_op jit(solution)/shard_map/group_grads/pallas_call | solution.py:437
  26.2 1.6 %collective-permute-start.7 = (bf16[2,128,256]{2,1,0:T(8,128)(2,1)S(1)}, bf16[2,128,256]{2,1,0:T(8,128)(2,1)S(1)}, u32[]{:S(2)}, u32[]{:S(2)}) collective-permute-start(bf16[2,128,256]{2,1,0:T(8,128)(2,1)S(1)} %get-tuple-element.37), channel_id=1, source_target_pairs={{0,4},{4,0},{8,12},{12,8},{1,5},{5,1},{9,13},{13,9},{2,6},{6,2},{1... | collective-permute-start | bytes 393224 | tf_op jit(solution)/shard_map/ppermute | solution.py:400
  27.8 2.5 %collective-permute-start.8 = (bf16[2,128,256]{2,1,0:T(8,128)(2,1)S(1)}, bf16[2,128,256]{2,1,0:T(8,128)(2,1)S(1)}, u32[]{:S(2)}, u32[]{:S(2)}) collective-permute-start(bf16[2,128,256]{2,1,0:T(8,128)(2,1)S(1)} %get-tuple-element.38), channel_id=1, source_target_pairs={{0,12},{4,8},{8,4},{12,0},{1,13},{5,9},{9,5},{13,1},{2,14},{6,10},... | collective-permute-start | bytes 393224 | tf_op jit(solution)/shard_map/ppermute | solution.py:400
  30.3 0.0 collective-permute-done.4.refs_10_
  30.3 0.0 copy-done
  30.3 4.9 %own_grads.1 = (bf16[1024,1280]{1,0:T(8,128)(2,1)}, bf16[2,1024,256]{2,1,0:T(8,128)(2,1)}, f32[2,128,256]{2,1,0:T(8,128)S(1)}) custom-call(s32[64]{0:T(128)S(1)} %copy-done.1, s32[16]{0:T(128)S(1)} %copy-done.2, f32[16]{0:T(128)S(1)} %copy-done.3, f32[16]{0:T(128)S(1)} %collective-permute-done.1.refs_3_, ...), custom_call_target="tpu_custom_call", output_to_operand_aliasing={{0}: (11, {}), {1}: (12, {})} | custom-call | tf_op jit(solution)/shard_map/own_grads/pallas_call | solution.py:437
  35.2 0.0 collective-permute-done.7
  35.3 0.0 collective-permute-done.8
  35.3 0.7 %add_convert_fusion = bf16[2,128,256]{2,1,0:T(8,128)(2,1)} fusion(f32[2,128,256]{2,1,0:T(8,128)S(1)} %get-tuple-element.36, bf16[2,128,256]{2,1,0:T(8,128)(2,1)S(1)} %collective-permute-done.8, bf16[2,128,256]{2,1,0:T(8,128)(2,1)S(1)} %collective-permute-done.7), kind=kLoop, calls=%fused_computation | loop fusion | flops 327680 | bytes 655360 | tf_op jit(solution)/shard_map/convert_element_type | solution.py:475
Async XLA Ops:
  0.6 14.6 %copy-start.3 = (f32[16]{0:T(128)S(1)}, f32[16]{0:T(128)}, u32[]{:S(2)}) copy-start(f32[16]{0:T(128)} %refs_2_.5) | copy-start | bytes 196
  0.6 14.6 %copy-start.1 = (s32[64]{0:T(128)S(1)}, s32[64]{0:T(128)}, u32[]{:S(2)}) copy-start(s32[64]{0:T(128)} %refs_0_.5) | copy-start | bytes 772
  0.7 14.6 %copy-start.2 = (s32[16]{0:T(128)S(1)}, s32[16]{0:T(128)}, u32[]{:S(2)}) copy-start(s32[16]{0:T(128)} %refs_1_.5) | copy-start | bytes 196
  0.7 13.1 %collective-permute-start = (bf16[2,128,256]{2,1,0:T(8,128)(2,1)}, bf16[2,128,256]{2,1,0:T(8,128)(2,1)S(1)}, u32[]{:S(2)}, u32[]{:S(2)}) collective-permute-start(bf16[2,128,256]{2,1,0:T(8,128)(2,1)} %refs_9_.1), channel_id=1, source_target_pairs={{0,8},{4,12},{8,0},{12,4},{1,9},{5,13},{9,1},{13,5},{2,10},{6,14},... | collective-permute-start | bytes 393224 | tf_op jit(solution)/shard_map/ppermute | solution.py:400
  4.8 9.0 %collective-permute-start.3 = (f32[16]{0:T(128)}, f32[16]{0:T(128)S(1)}, u32[]{:S(2)}, u32[]{:S(2)}) collective-permute-start(f32[16]{0:T(128)} %refs_2_.5), channel_id=1, source_target_pairs={{0,12},{4,8},{8,4},{12,0},{1,13},{5,9},{9,5},{13,1},{2,14},{6,10},... | collective-permute-start | bytes 200 | tf_op jit(solution)/shard_map/ppermute | solution.py:400
  6.1 7.7 %collective-permute-start.2 = (f32[16]{0:T(128)}, f32[16]{0:T(128)S(1)}, u32[]{:S(2)}, u32[]{:S(2)}) collective-permute-start(f32[16]{0:T(128)} %refs_2_.5), channel_id=1, source_target_pairs={{0,8},{4,12},{8,0},{12,4},{1,9},{5,13},{9,1},{13,5},{2,10},{6,14},... | collective-permute-start | bytes 200 | tf_op jit(solution)/shard_map/ppermute | solution.py:400
  7.8 6.0 %collective-permute-start.1 = (f32[16]{0:T(128)}, f32[16]{0:T(128)S(1)}, u32[]{:S(2)}, u32[]{:S(2)}) collective-permute-start(f32[16]{0:T(128)} %refs_2_.5), channel_id=1, source_target_pairs={{0,4},{4,0},{8,12},{12,8},{1,5},{5,1},{9,13},{13,9},{2,6},{6,2},{1... | collective-permute-start | bytes 200 | tf_op jit(solution)/shard_map/ppermute | solution.py:400
  9.2 10.8 %collective-permute-start.6 = (bf16[2,128,256]{2,1,0:T(8,128)(2,1)}, bf16[2,128,256]{2,1,0:T(8,128)(2,1)S(1)}, u32[]{:S(2)}, u32[]{:S(2)}) collective-permute-start(bf16[2,128,256]{2,1,0:T(8,128)(2,1)} %refs_9_.1), channel_id=1, source_target_pairs={{0,4},{4,0},{8,12},{12,8},{1,5},{5,1},{9,13},{13,9},{2,6},{6,2},{1... | collective-permute-start | bytes 393224 | tf_op jit(solution)/shard_map/ppermute | solution.py:400
  13.8 6.1 %collective-permute-start.5 = (bf16[2,128,256]{2,1,0:T(8,128)(2,1)S(1)}, bf16[2,128,256]{2,1,0:T(8,128)(2,1)S(1)}, u32[]{:S(2)}, u32[]{:S(2)}) collective-permute-start(bf16[2,128,256]{2,1,0:T(8,128)(2,1)S(1)} %collective-permute-done.refs_9_), channel_id=1, source_target_pairs={{0,4},{4,0},{8,12},{12,8},{1,5},{5,1},{9,13},{13,9},{2,6},{6,2},{1... | collective-permute-start | bytes 393224 | tf_op jit(solution)/shard_map/ppermute | solution.py:400
  19.5 10.8 %collective-permute-start.4 = (bf16[2,128,256]{2,1,0:T(8,128)(2,1)S(1)}, bf16[2,128,256]{2,1,0:T(8,128)(2,1)S(1)}, u32[]{:S(2)}, u32[]{:S(2)}) collective-permute-start(bf16[2,128,256]{2,1,0:T(8,128)(2,1)S(1)} %get-tuple-element.28), channel_id=1, source_target_pairs={{0,8},{4,12},{8,0},{12,4},{1,9},{5,13},{9,1},{13,5},{2,10},{6,14},... | collective-permute-start | bytes 393224 | tf_op jit(solution)/shard_map/ppermute | solution.py:400
  19.9 10.4 %copy-start = (bf16[2,128,256]{2,1,0:T(8,128)(2,1)S(1)}, bf16[2,128,256]{2,1,0:T(8,128)(2,1)}, u32[]{:S(2)}) copy-start(bf16[2,128,256]{2,1,0:T(8,128)(2,1)} %refs_9_.1) | copy-start | bytes 393220
  26.2 9.0 %collective-permute-start.7 = (bf16[2,128,256]{2,1,0:T(8,128)(2,1)S(1)}, bf16[2,128,256]{2,1,0:T(8,128)(2,1)S(1)}, u32[]{:S(2)}, u32[]{:S(2)}) collective-permute-start(bf16[2,128,256]{2,1,0:T(8,128)(2,1)S(1)} %get-tuple-element.37), channel_id=1, source_target_pairs={{0,4},{4,0},{8,12},{12,8},{1,5},{5,1},{9,13},{13,9},{2,6},{6,2},{1... | collective-permute-start | bytes 393224 | tf_op jit(solution)/shard_map/ppermute | solution.py:400
  27.8 7.4 %collective-permute-start.8 = (bf16[2,128,256]{2,1,0:T(8,128)(2,1)S(1)}, bf16[2,128,256]{2,1,0:T(8,128)(2,1)S(1)}, u32[]{:S(2)}, u32[]{:S(2)}) collective-permute-start(bf16[2,128,256]{2,1,0:T(8,128)(2,1)S(1)} %get-tuple-element.38), channel_id=1, source_target_pairs={{0,12},{4,8},{8,4},{12,0},{1,13},{5,9},{9,5},{13,1},{2,14},{6,10},... | collective-permute-start | bytes 393224 | tf_op jit(solution)/shard_map/ppermute | solution.py:400

commit v26 on v22

--- a/solution.py
+++ b/solution.py
@@ -425,8 +425,8 @@
         cost_estimate=cost,
         name="sort_rows",
     )(resp_prompt, *given)
-    onward, *barred = lax.optimization_barrier((prompts[2], *others, *in_order))
-    others, in_order = barred[: n_dp - 1], barred[n_dp - 1 :]
+    onward, *barred = lax.optimization_barrier((prompts[2], *others[::-1], *in_order))
+    others, in_order = barred[: n_dp - 1][::-1], barred[n_dp - 1 :]
     prompts[FAR] = swap(onward, 1)
 
     def grads_of(turns, ahead, written, come=(), kind=BF16):

time: 35.8 us -> 35.8 us (level)
  no operation moved by 1% of the time
where the time goes in v26:
time: 35.8 us; the launch traced here: 35.6 us
  Pallas kernels  19.4 us (54%)
  starting transfers between devices  14.2 us (40%)
  between operations  0.74 us (2%)
  other arithmetic  0.7 us (2%)
  waiting for transfers between devices  0.58 us (2%)
    pallas_call x3, Pallas kernels, grads_of(): pl.pallas_call(functools.partial(group_kernel, z, turns, ahead, len(come)...  15.5 us
    ppermute x9, starting transfers between devices, swap(): return lax.ppermute(x, 'dp', [(i, i ^ s) for i in range(n_dp)])  14.2 us
    pallas_call x1, Pallas kernels, near_shards(): pl.pallas_call(functools.partial(sort_kernel, z, (2, FAR)), out_shape=[sh...  3.92 us
  transfers between devices with their start and end apart: 9, of which 1 were waited for; matrix products, arithmetic and copies ran while one was open for 0% of the time, Pallas kernels for 54%

profile of v26, /device:TPU:0, one launch (start us, length us, event | category | flops | bytes accessed | tf_op | source)
XLA Modules:
  0.0 35.6 jit_solution(1501468656470865664)
XLA Ops:
  0.6 0.0 copy-start.3
  0.6 0.0 copy-start.1
  0.7 0.0 copy-start.2
  0.7 4.1 %collective-permute-start = (bf16[2,128,256]{2,1,0:T(8,128)(2,1)}, bf16[2,128,256]{2,1,0:T(8,128)(2,1)S(1)}, u32[]{:S(2)}, u32[]{:S(2)}) collective-permute-start(bf16[2,128,256]{2,1,0:T(8,128)(2,1)} %refs_9_.1), channel_id=1, source_target_pairs={{0,8},{4,12},{8,0},{12,4},{1,9},{5,13},{9,1},{13,5},{2,10},{6,14},... | collective-permute-start | bytes 393224 | tf_op jit(solution)/shard_map/ppermute | solution.py:400
  4.8 1.6 %collective-permute-start.3 = (f32[16]{0:T(128)}, f32[16]{0:T(128)S(1)}, u32[]{:S(2)}, u32[]{:S(2)}) collective-permute-start(f32[16]{0:T(128)} %refs_2_.5), channel_id=1, source_target_pairs={{0,4},{4,0},{8,12},{12,8},{1,5},{5,1},{9,13},{13,9},{2,6},{6,2},{1... | collective-permute-start | bytes 200 | tf_op jit(solution)/shard_map/ppermute | solution.py:400
  6.3 0.3 collective-permute-start.2
  6.7 2.5 %collective-permute-start.1 = (f32[16]{0:T(128)}, f32[16]{0:T(128)S(1)}, u32[]{:S(2)}, u32[]{:S(2)}) collective-permute-start(f32[16]{0:T(128)} %refs_2_.5), channel_id=1, source_target_pairs={{0,12},{4,8},{8,4},{12,0},{1,13},{5,9},{9,5},{13,1},{2,14},{6,10},... | collective-permute-start | bytes 200 | tf_op jit(solution)/shard_map/ppermute | solution.py:400
  9.2 0.7 %collective-permute-start.6 = (bf16[2,128,256]{2,1,0:T(8,128)(2,1)}, bf16[2,128,256]{2,1,0:T(8,128)(2,1)S(1)}, u32[]{:S(2)}, u32[]{:S(2)}) collective-permute-start(bf16[2,128,256]{2,1,0:T(8,128)(2,1)} %refs_9_.1), channel_id=1, source_target_pairs={{0,4},{4,0},{8,12},{12,8},{1,5},{5,1},{9,13},{13,9},{2,6},{6,2},{1... | collective-permute-start | bytes 393224 | tf_op jit(solution)/shard_map/ppermute | solution.py:400
  9.8 3.9 %sort_rows.1 = (bf16[2,512,1280]{2,1,0:T(8,128)(2,1)}, bf16[2,512,256]{2,1,0:T(8,128)(2,1)}) custom-call(s32[64]{0:T(128)} %refs_0_.5, bf16[1024,1280]{1,0:T(8,128)(2,1)} %refs_6_.5, bf16[1024,1280]{1,0:T(8,128)(2,1)} %refs_7_.5, bf16[2,1024,256]{2,1,0:T(8,128)(2,1)} %refs_8_.5), custom_call_target="tpu_custom_call" | custom-call | tf_op jit(solution)/shard_map/sort_rows/pallas_call | solution.py:409
  13.8 0.0 collective-permute-done.3.refs_3_
  13.8 0.0 collective-permute-done.2.refs_4_
  13.8 0.0 collective-permute-done.1.refs_5_
  13.8 0.0 collective-permute-done.refs_9_
  13.8 1.4 %collective-permute-start.5 = (bf16[2,128,256]{2,1,0:T(8,128)(2,1)S(1)}, bf16[2,128,256]{2,1,0:T(8,128)(2,1)S(1)}, u32[]{:S(2)}, u32[]{:S(2)}) collective-permute-start(bf16[2,128,256]{2,1,0:T(8,128)(2,1)S(1)} %collective-permute-done.refs_9_), channel_id=1, source_target_pairs={{0,4},{4,0},{8,12},{12,8},{1,5},{5,1},{9,13},{13,9},{2,6},{6,2},{1... | collective-permute-start | bytes 393224 | tf_op jit(solution)/shard_map/ppermute | solution.py:400
  15.2 0.0 copy-done.3
  15.2 0.0 copy-done.1
  15.2 0.0 copy-done.2
  15.2 4.3 %group_grads.2 = (bf16[1024,1280]{1,0:T(8,128)(2,1)}, bf16[2,1024,256]{2,1,0:T(8,128)(2,1)}, bf16[2,128,256]{2,1,0:T(8,128)(2,1)S(1)}) custom-call(s32[64]{0:T(128)S(1)} %copy-done.1, s32[16]{0:T(128)S(1)} %copy-done.2, f32[16]{0:T(128)S(1)} %copy-done.3, f32[16]{0:T(128)S(1)} %collective-permute-done.3.refs_3_, f32[16]{0:T(128)S(1)} %collective-permute-done.2.refs_4_, ...), custom_call_target="tpu_custom_call" | custom-call | tf_op jit(solution)/shard_map/group_grads/pallas_call | solution.py:437
  19.5 0.4 %collective-permute-start.4 = (bf16[2,128,256]{2,1,0:T(8,128)(2,1)S(1)}, bf16[2,128,256]{2,1,0:T(8,128)(2,1)S(1)}, u32[]{:S(2)}, u32[]{:S(2)}) collective-permute-start(bf16[2,128,256]{2,1,0:T(8,128)(2,1)S(1)} %get-tuple-element.28), channel_id=1, source_target_pairs={{0,8},{4,12},{8,0},{12,4},{1,9},{5,13},{9,1},{13,5},{2,10},{6,14},... | collective-permute-start | bytes 393224 | tf_op jit(solution)/shard_map/ppermute | solution.py:400
  19.9 0.0 collective-permute-done.6.refs_10_
  19.9 0.0 collective-permute-done.5.refs_9_
  19.9 0.0 copy-start
  19.9 6.3 %group_grads.3 = (bf16[1024,1280]{1,0:T(8,128)(2,1)}, bf16[2,1024,256]{2,1,0:T(8,128)(2,1)}, bf16[2,128,256]{2,1,0:T(8,128)(2,1)S(1)}, bf16[2,128,256]{2,1,0:T(8,128)(2,1)S(1)}) custom-call(s32[64]{0:T(128)S(1)} %copy-done.1, s32[16]{0:T(128)S(1)} %copy-done.2, f32[16]{0:T(128)S(1)} %copy-done.3, ...), custom_call_target="tpu_custom_call", output_to_operand_aliasing={{0}: (13, {}), {1}: (14, {})} | custom-call | tf_op jit(solution)/shard_map/group_grads/pallas_call | solution.py:437
  26.2 2.7 %collective-permute-start.7 = (bf16[2,128,256]{2,1,0:T(8,128)(2,1)S(1)}, bf16[2,128,256]{2,1,0:T(8,128)(2,1)S(1)}, u32[]{:S(2)}, u32[]{:S(2)}) collective-permute-start(bf16[2,128,256]{2,1,0:T(8,128)(2,1)S(1)} %get-tuple-element.37), channel_id=1, source_target_pairs={{0,12},{4,8},{8,4},{12,0},{1,13},{5,9},{9,5},{13,1},{2,14},{6,10},... | collective-permute-start | bytes 393224 | tf_op jit(solution)/shard_map/ppermute | solution.py:400
  29.0 0.5 %collective-permute-start.8 = (bf16[2,128,256]{2,1,0:T(8,128)(2,1)S(1)}, bf16[2,128,256]{2,1,0:T(8,128)(2,1)S(1)}, u32[]{:S(2)}, u32[]{:S(2)}) collective-permute-start(bf16[2,128,256]{2,1,0:T(8,128)(2,1)S(1)} %get-tuple-element.38), channel_id=1, source_target_pairs={{0,4},{4,0},{8,12},{12,8},{1,5},{5,1},{9,13},{13,9},{2,6},{6,2},{1... | collective-permute-start | bytes 393224 | tf_op jit(solution)/shard_map/ppermute | solution.py:400
  29.4 0.0 collective-permute-done.4.refs_10_
  29.4 0.0 copy-done
  29.4 4.9 %own_grads.1 = (bf16[1024,1280]{1,0:T(8,128)(2,1)}, bf16[2,1024,256]{2,1,0:T(8,128)(2,1)}, f32[2,128,256]{2,1,0:T(8,128)S(1)}) custom-call(s32[64]{0:T(128)S(1)} %copy-done.1, s32[16]{0:T(128)S(1)} %copy-done.2, f32[16]{0:T(128)S(1)} %copy-done.3, f32[16]{0:T(128)S(1)} %collective-permute-done.3.refs_3_, ...), custom_call_target="tpu_custom_call", output_to_operand_aliasing={{0}: (11, {}), {1}: (12, {})} | custom-call | tf_op jit(solution)/shard_map/own_grads/pallas_call | solution.py:437
  34.4 0.0 collective-permute-done.7
  34.4 0.6 %collective-permute-done.8 = bf16[2,128,256]{2,1,0:T(8,128)(2,1)S(1)} collective-permute-done((bf16[2,128,256]{2,1,0:T(8,128)(2,1)S(1)}, bf16[2,128,256]{2,1,0:T(8,128)(2,1)S(1)}, u32[]{:S(2)}, u32[]{:S(2)}) %collective-permute-start.8) | collective-permute-done | bytes 131104 | tf_op jit(solution)/shard_map/ppermute | solution.py:400
  34.9 0.7 %add_convert_fusion = bf16[2,128,256]{2,1,0:T(8,128)(2,1)} fusion(f32[2,128,256]{2,1,0:T(8,128)S(1)} %get-tuple-element.36, bf16[2,128,256]{2,1,0:T(8,128)(2,1)S(1)} %collective-permute-done.8, bf16[2,128,256]{2,1,0:T(8,128)(2,1)S(1)} %collective-permute-done.7), kind=kLoop, calls=%fused_computation | loop fusion | flops 327680 | bytes 655360 | tf_op jit(solution)/shard_map/convert_element_type | solution.py:475
Async XLA Ops:
  0.6 14.6 %copy-start.3 = (f32[16]{0:T(128)S(1)}, f32[16]{0:T(128)}, u32[]{:S(2)}) copy-start(f32[16]{0:T(128)} %refs_2_.5) | copy-start | bytes 196
  0.6 14.6 %copy-start.1 = (s32[64]{0:T(128)S(1)}, s32[64]{0:T(128)}, u32[]{:S(2)}) copy-start(s32[64]{0:T(128)} %refs_0_.5) | copy-start | bytes 772
  0.7 14.6 %copy-start.2 = (s32[16]{0:T(128)S(1)}, s32[16]{0:T(128)}, u32[]{:S(2)}) copy-start(s32[16]{0:T(128)} %refs_1_.5) | copy-start | bytes 196
  0.7 13.1 %collective-permute-start = (bf16[2,128,256]{2,1,0:T(8,128)(2,1)}, bf16[2,128,256]{2,1,0:T(8,128)(2,1)S(1)}, u32[]{:S(2)}, u32[]{:S(2)}) collective-permute-start(bf16[2,128,256]{2,1,0:T(8,128)(2,1)} %refs_9_.1), channel_id=1, source_target_pairs={{0,8},{4,12},{8,0},{12,4},{1,9},{5,13},{9,1},{13,5},{2,10},{6,14},... | collective-permute-start | bytes 393224 | tf_op jit(solution)/shard_map/ppermute | solution.py:400
  4.8 9.0 %collective-permute-start.3 = (f32[16]{0:T(128)}, f32[16]{0:T(128)S(1)}, u32[]{:S(2)}, u32[]{:S(2)}) collective-permute-start(f32[16]{0:T(128)} %refs_2_.5), channel_id=1, source_target_pairs={{0,4},{4,0},{8,12},{12,8},{1,5},{5,1},{9,13},{13,9},{2,6},{6,2},{1... | collective-permute-start | bytes 200 | tf_op jit(solution)/shard_map/ppermute | solution.py:400
  6.3 7.4 %collective-permute-start.2 = (f32[16]{0:T(128)}, f32[16]{0:T(128)S(1)}, u32[]{:S(2)}, u32[]{:S(2)}) collective-permute-start(f32[16]{0:T(128)} %refs_2_.5), channel_id=1, source_target_pairs={{0,8},{4,12},{8,0},{12,4},{1,9},{5,13},{9,1},{13,5},{2,10},{6,14},... | collective-permute-start | bytes 200 | tf_op jit(solution)/shard_map/ppermute | solution.py:400
  6.7 7.1 %collective-permute-start.1 = (f32[16]{0:T(128)}, f32[16]{0:T(128)S(1)}, u32[]{:S(2)}, u32[]{:S(2)}) collective-permute-start(f32[16]{0:T(128)} %refs_2_.5), channel_id=1, source_target_pairs={{0,12},{4,8},{8,4},{12,0},{1,13},{5,9},{9,5},{13,1},{2,14},{6,10},... | collective-permute-start | bytes 200 | tf_op jit(solution)/shard_map/ppermute | solution.py:400
  9.2 10.8 %collective-permute-start.6 = (bf16[2,128,256]{2,1,0:T(8,128)(2,1)}, bf16[2,128,256]{2,1,0:T(8,128)(2,1)S(1)}, u32[]{:S(2)}, u32[]{:S(2)}) collective-permute-start(bf16[2,128,256]{2,1,0:T(8,128)(2,1)} %refs_9_.1), channel_id=1, source_target_pairs={{0,4},{4,0},{8,12},{12,8},{1,5},{5,1},{9,13},{13,9},{2,6},{6,2},{1... | collective-permute-start | bytes 393224 | tf_op jit(solution)/shard_map/ppermute | solution.py:400
  13.8 6.1 %collective-permute-start.5 = (bf16[2,128,256]{2,1,0:T(8,128)(2,1)S(1)}, bf16[2,128,256]{2,1,0:T(8,128)(2,1)S(1)}, u32[]{:S(2)}, u32[]{:S(2)}) collective-permute-start(bf16[2,128,256]{2,1,0:T(8,128)(2,1)S(1)} %collective-permute-done.refs_9_), channel_id=1, source_target_pairs={{0,4},{4,0},{8,12},{12,8},{1,5},{5,1},{9,13},{13,9},{2,6},{6,2},{1... | collective-permute-start | bytes 393224 | tf_op jit(solution)/shard_map/ppermute | solution.py:400
  19.5 9.9 %collective-permute-start.4 = (bf16[2,128,256]{2,1,0:T(8,128)(2,1)S(1)}, bf16[2,128,256]{2,1,0:T(8,128)(2,1)S(1)}, u32[]{:S(2)}, u32[]{:S(2)}) collective-permute-start(bf16[2,128,256]{2,1,0:T(8,128)(2,1)S(1)} %get-tuple-element.28), channel_id=1, source_target_pairs={{0,8},{4,12},{8,0},{12,4},{1,9},{5,13},{9,1},{13,5},{2,10},{6,14},... | collective-permute-start | bytes 393224 | tf_op jit(solution)/shard_map/ppermute | solution.py:400
  19.9 9.5 %copy-start = (bf16[2,128,256]{2,1,0:T(8,128)(2,1)S(1)}, bf16[2,128,256]{2,1,0:T(8,128)(2,1)}, u32[]{:S(2)}) copy-start(bf16[2,128,256]{2,1,0:T(8,128)(2,1)} %refs_9_.1) | copy-start | bytes 393220
  26.2 8.1 %collective-permute-start.7 = (bf16[2,128,256]{2,1,0:T(8,128)(2,1)S(1)}, bf16[2,128,256]{2,1,0:T(8,128)(2,1)S(1)}, u32[]{:S(2)}, u32[]{:S(2)}) collective-permute-start(bf16[2,128,256]{2,1,0:T(8,128)(2,1)S(1)} %get-tuple-element.37), channel_id=1, source_target_pairs={{0,12},{4,8},{8,4},{12,0},{1,13},{5,9},{9,5},{13,1},{2,14},{6,10},... | collective-permute-start | bytes 393224 | tf_op jit(solution)/shard_map/ppermute | solution.py:400
  29.0 6.0 %collective-permute-start.8 = (bf16[2,128,256]{2,1,0:T(8,128)(2,1)S(1)}, bf16[2,128,256]{2,1,0:T(8,128)(2,1)S(1)}, u32[]{:S(2)}, u32[]{:S(2)}) collective-permute-start(bf16[2,128,256]{2,1,0:T(8,128)(2,1)S(1)} %get-tuple-element.38), channel_id=1, source_target_pairs={{0,4},{4,0},{8,12},{12,8},{1,5},{5,1},{9,13},{13,9},{2,6},{6,2},{1... | collective-permute-start | bytes 393224 | tf_op jit(solution)/shard_map/ppermute | solution.py:400
